TPU v7x, 32 devices: a whole 2x2x4 slice. The times are simulated.
32 devices in a mesh: ctx: 4 (over y, x), head: 8 (over z, core).
Axes of the slice: x: 2, y: 2, z: 4, core: 2. Of those that a mesh axis runs over, the one named last changes fastest.
Arguments:
- tokens: bfloat16 [4096, 4096], P('ctx', 'head'), may hold values from -6 to 6
- doc_ids: int32 [4096], P('ctx'), may hold values from 0 to 7, never falling along the last dimension, each value on 1 to 2048 neighbouring positions
- w_feat: bfloat16 [4096, 1024], P(None, 'head'), may hold values from -0.09375 to 0.09375
- w_value: bfloat16 [4096, 4096], P(None, 'head'), may hold values from -0.09375 to 0.09375
- w_window: bfloat16 [4096, 8192], P(None, 'head'), may hold values from -4 to 4
- w_out: bfloat16 [4096, 4096], P('head'), may hold values from -0.09375 to 0.09375
Outputs:
- layer_out: bfloat16 [4096, 4096], P('ctx', 'head')
Inputs may be any that keep to these rules, and one draw needn't show every extreme that they name: `doc_ids`: document ids never fall along the sequence; each of the 8 documents has 1 to 2048 tokens, and one has exactly 2048.
All inputs are finite; a program needn't handle non-finite values.
Results may differ from a plain program's by a relative error of at most 0.019.
Values may be sent and summed in bfloat16 or wider, within the bound.
No kernel may reach another device: no remote copies, remote signals or barrier semaphores. Data moves between devices by JAX's collectives and lax.ppermute only.
A program may use at most 128 MiB of HBM per device.

v0:
```python
import jax
import jax.numpy as jnp
from jax import lax
from jax.sharding import PartitionSpec as P

HEAD_DIM = 128
FEAT = 16
WIN = 64


def shifted(x, axis, by):
    devices = lax.axis_size(axis)
    pairs = [(i, i + by) for i in range(devices) if 0 <= i + by < devices]
    return lax.ppermute(x, axis, pairs)


def feature_map(projected):
    widened = projected.astype(jnp.float32)
    products = widened[..., :, None] * widened[..., None, :]
    products = products.reshape(widened.shape[:-1] + (FEAT * FEAT,))
    constant_term = jnp.ones(widened.shape[:-1] + (1,), jnp.float32)
    return jnp.concatenate(
        [constant_term, widened * FEAT ** (-0.25), products * (2.0 * FEAT) ** (-0.5)], -1
    ).astype(jnp.bfloat16)


def shards(tokens, doc_ids, w_feat, w_value, w_window, w_out):
    tok_rows = tokens.shape[0]
    head_count = w_value.shape[1] // HEAD_DIM
    highest = lax.Precision.HIGHEST
    zero_sums = (
        jnp.zeros((tok_rows, w_feat.shape[1]), jnp.float32),
        jnp.zeros((tok_rows, w_value.shape[1]), jnp.float32),
        jnp.zeros((tok_rows, w_window.shape[1]), jnp.float32),
    )
    column_piece = lax.all_gather(tokens, "head", axis=1, tiled=True)
    updated = []
    for running, weight in zip(zero_sums, (w_feat, w_value, w_window)):
        updated.append(jnp.dot(column_piece, weight, preferred_element_type=jnp.float32))
    feat_sum, value_sum, window_sum = tuple(updated)
    features = feat_sum.astype(jnp.bfloat16).reshape(tok_rows, head_count, 2 * FEAT)
    phi_query = feature_map(features[..., :FEAT])
    phi_key = feature_map(features[..., FEAT:])
    values_here = value_sum.astype(jnp.bfloat16).reshape(tok_rows, head_count, HEAD_DIM)
    window_proj = window_sum.astype(jnp.bfloat16).reshape(tok_rows, head_count, 2, HEAD_DIM)
    win_query = window_proj[:, :, 0]
    win_key = window_proj[:, :, 1]
    doc_float = doc_ids.astype(jnp.float32)
    positions = jnp.arange(tok_rows)
    allowed = (
        (doc_float[:, None] == doc_float[None, :]) & (positions[:, None] >= positions[None, :])
    ).astype(jnp.float32)
    scores = (
        jnp.einsum("thp,shp->hts", phi_query, phi_key, preferred_element_type=jnp.float32)
        * allowed[None]
    ).astype(jnp.bfloat16)
    inner = jnp.einsum("hts,shd->thd", scores, values_here, preferred_element_type=jnp.float32)
    keeps = doc_float == doc_float[-1]
    kept_keys = jnp.where(keeps[:, None, None], phi_key, jnp.zeros_like(phi_key))
    local_state = jnp.einsum(
        "shp,shd->hpd", kept_keys, values_here, preferred_element_type=jnp.float32
    )
    last_here = doc_float[tok_rows - 1 :]
    empty_state = jnp.zeros_like(local_state)
    my_index = lax.axis_index("ctx")
    first_doc = doc_float[0]
    piece_states = lax.all_gather(
        local_state[None].astype(jnp.bfloat16), "ctx", axis=0, tiled=True
    ).astype(jnp.float32)
    piece_docs = lax.all_gather(last_here.astype(jnp.bfloat16), "ctx", axis=0, tiled=True).astype(
        jnp.float32
    )
    device_ids = jnp.arange(piece_docs.shape[0], dtype=jnp.int32)
    chosen = ((device_ids < my_index) & (piece_docs == first_doc)).astype(jnp.float32)
    incoming = empty_state + jnp.tensordot(chosen, piece_states, 1, precision=highest)
    uses = doc_float == first_doc
    carried = jnp.einsum("thp,hpd->thd", phi_query.astype(jnp.float32), incoming, precision=highest)
    linear_out = inner + jnp.where(uses[:, None, None], carried, jnp.zeros_like(carried))
    mean_square = jnp.mean(linear_out * linear_out, -1, keepdims=True)
    normed = linear_out * lax.rsqrt(mean_square + 1e-05)
    tail_key, tail_value, tail_doc = shifted(
        (
            win_key[tok_rows - WIN :],
            values_here[tok_rows - WIN :],
            (doc_float[tok_rows - WIN :] + 1.0).astype(jnp.bfloat16),
        ),
        "ctx",
        1,
    )
    keys_all = jnp.concatenate([tail_key, win_key], 0)
    values_cat = jnp.concatenate([tail_value, values_here], 0)
    docs_cat = jnp.concatenate([tail_doc.astype(jnp.float32) - 1.0, doc_float], 0)
    key_pos = jnp.arange(WIN + tok_rows)
    within = (
        (key_pos[None, :] > positions[:, None])
        & (key_pos[None, :] <= positions[:, None] + WIN)
        & (docs_cat[None, :] == doc_float[:, None])
    )
    logits = jnp.einsum(
        "thd,shd->hts", win_query, keys_all, preferred_element_type=jnp.float32
    ) * HEAD_DIM ** (-0.5)
    logits = jnp.where(within[None], logits, -1e30)
    top_logit = jnp.max(logits, -1, keepdims=True)
    weights = jnp.exp(logits - top_logit) * within[None].astype(jnp.float32)
    probs = (weights / jnp.sum(weights, -1, keepdims=True)).astype(jnp.bfloat16)
    window_out = jnp.einsum("hts,shd->thd", probs, values_cat, preferred_element_type=jnp.float32)
    mixed = (normed + window_out).astype(jnp.bfloat16).reshape(tok_rows, head_count * HEAD_DIM)
    summed = lax.psum_scatter(
        lax.dot_general(
            w_out, mixed, (((0,), (1,)), ((), ())), preferred_element_type=jnp.float32
        ).astype(jnp.bfloat16),
        "head",
        scatter_dimension=0,
        tiled=True,
    ).astype(jnp.float32)
    return summed.T.astype(jnp.bfloat16)


def solution(mesh):
    return jax.shard_map(
        shards,
        mesh=mesh,
        in_specs=(
            P("ctx", "head"),
            P("ctx"),
            P(None, "head"),
            P(None, "head"),
            P(None, "head"),
            P("head", None),
        ),
        out_specs=P("ctx", "head"),
        check_vma=False,
    )
```

profile of v0, /device:TPU:0, one launch (start us, length us, event | category | flops | bytes accessed | tf_op | source)
XLA Modules:
  0.0 280.4 jit_solution(6930500385219124066)
XLA Ops:
  6.5 0.7 all-gather.4.cloned.1.call-update
  7.3 0.7 convert_element_type.80
  8.0 0.6 slice.67
  8.6 1.2 dynamic-slice
  9.8 1.3 dynamic-update-slice
  11.2 4.8 %collective-permute-start.1 = (bf16[64]{0:T(256)(128)(2,1)S(1)}, bf16[64]{0:T(256)(128)(2,1)S(1)}, u32[]{:S(2)}, u32[]{:S(2)}) collective-permute-start(bf16[64]{0:T(256)(128)(2,1)S(1)} %add_convert_fusion), channel_id=1, source_target_pairs={{0,8},{8,16},{16,24},{1,9},{9,17},{17,25},{2,10},{10,18},{18,26},{... | collective-permute-start | bytes 392 | tf_op jit(solution)/shard_map/ppermute | solution.py:14
  16.1 9.0 %all-reduce = bf16[4]{0:T(256)(128)(2,1)S(1)} all-reduce(bf16[4]{0:T(256)(128)(2,1)S(1)} %dynamic-update-slice), channel_id=1, replica_groups=mesh['ctx'=4,'head'=8] {'ctx'}, use_global_device_ids=true, to_apply=%add | all-reduce | flops 4 | bytes 16
  25.0 0.6 fusion.48
  25.6 1.9 broadcast_compare_fusion
  27.5 2.6 fusion.7
  30.2 3.6 %fusion.5 = (pred[1024,1088]{0,1:T(8,128)(4,1)}, f32[1024,1088]{0,1:T(8,128)}) fusion(f32[1024]{0:T(1024)S(1)} %convert_element_type.80, s32[1024]{0:T(1024)S(1)} %iota_add_fusion, f32[1088]{0:T(1024)S(1)} %pad_maximum_fusion.12), kind=kLoop, calls=%fused_computation.12 | loop fusion | flops 6684672 | bytes 5583104 | tf_op jit(solution)/shard_map/and | solution.py:95
  33.8 60.0 %all-gather.4.cloned.1.call-done = bf16[1024,4096]{1,0:T(8,128)(2,1)} async-done(((bf16[1024,512]{1,0:T(8,128)(2,1)}), bf16[1024,4096]{1,0:T(8,128)(2,1)}) %all-gather.4.cloned.1.call-update) | async-done | bytes 8388624 | tf_op jit(solution)/shard_map/all_gather | solution.py:36
  93.8 6.4 %convolution_convert_fusion.2 = bf16[1024,128]{0,1:T(8,128)(2,1)S(1)} fusion(bf16[1024,4096]{1,0:T(8,128)(2,1)} %all-gather.4.cloned.1.call-done, bf16[4096,128]{1,0:T(8,128)(2,1)S(1)} %copy-done), kind=kOutput, calls=%fused_computation.33 | convolution fusion | flops 1073872896 | bytes 9699328 | tf_op jit(solution)/shard_map/dot_general | solution.py:39
  100.7 4.5 %convolution_convert_fusion.1 = bf16[1024,512]{1,0:T(8,128)(2,1)S(1)} fusion(bf16[1024,4096]{1,0:T(8,128)(2,1)S(1)} %copy-done.2, bf16[4096,512]{1,0:T(8,128)(2,1)S(1)} %copy-done.8), kind=kOutput, calls=%fused_computation.31 | convolution fusion | flops 4295491584 | bytes 13631488 | tf_op jit(solution)/shard_map/dot_general | solution.py:39
  105.2 1.4 copy_bitcast_fusion
  106.6 0.6 copy_bitcast_fusion.1
  107.8 1.3 copy-done.3
  109.1 1.7 fusion.14
  111.6 13.9 %convolution_convert_fusion = bf16[1024,1024]{0,1:T(8,128)(2,1)S(1)} fusion(bf16[1024,4096]{1,0:T(8,128)(2,1)} %all-gather.4.cloned.1.call-done, bf16[4096,1024]{1,0:T(8,128)(2,1)} %param.10), kind=kOutput, calls=%fused_computation.29 | convolution fusion | flops 8590983168 | bytes 18874368 | tf_op jit(solution)/shard_map/dot_general | solution.py:39
  125.5 1.4 copy-done.7
  127.0 0.7 copy.25
  127.8 3.9 %collective-permute-start.2 = (bf16[64,4,128]{2,0,1:T(8,128)(2,1)}, bf16[64,4,128]{2,0,1:T(8,128)(2,1)}, u32[]{:S(2)}, u32[]{:S(2)}) collective-permute-start(bf16[64,4,128]{2,0,1:T(8,128)(2,1)} %bitcast.82), channel_id=1, source_target_pairs={{0,8},{8,16},{16,24},{1,9},{9,17},{17,25},{2,10},{10,18},{18,26},{... | collective-permute-start | bytes 196616 | tf_op jit(solution)/shard_map/ppermute | solution.py:14
  131.7 2.8 collective-permute-start
  134.5 12.1 %fusion.13 = f32[4,128,1024]{2,1,0:T(8,128)} fusion(f32[1024,1024]{1,0:T(8,128)} %fusion.7, bf16[1024,4,256]{0,2,1:T(8,128)(2,1)} %bitcast.77, bf16[1024,4,16]{0,2,1:T(8,128)(2,1)S(1)} %get-tuple-element.6, bf16[1024,4,256]{0,2,1:T(8,128)(2,1)S(1)} %bitcast.74, bf16[1024,4,16]{0,2,1:T(8,128)(2,1)S(1)} %get-tuple-element.5, bf16[273]{0:T(512)(128)(2,1)S(1)} %pad.9.clone, ...), kind=kOutput, calls=%fused_computation.30 | convolution fusion | flops 3385638912 | bytes 11797026 | tf_op jit(solution)/shard_map/hts,shd->thd/dot_general | solution.py:57
  146.6 1.3 slice.50
  147.9 1.5 copy.26
  149.4 15.2 %fusion.49 = (f32[4,1024]{1,0:T(4,128)S(1)}, f32[4,1024,1088]{1,2,0:T(8,128)}) fusion(f32[1024,1088]{0,1:T(8,128)} %get-tuple-element.10, pred[1024,1088]{0,1:T(8,128)(4,1)} %get-tuple-element.9, bf16[1024,4,2,128]{0,3,2,1:T(8,128)(2,1)} %bitcast.81, bf16[1024,4,128]{2,0,1:T(8,128)(2,1)} %bitcast.78, bf16[64,4,128]{2,0,1:T(8,128)(2,1)} %collective-permute-done.2), kind=kOutput, calls=%fused_computation.81 | convolution fusion | flops 1165362176 | bytes 25575424 | tf_op jit(solution)/shard_map/sub | solution.py:104
  164.6 2.5 fusion.22
  167.2 4.1 %fusion.12 = (f32[1024,4]{0,1:T(4,128)S(1)}, f32[4,128,1024]{2,1,0:T(8,128)S(1)}) fusion(f32[4,128,1024]{2,1,0:T(8,128)} %fusion.13, bf16[1024,4,256]{0,2,1:T(8,128)(2,1)S(1)} %bitcast.75, bf16[1024,4,16]{0,2,1:T(8,128)(2,1)S(1)} %get-tuple-element.5, bf16[273]{0:T(512)(128)(2,1)S(1)} %pad.9.clone, f32[1,4,273,128]{3,0,2,1:T(1,128)S(1)} %fusion.22, ...), kind=kOutput, calls=%fused_computation.27 | convolution fusion | flops 1726369792 | bytes 6999586 | tf_op jit(solution)/shard_map/thp,hpd->thd/dot_general | solution.py:77
  171.3 8.2 %fusion.11 = bf16[1024,4,128]{0,2,1:T(8,128)(2,1)S(1)} fusion(f32[4,128,1024]{2,1,0:T(8,128)S(1)} %get-tuple-element.18, f32[4,1024,1088]{1,2,0:T(8,128)} %get-tuple-element.16, f32[4,1024]{1,0:T(4,128)S(1)} %get-tuple-element.15, bf16[1024,4,128]{2,0,1:T(8,128)(2,1)S(1)} %copy-done.6, bf16[64,4,128]{2,0,1:T(8,128)(2,1)S(1)} %collective-permute-done, ...), kind=kOutput, calls=%fused_computation.24 | convolution fusion | flops 1153564672 | bytes 22118400 | tf_op jit(solution)/shard_map/hts,shd->thd/dot_general | solution.py:106
  179.5 6.9 %convert_bitcast_fusion = bf16[4096,1024]{0,1:T(8,128)(2,1)} fusion(bf16[1024,512]{0,1:T(8,128)(2,1)S(1)} %bitcast.84, bf16[512,4096]{1,0:T(8,128)(2,1)S(1)} %copy-done.9), kind=kOutput, calls=%fused_computation.8 | convolution fusion | flops 4299161600 | bytes 13631488 | tf_op jit(solution)/shard_map/dot_general | solution.py:109
  186.5 87.4 %reduce-scatter.2.cloned.1.call-done = bf16[512,1024]{0,1:T(8,128)(2,1)} async-done(((bf16[4096,1024]{0,1:T(8,128)(2,1)}), bf16[512,1024]{0,1:T(8,128)(2,1)}) %reduce-scatter.2.cloned.1.call-update) | async-done | bytes 1048592 | tf_op jit(solution)/shard_map/reduce_scatter | solution.py:108
  (39 shorter events, 2.2 us)
Async XLA Ops:
  6.5 87.2 %copy-start = (bf16[4096,128]{1,0:T(8,128)(2,1)S(1)}, bf16[4096,128]{1,0:T(8,128)(2,1)}, u32[]{:S(2)}) copy-start(bf16[4096,128]{1,0:T(8,128)(2,1)} %param.8) | copy-start | bytes 3145732
  6.5 87.2 %all-gather.4.cloned.1.call-start = ((), (), s32[]{:S(2)}) async-start(), calls=%async_computation.1 | async-start | bytes 9437184 | tf_op jit(solution)/shard_map/all_gather | solution.py:36
  7.3 157.4 %all-gather.6.cloned.1.call-start = ((), (), s32[]{:S(2)}) async-start(), calls=%async_computation.3 | async-start | bytes 1433600 | tf_op jit(solution)/shard_map/all_gather | solution.py:67
  11.2 18.9 %collective-permute-start.1 = (bf16[64]{0:T(256)(128)(2,1)S(1)}, bf16[64]{0:T(256)(128)(2,1)S(1)}, u32[]{:S(2)}, u32[]{:S(2)}) collective-permute-start(bf16[64]{0:T(256)(128)(2,1)S(1)} %add_convert_fusion), channel_id=1, source_target_pairs={{0,8},{8,16},{16,24},{1,9},{9,17},{17,25},{2,10},{10,18},{18,26},{... | collective-permute-start | bytes 392 | tf_op jit(solution)/shard_map/ppermute | solution.py:14
  93.8 6.5 %copy-start.2 = (bf16[1024,4096]{1,0:T(8,128)(2,1)S(1)}, bf16[1024,4096]{1,0:T(8,128)(2,1)}, u32[]{:S(2)}) copy-start(bf16[1024,4096]{1,0:T(8,128)(2,1)} %all-gather.4.cloned.1.call-done) | copy-start | bytes 25165828
  93.8 7.0 %copy-start.8 = (bf16[4096,512]{1,0:T(8,128)(2,1)S(1)}, bf16[4096,512]{1,0:T(8,128)(2,1)}, u32[]{:S(2)}) copy-start(bf16[4096,512]{1,0:T(8,128)(2,1)} %param.9) | copy-start | bytes 12582916
  105.2 2.6 copy-start.4
  107.8 1.3 copy-start.3
  110.8 163.0 %reduce-scatter.2.cloned.1.call-start = ((), (), s32[]{:S(2)}) async-start(), calls=%async_computation.2 | async-start | bytes 9437184 | tf_op jit(solution)/shard_map/reduce_scatter | solution.py:108
  111.6 22.9 %copy-start.5 = (bf16[1024,512]{1,0:T(8,128)(2,1)S(1)}, bf16[1024,512]{1,0:T(8,128)(2,1)}, u32[]{:S(2)}) copy-start(bf16[1024,512]{1,0:T(8,128)(2,1)} %copy-done.4) | copy-start | bytes 3145732
  125.5 1.4 copy-start.7
  127.8 21.6 %collective-permute-start.2 = (bf16[64,4,128]{2,0,1:T(8,128)(2,1)}, bf16[64,4,128]{2,0,1:T(8,128)(2,1)}, u32[]{:S(2)}, u32[]{:S(2)}) collective-permute-start(bf16[64,4,128]{2,0,1:T(8,128)(2,1)} %bitcast.82), channel_id=1, source_target_pairs={{0,8},{8,16},{16,24},{1,9},{9,17},{17,25},{2,10},{10,18},{18,26},{... | collective-permute-start | bytes 196616 | tf_op jit(solution)/shard_map/ppermute | solution.py:14
  131.7 39.6 %collective-permute-start = (bf16[64,4,128]{2,0,1:T(8,128)(2,1)}, bf16[64,4,128]{2,0,1:T(8,128)(2,1)S(1)}, u32[]{:S(2)}, u32[]{:S(2)}) collective-permute-start(bf16[64,4,128]{2,0,1:T(8,128)(2,1)} %copy_bitcast_fusion.1), channel_id=1, source_target_pairs={{0,8},{8,16},{16,24},{1,9},{9,17},{17,25},{2,10},{10,18},{18,26},{... | collective-permute-start | bytes 196616 | tf_op jit(solution)/shard_map/ppermute | solution.py:14
  167.2 4.1 %copy-start.6 = (bf16[1024,4,128]{2,0,1:T(8,128)(2,1)S(1)}, bf16[1024,4,128]{2,0,1:T(8,128)(2,1)}, u32[]{:S(2)}) copy-start(bf16[1024,4,128]{2,0,1:T(8,128)(2,1)} %copy_bitcast_fusion) | copy-start | bytes 3145732
  171.3 8.2 %copy-start.9 = (bf16[512,4096]{1,0:T(8,128)(2,1)S(1)}, bf16[512,4096]{1,0:T(8,128)(2,1)}, u32[]{:S(2)}) copy-start(bf16[512,4096]{1,0:T(8,128)(2,1)} %param.11) | copy-start | bytes 12582916
  186.5 87.4 %copy-start.1 = (bf16[4096,128]{1,0:T(8,128)(2,1)S(1)}, bf16[4096,128]{1,0:T(8,128)(2,1)}, u32[]{:S(2)}) copy-start(bf16[4096,128]{1,0:T(8,128)(2,1)} %param.8) | copy-start | bytes 3145732
Sparse Core Ops, SparseCore 0:
  9.0 84.7 all-gather.3
  110.9 28.4 all-gather.5
  186.6 87.2 reduce-scatter.1
where the time goes:
time: 281 us; the launch traced here: 280 us
  waiting for transfers between devices  148 us (53%)
  matrix products  75.5 us (27%)
  between operations  13.3 us (5%)
  local copies, waits for them, and re-layouts  12.5 us (4%)
  starting transfers between devices  11.8 us (4%)
  other arithmetic  10.1 us (4%)
  blocking collectives  8.97 us (3%)
    reduce_scatter x1, waiting for transfers between devices, shards(): lax.psum_scatter(lax.dot_general(w_out, mixed, (((0,), (1,)), ((), ())),...  87.4 us
    all_gather x1, waiting for transfers between devices, shards(): column_piece = lax.all_gather(tokens, 'head', axis=1, tiled=True)  60 us
    dot_general x3, matrix products, shards(): jnp.dot(column_piece, weight, preferred_element_type=jnp.float32)  24.8 us
    sub x1, matrix products, shards(): weights = jnp.exp(logits - top_logit) * within[None].astype(jnp.float32)  15.2 us
    dot_general x1, matrix products, shards(): jnp.einsum('hts,shd->thd', scores, values_here, preferred_element_type=jn...  12.1 us
    ppermute x3, starting transfers between devices, shifted(): return lax.ppermute(x, axis, pairs)  11.5 us
    unnamed x1, blocking collectives  8.97 us
    dot_general x1, matrix products, shards(): jnp.einsum('hts,shd->thd', probs, values_cat, preferred_element_type=jnp....  8.17 us
  transfers between devices with their start and end apart: 6, of which 2 were waited for; matrix products, arithmetic and copies ran while one was open for 23% of the time, Pallas kernels for 0%

commit v1 on v0

v1 whole, which is shorter than its diff:
```python
import functools

import jax
import jax.numpy as jnp
import numpy as np
from jax import lax
from jax.experimental import pallas as pl
from jax.experimental.pallas import tpu as pltpu
from jax.sharding import PartitionSpec as P

HEAD_DIM = 128
FEAT = 16
WIN = 64
PAIRS = [(i, j) for i in range(FEAT) for j in range(i, FEAT)]
WIDE = 256
STATE = -(-(len(PAIRS) + FEAT + 1) // 16) * 16
VMEM = 60 * 1024 * 1024
F32 = jnp.float32
BF16 = jnp.bfloat16


def params():
    return pltpu.CompilerParams(vmem_limit_bytes=VMEM, dimension_semantics=("arbitrary",))


def line(count, step, sources):
    return [(2 * z + c, 2 * (z + step) + c) for z in sources for c in (0, 1) if 0 <= z + step < count]


def swap(x, count):
    return lax.ppermute(x, "head", [(h, h ^ 1) for h in range(2 * count)])


def gather_pieces(x, count):
    mine = [x]
    up = down = x
    for s in range(1, count):
        up = lax.ppermute(up, "head", line(count, 1, range(s - 1, count)))
        down = lax.ppermute(down, "head", line(count, -1, range(0, count - s + 1)))
        mine += [up, down]
    return mine, [swap(p, count) for p in mine]


def project_kernel(count, extra, place, *refs):
    slots = 2 * count - 1
    pieces = refs[: 2 * slots]
    weights = refs[2 * slots : 2 * slots + 1 + extra]
    outs = refs[2 * slots + 1 + extra : 2 * slots + 2 * (1 + extra)]
    x, sems = refs[-2:]
    width = pieces[0].shape[1]

    @pl.when(pl.program_id(0) == 0)
    def _():
        z, c = place[0], place[1]

        def copy(slot, other, source):
            column = pl.multiple_of((2 * source + lax.rem(c + other, 2)) * width, width)
            return pltpu.make_async_copy(
                pieces[other * slots + slot], x.at[:, pl.ds(column, width)], sems.at[other, slot]
            )

        def visit(do):
            for other in (0, 1):
                do(copy(0, other, z))
            for s in range(1, count):

                @pl.when(z >= s)
                def _():
                    for other in (0, 1):
                        do(copy(2 * s - 1, other, z - s))

                @pl.when(z + s < count)
                def _():
                    for other in (0, 1):
                        do(copy(2 * s, other, z + s))

        visit(lambda one: one.start())
        visit(lambda one: one.wait())
        if extra:
            outs[1][...] = jnp.dot(x[...], weights[1][...], preferred_element_type=F32).astype(BF16)

    outs[0][...] = jnp.dot(x[...], weights[0][...], preferred_element_type=F32).astype(BF16)


def project(place, mine, theirs, weight, extra=None):
    count = (len(mine) + 1) // 2
    rows = mine[0].shape[0]
    depth, columns = weight.shape
    tile = min(256, columns)
    specs = [pl.BlockSpec(memory_space=pl.ANY)] * (2 * len(mine))
    specs += [pl.BlockSpec((depth, tile), lambda j, _: (0, j))]
    out_specs = [pl.BlockSpec((rows, tile), lambda j, _: (0, j))]
    shapes = [jax.ShapeDtypeStruct((rows, columns), BF16)]
    args = [weight]
    if extra is not None:
        args.append(extra)
        specs.append(pl.BlockSpec(extra.shape, lambda j, _: (0, 0)))
        out_specs.append(pl.BlockSpec((rows, extra.shape[1]), lambda j, _: (0, 0)))
        shapes.append(jax.ShapeDtypeStruct((rows, extra.shape[1]), BF16))
    return pl.pallas_call(
        functools.partial(project_kernel, count, len(args) - 1),
        grid_spec=pltpu.PrefetchScalarGridSpec(
            num_scalar_prefetch=1,
            grid=(columns // tile,),
            in_specs=specs,
            out_specs=out_specs,
            scratch_shapes=[
                pltpu.VMEM((rows, depth), BF16),
                pltpu.SemaphoreType.DMA((2, len(mine))),
            ],
        ),
        out_shape=shapes,
        compiler_params=params(),
    )(place, *mine, *theirs, *args)


def expansions(heads):
    lanes = heads * 2 * FEAT
    maps = np.zeros((2, heads, lanes, 2 * WIDE), np.float32)
    rows = np.zeros((3, WIDE), np.float32)
    for h in range(heads):
        for side in (0, 1):
            base = h * 2 * FEAT + side * FEAT
            for n, (i, j) in enumerate(PAIRS):
                maps[side, h, base + i, n] = 1.0
                maps[side, h, base + j, WIDE + n] = 1.0
            for i in range(FEAT):
                maps[side, h, base + i, len(PAIRS) + i] = 1.0
    for n, (i, j) in enumerate(PAIRS):
        rows[2, n] = (2.0 * FEAT) ** -0.5 * (1.0 if i == j else 2.0**0.5)
    rows[1, len(PAIRS) : len(PAIRS) + FEAT + 1] = 1.0
    rows[0, len(PAIRS) + FEAT] = 1.0
    rows[2, len(PAIRS) : len(PAIRS) + FEAT] = FEAT**-0.25
    rows[2, len(PAIRS) + FEAT] = 1.0
    return maps.astype(jnp.bfloat16), rows


def picks(heads):
    lanes = heads * 2 * FEAT
    maps = np.zeros((heads, lanes, 256), np.float32)
    for h in range(heads):
        for i in range(FEAT):
            maps[h, h * 2 * FEAT + i, i] = 1.0
            maps[h, h * 2 * FEAT + FEAT + i, 128 + i] = 1.0
    return maps.astype(jnp.bfloat16)


def phi(features, expand, rows):
    factors = jnp.dot(features, expand, preferred_element_type=F32)
    left = factors[:, :WIDE] + rows[0:1]
    right = factors[:, WIDE:] + rows[1:2]
    return (left * right * rows[2:3]).astype(BF16)


def state_kernel(final, features, values, keep, expand, rows, *refs):
    phi_key = phi(features[...], expand[0], rows[...])
    kept = jnp.where(keep[...] > 0, values[...].astype(F32), 0.0).astype(BF16)
    state = lax.dot_general(phi_key, kept, (((0,), (0,)), ((), ())), preferred_element_type=F32)
    state = state[:STATE]
    if final:
        state = state + refs[0][0]
    refs[-1][0] = state.astype(refs[-1].dtype)


def local_state(features, values, keep, expand, rows, before=None):
    heads = values.shape[1] // HEAD_DIM
    count = features.shape[0]
    specs = [
        pl.BlockSpec(features.shape, lambda h: (0, 0)),
        pl.BlockSpec((count, HEAD_DIM), lambda h: (0, h)),
        pl.BlockSpec((count, 1), lambda h: (0, 0)),
        pl.BlockSpec((1,) + expand.shape[1:], lambda h: (h, 0, 0)),
        pl.BlockSpec(rows.shape, lambda h: (0, 0)),
    ]
    block = pl.BlockSpec((1, STATE, HEAD_DIM), lambda h: (h, 0, 0))
    args = [features, values, keep, expand, rows]
    if before is not None:
        specs.append(block)
        args.append(before)
    return pl.pallas_call(
        functools.partial(state_kernel, before is not None),
        grid=(heads,),
        in_specs=specs,
        out_specs=block,
        out_shape=jax.ShapeDtypeStruct((heads, STATE, HEAD_DIM), F32 if before is None else BF16),
        compiler_params=params(),
    )(*args)


def attention_kernel(
    feat_low, feat_high, val_low, val_high, win_low, win_high, tail_win, tail_val, bounds, pick,
    inner, windowed, query, key
):
    half = feat_low.shape[0]
    rows = 2 * half
    for part, ref in enumerate((feat_low, feat_high)):
        both = jnp.dot(ref[...], pick[0], preferred_element_type=F32).astype(BF16)
        query[part * half : (part + 1) * half] = both[:, :128]
        key[part * half : (part + 1) * half] = both[:, 128:]

    def rows_of(low, high, start, size):
        if start >= half:
            return high[start - half : start - half + size]
        if start + size <= half:
            return low[start : start + size]
        return jnp.concatenate([low[start:half], high[0 : start + size - half]], 0)

    tile = min(256, half)
    for q in range(rows // tile):
        here = slice(q * tile, (q + 1) * tile)
        first = bounds[here, 0:1]
        total = jnp.zeros((tile, HEAD_DIM), F32)
        for k in range(q + 1):
            dots = lax.dot_general(
                query[here], key[k * tile : (k + 1) * tile], (((1,), (1,)), ((), ())),
                preferred_element_type=F32,
            )
            score = dots * (dots * (0.5 / FEAT) + FEAT**-0.5) + 1.0
            at = lax.broadcasted_iota(jnp.int32, (tile, tile), 1) + k * tile
            good = at >= first
            if k == q:
                good &= at <= lax.broadcasted_iota(jnp.int32, (tile, tile), 0) + q * tile
            score = jnp.where(good, score, 0.0).astype(BF16)
            total += jnp.dot(
                score, rows_of(val_low, val_high, k * tile, tile), preferred_element_type=F32
            )
        inner[here] = total

    tile = min(128, half)
    for q in range(rows // tile):
        here = slice(q * tile, (q + 1) * tile)
        start = q * tile - WIN
        wide = tile + WIN
        queries = rows_of(win_low, win_high, q * tile, tile)[:, :HEAD_DIM]
        if q:
            keys = rows_of(win_low, win_high, start, wide)[:, HEAD_DIM:]
            values = rows_of(val_low, val_high, start, wide)
        else:
            keys = jnp.concatenate([tail_win[...], win_low[0:tile]], 0)[:, HEAD_DIM:]
            values = jnp.concatenate([tail_val[...], val_low[0:tile]], 0)
        logits = lax.dot_general(
            queries, keys, (((1,), (1,)), ((), ())), preferred_element_type=F32
        ) * HEAD_DIM**-0.5
        at = lax.broadcasted_iota(jnp.int32, (tile, wide), 1)
        row = lax.broadcasted_iota(jnp.int32, (tile, wide), 0)
        good = (at >= bounds[here, 1:2] - start) & (at <= row + WIN)
        logits = jnp.where(good, logits, -1e30)
        top = jnp.max(logits, 1, keepdims=True)
        weight = jnp.where(good, jnp.exp(logits - top), 0.0)
        probs = (weight / jnp.sum(weight, 1, keepdims=True)).astype(BF16)
        windowed[here] = jnp.dot(probs, values, preferred_element_type=F32)


def attention(feats, vals, wins, tail_win, tail_val, bounds, pick):
    half, columns = vals[0].shape
    heads = columns // HEAD_DIM
    rows = 2 * half

    def full(a):
        return pl.BlockSpec(a.shape, lambda h: (0,) * a.ndim)

    value = pl.BlockSpec((half, HEAD_DIM), lambda h: (0, h))
    window = pl.BlockSpec((half, 2 * HEAD_DIM), lambda h: (0, h))
    out = pl.BlockSpec((rows, HEAD_DIM), lambda h: (0, h))
    return pl.pallas_call(
        attention_kernel,
        grid=(heads,),
        in_specs=[
            full(feats[0]), full(feats[1]), value, value, window, window,
            pl.BlockSpec((WIN, 2 * HEAD_DIM), lambda h: (0, h)),
            pl.BlockSpec((WIN, HEAD_DIM), lambda h: (0, h)),
            full(bounds),
            pl.BlockSpec((1,) + pick.shape[1:], lambda h: (h, 0, 0)),
        ],
        out_specs=[out, out],
        out_shape=[jax.ShapeDtypeStruct((rows, columns), F32)] * 2,
        scratch_shapes=[pltpu.VMEM((rows, 128), BF16)] * 2,
        compiler_params=params(),
    )(*feats, *vals, *wins, tail_win, tail_val, bounds, pick)


def finish_kernel(shifts, chosen, feat_low, feat_high, uses, expand, rows, inner, windowed, *refs):
    half = feat_low.shape[0]
    states, outs = refs[:shifts], refs[shifts:]
    incoming = jnp.zeros((STATE, HEAD_DIM), F32)
    for k in range(shifts):
        incoming += jnp.where(chosen[k] > 0, states[k][0].astype(F32), 0.0)
    incoming = jnp.concatenate([incoming, jnp.zeros((WIDE - STATE, HEAD_DIM), F32)], 0).astype(BF16)
    for part, ref in enumerate((feat_low, feat_high)):
        here = slice(part * half, (part + 1) * half)
        phi_query = phi(ref[...], expand[0], rows[...])
        carried = jnp.dot(phi_query, incoming, preferred_element_type=F32)
        linear = inner[here] + jnp.where(uses[here] == 0, carried, 0.0)
        mean = jnp.mean(linear * linear, 1, keepdims=True)
        outs[part][...] = (linear * lax.rsqrt(mean + 1e-5) + windowed[here]).astype(BF16)


def finish(chosen, feats, uses, expand, rows, inner, windowed, states):
    count, columns = inner.shape
    half = count // 2
    heads = columns // HEAD_DIM

    def full(a):
        return pl.BlockSpec(a.shape, lambda h, _: (0,) * a.ndim)

    block = pl.BlockSpec((count, HEAD_DIM), lambda h, _: (0, h))
    out = pl.BlockSpec((half, HEAD_DIM), lambda h, _: (0, h))
    state = pl.BlockSpec((1, STATE, HEAD_DIM), lambda h, _: (h, 0, 0))
    return pl.pallas_call(
        functools.partial(finish_kernel, len(states)),
        grid_spec=pltpu.PrefetchScalarGridSpec(
            num_scalar_prefetch=1,
            grid=(heads,),
            in_specs=[
                full(feats[0]), full(feats[1]), full(uses),
                pl.BlockSpec((1,) + expand.shape[1:], lambda h, _: (h, 0, 0)),
                full(rows), block, block,
            ] + [state] * len(states),
            out_specs=[out, out],
        ),
        out_shape=[jax.ShapeDtypeStruct((half, columns), BF16)] * 2,
        compiler_params=params(),
    )(chosen, *feats, uses, expand, rows, inner, windowed, *states)


def shards(tokens, doc_ids, w_feat, w_value, w_window, w_out):
    rows = tokens.shape[0]
    half = rows // 2
    heads = w_value.shape[1] // HEAD_DIM
    count = lax.axis_size("head") // 2
    blocks = lax.axis_size("ctx")
    me = lax.axis_index("head")
    z, c = me // 2, me % 2
    place = jnp.stack([z, c]).astype(jnp.int32)

    high_mine, high_theirs = gather_pieces(tokens[half:], count)
    low_mine, low_theirs = gather_pieces(tokens[:half], count)

    docs = doc_ids.astype(F32)
    doc_tails = [
        lax.ppermute(docs[rows - WIN :] + 1.0, "ctx", [(i, i + k) for i in range(blocks - k)])
        for k in range(1, blocks)
    ]
    chosen = jnp.stack([t[WIN - 1] == docs[0] + 1.0 for t in doc_tails]).astype(jnp.int32)
    first = jnp.sum((docs[None, :] < docs[:, None]).astype(F32), 1).astype(jnp.int32)
    in_tail = jnp.sum((doc_tails[0] == docs[0] + 1.0).astype(jnp.int32))
    at = jnp.arange(rows, dtype=jnp.int32)
    window_first = jnp.maximum(jnp.where(first == 0, -in_tail, first), at - (WIN - 1))
    bounds = jnp.stack([first, window_first], 1)
    uses = first[:, None]
    keep = (docs == docs[-1]).astype(jnp.int32)[:, None]

    maps, scale_rows = expansions(heads)
    query_map, key_map = jnp.asarray(maps[0]), jnp.asarray(maps[1])
    scale_rows = jnp.asarray(scale_rows)
    pick = jnp.asarray(picks(heads))

    features_out = w_out.shape[1] // (2 * count)
    split_out = w_out.reshape(w_out.shape[0], count, 2, features_out)
    my_out = lax.dynamic_index_in_dim(split_out, c, 2, keepdims=False)
    their_out = swap(lax.dynamic_index_in_dim(split_out, 1 - c, 2, keepdims=False), count)
    chip_out = jnp.concatenate([my_out, their_out], 0)

    def out_for(chip):
        return lax.dynamic_index_in_dim(chip_out, jnp.clip(chip, 0, count - 1), 1, keepdims=False)

    out_up = [out_for(z + count - s) for s in range(1, count)]
    out_down = [out_for(z - count + s) for s in range(1, count)]
    out_here = out_for(z)

    value_high, feat_high = project(place, high_mine, high_theirs, w_value, w_feat)
    (win_high,) = project(place, high_mine, high_theirs, w_window)
    tail_win, tail_val = (
        lax.ppermute(a[half - WIN :], "ctx", [(i, i + 1) for i in range(blocks - 1)])
        for a in (win_high, value_high)
    )
    state_high = local_state(feat_high, value_high, keep[half:], key_map, scale_rows)

    value_low, feat_low = project(place, low_mine, low_theirs, w_value, w_feat)
    state = local_state(feat_low, value_low, keep[:half], key_map, scale_rows, state_high)
    states = [
        lax.ppermute(state, "ctx", [(i, i + k) for i in range(blocks - k)])
        for k in range(1, blocks)
    ]
    (win_low,) = project(place, low_mine, low_theirs, w_window)
    feats = (feat_low, feat_high)
    inner, windowed = attention(
        feats, (value_low, value_high), (win_low, win_high), tail_win, tail_val, bounds, pick
    )
    mixed = finish(chosen, feats, uses, query_map, scale_rows, inner, windowed, states)

    outs = []
    for mine in mixed:
        chip = jnp.concatenate([mine, swap(mine, count)], 1)

        def partial(weight, *received):
            total = jnp.dot(chip, weight, preferred_element_type=F32)
            for r in received:
                total += r.astype(F32)
            return total.astype(BF16)

        up, down = (), ()
        for s in range(1, count):
            up = (
                lax.ppermute(
                    partial(out_up[s - 1], *up), "head", line(count, 1, range(0, s))
                ),
            )
            down = (
                lax.ppermute(
                    partial(out_down[s - 1], *down), "head", line(count, -1, range(count - s, count))
                ),
            )
        outs.append(partial(out_here, *up, *down))
    return jnp.concatenate(outs, 0)


def solution(mesh):
    return jax.shard_map(
        shards,
        mesh=mesh,
        in_specs=(
            P("ctx", "head"),
            P("ctx"),
            P(None, "head"),
            P(None, "head"),
            P(None, "head"),
            P("head", None),
        ),
        out_specs=P("ctx", "head"),
        check_vma=False,
    )
```

time: 281 us -> 279 us (level)
  waiting for transfers between devices: 148 us -> 63.2 us
  Pallas kernels: 0 us -> 75.6 us
  starting transfers between devices: 11.8 us -> 71.2 us
  matrix products: 75.5 us -> 29.2 us
  local copies, waits for them, and re-layouts: 12.5 us -> 29.2 us
  between operations: 13.3 us -> 4.11 us
  blocking collectives: 8.97 us -> 0 us
  other arithmetic: 10.1 us -> 4.23 us
    reduce_scatter x1 -> x0, waiting for transfers between devices: 87.4 us -> none  [shards(): lax.psum_scatter(lax.dot_general(w_out, mixed, (((0,), (1,)), ((), ())),...]
    pallas_call x0 -> x8, Pallas kernels: none -> 75.6 us  [the longest x4 40.9 us: project(): pl.pallas_call(functools.partial(project_kernel, count, len(args) - 1), g...]
    ppermute x3 -> x49, waiting for transfers between devices: 0.01 us -> 63.2 us  [the longest x6 38.6 us: gather_pieces(): down = lax.ppermute(down, 'head', line(count, -1, range(0, count - s + 1)))]
    all_gather x2 -> x0, waiting for transfers between devices: 60 us -> none  [the longest x1 60 us: shards(): column_piece = lax.all_gather(tokens, 'head', axis=1, tiled=True)]
    ppermute x3 -> x49, starting transfers between devices: 11.5 us -> 71.2 us  [the longest x6 22.2 us: shards(): lax.ppermute(partial(out_up[s - 1], *up), 'head', line(count, 1, range(0,...]
    dot_general x9 -> x14, matrix products: 60.3 us -> 29.2 us  [partial(): total = jnp.dot(chip, weight, preferred_element_type=F32)]
    sub x1 -> x0, matrix products: 15.2 us -> none  [shards(): weights = jnp.exp(logits - top_logit) * within[None].astype(jnp.float32)]
    dynamic_slice x0 -> x3, local copies, waits for them, and re-layouts: none -> 9.14 us  [the longest x2 6.35 us: shards(): lax.dynamic_index_in_dim(split_out, 1 - c, 2, keepdims=False)]
  transfers between devices with their start and end apart: 6 -> 49, of which waited for: 2 -> 14; matrix products, arithmetic and copies ran while one was open for 23% -> 20% of each run, Pallas kernels for 0% -> 27%
where the time goes in v1:
time: 279 us; the launch traced here: 277 us
  Pallas kernels  75.6 us (27%)
  starting transfers between devices  71.2 us (26%)
  waiting for transfers between devices  63.2 us (23%)
  local copies, waits for them, and re-layouts  29.2 us (10%)
  matrix products  29.2 us (10%)
  other arithmetic  4.23 us (2%)
  between operations  4.11 us (1%)
    pallas_call x4, Pallas kernels, project(): pl.pallas_call(functools.partial(project_kernel, count, len(args) - 1), g...  40.9 us
    ppermute x6, waiting for transfers between devices, gather_pieces(): down = lax.ppermute(down, 'head', line(count, -1, range(0, count - s + 1)))  38.6 us
    dot_general x14, matrix products, partial(): total = jnp.dot(chip, weight, preferred_element_type=F32)  29.2 us
    ppermute x6, starting transfers between devices, shards(): lax.ppermute(partial(out_up[s - 1], *up), 'head', line(count, 1, range(0,...  22.2 us
    pallas_call x1, Pallas kernels, attention(): pl.pallas_call(attention_kernel, grid=(heads,), in_specs=[full(feats[0]),...  18.7 us
    ppermute x6, waiting for transfers between devices, shards(): lax.ppermute(partial(out_up[s - 1], *up), 'head', line(count, 1, range(0,...  15.3 us
    ppermute x6, starting transfers between devices, gather_pieces(): up = lax.ppermute(up, 'head', line(count, 1, range(s - 1, count)))  14.6 us
    unnamed x56, local copies, waits for them, and re-layouts  9.68 us
  transfers between devices with their start and end apart: 49, of which 14 were waited for; matrix products, arithmetic and copies ran while one was open for 20% of the time, Pallas kernels for 27%

profile of v1, /device:TPU:0, one launch (start us, length us, event | category | flops | bytes accessed | tf_op | source)
XLA Modules:
  0.0 276.7 jit_solution(3986471321766483139)
XLA Ops:
  1.3 5.0 %collective-permute-start.16 = (bf16[512,512]{1,0:T(8,128)(2,1)S(1)}, bf16[512,512]{1,0:T(8,128)(2,1)S(1)}, u32[]{:S(2)}, u32[]{:S(2)}) collective-permute-start(bf16[512,512]{1,0:T(8,128)(2,1)S(1)} %get-tuple-element.23.refs_0_), channel_id=1, source_target_pairs={{0,2},{1,3},{2,4},{3,5},{4,6},{5,7},{8,10},{9,11},{10,12},{11,13},... | collective-permute-start | bytes 1572872 | tf_op jit(solution)/shard_map/ppermute | solution.py:38
  7.7 4.6 %collective-permute-start.3 = (bf16[512,512]{1,0:T(8,128)(2,1)S(1)}, bf16[512,512]{1,0:T(8,128)(2,1)S(1)}, u32[]{:S(2)}, u32[]{:S(2)}) collective-permute-start(bf16[512,512]{1,0:T(8,128)(2,1)S(1)} %get-tuple-element.24.refs_0_), channel_id=1, source_target_pairs={{0,2},{1,3},{2,4},{3,5},{4,6},{5,7},{8,10},{9,11},{10,12},{11,13},... | collective-permute-start | bytes 1572872 | tf_op jit(solution)/shard_map/ppermute | solution.py:38
  12.3 3.4 %collective-permute-start = (f32[64]{0:T(128)S(1)}, f32[64]{0:T(128)S(1)}, u32[]{:S(2)}, u32[]{:S(2)}) collective-permute-start(f32[64]{0:T(128)S(1)} %slice_add_fusion), channel_id=1, source_target_pairs={{0,8},{8,16},{16,24},{1,9},{9,17},{17,25},{2,10},{10,18},{18,26},{... | collective-permute-start | bytes 776 | tf_op jit(solution)/shard_map/ppermute | solution.py:341
  18.6 3.6 %collective-permute-done.17.refs_2_ = bf16[512,512]{1,0:T(8,128)(2,1)S(1)} collective-permute-done((bf16[512,512]{1,0:T(8,128)(2,1)S(1)}, bf16[512,512]{1,0:T(8,128)(2,1)S(1)}, u32[]{:S(2)}, u32[]{:S(2)}) %collective-permute-start.17) | collective-permute-done | bytes 524320 | tf_op jit(solution)/shard_map/ppermute | solution.py:39
  25.0 3.7 %collective-permute-done.3.refs_1_ = bf16[512,512]{1,0:T(8,128)(2,1)S(1)} collective-permute-done((bf16[512,512]{1,0:T(8,128)(2,1)S(1)}, bf16[512,512]{1,0:T(8,128)(2,1)S(1)}, u32[]{:S(2)}, u32[]{:S(2)}) %collective-permute-start.3) | collective-permute-done | bytes 524320 | tf_op jit(solution)/shard_map/ppermute | solution.py:38
  28.6 5.1 %collective-permute-done.4.refs_2_ = bf16[512,512]{1,0:T(8,128)(2,1)S(1)} collective-permute-done((bf16[512,512]{1,0:T(8,128)(2,1)S(1)}, bf16[512,512]{1,0:T(8,128)(2,1)S(1)}, u32[]{:S(2)}, u32[]{:S(2)}) %collective-permute-start.4) | collective-permute-done | bytes 524320 | tf_op jit(solution)/shard_map/ppermute | solution.py:39
  35.8 9.1 %collective-permute-done.19.refs_4_ = bf16[512,512]{1,0:T(8,128)(2,1)} collective-permute-done((bf16[512,512]{1,0:T(8,128)(2,1)S(1)}, bf16[512,512]{1,0:T(8,128)(2,1)}, u32[]{:S(2)}, u32[]{:S(2)}) %collective-permute-start.19) | collective-permute-done | bytes 524320 | tf_op jit(solution)/shard_map/ppermute | solution.py:39
  48.2 8.3 %collective-permute-done.6.refs_4_ = bf16[512,512]{1,0:T(8,128)(2,1)S(1)} collective-permute-done((bf16[512,512]{1,0:T(8,128)(2,1)S(1)}, bf16[512,512]{1,0:T(8,128)(2,1)S(1)}, u32[]{:S(2)}, u32[]{:S(2)}) %collective-permute-start.6) | collective-permute-done | bytes 524320 | tf_op jit(solution)/shard_map/ppermute | solution.py:39
  57.4 6.5 %copy.37 = bf16[512,4096]{0,1:T(8,128)(2,1)} copy(bf16[512,4096]{1,0:T(8,128)(2,1)} %param.15) | data formatting | bytes 8388608 | tf_op args[5]
  65.4 4.0 %constant_dynamic-slice_fusion = (bf16[512,4,1,512]{0,3,2,1:T(8,128)(2,1)S(1)}, bf16[512,4,1,512]{0,3,2,1:T(8,128)(2,1)}) fusion(bf16[512,4,2,512]{0,3,2,1:T(8,128)(2,1)} %bitcast.72, s32[]{:T(128)S(6)} %select_n.41, s32[]{:T(128)S(6)} %select_n.40), kind=kLoop, calls=%fused_computation.63 | loop fusion | bytes 8388616 | tf_op jit(solution)/shard_map/jit(dynamic_index_in_dim)/dynamic_slice | solution.py:361
  75.5 12.5 %collective-permute-done.8.refs_6_ = bf16[512,512]{1,0:T(8,128)(2,1)S(1)} collective-permute-done((bf16[512,512]{1,0:T(8,128)(2,1)S(1)}, bf16[512,512]{1,0:T(8,128)(2,1)S(1)}, u32[]{:S(2)}, u32[]{:S(2)}) %collective-permute-start.8) | collective-permute-done | bytes 524320 | tf_op jit(solution)/shard_map/ppermute | solution.py:39
  94.5 9.5 %shard_map.101 = (bf16[512,512]{1,0:T(8,128)(2,1)}, bf16[512,128]{1,0:T(8,128)(2,1)}) custom-call(s32[2]{0:T(128)} %pad_add_fusion.1.place, bf16[512,512]{1,0:T(8,128)(2,1)} %copy-done.2, bf16[512,512]{1,0:T(8,128)(2,1)} %copy-done.6, bf16[512,512]{1,0:T(8,128)(2,1)} %copy-done.7, bf16[512,512]{1,0:T(8,128)(2,1)} %collective-permute-done.18.refs_3_, ...), custom_call_target="tpu_custom_call" | custom-call | tf_op jit(solution)/shard_map/pallas_call | solution.py:100
  104.9 3.5 %collective-permute-start.30 = (bf16[64,512]{1,0:T(8,128)(2,1)S(1)}, bf16[64,512]{1,0:T(8,128)(2,1)S(1)}, u32[]{:S(2)}, u32[]{:S(2)}) collective-permute-start(bf16[64,512]{1,0:T(8,128)(2,1)S(1)} %slice.55), channel_id=1, source_target_pairs={{0,8},{8,16},{16,24},{1,9},{9,17},{17,25},{2,10},{10,18},{18,26},{... | collective-permute-start | bytes 196616 | tf_op jit(solution)/shard_map/ppermute | solution.py:374
  108.3 4.4 %shard_map.105.refs_0_ = f32[4,160,128]{2,1,0:T(8,128)} custom-call(bf16[512,128]{1,0:T(8,128)(2,1)} %get-tuple-element.14.feat_high.features, bf16[512,512]{1,0:T(8,128)(2,1)} %get-tuple-element.16.val_high.values, s32[512,1]{1,0:T(8,128)} %copy.34.keep, bf16[4,128,512]{2,1,0:T(8,128)(2,1)} %constant.95.clone.expand, f32[3,256]{1,0:T(4,128)} %constant.96.clone.rows), custom_call_target="tpu_custom_call" | custom-call | tf_op jit(solution)/shard_map/pallas_call | solution.py:180
  112.8 3.4 %collective-permute-start.1 = (f32[64]{0:T(128)S(1)}, f32[64]{0:T(128)S(1)}, u32[]{:S(2)}, u32[]{:S(2)}) collective-permute-start(f32[64]{0:T(128)S(1)} %slice_add_fusion), channel_id=1, source_target_pairs={{0,16},{8,24},{1,17},{9,25},{2,18},{10,26},{3,19},{11,27},{4,20},{... | collective-permute-start | bytes 776 | tf_op jit(solution)/shard_map/ppermute | solution.py:341
  117.6 9.5 %shard_map.100 = (bf16[512,512]{1,0:T(8,128)(2,1)}, bf16[512,128]{1,0:T(8,128)(2,1)}) custom-call(s32[2]{0:T(128)} %pad_add_fusion.1.place, bf16[512,512]{1,0:T(8,128)(2,1)} %copy-done.1, bf16[512,512]{1,0:T(8,128)(2,1)} %copy-done.3, bf16[512,512]{1,0:T(8,128)(2,1)} %copy-done.4, bf16[512,512]{1,0:T(8,128)(2,1)} %copy-done.8, bf16[512,512]{1,0:T(8,128)(2,1)} %copy-done.11, ...), custom_call_target="tpu_custom_call" | custom-call | tf_op jit(solution)/shard_map/pallas_call | solution.py:100
  127.1 4.6 %shard_map.106 = bf16[4,160,128]{2,1,0:T(8,128)(2,1)} custom-call(bf16[512,128]{1,0:T(8,128)(2,1)} %get-tuple-element.13.feat_low.features, bf16[512,512]{1,0:T(8,128)(2,1)} %get-tuple-element.15.val_low.values, s32[512,1]{1,0:T(8,128)} %copy.35.keep, bf16[4,128,512]{2,1,0:T(8,128)(2,1)} %constant.95.clone.expand, f32[3,256]{1,0:T(4,128)} %constant.96.clone.rows, ...), custom_call_target="tpu_custom_call" | custom-call | tf_op jit(solution)/shard_map/pallas_call | solution.py:180
  133.3 11.0 %shard_map.103.win_high = bf16[512,1024]{1,0:T(8,128)(2,1)} custom-call(s32[2]{0:T(128)} %pad_add_fusion.1.place, bf16[512,512]{1,0:T(8,128)(2,1)} %copy-done.2, bf16[512,512]{1,0:T(8,128)(2,1)} %copy-done.6, bf16[512,512]{1,0:T(8,128)(2,1)} %copy-done.7, bf16[512,512]{1,0:T(8,128)(2,1)} %collective-permute-done.18.refs_3_, ...), custom_call_target="tpu_custom_call" | custom-call | tf_op jit(solution)/shard_map/pallas_call | solution.py:100
  155.4 11.0 %shard_map.102.win_low = bf16[512,1024]{1,0:T(8,128)(2,1)} custom-call(s32[2]{0:T(128)} %pad_add_fusion.1.place, bf16[512,512]{1,0:T(8,128)(2,1)} %copy-done.1, bf16[512,512]{1,0:T(8,128)(2,1)} %copy-done.3, bf16[512,512]{1,0:T(8,128)(2,1)} %copy-done.4, bf16[512,512]{1,0:T(8,128)(2,1)} %copy-done.8, bf16[512,512]{1,0:T(8,128)(2,1)} %copy-done.11, ...), custom_call_target="tpu_custom_call" | custom-call | tf_op jit(solution)/shard_map/pallas_call | solution.py:100
  167.1 18.7 %shard_map.104 = (f32[1024,512]{1,0:T(8,128)}, f32[1024,512]{1,0:T(8,128)}) custom-call(bf16[512,128]{1,0:T(8,128)(2,1)} %get-tuple-element.13.feat_low.features, bf16[512,128]{1,0:T(8,128)(2,1)} %get-tuple-element.14.feat_high.features, bf16[512,512]{1,0:T(8,128)(2,1)} %get-tuple-element.15.val_low.values, ...), custom_call_target="tpu_custom_call" | custom-call | tf_op jit(solution)/shard_map/pallas_call | solution.py:265
  186.6 6.9 %shard_map.107 = (bf16[512,512]{1,0:T(8,128)(2,1)}, bf16[512,512]{1,0:T(8,128)(2,1)}) custom-call(s32[3]{0:T(128)} %add_convert_fusion.chosen, bf16[512,128]{1,0:T(8,128)(2,1)} %get-tuple-element.13.feat_low.features, bf16[512,128]{1,0:T(8,128)(2,1)} %get-tuple-element.14.feat_high.features, s32[1024,1]{1,0:T(8,128)} %copy.36.uses, ...), custom_call_target="tpu_custom_call" | custom-call | tf_op jit(solution)/shard_map/pallas_call | solution.py:309
  193.6 2.8 %copy.38 = bf16[512,4,1,512]{3,0,2,1:T(8,128)(2,1)S(1)} copy(bf16[512,4,1,512]{0,3,2,1:T(8,128)(2,1)} %get-tuple-element.22) | data formatting | bytes 4194304 | tf_op jit(solution)/shard_map/jit(dynamic_index_in_dim)/dynamic_slice | solution.py:360
  211.2 4.1 %collective-permute-done.36 = bf16[512,512]{1,0:T(8,128)(2,1)S(1)} collective-permute-done((bf16[512,512]{1,0:T(8,128)(2,1)S(1)}, bf16[512,512]{1,0:T(8,128)(2,1)S(1)}, u32[]{:S(2)}, u32[]{:S(2)}) %collective-permute-start.36) | collective-permute-done | bytes 524320 | tf_op jit(solution)/shard_map/ppermute | solution.py:405
  217.1 4.4 %collective-permute-start.37 = (bf16[512,512]{1,0:T(8,128)(2,1)S(1)}, bf16[512,512]{1,0:T(8,128)(2,1)S(1)}, u32[]{:S(2)}, u32[]{:S(2)}) collective-permute-start(bf16[512,512]{1,0:T(8,128)(2,1)S(1)} %fusion.3), channel_id=1, source_target_pairs={{0,2},{1,3},{2,4},{3,5},{8,10},{9,11},{10,12},{11,13},{16,18},{17,... | collective-permute-start | bytes 1572872 | tf_op jit(solution)/shard_map/ppermute | solution.py:405
  224.0 2.6 collective-permute-done.43
  228.3 4.4 %collective-permute-start.44 = (bf16[512,512]{1,0:T(8,128)(2,1)S(1)}, bf16[512,512]{1,0:T(8,128)(2,1)S(1)}, u32[]{:S(2)}, u32[]{:S(2)}) collective-permute-start(bf16[512,512]{1,0:T(8,128)(2,1)S(1)} %fusion.7), channel_id=1, source_target_pairs={{0,2},{1,3},{2,4},{3,5},{8,10},{9,11},{10,12},{11,13},{16,18},{17,... | collective-permute-start | bytes 1572872 | tf_op jit(solution)/shard_map/ppermute | solution.py:405
  235.2 2.6 collective-permute-done.37
  240.3 5.2 %collective-permute-start.38 = (bf16[512,512]{1,0:T(8,128)(2,1)}, bf16[512,512]{1,0:T(8,128)(2,1)}, u32[]{:S(2)}, u32[]{:S(2)}) collective-permute-start(bf16[512,512]{1,0:T(8,128)(2,1)} %fusion.2), channel_id=1, source_target_pairs={{0,2},{1,3},{2,4},{3,5},{4,6},{5,7},{8,10},{9,11},{10,12},{11,13},... | collective-permute-start | bytes 1572872 | tf_op jit(solution)/shard_map/ppermute | solution.py:405
  251.9 5.3 %collective-permute-start.45 = (bf16[512,512]{1,0:T(8,128)(2,1)}, bf16[512,512]{1,0:T(8,128)(2,1)}, u32[]{:S(2)}, u32[]{:S(2)}) collective-permute-start(bf16[512,512]{1,0:T(8,128)(2,1)} %fusion.6), channel_id=1, source_target_pairs={{0,2},{1,3},{2,4},{3,5},{4,6},{5,7},{8,10},{9,11},{10,12},{11,13},... | collective-permute-start | bytes 1572872 | tf_op jit(solution)/shard_map/ppermute | solution.py:405
  257.3 2.6 fusion.8
  264.8 6.0 %collective-permute-done.45 = bf16[512,512]{1,0:T(8,128)(2,1)} collective-permute-done((bf16[512,512]{1,0:T(8,128)(2,1)}, bf16[512,512]{1,0:T(8,128)(2,1)}, u32[]{:S(2)}, u32[]{:S(2)}) %collective-permute-start.45) | collective-permute-done | bytes 524320 | tf_op jit(solution)/shard_map/ppermute | solution.py:405
  270.8 2.8 %collective-permute-done.48 = bf16[512,512]{1,0:T(8,128)(2,1)} collective-permute-done((bf16[512,512]{1,0:T(8,128)(2,1)}, bf16[512,512]{1,0:T(8,128)(2,1)}, u32[]{:S(2)}, u32[]{:S(2)}) %collective-permute-start.48) | collective-permute-done | bytes 524320 | tf_op jit(solution)/shard_map/ppermute | solution.py:410
  (172 shorter events, 81.7 us)
Async XLA Ops:
  1.3 17.2 %collective-permute-start.16 = (bf16[512,512]{1,0:T(8,128)(2,1)S(1)}, bf16[512,512]{1,0:T(8,128)(2,1)S(1)}, u32[]{:S(2)}, u32[]{:S(2)}) collective-permute-start(bf16[512,512]{1,0:T(8,128)(2,1)S(1)} %get-tuple-element.23.refs_0_), channel_id=1, source_target_pairs={{0,2},{1,3},{2,4},{3,5},{4,6},{5,7},{8,10},{9,11},{10,12},{11,13},... | collective-permute-start | bytes 1572872 | tf_op jit(solution)/shard_map/ppermute | solution.py:38
  7.7 21.0 %collective-permute-start.3 = (bf16[512,512]{1,0:T(8,128)(2,1)S(1)}, bf16[512,512]{1,0:T(8,128)(2,1)S(1)}, u32[]{:S(2)}, u32[]{:S(2)}) collective-permute-start(bf16[512,512]{1,0:T(8,128)(2,1)S(1)} %get-tuple-element.24.refs_0_), channel_id=1, source_target_pairs={{0,2},{1,3},{2,4},{3,5},{4,6},{5,7},{8,10},{9,11},{10,12},{11,13},... | collective-permute-start | bytes 1572872 | tf_op jit(solution)/shard_map/ppermute | solution.py:38
  17.0 16.7 %collective-permute-start.4 = (bf16[512,512]{1,0:T(8,128)(2,1)S(1)}, bf16[512,512]{1,0:T(8,128)(2,1)S(1)}, u32[]{:S(2)}, u32[]{:S(2)}) collective-permute-start(bf16[512,512]{1,0:T(8,128)(2,1)S(1)} %get-tuple-element.24.refs_0_), channel_id=1, source_target_pairs={{2,0},{3,1},{4,2},{5,3},{6,4},{7,5},{10,8},{11,9},{12,10},{13,11},... | collective-permute-start | bytes 1572872 | tf_op jit(solution)/shard_map/ppermute | solution.py:39
  23.7 21.2 %collective-permute-start.19 = (bf16[512,512]{1,0:T(8,128)(2,1)S(1)}, bf16[512,512]{1,0:T(8,128)(2,1)}, u32[]{:S(2)}, u32[]{:S(2)}) collective-permute-start(bf16[512,512]{1,0:T(8,128)(2,1)S(1)} %collective-permute-done.17.refs_2_), channel_id=1, source_target_pairs={{2,0},{3,1},{4,2},{5,3},{10,8},{11,9},{12,10},{13,11},{18,16},{19,... | collective-permute-start | bytes 1572872 | tf_op jit(solution)/shard_map/ppermute | solution.py:39
  28.6 16.3 %collective-permute-start.23 = (bf16[512,512]{1,0:T(8,128)(2,1)S(1)}, bf16[512,512]{1,0:T(8,128)(2,1)S(1)}, u32[]{:S(2)}, u32[]{:S(2)}) collective-permute-start(bf16[512,512]{1,0:T(8,128)(2,1)S(1)} %collective-permute-done.16.refs_1_), channel_id=1, source_target_pairs={{0,1},{1,0},{2,3},{3,2},{4,5},{5,4},{6,7},{7,6},{8,9},{9,8},{10,11... | collective-permute-start | bytes 1572872 | tf_op jit(solution)/shard_map/ppermute | solution.py:31
  34.5 22.0 %collective-permute-start.6 = (bf16[512,512]{1,0:T(8,128)(2,1)S(1)}, bf16[512,512]{1,0:T(8,128)(2,1)S(1)}, u32[]{:S(2)}, u32[]{:S(2)}) collective-permute-start(bf16[512,512]{1,0:T(8,128)(2,1)S(1)} %collective-permute-done.4.refs_2_), channel_id=1, source_target_pairs={{2,0},{3,1},{4,2},{5,3},{10,8},{11,9},{12,10},{13,11},{18,16},{19,... | collective-permute-start | bytes 1572872 | tf_op jit(solution)/shard_map/ppermute | solution.py:39
  44.9 19.0 %collective-permute-start.11 = (bf16[512,512]{1,0:T(8,128)(2,1)S(1)}, bf16[512,512]{1,0:T(8,128)(2,1)}, u32[]{:S(2)}, u32[]{:S(2)}) collective-permute-start(bf16[512,512]{1,0:T(8,128)(2,1)S(1)} %collective-permute-done.4.refs_2_), channel_id=1, source_target_pairs={{0,1},{1,0},{2,3},{3,2},{4,5},{5,4},{6,7},{7,6},{8,9},{9,8},{10,11... | collective-permute-start | bytes 1572872 | tf_op jit(solution)/shard_map/ppermute | solution.py:31
  45.5 26.3 %collective-permute-start.20 = (bf16[512,512]{1,0:T(8,128)(2,1)}, bf16[512,512]{1,0:T(8,128)(2,1)}, u32[]{:S(2)}, u32[]{:S(2)}) collective-permute-start(bf16[512,512]{1,0:T(8,128)(2,1)} %collective-permute-done.18.refs_3_), channel_id=1, source_target_pairs={{4,6},{5,7},{12,14},{13,15},{20,22},{21,23},{28,30},{29,31}} | collective-permute-start | bytes 1572872 | tf_op jit(solution)/shard_map/ppermute | solution.py:38
  46.9 25.2 %collective-permute-start.21 = (bf16[512,512]{1,0:T(8,128)(2,1)}, bf16[512,512]{1,0:T(8,128)(2,1)}, u32[]{:S(2)}, u32[]{:S(2)}) collective-permute-start(bf16[512,512]{1,0:T(8,128)(2,1)} %collective-permute-done.19.refs_4_), channel_id=1, source_target_pairs={{2,0},{3,1},{10,8},{11,9},{18,16},{19,17},{26,24},{27,25}} | collective-permute-start | bytes 1572872 | tf_op jit(solution)/shard_map/ppermute | solution.py:39
  56.5 17.0 %collective-permute-start.25 = (bf16[512,512]{1,0:T(8,128)(2,1)}, bf16[512,512]{1,0:T(8,128)(2,1)}, u32[]{:S(2)}, u32[]{:S(2)}) collective-permute-start(bf16[512,512]{1,0:T(8,128)(2,1)} %collective-permute-done.18.refs_3_), channel_id=1, source_target_pairs={{0,1},{1,0},{2,3},{3,2},{4,5},{5,4},{6,7},{7,6},{8,9},{9,8},{10,11... | collective-permute-start | bytes 1572872 | tf_op jit(solution)/shard_map/ppermute | solution.py:31
  56.5 17.2 %collective-permute-start.26 = (bf16[512,512]{1,0:T(8,128)(2,1)}, bf16[512,512]{1,0:T(8,128)(2,1)}, u32[]{:S(2)}, u32[]{:S(2)}) collective-permute-start(bf16[512,512]{1,0:T(8,128)(2,1)} %collective-permute-done.19.refs_4_), channel_id=1, source_target_pairs={{0,1},{1,0},{2,3},{3,2},{4,5},{5,4},{6,7},{7,6},{8,9},{9,8},{10,11... | collective-permute-start | bytes 1572872 | tf_op jit(solution)/shard_map/ppermute | solution.py:31
  71.8 127.6 %collective-permute-start.35 = (bf16[512,4,512]{2,0,1:T(8,128)(2,1)}, bf16[512,4,512]{2,0,1:T(8,128)(2,1)}, u32[]{:S(2)}, u32[]{:S(2)}) collective-permute-start(bf16[512,4,512]{2,0,1:T(8,128)(2,1)} %bitcast.73), channel_id=1, source_target_pairs={{0,1},{1,0},{2,3},{3,2},{4,5},{5,4},{6,7},{7,6},{8,9},{9,8},{10,11... | collective-permute-start | bytes 6291464 | tf_op jit(solution)/shard_map/ppermute | solution.py:31
  75.3 29.5 %collective-permute-start.12 = (bf16[512,512]{1,0:T(8,128)(2,1)S(1)}, bf16[512,512]{1,0:T(8,128)(2,1)S(1)}, u32[]{:S(2)}, u32[]{:S(2)}) collective-permute-start(bf16[512,512]{1,0:T(8,128)(2,1)S(1)} %copy-done.9), channel_id=1, source_target_pairs={{0,1},{1,0},{2,3},{3,2},{4,5},{5,4},{6,7},{7,6},{8,9},{9,8},{10,11... | collective-permute-start | bytes 1572872 | tf_op jit(solution)/shard_map/ppermute | solution.py:31
  88.0 24.8 %collective-permute-start.13 = (bf16[512,512]{1,0:T(8,128)(2,1)S(1)}, bf16[512,512]{1,0:T(8,128)(2,1)S(1)}, u32[]{:S(2)}, u32[]{:S(2)}) collective-permute-start(bf16[512,512]{1,0:T(8,128)(2,1)S(1)} %copy-done.12), channel_id=1, source_target_pairs={{0,1},{1,0},{2,3},{3,2},{4,5},{5,4},{6,7},{7,6},{8,9},{9,8},{10,11... | collective-permute-start | bytes 1572872 | tf_op jit(solution)/shard_map/ppermute | solution.py:31
  88.0 28.2 %collective-permute-start.14 = (bf16[512,512]{1,0:T(8,128)(2,1)}, bf16[512,512]{1,0:T(8,128)(2,1)S(1)}, u32[]{:S(2)}, u32[]{:S(2)}) collective-permute-start(bf16[512,512]{1,0:T(8,128)(2,1)} %collective-permute-done.7.refs_5_), channel_id=1, source_target_pairs={{0,1},{1,0},{2,3},{3,2},{4,5},{5,4},{6,7},{7,6},{8,9},{9,8},{10,11... | collective-permute-start | bytes 1572872 | tf_op jit(solution)/shard_map/ppermute | solution.py:31
  88.5 29.0 %collective-permute-start.15 = (bf16[512,512]{1,0:T(8,128)(2,1)S(1)}, bf16[512,512]{1,0:T(8,128)(2,1)}, u32[]{:S(2)}, u32[]{:S(2)}) collective-permute-start(bf16[512,512]{1,0:T(8,128)(2,1)S(1)} %collective-permute-done.8.refs_6_), channel_id=1, source_target_pairs={{0,1},{1,0},{2,3},{3,2},{4,5},{5,4},{6,7},{7,6},{8,9},{9,8},{10,11... | collective-permute-start | bytes 1572872 | tf_op jit(solution)/shard_map/ppermute | solution.py:31
  104.9 43.0 %collective-permute-start.30 = (bf16[64,512]{1,0:T(8,128)(2,1)S(1)}, bf16[64,512]{1,0:T(8,128)(2,1)S(1)}, u32[]{:S(2)}, u32[]{:S(2)}) collective-permute-start(bf16[64,512]{1,0:T(8,128)(2,1)S(1)} %slice.55), channel_id=1, source_target_pairs={{0,8},{8,16},{16,24},{1,9},{9,17},{17,25},{2,10},{10,18},{18,26},{... | collective-permute-start | bytes 196616 | tf_op jit(solution)/shard_map/ppermute | solution.py:374
  112.8 32.4 %collective-permute-start.1 = (f32[64]{0:T(128)S(1)}, f32[64]{0:T(128)S(1)}, u32[]{:S(2)}, u32[]{:S(2)}) collective-permute-start(f32[64]{0:T(128)S(1)} %slice_add_fusion), channel_id=1, source_target_pairs={{0,16},{8,24},{1,17},{9,25},{2,18},{10,26},{3,19},{11,27},{4,20},{... | collective-permute-start | bytes 776 | tf_op jit(solution)/shard_map/ppermute | solution.py:341
  116.2 30.3 %collective-permute-start.2 = (f32[64]{0:T(128)S(1)}, f32[64]{0:T(128)S(1)}, u32[]{:S(2)}, u32[]{:S(2)}) collective-permute-start(f32[64]{0:T(128)S(1)} %slice_add_fusion), channel_id=1, source_target_pairs={{0,24},{1,25},{2,26},{3,27},{4,28},{5,29},{6,30},{7,31}} | collective-permute-start | bytes 776 | tf_op jit(solution)/shard_map/ppermute | solution.py:341
  131.6 54.2 %collective-permute-start.31 = (bf16[4,160,128]{2,1,0:T(8,128)(2,1)}, bf16[4,160,128]{2,1,0:T(8,128)(2,1)S(1)}, u32[]{:S(2)}, u32[]{:S(2)}) collective-permute-start(bf16[4,160,128]{2,1,0:T(8,128)(2,1)} %shard_map.106), channel_id=1, source_target_pairs={{0,8},{8,16},{16,24},{1,9},{9,17},{17,25},{2,10},{10,18},{18,26},{... | collective-permute-start | bytes 491528 | tf_op jit(solution)/shard_map/ppermute | solution.py:382
  145.2 40.6 %collective-permute-start.32 = (bf16[4,160,128]{2,1,0:T(8,128)(2,1)S(1)}, bf16[4,160,128]{2,1,0:T(8,128)(2,1)S(1)}, u32[]{:S(2)}, u32[]{:S(2)}) collective-permute-start(bf16[4,160,128]{2,1,0:T(8,128)(2,1)S(1)} %copy-done.23), channel_id=1, source_target_pairs={{0,16},{8,24},{1,17},{9,25},{2,18},{10,26},{3,19},{11,27},{4,20},{... | collective-permute-start | bytes 491528 | tf_op jit(solution)/shard_map/ppermute | solution.py:382
  146.5 39.3 %collective-permute-start.33 = (bf16[4,160,128]{2,1,0:T(8,128)(2,1)S(1)}, bf16[4,160,128]{2,1,0:T(8,128)(2,1)S(1)}, u32[]{:S(2)}, u32[]{:S(2)}) collective-permute-start(bf16[4,160,128]{2,1,0:T(8,128)(2,1)S(1)} %copy-done.23), channel_id=1, source_target_pairs={{0,24},{1,25},{2,26},{3,27},{4,28},{5,29},{6,30},{7,31}} | collective-permute-start | bytes 491528 | tf_op jit(solution)/shard_map/ppermute | solution.py:382
  147.8 18.6 %collective-permute-start.29 = (bf16[64,1024]{1,0:T(8,128)(2,1)S(1)}, bf16[64,1024]{1,0:T(8,128)(2,1)S(1)}, u32[]{:S(2)}, u32[]{:S(2)}) collective-permute-start(bf16[64,1024]{1,0:T(8,128)(2,1)S(1)} %slice.61), channel_id=1, source_target_pairs={{0,8},{8,16},{16,24},{1,9},{9,17},{17,25},{2,10},{10,18},{18,26},{... | collective-permute-start | bytes 393224 | tf_op jit(solution)/shard_map/ppermute | solution.py:374
  204.9 16.7 %collective-permute-start.39 = (bf16[512,512]{1,0:T(8,128)(2,1)S(1)}, bf16[512,512]{1,0:T(8,128)(2,1)S(1)}, u32[]{:S(2)}, u32[]{:S(2)}) collective-permute-start(bf16[512,512]{1,0:T(8,128)(2,1)S(1)} %convolution_convert_fusion.2), channel_id=1, source_target_pairs={{6,4},{7,5},{14,12},{15,13},{22,20},{23,21},{30,28},{31,29}} | collective-permute-start | bytes 1572872 | tf_op jit(solution)/shard_map/ppermute | solution.py:410
  207.4 19.2 %collective-permute-start.43 = (bf16[512,512]{1,0:T(8,128)(2,1)S(1)}, bf16[512,512]{1,0:T(8,128)(2,1)S(1)}, u32[]{:S(2)}, u32[]{:S(2)}) collective-permute-start(bf16[512,512]{1,0:T(8,128)(2,1)S(1)} %convolution_convert_fusion.1), channel_id=1, source_target_pairs={{0,2},{1,3},{8,10},{9,11},{16,18},{17,19},{24,26},{25,27}} | collective-permute-start | bytes 1572872 | tf_op jit(solution)/shard_map/ppermute | solution.py:405
  210.5 22.2 %collective-permute-start.46 = (bf16[512,512]{1,0:T(8,128)(2,1)S(1)}, bf16[512,512]{1,0:T(8,128)(2,1)S(1)}, u32[]{:S(2)}, u32[]{:S(2)}) collective-permute-start(bf16[512,512]{1,0:T(8,128)(2,1)S(1)} %convolution_convert_fusion), channel_id=1, source_target_pairs={{6,4},{7,5},{14,12},{15,13},{22,20},{23,21},{30,28},{31,29}} | collective-permute-start | bytes 1572872 | tf_op jit(solution)/shard_map/ppermute | solution.py:410
  217.1 20.7 %collective-permute-start.37 = (bf16[512,512]{1,0:T(8,128)(2,1)S(1)}, bf16[512,512]{1,0:T(8,128)(2,1)S(1)}, u32[]{:S(2)}, u32[]{:S(2)}) collective-permute-start(bf16[512,512]{1,0:T(8,128)(2,1)S(1)} %fusion.3), channel_id=1, source_target_pairs={{0,2},{1,3},{2,4},{3,5},{8,10},{9,11},{10,12},{11,13},{16,18},{17,... | collective-permute-start | bytes 1572872 | tf_op jit(solution)/shard_map/ppermute | solution.py:405
  223.3 22.3 %collective-permute-start.40 = (bf16[512,512]{1,0:T(8,128)(2,1)S(1)}, bf16[512,512]{1,0:T(8,128)(2,1)S(1)}, u32[]{:S(2)}, u32[]{:S(2)}) collective-permute-start(bf16[512,512]{1,0:T(8,128)(2,1)S(1)} %fusion.5), channel_id=1, source_target_pairs={{4,2},{5,3},{6,4},{7,5},{12,10},{13,11},{14,12},{15,13},{20,18},{2... | collective-permute-start | bytes 1572872 | tf_op jit(solution)/shard_map/ppermute | solution.py:410
  228.3 21.1 %collective-permute-start.44 = (bf16[512,512]{1,0:T(8,128)(2,1)S(1)}, bf16[512,512]{1,0:T(8,128)(2,1)S(1)}, u32[]{:S(2)}, u32[]{:S(2)}) collective-permute-start(bf16[512,512]{1,0:T(8,128)(2,1)S(1)} %fusion.7), channel_id=1, source_target_pairs={{0,2},{1,3},{2,4},{3,5},{8,10},{9,11},{10,12},{11,13},{16,18},{17,... | collective-permute-start | bytes 1572872 | tf_op jit(solution)/shard_map/ppermute | solution.py:405
  234.5 22.8 %collective-permute-start.47 = (bf16[512,512]{1,0:T(8,128)(2,1)S(1)}, bf16[512,512]{1,0:T(8,128)(2,1)S(1)}, u32[]{:S(2)}, u32[]{:S(2)}) collective-permute-start(bf16[512,512]{1,0:T(8,128)(2,1)S(1)} %fusion.9), channel_id=1, source_target_pairs={{4,2},{5,3},{6,4},{7,5},{12,10},{13,11},{14,12},{15,13},{20,18},{2... | collective-permute-start | bytes 1572872 | tf_op jit(solution)/shard_map/ppermute | solution.py:410
  240.3 20.8 %collective-permute-start.38 = (bf16[512,512]{1,0:T(8,128)(2,1)}, bf16[512,512]{1,0:T(8,128)(2,1)}, u32[]{:S(2)}, u32[]{:S(2)}) collective-permute-start(bf16[512,512]{1,0:T(8,128)(2,1)} %fusion.2), channel_id=1, source_target_pairs={{0,2},{1,3},{2,4},{3,5},{4,6},{5,7},{8,10},{9,11},{10,12},{11,13},... | collective-permute-start | bytes 1572872 | tf_op jit(solution)/shard_map/ppermute | solution.py:405
  251.9 18.9 %collective-permute-start.45 = (bf16[512,512]{1,0:T(8,128)(2,1)}, bf16[512,512]{1,0:T(8,128)(2,1)}, u32[]{:S(2)}, u32[]{:S(2)}) collective-permute-start(bf16[512,512]{1,0:T(8,128)(2,1)} %fusion.6), channel_id=1, source_target_pairs={{0,2},{1,3},{2,4},{3,5},{4,6},{5,7},{8,10},{9,11},{10,12},{11,13},... | collective-permute-start | bytes 1572872 | tf_op jit(solution)/shard_map/ppermute | solution.py:405
  (44 other events, 709.9 us)

commit v2 on v0

v2 whole, which is shorter than its diff:
```python
import functools

import jax
import jax.numpy as jnp
import numpy as np
from jax import lax
from jax.experimental import pallas as pl
from jax.experimental.pallas import tpu as pltpu
from jax.sharding import PartitionSpec as P

HEAD_DIM = 128
FEAT = 16
WIN = 64
PAIRS = [(i, j) for i in range(FEAT) for j in range(i, FEAT)]
WIDE = 256
CHUNK = 256
GROUP = 2
STATE = -(-(len(PAIRS) + FEAT + 1) // 16) * 16
VMEM = 60 * 1024 * 1024
F32 = jnp.float32
BF16 = jnp.bfloat16


def params():
    return pltpu.CompilerParams(vmem_limit_bytes=VMEM, dimension_semantics=("arbitrary",))


def line(count, step, sources):
    return [(2 * z + c, 2 * (z + step) + c) for z in sources for c in (0, 1) if 0 <= z + step < count]


def swap(x, count):
    return lax.ppermute(x, "head", [(h, h ^ 1) for h in range(2 * count)])


def project_kernel(parts, first, last, place, mine, theirs, *refs):
    weights, before = refs[:parts], refs[parts : 2 * parts] if first else ()
    outs, sums = refs[-2 * parts : -parts], refs[-parts:]
    width = mine.shape[1]
    step = pl.program_id(0)

    @pl.when(step == 0)
    def _():
        for n in range(parts):
            sums[n][...] = before[n][...] if first else jnp.zeros_like(sums[n])

    c = place[1]
    own = pl.ds(pl.multiple_of(c * width, width), width)
    other = pl.ds(pl.multiple_of((1 - c) * width, width), width)
    for n in range(parts):
        sums[n][...] += jnp.dot(mine[...], weights[n][own, :], preferred_element_type=F32)
        sums[n][...] += jnp.dot(theirs[...], weights[n][other, :], preferred_element_type=F32)

    @pl.when(step == pl.num_programs(0) - 1)
    def _():
        for n in range(parts):
            outs[n][...] = sums[n][...].astype(outs[n].dtype)


def project(place, chips, mine, theirs, weights, before=None, dtype=BF16):
    rows = mine.shape[0]
    width = mine.shape[1] // len(chips)
    count = weights[0].shape[0] // (2 * width)
    if len(chips) == 1:
        pick = lambda j, p: p[0] + chips[0]
    else:
        early = chips == (0, 1, count - 1)
        pick = lambda j, p: p[0] + (jnp.where(j == 2, count - 1, j) if early else j + chips[0])
    piece = pl.BlockSpec((rows, width), lambda j, p: (0, j))
    specs = [piece, piece]
    specs += [
        pl.BlockSpec((2 * width, w.shape[1]), lambda j, p: (lax.rem(pick(j, p), count), 0))
        for w in weights
    ]
    wholes = [pl.BlockSpec((rows, w.shape[1]), lambda j, p: (0, 0)) for w in weights]
    args = [mine, theirs, *weights]
    if before is not None:
        specs += wholes
        args += list(before)
    return pl.pallas_call(
        functools.partial(project_kernel, len(weights), before is not None, dtype == BF16),
        grid_spec=pltpu.PrefetchScalarGridSpec(
            num_scalar_prefetch=1,
            grid=(len(chips),),
            in_specs=specs,
            out_specs=wholes,
            scratch_shapes=[pltpu.VMEM((rows, w.shape[1]), F32) for w in weights],
        ),
        out_shape=[jax.ShapeDtypeStruct((rows, w.shape[1]), dtype) for w in weights],
        compiler_params=params(),
    )(place, *args)


def expansions(heads):
    lanes = heads * 2 * FEAT
    maps = np.zeros((2, heads, lanes, 2 * WIDE), np.float32)
    rows = np.zeros((3, WIDE), np.float32)
    for h in range(heads):
        for side in (0, 1):
            base = h * 2 * FEAT + side * FEAT
            for n, (i, j) in enumerate(PAIRS):
                maps[side, h, base + i, n] = 1.0
                maps[side, h, base + j, WIDE + n] = 1.0
            for i in range(FEAT):
                maps[side, h, base + i, len(PAIRS) + i] = 1.0
    for n, (i, j) in enumerate(PAIRS):
        rows[2, n] = (2.0 * FEAT) ** -0.5 * (1.0 if i == j else 2.0**0.5)
    rows[1, len(PAIRS) : len(PAIRS) + FEAT + 1] = 1.0
    rows[0, len(PAIRS) + FEAT] = 1.0
    rows[2, len(PAIRS) : len(PAIRS) + FEAT] = FEAT**-0.25
    rows[2, len(PAIRS) + FEAT] = 1.0
    return maps.astype(jnp.bfloat16), rows


def picks(heads):
    lanes = heads * 2 * FEAT
    maps = np.zeros((heads, lanes, 256), np.float32)
    for h in range(heads):
        for i in range(FEAT):
            maps[h, h * 2 * FEAT + i, i] = 1.0
            maps[h, h * 2 * FEAT + FEAT + i, 128 + i] = 1.0
    return maps.astype(jnp.bfloat16)


def phi(features, expand, rows):
    factors = jnp.dot(features, expand, preferred_element_type=F32)
    left = factors[:, :WIDE] + rows[0:1]
    right = factors[:, WIDE:] + rows[1:2]
    return (left * right * rows[2:3]).astype(BF16)


def chunk_sums(limits, start, features, values, expand, rows, heads):
    sums = []
    for n in range(features.shape[0] // CHUNK):
        here = slice(n * CHUNK, (n + 1) * CHUNK)
        at = lax.broadcasted_iota(jnp.int32, (CHUNK, HEAD_DIM), 0) + (start + n) * CHUNK
        good = at >= limits[start + n]
        one = []
        for h in range(heads):
            phi_key = phi(features[here], expand[h], rows[...])
            kept = jnp.where(good, values[here, h * HEAD_DIM : (h + 1) * HEAD_DIM].astype(F32), 0.0)
            one.append(
                lax.dot_general(
                    phi_key, kept.astype(BF16), (((0,), (0,)), ((), ())), preferred_element_type=F32
                )[:STATE]
            )
        sums.append(one)
    return sums


def high_sums_kernel(start, limits, features, values, expand, rows, out):
    heads = out.shape[1]
    for n, one in enumerate(chunk_sums(limits, start, features, values, expand, rows, heads)):
        for h in range(heads):
            out[n, h] = one[h]


def low_sums_kernel(limits, features, values, expand, rows, high, prefix, end):
    heads = high.shape[1]
    low = chunk_sums(limits, 0, features, values, expand, rows, heads)
    for h in range(heads):
        state = jnp.zeros((STATE, HEAD_DIM), F32)
        for n in range(len(low) + high.shape[0]):
            prefix[n, h] = state
            chunk = low[n][h] if n < len(low) else high[n - len(low), h]
            state = chunk + jnp.where(limits[n] <= n * CHUNK, state, 0.0)
        end[h] = state.astype(BF16)


def sums(limits, features, values, expand, rows, high=None):
    count, columns = values.shape
    heads = columns // HEAD_DIM
    chunks = count // CHUNK
    shape = jax.ShapeDtypeStruct((chunks, heads, STATE, HEAD_DIM), F32)
    vmem = pl.BlockSpec(memory_space=pltpu.VMEM)
    smem = pl.BlockSpec(memory_space=pltpu.SMEM)
    if high is None:
        return pl.pallas_call(
            functools.partial(high_sums_kernel, chunks),
            in_specs=[smem] + [vmem] * 4,
            out_specs=vmem,
            out_shape=shape,
            compiler_params=pltpu.CompilerParams(vmem_limit_bytes=VMEM),
        )(limits, features, values, expand, rows)
    return pl.pallas_call(
        low_sums_kernel,
        in_specs=[smem] + [vmem] * 5,
        out_specs=[vmem, vmem],
        out_shape=[
            jax.ShapeDtypeStruct((2 * chunks, heads, STATE, HEAD_DIM), F32),
            jax.ShapeDtypeStruct((heads, STATE, HEAD_DIM), BF16),
        ],
        compiler_params=pltpu.CompilerParams(vmem_limit_bytes=VMEM),
    )(limits, features, values, expand, rows, high)


TILE = 128


def window_tile(queries, keys, values, window_first, start):
    wide = TILE + WIN
    logits = lax.dot_general(
        queries, keys, (((1,), (1,)), ((), ())), preferred_element_type=F32
    ) * HEAD_DIM**-0.5
    at = lax.broadcasted_iota(jnp.int32, (TILE, wide), 1)
    row = lax.broadcasted_iota(jnp.int32, (TILE, wide), 0)
    good = (at >= window_first - start) & (at <= row + WIN)
    logits = jnp.where(good, logits, -1e30)
    top = jnp.max(logits, 1, keepdims=True)
    weight = jnp.where(good, jnp.exp(logits - top), 0.0)
    probs = (weight / jnp.sum(weight, 1, keepdims=True)).astype(BF16)
    return jnp.dot(probs, values, preferred_element_type=F32)


def local_kernel(low, features, values, window, bounds, pick, expand, rows, *refs):
    if low:
        tail_values, tail_window, next_values, next_window = refs[:4]
        inner, windowed, phi_query, next_windowed = refs[4:]
    else:
        inner, windowed, phi_query = refs
    half = features.shape[0]
    base = 0 if low else half
    for h in range(values.shape[1] // HEAD_DIM):
        column = slice(h * HEAD_DIM, (h + 1) * HEAD_DIM)
        query = slice(2 * h * HEAD_DIM, (2 * h + 1) * HEAD_DIM)
        key = slice((2 * h + 1) * HEAD_DIM, (2 * h + 2) * HEAD_DIM)
        phi_query[:, h * WIDE : (h + 1) * WIDE] = phi(features[...], expand[h], rows[...])
        for n in range(half // CHUNK):
            here = slice(n * CHUNK, (n + 1) * CHUNK)
            both = jnp.dot(features[here], pick[h], preferred_element_type=F32).astype(BF16)
            dots = lax.dot_general(
                both[:, :128], both[:, 128:], (((1,), (1,)), ((), ())), preferred_element_type=F32
            )
            score = dots * (dots * (0.5 / FEAT) + FEAT**-0.5) + 1.0
            at = lax.broadcasted_iota(jnp.int32, (CHUNK, CHUNK), 1)
            row = lax.broadcasted_iota(jnp.int32, (CHUNK, CHUNK), 0)
            first = bounds[base + n * CHUNK : base + (n + 1) * CHUNK, 0:1] - (base + n * CHUNK)
            score = jnp.where((at >= first) & (at <= row), score, 0.0).astype(BF16)
            inner[here, column] = jnp.dot(
                score, values[here, column], preferred_element_type=F32
            )
        for n in range(half // TILE):
            here = slice(n * TILE, (n + 1) * TILE)
            near = slice(n * TILE - WIN, (n + 1) * TILE)
            start = base + n * TILE - WIN
            first = bounds[base + n * TILE : base + (n + 1) * TILE, 1:2]
            if n:
                keys, vals = window[near, key], values[near, column]
            elif low:
                keys = jnp.concatenate([tail_window[:, key], window[:TILE, key]], 0)
                vals = jnp.concatenate([tail_values[:, column], values[:TILE, column]], 0)
            else:
                continue
            windowed[here, column] = window_tile(window[here, query], keys, vals, first, start)
        if low:
            keys = jnp.concatenate([window[half - WIN :, key], next_window[:, key]], 0)
            vals = jnp.concatenate([values[half - WIN :, column], next_values[:, column]], 0)
            first = bounds[half : half + TILE, 1:2]
            next_windowed[:, column] = window_tile(
                next_window[:, query], keys, vals, first, half - WIN
            )


def local(low, features, values, window, bounds, pick, expand, rows, tails=(), after=()):
    half, columns = values.shape
    heads = columns // HEAD_DIM
    group = min(GROUP, heads)

    def full(a):
        return pl.BlockSpec(a.shape, lambda g: (0,) * a.ndim)

    def some(count, width):
        return pl.BlockSpec((count, group * width), lambda g: (0, g))

    def per_head(a):
        return pl.BlockSpec((group,) + a.shape[1:], lambda g: (g, 0, 0))

    specs = [
        full(features), some(half, HEAD_DIM), some(half, 2 * HEAD_DIM), full(bounds),
        per_head(pick), per_head(expand), full(rows),
    ]
    out_specs = [some(half, HEAD_DIM), some(half, HEAD_DIM), some(half, WIDE)]
    shapes = [
        jax.ShapeDtypeStruct((half, columns), F32),
        jax.ShapeDtypeStruct((half, columns), F32),
        jax.ShapeDtypeStruct((half, heads * WIDE), BF16),
    ]
    if low:
        specs += [
            some(WIN, HEAD_DIM), some(WIN, 2 * HEAD_DIM), some(TILE, HEAD_DIM), some(TILE, 2 * HEAD_DIM)
        ]
        out_specs.append(some(TILE, HEAD_DIM))
        shapes.append(jax.ShapeDtypeStruct((TILE, columns), F32))
    return pl.pallas_call(
        functools.partial(local_kernel, low),
        grid=(heads // group,),
        in_specs=specs,
        out_specs=out_specs,
        out_shape=shapes,
        compiler_params=params(),
    )(features, values, window, bounds, pick, expand, rows, *tails, *after)


def finish_kernel(start, shifts, limits, chosen, phi_query, bounds, inner, windowed, prefix, *refs):
    states, out = refs[:shifts], refs[-1]
    head_first = refs[shifts] if len(refs) == shifts + 2 else None
    for h in range(inner.shape[1] // HEAD_DIM):
        column = slice(h * HEAD_DIM, (h + 1) * HEAD_DIM)
        incoming = jnp.zeros((STATE, HEAD_DIM), F32)
        for k in range(shifts):
            incoming += jnp.where(chosen[k] > 0, states[k][h].astype(F32), 0.0)
        for n in range(inner.shape[0] // CHUNK):
            here = slice(n * CHUNK, (n + 1) * CHUNK)
            chunk = start + n
            state = incoming
            if chunk:
                state = jnp.where(limits[chunk - 1] <= 0, incoming, 0.0) + prefix[n, h]
            state = jnp.concatenate([state, jnp.zeros((WIDE - STATE, HEAD_DIM), F32)], 0)
            carried = jnp.dot(
                phi_query[here, h * WIDE : (h + 1) * WIDE], state.astype(BF16),
                preferred_element_type=F32,
            )
            first = bounds[chunk * CHUNK : (chunk + 1) * CHUNK, 0:1]
            linear = inner[here, column] + jnp.where(first <= chunk * CHUNK, carried, 0.0)
            mean = jnp.mean(linear * linear, 1, keepdims=True)
            normed = linear * lax.rsqrt(mean + 1e-5)
            if n == 0 and head_first is not None:
                out[:TILE, column] = (normed[:TILE] + head_first[:, column]).astype(BF16)
                out[TILE:CHUNK, column] = (normed[TILE:] + windowed[TILE:CHUNK, column]).astype(BF16)
            else:
                out[here, column] = (normed + windowed[here, column]).astype(BF16)


def finish(start, limits, chosen, phi_query, bounds, inner, windowed, prefix, states, head_first=None):
    half, columns = inner.shape
    heads = columns // HEAD_DIM
    group = min(GROUP, heads)
    chunks = half // CHUNK

    def some(count, width):
        return pl.BlockSpec((count, group * width), lambda g, *_: (0, g))

    specs = [
        some(half, WIDE), pl.BlockSpec(bounds.shape, lambda g, *_: (0, 0)),
        some(half, HEAD_DIM), some(half, HEAD_DIM),
        pl.BlockSpec((chunks, group, STATE, HEAD_DIM), lambda g, *_: (start // chunks, g, 0, 0)),
    ]
    specs += [pl.BlockSpec((group, STATE, HEAD_DIM), lambda g, *_: (g, 0, 0))] * len(states)
    args = [phi_query, bounds, inner, windowed, prefix, *states]
    if head_first is not None:
        specs.append(some(TILE, HEAD_DIM))
        args.append(head_first)
    return pl.pallas_call(
        functools.partial(finish_kernel, start, len(states)),
        grid_spec=pltpu.PrefetchScalarGridSpec(
            num_scalar_prefetch=2,
            grid=(heads // group,),
            in_specs=specs,
            out_specs=some(half, HEAD_DIM),
        ),
        out_shape=jax.ShapeDtypeStruct((half, columns), BF16),
        compiler_params=params(),
    )(limits, chosen, *args)


def output_kernel(received, place, mine, theirs, own_rows, other_rows, *refs):
    total = jnp.dot(mine[...], own_rows[...], preferred_element_type=F32)
    total += jnp.dot(theirs[...], other_rows[...], preferred_element_type=F32)
    for n in range(received):
        total += refs[n][...].astype(F32)
    refs[-1][...] = total.astype(BF16)


def output(where, mine, theirs, own_rows, other_rows, received):
    rows, depth = mine.shape
    width = other_rows.shape[2]
    tile = min(256, width)
    cuts = width // tile
    result = pl.BlockSpec((rows, tile), lambda j, p: (0, j))
    whole = pl.BlockSpec((rows, depth), lambda j, p: (0, 0))
    return pl.pallas_call(
        functools.partial(output_kernel, len(received)),
        grid_spec=pltpu.PrefetchScalarGridSpec(
            num_scalar_prefetch=1,
            grid=(cuts,),
            in_specs=[
                whole, whole,
                pl.BlockSpec((depth, tile), lambda j, p: (0, (2 * p[0] + p[1]) * cuts + j)),
                pl.BlockSpec((None, depth, tile), lambda j, p: (p[0], 0, j)),
            ] + [result] * len(received),
            out_specs=result,
        ),
        out_shape=jax.ShapeDtypeStruct((rows, width), BF16),
        compiler_params=params(),
    )(where, mine, theirs, own_rows, other_rows, *received)


def after(x, *others):
    return lax.optimization_barrier((x, *others))[0]


def shards(tokens, doc_ids, w_feat, w_value, w_window, w_out):
    rows = tokens.shape[0]
    half = rows // 2
    chunks = rows // CHUNK
    heads = w_value.shape[1] // HEAD_DIM
    count = lax.axis_size("head") // 2
    blocks = lax.axis_size("ctx")
    me = lax.axis_index("head")
    z, c = me // 2, me % 2
    place = jnp.stack([z, c]).astype(jnp.int32)

    def hop(x, step, sources):
        return lax.ppermute(x, "head", line(count, step, sources))

    def near(x):
        return hop(x, 1, range(count)), hop(x, -1, range(count))

    def far(x):
        return hop(x, count - 1, [0]), hop(x, 1 - count, [count - 1])

    def chain(up, down):
        ups, downs = [up], [down]
        for s in range(2, count - 1):
            ups.append(hop(ups[-1], 1, range(s - 1, count)))
            downs.append(hop(downs[-1], -1, range(0, count - s + 1)))
        return ups, downs

    def early_pieces(x, up, down, far_up, far_down):
        mine = jnp.concatenate([x, down + far_up, far_down + up], 1)
        return mine, swap(mine, count)

    def late_pieces(ups, downs):
        mine = jnp.concatenate(
            [downs[s - 1] + ups[count - s - 1] for s in range(2, count - 1)], 1
        )
        return mine, swap(mine, count)

    high, low = tokens[half:], tokens[:half]
    high_near = near(high)
    high_far = far(high)

    docs = doc_ids.astype(F32)
    doc_tails = [
        lax.ppermute(docs[rows - WIN :] + 1.0, "ctx", [(i, i + k) for i in range(blocks - k)])
        for k in range(1, blocks)
    ]
    chosen = jnp.stack([t[WIN - 1] == docs[0] + 1.0 for t in doc_tails]).astype(jnp.int32)
    first = jnp.sum((docs[None, :] < docs[:, None]).astype(F32), 1).astype(jnp.int32)
    in_tail = jnp.sum((doc_tails[0] == docs[0] + 1.0).astype(jnp.int32))
    at = jnp.arange(rows, dtype=jnp.int32)
    window_first = jnp.maximum(jnp.where(first == 0, -in_tail, first), at - (WIN - 1))
    bounds = jnp.stack([first, window_first], 1)
    limits = jnp.stack([first[min((n + 1) * CHUNK, rows - 1)] for n in range(chunks)])

    maps, scale_rows = expansions(heads)
    query_map, key_map = jnp.asarray(maps[0]), jnp.asarray(maps[1])
    scale_rows = jnp.asarray(scale_rows)
    pick = jnp.asarray(picks(heads))

    depth, columns = w_out.shape
    width = columns // (2 * count)
    other_rows = swap(
        jnp.stack(
            [
                lax.dynamic_slice(w_out, (0, (2 * chip + 1 - c) * width), (depth, width))
                for chip in range(count)
            ]
        ),
        count,
    )

    weights = (w_feat, w_value, w_window)
    early = (0, 1, count - 1)
    late = tuple(range(2, count - 1))

    high_ups, high_downs = chain(*high_near)
    low_far = far(after(low, *high_near))
    mine, theirs = early_pieces(high, *high_near, *high_far)
    part = project(place, early, mine, theirs, weights, None, F32)
    high_ups[-1], high_downs[-1], other_rows, bounds, chosen = lax.optimization_barrier(
        (high_ups[-1], high_downs[-1], other_rows, bounds, chosen, part[0])
    )[:5]
    low_near = near(after(low, high_ups[-1], high_downs[-1], other_rows, bounds, chosen))
    mine, theirs = late_pieces(high_ups, high_downs)
    feat_high, value_high, win_high = project(place, late, mine, theirs, weights, part)
    tail_win, tail_value = (
        lax.ppermute(a[half - WIN :], "ctx", [(i, i + 1) for i in range(blocks - 1)])
        for a in (win_high, value_high)
    )
    high_sums = sums(limits, feat_high, value_high, key_map, scale_rows)
    inner_high, windowed_high, phi_high = local(
        False, feat_high, value_high, win_high, bounds, pick, query_map, scale_rows
    )

    *low_near, far_up, far_down, tail_win, tail_value = lax.optimization_barrier(
        (*low_near, *low_far, tail_win, tail_value, inner_high, high_sums)
    )[:6]
    low_ups, low_downs = chain(*low_near)
    mine, theirs = early_pieces(low, *low_near, far_up, far_down)
    part = project(place, early, mine, theirs, weights, None, F32)
    low_ups[-1], low_downs[-1] = lax.optimization_barrier((low_ups[-1], low_downs[-1], part[0]))[:2]
    mine, theirs = late_pieces(low_ups, low_downs)
    feat_low, value_low = project(place, late, mine, theirs, weights[:2], part[:2])
    prefix, state = sums(limits, feat_low, value_low, key_map, scale_rows, high_sums)
    states = [
        lax.ppermute(state, "ctx", [(i, i + k) for i in range(blocks - k)])
        for k in range(1, blocks)
    ]
    (win_low,) = project(place, late, after(mine, state), theirs, weights[2:], part[2:])
    inner_low, windowed_low, phi_low, windowed_next = local(
        True, feat_low, value_low, win_low, bounds, pick, query_map, scale_rows,
        (tail_value, tail_win), (value_high, win_high),
    )
    mixed_high = finish(
        chunks // 2, limits, chosen, phi_high, bounds, inner_high, windowed_high, prefix, states,
        windowed_next,
    )
    mixed_low = finish(
        0, limits, chosen, phi_low, bounds, inner_low, windowed_low, prefix, states
    )

    outs = []
    for mixed in (mixed_low, mixed_high):
        swapped = swap(mixed, count)

        def part_of(chip, *received):
            where = jnp.stack([jnp.clip(chip, 0, count - 1), c]).astype(jnp.int32)
            return output(where, mixed, swapped, w_out, other_rows, received)

        up, down = (), ()
        for s in range(1, count):
            up = (hop(part_of(z + count - s, *up), 1, range(0, s)),)
            down = (hop(part_of(z - count + s, *down), -1, range(count - s, count)),)
        outs.append(part_of(z, *up, *down))
    return jnp.concatenate(outs, 0)


def solution(mesh):
    return jax.shard_map(
        shards,
        mesh=mesh,
        in_specs=(
            P("ctx", "head"),
            P("ctx"),
            P(None, "head"),
            P(None, "head"),
            P(None, "head"),
            P("head", None),
        ),
        out_specs=P("ctx", "head"),
        check_vma=False,
    )
```

time: 281 us -> 287 us (1.021)
  Pallas kernels: 0 us -> 133 us
  waiting for transfers between devices: 148 us -> 26.7 us
  matrix products: 75.5 us -> 0 us
  starting transfers between devices: 11.8 us -> 75.3 us
  other arithmetic: 10.1 us -> 23.2 us
  local copies, waits for them, and re-layouts: 12.5 us -> 22.6 us
  between operations: 13.3 us -> 3.99 us
  blocking collectives: 8.97 us -> 0 us
    pallas_call x0 -> x25, Pallas kernels: none -> 133 us  [the longest x14 53.7 us: output(): pl.pallas_call(functools.partial(output_kernel, len(received)), grid_spec...]
    reduce_scatter x1 -> x0, waiting for transfers between devices: 87.4 us -> none  [shards(): lax.psum_scatter(lax.dot_general(w_out, mixed, (((0,), (1,)), ((), ())),...]
    ppermute x3 -> x39, starting transfers between devices: 11.5 us -> 75.3 us  [the longest x24 56.9 us: hop(): return lax.ppermute(x, 'head', line(count, step, sources))]
    dot_general x9 -> x0, matrix products: 60.3 us -> none  [the longest x3 24.8 us: shards(): jnp.dot(column_piece, weight, preferred_element_type=jnp.float32)]
    all_gather x2 -> x0, waiting for transfers between devices: 60 us -> none  [the longest x1 60 us: shards(): column_piece = lax.all_gather(tokens, 'head', axis=1, tiled=True)]
    ppermute x3 -> x39, waiting for transfers between devices: 0.01 us -> 26.7 us  [the longest x24 24.4 us: hop(): return lax.ppermute(x, 'head', line(count, step, sources))]
    sub x1 -> x0, matrix products: 15.2 us -> none  [shards(): weights = jnp.exp(logits - top_logit) * within[None].astype(jnp.float32)]
    unnamed x1 -> x0, blocking collectives: 8.97 us -> none
  transfers between devices with their start and end apart: 6 -> 39, of which waited for: 2 -> 7; matrix products, arithmetic and copies ran while one was open for 23% -> 8% of each run, Pallas kernels for 0% -> 40%
where the time goes in v2:
time: 287 us; the launch traced here: 285 us
  Pallas kernels  133 us (46%)
  starting transfers between devices  75.3 us (26%)
  waiting for transfers between devices  26.7 us (9%)
  other arithmetic  23.2 us (8%)
  local copies, waits for them, and re-layouts  22.6 us (8%)
  between operations  3.99 us (1%)
    ppermute x24, starting transfers between devices, hop(): return lax.ppermute(x, 'head', line(count, step, sources))  56.9 us
    pallas_call x14, Pallas kernels, output(): pl.pallas_call(functools.partial(output_kernel, len(received)), grid_spec...  53.7 us
    pallas_call x5, Pallas kernels, project(): pl.pallas_call(functools.partial(project_kernel, len(weights), before is...  40.5 us
    ppermute x24, waiting for transfers between devices, hop(): return lax.ppermute(x, 'head', line(count, step, sources))  24.4 us
    pallas_call x2, Pallas kernels, local(): pl.pallas_call(functools.partial(local_kernel, low), grid=(heads // group...  20.4 us
    unnamed x56, local copies, waits for them, and re-layouts  14 us
    pallas_call x2, Pallas kernels, finish(): pl.pallas_call(functools.partial(finish_kernel, start, len(states)), grid...  8.73 us
    ppermute x3, starting transfers between devices, shards(): lax.ppermute(docs[rows - WIN:] + 1.0, 'ctx', [(i, i + k) for i in range(b...  8.1 us
  transfers between devices with their start and end apart: 39, of which 7 were waited for; matrix products, arithmetic and copies ran while one was open for 8% of the time, Pallas kernels for 40%

profile of v2, /device:TPU:0, one launch (start us, length us, event | category | flops | bytes accessed | tf_op | source)
XLA Modules:
  0.0 284.8 jit_solution(14480047970378690197)
XLA Ops:
  1.3 5.8 %collective-permute-start = (bf16[512,512]{1,0:T(8,128)(2,1)S(1)}, bf16[512,512]{1,0:T(8,128)(2,1)}, u32[]{:S(2)}, u32[]{:S(2)}) collective-permute-start(bf16[512,512]{1,0:T(8,128)(2,1)S(1)} %get-tuple-element.82), channel_id=1, source_target_pairs={{0,2},{1,3},{2,4},{3,5},{4,6},{5,7},{8,10},{9,11},{10,12},{11,13},... | collective-permute-start | bytes 1572872 | tf_op jit(solution)/shard_map/ppermute | solution.py:414
  9.6 8.7 %collective-permute-start.8 = (bf16[512,512]{1,0:T(8,128)(2,1)S(1)}, bf16[512,512]{1,0:T(8,128)(2,1)}, u32[]{:S(2)}, u32[]{:S(2)}) collective-permute-start(bf16[512,512]{1,0:T(8,128)(2,1)S(1)} %get-tuple-element.82), channel_id=1, source_target_pairs={{0,6},{1,7},{8,14},{9,15},{16,22},{17,23},{24,30},{25,31}} | collective-permute-start | bytes 1572872 | tf_op jit(solution)/shard_map/ppermute | solution.py:414
  21.6 4.0 %collective-permute-done.9 = bf16[512,512]{1,0:T(8,128)(2,1)} collective-permute-done((bf16[512,512]{1,0:T(8,128)(2,1)S(1)}, bf16[512,512]{1,0:T(8,128)(2,1)}, u32[]{:S(2)}, u32[]{:S(2)}) %collective-permute-start.9) | collective-permute-done | bytes 524320 | tf_op jit(solution)/shard_map/ppermute | solution.py:414
  27.0 7.9 %collective-permute-done.2 = bf16[512,512]{1,0:T(8,128)(2,1)} collective-permute-done((bf16[512,512]{1,0:T(8,128)(2,1)S(1)}, bf16[512,512]{1,0:T(8,128)(2,1)}, u32[]{:S(2)}, u32[]{:S(2)}) %collective-permute-start.2) | collective-permute-done | bytes 524320 | tf_op jit(solution)/shard_map/ppermute | solution.py:414
  55.9 11.8 %shard_map.100 = (f32[512,128]{1,0:T(8,128)}, f32[512,512]{1,0:T(8,128)}, f32[512,1024]{1,0:T(8,128)}) custom-call(s32[2]{0:T(128)} %pad_add_fusion.3.place, bf16[512,1536]{1,0:T(8,128)(2,1)} %pad_maximum_fusion.1.mine, bf16[512,1536]{1,0:T(8,128)(2,1)} %collective-permute-done.10.theirs, bf16[4096,128]{1,0:T(8,128)(2,1)} %refs_0_.8, ...), custom_call_target="tpu_custom_call" | custom-call | tf_op jit(solution)/shard_map/pallas_call | solution.py:80
  79.9 7.1 %shard_map.101 = (bf16[512,128]{1,0:T(8,128)(2,1)}, bf16[512,512]{1,0:T(8,128)(2,1)}, bf16[512,1024]{1,0:T(8,128)(2,1)}) custom-call(s32[2]{0:T(128)} %pad_add_fusion.3.place, bf16[512,512]{1,0:T(8,128)(2,1)} %copy-done.7, bf16[512,512]{1,0:T(8,128)(2,1)} %copy-done.24, bf16[4096,128]{1,0:T(8,128)(2,1)} %refs_0_.8, bf16[4096,512]{1,0:T(8,128)(2,1)} %refs_1_.7, ...), custom_call_target="tpu_custom_call" | custom-call | tf_op jit(solution)/shard_map/pallas_call | solution.py:80
  97.7 4.6 %shard_map.103.high = f32[2,4,160,128]{3,2,1,0:T(8,128)} custom-call(s32[4]{0:T(128)} %pad_add_fusion.2.limits, bf16[512,128]{1,0:T(8,128)(2,1)} %get-tuple-element.53.features, bf16[512,512]{1,0:T(8,128)(2,1)} %get-tuple-element.52.values.refs_2_, bf16[4,128,512]{2,1,0:T(8,128)(2,1)} %constant.73.clone.expand, f32[3,256]{1,0:T(4,128)} %constant.74.clone.rows), custom_call_target="tpu_custom_call" | custom-call | tf_op jit(solution)/shard_map/pallas_call | solution.py:178
  102.3 8.6 %shard_map.102 = (f32[512,512]{1,0:T(8,128)}, f32[512,512]{1,0:T(8,128)}, bf16[512,1024]{1,0:T(8,128)(2,1)}) custom-call(bf16[512,128]{1,0:T(8,128)(2,1)} %get-tuple-element.53.features, bf16[512,512]{1,0:T(8,128)(2,1)} %get-tuple-element.52.values.refs_2_, bf16[512,1024]{1,0:T(8,128)(2,1)} %get-tuple-element.51.window.refs_3_, s32[1024,2]{1,0:T(8,128)} %copy.18.bounds, ...), custom_call_target="tpu_custom_call" | custom-call | tf_op jit(solution)/shard_map/pallas_call | solution.py:294
  118.4 11.7 %shard_map.104 = (f32[512,128]{1,0:T(8,128)}, f32[512,512]{1,0:T(8,128)}, f32[512,1024]{1,0:T(8,128)}) custom-call(s32[2]{0:T(128)} %pad_add_fusion.3.place, bf16[512,1536]{1,0:T(8,128)(2,1)} %copy-done.3, bf16[512,1536]{1,0:T(8,128)(2,1)} %copy-done.8, bf16[4096,128]{1,0:T(8,128)(2,1)} %refs_0_.8, bf16[4096,512]{1,0:T(8,128)(2,1)} %refs_1_.7, ...), custom_call_target="tpu_custom_call" | custom-call | tf_op jit(solution)/shard_map/pallas_call | solution.py:80
  130.1 6.8 %collective-permute-done.19 = bf16[512,512]{1,0:T(8,128)(2,1)} collective-permute-done((bf16[512,512]{1,0:T(8,128)(2,1)}, bf16[512,512]{1,0:T(8,128)(2,1)}, u32[]{:S(2)}, u32[]{:S(2)}) %collective-permute-start.19) | collective-permute-done | bytes 524320 | tf_op jit(solution)/shard_map/ppermute | solution.py:414
  141.0 4.5 %shard_map.105 = (bf16[512,128]{1,0:T(8,128)(2,1)}, bf16[512,512]{1,0:T(8,128)(2,1)}) custom-call(s32[2]{0:T(128)} %pad_add_fusion.3.place, bf16[512,512]{1,0:T(8,128)(2,1)} %copy-done.4, bf16[512,512]{1,0:T(8,128)(2,1)} %copy-done.6, bf16[4096,128]{1,0:T(8,128)(2,1)} %refs_0_.8, bf16[4096,512]{1,0:T(8,128)(2,1)} %refs_1_.7, ...), custom_call_target="tpu_custom_call" | custom-call | tf_op jit(solution)/shard_map/pallas_call | solution.py:80
  145.5 5.1 %shard_map.106 = (f32[4,4,160,128]{3,2,1,0:T(8,128)}, bf16[4,160,128]{2,1,0:T(8,128)(2,1)}) custom-call(s32[4]{0:T(128)} %pad_add_fusion.2.limits, bf16[512,128]{1,0:T(8,128)(2,1)} %get-tuple-element.63.features, bf16[512,512]{1,0:T(8,128)(2,1)} %get-tuple-element.64.values, bf16[4,128,512]{2,1,0:T(8,128)(2,1)} %constant.73.clone.expand, ...), custom_call_target="tpu_custom_call" | custom-call | tf_op jit(solution)/shard_map/pallas_call | solution.py:185
  155.9 5.5 %shard_map.107.window = bf16[512,1024]{1,0:T(8,128)(2,1)} custom-call(s32[2]{0:T(128)} %pad_add_fusion.3.place, bf16[512,512]{1,0:T(8,128)(2,1)} %copy-done.4, bf16[512,512]{1,0:T(8,128)(2,1)} %copy-done.6, bf16[4096,1024]{1,0:T(8,128)(2,1)} %refs_0_.9, f32[512,1024]{1,0:T(8,128)} %get-tuple-element.67.refs_1_), custom_call_target="tpu_custom_call" | custom-call | tf_op jit(solution)/shard_map/pallas_call | solution.py:80
  161.4 11.8 %shard_map.108 = (f32[512,512]{1,0:T(8,128)}, f32[512,512]{1,0:T(8,128)}, bf16[512,1024]{1,0:T(8,128)(2,1)}, f32[128,512]{1,0:T(8,128)}) custom-call(bf16[512,128]{1,0:T(8,128)(2,1)} %get-tuple-element.63.features, bf16[512,512]{1,0:T(8,128)(2,1)} %get-tuple-element.64.values, bf16[512,1024]{1,0:T(8,128)(2,1)} %shard_map.107.window, s32[1024,2]{1,0:T(8,128)} %copy.18.bounds, ...), custom_call_target="tpu_custom_call" | custom-call | tf_op jit(solution)/shard_map/pallas_call | solution.py:294
  174.0 4.3 %shard_map.109.mine = bf16[512,512]{1,0:T(8,128)(2,1)} custom-call(s32[4]{0:T(128)} %pad_add_fusion.2.limits, s32[3]{0:T(128)} %add_convert_fusion.chosen, bf16[512,1024]{1,0:T(8,128)(2,1)} %get-tuple-element.70.phi_query, s32[1024,2]{1,0:T(8,128)} %copy.18.bounds, f32[512,512]{1,0:T(8,128)} %get-tuple-element.71.inner, ...), custom_call_target="tpu_custom_call" | custom-call | tf_op jit(solution)/shard_map/pallas_call | solution.py:353
  178.3 4.4 %shard_map.117.mine = bf16[512,512]{1,0:T(8,128)(2,1)} custom-call(s32[4]{0:T(128)} %pad_add_fusion.2.limits, s32[3]{0:T(128)} %add_convert_fusion.chosen, bf16[512,1024]{1,0:T(8,128)(2,1)} %get-tuple-element.74.phi_query, s32[1024,2]{1,0:T(8,128)} %copy.18.bounds, f32[512,512]{1,0:T(8,128)} %get-tuple-element.54.inner, ...), custom_call_target="tpu_custom_call" | custom-call | tf_op jit(solution)/shard_map/pallas_call | solution.py:353
  184.6 3.7 %shard_map.113 = bf16[512,512]{1,0:T(8,128)(2,1)} custom-call(s32[2]{0:T(128)} %pad_add_fusion.9.place, bf16[512,512]{1,0:T(8,128)(2,1)} %shard_map.109.mine, bf16[512,512]{1,0:T(8,128)(2,1)} %copy-done.1, bf16[512,4096]{1,0:T(8,128)(2,1)} %own_rows.27, bf16[4,512,512]{2,1,0:T(8,128)(2,1)} %copy-done), custom_call_target="tpu_custom_call" | custom-call | tf_op jit(solution)/shard_map/pallas_call | solution.py:381
  197.5 3.7 %shard_map.121 = bf16[512,512]{1,0:T(8,128)(2,1)} custom-call(s32[2]{0:T(128)} %pad_add_fusion.9.place, bf16[512,512]{1,0:T(8,128)(2,1)} %shard_map.117.mine, bf16[512,512]{1,0:T(8,128)(2,1)} %copy-done.2, bf16[512,4096]{1,0:T(8,128)(2,1)} %own_rows.27, bf16[4,512,512]{2,1,0:T(8,128)(2,1)} %copy-done), custom_call_target="tpu_custom_call" | custom-call | tf_op jit(solution)/shard_map/pallas_call | solution.py:381
  209.3 3.9 %shard_map.114 = bf16[512,512]{1,0:T(8,128)(2,1)} custom-call(s32[2]{0:T(128)} %pad_add_fusion.8.place, bf16[512,512]{1,0:T(8,128)(2,1)} %shard_map.109.mine, bf16[512,512]{1,0:T(8,128)(2,1)} %copy-done.1, bf16[512,4096]{1,0:T(8,128)(2,1)} %own_rows.27, bf16[4,512,512]{2,1,0:T(8,128)(2,1)} %copy-done, bf16[512,512]{1,0:T(8,128)(2,1)} %copy-done.21), custom_call_target="tpu_custom_call" | custom-call | tf_op jit(solution)/shard_map/pallas_call | solution.py:381
  214.7 3.9 %shard_map.111 = bf16[512,512]{1,0:T(8,128)(2,1)} custom-call(s32[2]{0:T(128)} %pad_add_fusion.5.place, bf16[512,512]{1,0:T(8,128)(2,1)} %shard_map.109.mine, bf16[512,512]{1,0:T(8,128)(2,1)} %copy-done.1, bf16[512,4096]{1,0:T(8,128)(2,1)} %own_rows.27, bf16[4,512,512]{2,1,0:T(8,128)(2,1)} %copy-done, bf16[512,512]{1,0:T(8,128)(2,1)} %copy-done.19), custom_call_target="tpu_custom_call" | custom-call | tf_op jit(solution)/shard_map/pallas_call | solution.py:381
  221.2 3.9 %shard_map.122 = bf16[512,512]{1,0:T(8,128)(2,1)} custom-call(s32[2]{0:T(128)} %pad_add_fusion.8.place, bf16[512,512]{1,0:T(8,128)(2,1)} %shard_map.117.mine, bf16[512,512]{1,0:T(8,128)(2,1)} %copy-done.2, bf16[512,4096]{1,0:T(8,128)(2,1)} %own_rows.27, bf16[4,512,512]{2,1,0:T(8,128)(2,1)} %copy-done, bf16[512,512]{1,0:T(8,128)(2,1)} %copy-done.18), custom_call_target="tpu_custom_call" | custom-call | tf_op jit(solution)/shard_map/pallas_call | solution.py:381
  226.6 3.9 %shard_map.119 = bf16[512,512]{1,0:T(8,128)(2,1)} custom-call(s32[2]{0:T(128)} %pad_add_fusion.5.place, bf16[512,512]{1,0:T(8,128)(2,1)} %shard_map.117.mine, bf16[512,512]{1,0:T(8,128)(2,1)} %copy-done.2, bf16[512,4096]{1,0:T(8,128)(2,1)} %own_rows.27, bf16[4,512,512]{2,1,0:T(8,128)(2,1)} %copy-done, bf16[512,512]{1,0:T(8,128)(2,1)} %copy-done.14), custom_call_target="tpu_custom_call" | custom-call | tf_op jit(solution)/shard_map/pallas_call | solution.py:381
  230.5 5.1 %collective-permute-start.34 = (bf16[512,512]{1,0:T(8,128)(2,1)}, bf16[512,512]{1,0:T(8,128)(2,1)S(1)}, u32[]{:S(2)}, u32[]{:S(2)}) collective-permute-start(bf16[512,512]{1,0:T(8,128)(2,1)} %shard_map.119), channel_id=1, source_target_pairs={{0,2},{1,3},{2,4},{3,5},{8,10},{9,11},{10,12},{11,13},{16,18},{17,... | collective-permute-start | bytes 1572872 | tf_op jit(solution)/shard_map/ppermute | solution.py:414
  237.7 3.9 %shard_map.115 = bf16[512,512]{1,0:T(8,128)(2,1)} custom-call(s32[2]{0:T(128)} %pad_add_fusion.7.place, bf16[512,512]{1,0:T(8,128)(2,1)} %shard_map.109.mine, bf16[512,512]{1,0:T(8,128)(2,1)} %copy-done.1, bf16[512,4096]{1,0:T(8,128)(2,1)} %own_rows.27, bf16[4,512,512]{2,1,0:T(8,128)(2,1)} %copy-done, bf16[512,512]{1,0:T(8,128)(2,1)} %copy-done.12), custom_call_target="tpu_custom_call" | custom-call | tf_op jit(solution)/shard_map/pallas_call | solution.py:381
  243.7 3.9 %shard_map.112 = bf16[512,512]{1,0:T(8,128)(2,1)} custom-call(s32[2]{0:T(128)} %pad_add_fusion.4.place, bf16[512,512]{1,0:T(8,128)(2,1)} %shard_map.109.mine, bf16[512,512]{1,0:T(8,128)(2,1)} %copy-done.1, bf16[512,4096]{1,0:T(8,128)(2,1)} %own_rows.27, bf16[4,512,512]{2,1,0:T(8,128)(2,1)} %copy-done, bf16[512,512]{1,0:T(8,128)(2,1)} %copy-done.13), custom_call_target="tpu_custom_call" | custom-call | tf_op jit(solution)/shard_map/pallas_call | solution.py:381
  247.6 5.2 %collective-permute-start.28 = (bf16[512,512]{1,0:T(8,128)(2,1)}, bf16[512,512]{1,0:T(8,128)(2,1)S(1)}, u32[]{:S(2)}, u32[]{:S(2)}) collective-permute-start(bf16[512,512]{1,0:T(8,128)(2,1)} %shard_map.112), channel_id=1, source_target_pairs={{0,2},{1,3},{2,4},{3,5},{4,6},{5,7},{8,10},{9,11},{10,12},{11,13},... | collective-permute-start | bytes 1572872 | tf_op jit(solution)/shard_map/ppermute | solution.py:414
  253.6 3.9 %shard_map.123 = bf16[512,512]{1,0:T(8,128)(2,1)} custom-call(s32[2]{0:T(128)} %pad_add_fusion.7.place, bf16[512,512]{1,0:T(8,128)(2,1)} %shard_map.117.mine, bf16[512,512]{1,0:T(8,128)(2,1)} %copy-done.2, bf16[512,4096]{1,0:T(8,128)(2,1)} %own_rows.27, bf16[4,512,512]{2,1,0:T(8,128)(2,1)} %copy-done, bf16[512,512]{1,0:T(8,128)(2,1)} %copy-done.15), custom_call_target="tpu_custom_call" | custom-call | tf_op jit(solution)/shard_map/pallas_call | solution.py:381
  259.5 3.9 %shard_map.120 = bf16[512,512]{1,0:T(8,128)(2,1)} custom-call(s32[2]{0:T(128)} %pad_add_fusion.4.place, bf16[512,512]{1,0:T(8,128)(2,1)} %shard_map.117.mine, bf16[512,512]{1,0:T(8,128)(2,1)} %copy-done.2, bf16[512,4096]{1,0:T(8,128)(2,1)} %own_rows.27, bf16[4,512,512]{2,1,0:T(8,128)(2,1)} %copy-done, bf16[512,512]{1,0:T(8,128)(2,1)} %copy-done.16), custom_call_target="tpu_custom_call" | custom-call | tf_op jit(solution)/shard_map/pallas_call | solution.py:381
  263.4 4.6 %collective-permute-start.35 = (bf16[512,512]{1,0:T(8,128)(2,1)}, bf16[512,512]{1,0:T(8,128)(2,1)S(1)}, u32[]{:S(2)}, u32[]{:S(2)}) collective-permute-start(bf16[512,512]{1,0:T(8,128)(2,1)} %shard_map.120), channel_id=1, source_target_pairs={{0,2},{1,3},{2,4},{3,5},{4,6},{5,7},{8,10},{9,11},{10,12},{11,13},... | collective-permute-start | bytes 1572872 | tf_op jit(solution)/shard_map/ppermute | solution.py:414
  270.3 3.9 %shard_map.116 = bf16[512,512]{1,0:T(8,128)(2,1)} custom-call(s32[2]{0:T(128)} %pad_add_fusion.1.place, bf16[512,512]{1,0:T(8,128)(2,1)} %shard_map.109.mine, bf16[512,512]{1,0:T(8,128)(2,1)} %copy-done.1, bf16[512,4096]{1,0:T(8,128)(2,1)} %own_rows.27, bf16[4,512,512]{2,1,0:T(8,128)(2,1)} %copy-done, bf16[512,512]{1,0:T(8,128)(2,1)} %copy-done.22, ...), custom_call_target="tpu_custom_call" | custom-call | tf_op jit(solution)/shard_map/pallas_call | solution.py:381
  274.2 3.7 %collective-permute-done.35.refs_0_ = bf16[512,512]{1,0:T(8,128)(2,1)S(1)} collective-permute-done((bf16[512,512]{1,0:T(8,128)(2,1)}, bf16[512,512]{1,0:T(8,128)(2,1)S(1)}, u32[]{:S(2)}, u32[]{:S(2)}) %collective-permute-start.35) | collective-permute-done | bytes 524320 | tf_op jit(solution)/shard_map/ppermute | solution.py:414
  278.7 4.0 %shard_map.124 = bf16[512,512]{1,0:T(8,128)(2,1)} custom-call(s32[2]{0:T(128)} %pad_add_fusion.1.place, bf16[512,512]{1,0:T(8,128)(2,1)} %shard_map.117.mine, bf16[512,512]{1,0:T(8,128)(2,1)} %copy-done.2, bf16[512,4096]{1,0:T(8,128)(2,1)} %own_rows.27, bf16[4,512,512]{2,1,0:T(8,128)(2,1)} %copy-done, bf16[512,512]{1,0:T(8,128)(2,1)} %copy-done.23, ...), custom_call_target="tpu_custom_call" | custom-call | tf_op jit(solution)/shard_map/pallas_call | solution.py:381
  (164 shorter events, 103.3 us)
Async XLA Ops:
  1.3 20.4 %collective-permute-start = (bf16[512,512]{1,0:T(8,128)(2,1)S(1)}, bf16[512,512]{1,0:T(8,128)(2,1)}, u32[]{:S(2)}, u32[]{:S(2)}) collective-permute-start(bf16[512,512]{1,0:T(8,128)(2,1)S(1)} %get-tuple-element.82), channel_id=1, source_target_pairs={{0,2},{1,3},{2,4},{3,5},{4,6},{5,7},{8,10},{9,11},{10,12},{11,13},... | collective-permute-start | bytes 1572872 | tf_op jit(solution)/shard_map/ppermute | solution.py:414
  7.0 18.6 %collective-permute-start.9 = (bf16[512,512]{1,0:T(8,128)(2,1)S(1)}, bf16[512,512]{1,0:T(8,128)(2,1)}, u32[]{:S(2)}, u32[]{:S(2)}) collective-permute-start(bf16[512,512]{1,0:T(8,128)(2,1)S(1)} %get-tuple-element.82), channel_id=1, source_target_pairs={{6,0},{7,1},{14,8},{15,9},{22,16},{23,17},{30,24},{31,25}} | collective-permute-start | bytes 1572872 | tf_op jit(solution)/shard_map/ppermute | solution.py:414
  8.3 26.6 %collective-permute-start.2 = (bf16[512,512]{1,0:T(8,128)(2,1)S(1)}, bf16[512,512]{1,0:T(8,128)(2,1)}, u32[]{:S(2)}, u32[]{:S(2)}) collective-permute-start(bf16[512,512]{1,0:T(8,128)(2,1)S(1)} %get-tuple-element.82), channel_id=1, source_target_pairs={{2,0},{3,1},{4,2},{5,3},{6,4},{7,5},{10,8},{11,9},{12,10},{13,11},... | collective-permute-start | bytes 1572872 | tf_op jit(solution)/shard_map/ppermute | solution.py:414
  9.6 25.3 %collective-permute-start.8 = (bf16[512,512]{1,0:T(8,128)(2,1)S(1)}, bf16[512,512]{1,0:T(8,128)(2,1)}, u32[]{:S(2)}, u32[]{:S(2)}) collective-permute-start(bf16[512,512]{1,0:T(8,128)(2,1)S(1)} %get-tuple-element.82), channel_id=1, source_target_pairs={{0,6},{1,7},{8,14},{9,15},{16,22},{17,23},{24,30},{25,31}} | collective-permute-start | bytes 1572872 | tf_op jit(solution)/shard_map/ppermute | solution.py:414
  21.6 47.9 %collective-permute-start.4 = (bf16[4,512,512]{2,1,0:T(8,128)(2,1)}, bf16[4,512,512]{2,1,0:T(8,128)(2,1)S(1)}, u32[]{:S(2)}, u32[]{:S(2)}) collective-permute-start(bf16[4,512,512]{2,1,0:T(8,128)(2,1)} %pad_maximum_fusion), channel_id=1, source_target_pairs={{0,1},{1,0},{2,3},{3,2},{4,5},{5,4},{6,7},{7,6},{8,9},{9,8},{10,11... | collective-permute-start | bytes 6291464 | tf_op jit(solution)/shard_map/ppermute | solution.py:33
  37.6 18.3 %collective-permute-start.10 = (bf16[512,1536]{1,0:T(8,128)(2,1)}, bf16[512,1536]{1,0:T(8,128)(2,1)}, u32[]{:S(2)}, u32[]{:S(2)}) collective-permute-start(bf16[512,1536]{1,0:T(8,128)(2,1)} %pad_maximum_fusion.1.mine), channel_id=1, source_target_pairs={{0,1},{1,0},{2,3},{3,2},{4,5},{5,4},{6,7},{7,6},{8,9},{9,8},{10,11... | collective-permute-start | bytes 4718600 | tf_op jit(solution)/shard_map/ppermute | solution.py:33
  52.0 15.7 %collective-permute-start.1 = (bf16[512,512]{1,0:T(8,128)(2,1)}, bf16[512,512]{1,0:T(8,128)(2,1)S(1)}, u32[]{:S(2)}, u32[]{:S(2)}) collective-permute-start(bf16[512,512]{1,0:T(8,128)(2,1)} %collective-permute-done), channel_id=1, source_target_pairs={{2,4},{3,5},{4,6},{5,7},{10,12},{11,13},{12,14},{13,15},{18,20},{1... | collective-permute-start | bytes 1572872 | tf_op jit(solution)/shard_map/ppermute | solution.py:414
  52.7 16.9 %collective-permute-start.3 = (bf16[512,512]{1,0:T(8,128)(2,1)}, bf16[512,512]{1,0:T(8,128)(2,1)}, u32[]{:S(2)}, u32[]{:S(2)}) collective-permute-start(bf16[512,512]{1,0:T(8,128)(2,1)} %collective-permute-done.2), channel_id=1, source_target_pairs={{2,0},{3,1},{4,2},{5,3},{10,8},{11,9},{12,10},{13,11},{18,16},{19,... | collective-permute-start | bytes 1572872 | tf_op jit(solution)/shard_map/ppermute | solution.py:414
  71.2 19.5 %collective-permute-start.13 = (bf16[512,512]{1,0:T(8,128)(2,1)S(1)}, bf16[512,512]{1,0:T(8,128)(2,1)}, u32[]{:S(2)}, u32[]{:S(2)}) collective-permute-start(bf16[512,512]{1,0:T(8,128)(2,1)S(1)} %get-tuple-element.48), channel_id=1, source_target_pairs={{0,6},{1,7},{8,14},{9,15},{16,22},{17,23},{24,30},{25,31}} | collective-permute-start | bytes 1572872 | tf_op jit(solution)/shard_map/ppermute | solution.py:414
  73.3 37.7 %collective-permute-start.14 = (bf16[512,512]{1,0:T(8,128)(2,1)S(1)}, bf16[512,512]{1,0:T(8,128)(2,1)}, u32[]{:S(2)}, u32[]{:S(2)}) collective-permute-start(bf16[512,512]{1,0:T(8,128)(2,1)S(1)} %get-tuple-element.48), channel_id=1, source_target_pairs={{6,0},{7,1},{14,8},{15,9},{22,16},{23,17},{30,24},{31,25}} | collective-permute-start | bytes 1572872 | tf_op jit(solution)/shard_map/ppermute | solution.py:414
  74.6 36.4 %collective-permute-start.11 = (bf16[512,512]{1,0:T(8,128)(2,1)S(1)}, bf16[512,512]{1,0:T(8,128)(2,1)S(1)}, u32[]{:S(2)}, u32[]{:S(2)}) collective-permute-start(bf16[512,512]{1,0:T(8,128)(2,1)S(1)} %get-tuple-element.48), channel_id=1, source_target_pairs={{0,2},{1,3},{2,4},{3,5},{4,6},{5,7},{8,10},{9,11},{10,12},{11,13},... | collective-permute-start | bytes 1572872 | tf_op jit(solution)/shard_map/ppermute | solution.py:414
  77.8 33.2 %collective-permute-start.12 = (bf16[512,512]{1,0:T(8,128)(2,1)S(1)}, bf16[512,512]{1,0:T(8,128)(2,1)}, u32[]{:S(2)}, u32[]{:S(2)}) collective-permute-start(bf16[512,512]{1,0:T(8,128)(2,1)S(1)} %get-tuple-element.48), channel_id=1, source_target_pairs={{2,0},{3,1},{4,2},{5,3},{6,4},{7,5},{10,8},{11,9},{12,10},{13,11},... | collective-permute-start | bytes 1572872 | tf_op jit(solution)/shard_map/ppermute | solution.py:414
  87.9 23.1 %collective-permute-start.16 = (bf16[64,1024]{1,0:T(8,128)(2,1)S(1)}, bf16[64,1024]{1,0:T(8,128)(2,1)S(1)}, u32[]{:S(2)}, u32[]{:S(2)}) collective-permute-start(bf16[64,1024]{1,0:T(8,128)(2,1)S(1)} %slice.55), channel_id=1, source_target_pairs={{0,8},{8,16},{16,24},{1,9},{9,17},{17,25},{2,10},{10,18},{18,26},{... | collective-permute-start | bytes 393224 | tf_op jit(solution)/shard_map/ppermute | solution.py:488
  90.7 20.3 %collective-permute-start.17 = (bf16[64,512]{1,0:T(8,128)(2,1)S(1)}, bf16[64,512]{1,0:T(8,128)(2,1)S(1)}, u32[]{:S(2)}, u32[]{:S(2)}) collective-permute-start(bf16[64,512]{1,0:T(8,128)(2,1)S(1)} %slice.56), channel_id=1, source_target_pairs={{0,8},{8,16},{16,24},{1,9},{9,17},{17,25},{2,10},{10,18},{18,26},{... | collective-permute-start | bytes 196616 | tf_op jit(solution)/shard_map/ppermute | solution.py:488
  113.8 16.3 %collective-permute-start.18 = (bf16[512,512]{1,0:T(8,128)(2,1)S(1)}, bf16[512,512]{1,0:T(8,128)(2,1)}, u32[]{:S(2)}, u32[]{:S(2)}) collective-permute-start(bf16[512,512]{1,0:T(8,128)(2,1)S(1)} %collective-permute-done.11), channel_id=1, source_target_pairs={{2,4},{3,5},{4,6},{5,7},{10,12},{11,13},{12,14},{13,15},{18,20},{1... | collective-permute-start | bytes 1572872 | tf_op jit(solution)/shard_map/ppermute | solution.py:414
  115.3 21.6 %collective-permute-start.19 = (bf16[512,512]{1,0:T(8,128)(2,1)}, bf16[512,512]{1,0:T(8,128)(2,1)}, u32[]{:S(2)}, u32[]{:S(2)}) collective-permute-start(bf16[512,512]{1,0:T(8,128)(2,1)} %collective-permute-done.12), channel_id=1, source_target_pairs={{2,0},{3,1},{4,2},{5,3},{10,8},{11,9},{12,10},{13,11},{18,16},{19,... | collective-permute-start | bytes 1572872 | tf_op jit(solution)/shard_map/ppermute | solution.py:414
  150.6 22.6 %collective-permute-start.22 = (bf16[4,160,128]{2,1,0:T(8,128)(2,1)}, bf16[4,160,128]{2,1,0:T(8,128)(2,1)S(1)}, u32[]{:S(2)}, u32[]{:S(2)}) collective-permute-start(bf16[4,160,128]{2,1,0:T(8,128)(2,1)} %get-tuple-element.65), channel_id=1, source_target_pairs={{0,8},{8,16},{16,24},{1,9},{9,17},{17,25},{2,10},{10,18},{18,26},{... | collective-permute-start | bytes 491528 | tf_op jit(solution)/shard_map/ppermute | solution.py:507
  153.3 19.9 %collective-permute-start.23 = (bf16[4,160,128]{2,1,0:T(8,128)(2,1)}, bf16[4,160,128]{2,1,0:T(8,128)(2,1)S(1)}, u32[]{:S(2)}, u32[]{:S(2)}) collective-permute-start(bf16[4,160,128]{2,1,0:T(8,128)(2,1)} %get-tuple-element.65), channel_id=1, source_target_pairs={{0,16},{8,24},{1,17},{9,25},{2,18},{10,26},{3,19},{11,27},{4,20},{... | collective-permute-start | bytes 491528 | tf_op jit(solution)/shard_map/ppermute | solution.py:507
  154.6 18.6 %collective-permute-start.24 = (bf16[4,160,128]{2,1,0:T(8,128)(2,1)}, bf16[4,160,128]{2,1,0:T(8,128)(2,1)S(1)}, u32[]{:S(2)}, u32[]{:S(2)}) collective-permute-start(bf16[4,160,128]{2,1,0:T(8,128)(2,1)} %get-tuple-element.65), channel_id=1, source_target_pairs={{0,24},{1,25},{2,26},{3,27},{4,28},{5,29},{6,30},{7,31}} | collective-permute-start | bytes 491528 | tf_op jit(solution)/shard_map/ppermute | solution.py:507
  182.7 14.0 %collective-permute-start.32 = (bf16[512,512]{1,0:T(8,128)(2,1)}, bf16[512,512]{1,0:T(8,128)(2,1)S(1)}, u32[]{:S(2)}, u32[]{:S(2)}) collective-permute-start(bf16[512,512]{1,0:T(8,128)(2,1)} %shard_map.117.mine), channel_id=1, source_target_pairs={{0,1},{1,0},{2,3},{3,2},{4,5},{5,4},{6,7},{7,6},{8,9},{9,8},{10,11... | collective-permute-start | bytes 1572872 | tf_op jit(solution)/shard_map/ppermute | solution.py:33
  188.3 20.2 %collective-permute-start.29 = (bf16[512,512]{1,0:T(8,128)(2,1)}, bf16[512,512]{1,0:T(8,128)(2,1)S(1)}, u32[]{:S(2)}, u32[]{:S(2)}) collective-permute-start(bf16[512,512]{1,0:T(8,128)(2,1)} %shard_map.113), channel_id=1, source_target_pairs={{6,4},{7,5},{14,12},{15,13},{22,20},{23,21},{30,28},{31,29}} | collective-permute-start | bytes 1572872 | tf_op jit(solution)/shard_map/ppermute | solution.py:414
  193.3 20.6 %collective-permute-start.26 = (bf16[512,512]{1,0:T(8,128)(2,1)}, bf16[512,512]{1,0:T(8,128)(2,1)S(1)}, u32[]{:S(2)}, u32[]{:S(2)}) collective-permute-start(bf16[512,512]{1,0:T(8,128)(2,1)} %shard_map.110), channel_id=1, source_target_pairs={{0,2},{1,3},{8,10},{9,11},{16,18},{17,19},{24,26},{25,27}} | collective-permute-start | bytes 1572872 | tf_op jit(solution)/shard_map/ppermute | solution.py:414
  201.3 19.1 %collective-permute-start.36 = (bf16[512,512]{1,0:T(8,128)(2,1)}, bf16[512,512]{1,0:T(8,128)(2,1)S(1)}, u32[]{:S(2)}, u32[]{:S(2)}) collective-permute-start(bf16[512,512]{1,0:T(8,128)(2,1)} %shard_map.121), channel_id=1, source_target_pairs={{6,4},{7,5},{14,12},{15,13},{22,20},{23,21},{30,28},{31,29}} | collective-permute-start | bytes 1572872 | tf_op jit(solution)/shard_map/ppermute | solution.py:414
  205.6 20.1 %collective-permute-start.33 = (bf16[512,512]{1,0:T(8,128)(2,1)}, bf16[512,512]{1,0:T(8,128)(2,1)S(1)}, u32[]{:S(2)}, u32[]{:S(2)}) collective-permute-start(bf16[512,512]{1,0:T(8,128)(2,1)} %shard_map.118), channel_id=1, source_target_pairs={{0,2},{1,3},{8,10},{9,11},{16,18},{17,19},{24,26},{25,27}} | collective-permute-start | bytes 1572872 | tf_op jit(solution)/shard_map/ppermute | solution.py:414
  213.2 23.7 %collective-permute-start.30 = (bf16[512,512]{1,0:T(8,128)(2,1)}, bf16[512,512]{1,0:T(8,128)(2,1)S(1)}, u32[]{:S(2)}, u32[]{:S(2)}) collective-permute-start(bf16[512,512]{1,0:T(8,128)(2,1)} %shard_map.114), channel_id=1, source_target_pairs={{4,2},{5,3},{6,4},{7,5},{12,10},{13,11},{14,12},{15,13},{20,18},{2... | collective-permute-start | bytes 1572872 | tf_op jit(solution)/shard_map/ppermute | solution.py:414
  218.5 24.3 %collective-permute-start.27 = (bf16[512,512]{1,0:T(8,128)(2,1)}, bf16[512,512]{1,0:T(8,128)(2,1)S(1)}, u32[]{:S(2)}, u32[]{:S(2)}) collective-permute-start(bf16[512,512]{1,0:T(8,128)(2,1)} %shard_map.111), channel_id=1, source_target_pairs={{0,2},{1,3},{2,4},{3,5},{8,10},{9,11},{10,12},{11,13},{16,18},{17,... | collective-permute-start | bytes 1572872 | tf_op jit(solution)/shard_map/ppermute | solution.py:414
  225.1 27.6 %collective-permute-start.37 = (bf16[512,512]{1,0:T(8,128)(2,1)}, bf16[512,512]{1,0:T(8,128)(2,1)S(1)}, u32[]{:S(2)}, u32[]{:S(2)}) collective-permute-start(bf16[512,512]{1,0:T(8,128)(2,1)} %shard_map.122), channel_id=1, source_target_pairs={{4,2},{5,3},{6,4},{7,5},{12,10},{13,11},{14,12},{15,13},{20,18},{2... | collective-permute-start | bytes 1572872 | tf_op jit(solution)/shard_map/ppermute | solution.py:414
  230.5 28.3 %collective-permute-start.34 = (bf16[512,512]{1,0:T(8,128)(2,1)}, bf16[512,512]{1,0:T(8,128)(2,1)S(1)}, u32[]{:S(2)}, u32[]{:S(2)}) collective-permute-start(bf16[512,512]{1,0:T(8,128)(2,1)} %shard_map.119), channel_id=1, source_target_pairs={{0,2},{1,3},{2,4},{3,5},{8,10},{9,11},{10,12},{11,13},{16,18},{17,... | collective-permute-start | bytes 1572872 | tf_op jit(solution)/shard_map/ppermute | solution.py:414
  241.6 27.1 %collective-permute-start.31 = (bf16[512,512]{1,0:T(8,128)(2,1)}, bf16[512,512]{1,0:T(8,128)(2,1)S(1)}, u32[]{:S(2)}, u32[]{:S(2)}) collective-permute-start(bf16[512,512]{1,0:T(8,128)(2,1)} %shard_map.115), channel_id=1, source_target_pairs={{2,0},{3,1},{4,2},{5,3},{6,4},{7,5},{10,8},{11,9},{12,10},{13,11},... | collective-permute-start | bytes 1572872 | tf_op jit(solution)/shard_map/ppermute | solution.py:414
  247.6 21.1 %collective-permute-start.28 = (bf16[512,512]{1,0:T(8,128)(2,1)}, bf16[512,512]{1,0:T(8,128)(2,1)S(1)}, u32[]{:S(2)}, u32[]{:S(2)}) collective-permute-start(bf16[512,512]{1,0:T(8,128)(2,1)} %shard_map.112), channel_id=1, source_target_pairs={{0,2},{1,3},{2,4},{3,5},{4,6},{5,7},{8,10},{9,11},{10,12},{11,13},... | collective-permute-start | bytes 1572872 | tf_op jit(solution)/shard_map/ppermute | solution.py:414
  257.4 16.8 %collective-permute-start.38 = (bf16[512,512]{1,0:T(8,128)(2,1)}, bf16[512,512]{1,0:T(8,128)(2,1)S(1)}, u32[]{:S(2)}, u32[]{:S(2)}) collective-permute-start(bf16[512,512]{1,0:T(8,128)(2,1)} %shard_map.123), channel_id=1, source_target_pairs={{2,0},{3,1},{4,2},{5,3},{6,4},{7,5},{10,8},{11,9},{12,10},{13,11},... | collective-permute-start | bytes 1572872 | tf_op jit(solution)/shard_map/ppermute | solution.py:414
  263.4 14.5 %collective-permute-start.35 = (bf16[512,512]{1,0:T(8,128)(2,1)}, bf16[512,512]{1,0:T(8,128)(2,1)S(1)}, u32[]{:S(2)}, u32[]{:S(2)}) collective-permute-start(bf16[512,512]{1,0:T(8,128)(2,1)} %shard_map.120), channel_id=1, source_target_pairs={{0,2},{1,3},{2,4},{3,5},{4,6},{5,7},{8,10},{9,11},{10,12},{11,13},... | collective-permute-start | bytes 1572872 | tf_op jit(solution)/shard_map/ppermute | solution.py:414
  (35 other events, 119.4 us)

commit v3 on v2

v3 whole, which is shorter than its diff:
```python
import functools

import jax
import jax.numpy as jnp
import numpy as np
from jax import lax
from jax.experimental import pallas as pl
from jax.experimental.pallas import tpu as pltpu
from jax.sharding import PartitionSpec as P

HEAD_DIM = 128
FEAT = 16
WIN = 64
PAIRS = [(i, j) for i in range(FEAT) for j in range(i, FEAT)]
WIDE = 256
CHUNK = 256
GROUP = 2
STATE = -(-(len(PAIRS) + FEAT + 1) // 16) * 16
VMEM = 60 * 1024 * 1024
F32 = jnp.float32
BF16 = jnp.bfloat16


def params():
    return pltpu.CompilerParams(vmem_limit_bytes=VMEM, dimension_semantics=("arbitrary",))


def line(count, step, sources):
    return [(2 * z + c, 2 * (z + step) + c) for z in sources for c in (0, 1) if 0 <= z + step < count]


def swap(x, count):
    return lax.ppermute(x, "head", [(h, h ^ 1) for h in range(2 * count)])


def project_kernel(parts, place, mine, theirs, mine_late, theirs_late, *refs):
    weights, outs = refs[:parts], refs[parts : 2 * parts]
    sums, both = refs[2 * parts : -1], refs[-1]
    width = mine.shape[1]
    step = pl.program_id(0)
    c = place[1]
    own = pl.ds(pl.multiple_of(c * width, width), width)
    other = pl.ds(pl.multiple_of((1 - c) * width, width), width)

    @pl.when(step < 3)
    def _():
        both[:, own] = mine[...]
        both[:, other] = theirs[...]

    @pl.when(step >= 3)
    def _():
        both[:, own] = mine_late[...]
        both[:, other] = theirs_late[...]

    @pl.when(step == 0)
    def _():
        for n in range(parts):
            sums[n][...] = jnp.dot(both[...], weights[n][...], preferred_element_type=F32)

    @pl.when(step > 0)
    def _():
        for n in range(parts):
            sums[n][...] += jnp.dot(both[...], weights[n][...], preferred_element_type=F32)

    @pl.when(step == pl.num_programs(0) - 1)
    def _():
        for n in range(parts):
            outs[n][...] = sums[n][...].astype(outs[n].dtype)


def project(place, early, late, weights):
    rows = early[0].shape[0]
    width = early[0].shape[1] // 3
    count = weights[0].shape[0] // (2 * width)

    def chip(j, p):
        away = jnp.where(j < 2, j, jnp.where(j == 2, count - 1, j - 1))
        return lax.rem(p[0] + away, count), 0

    piece = pl.BlockSpec((rows, width), lambda j, p: (0, jnp.minimum(j, 2)))
    later = pl.BlockSpec((rows, width), lambda j, p: (0, jnp.maximum(j - 3, 0)))
    return pl.pallas_call(
        functools.partial(project_kernel, len(weights)),
        grid_spec=pltpu.PrefetchScalarGridSpec(
            num_scalar_prefetch=1,
            grid=(count,),
            in_specs=[piece, piece, later, later]
            + [pl.BlockSpec((2 * width, w.shape[1]), chip) for w in weights],
            out_specs=[pl.BlockSpec((rows, w.shape[1]), lambda j, p: (0, 0)) for w in weights],
            scratch_shapes=[pltpu.VMEM((rows, w.shape[1]), F32) for w in weights]
            + [pltpu.VMEM((rows, 2 * width), BF16)],
        ),
        out_shape=[jax.ShapeDtypeStruct((rows, w.shape[1]), BF16) for w in weights],
        compiler_params=params(),
    )(place, *early, *late, *weights)


def expansions(heads):
    lanes = heads * 2 * FEAT
    maps = np.zeros((2, heads, lanes, 2 * WIDE), np.float32)
    rows = np.zeros((3, WIDE), np.float32)
    for h in range(heads):
        for side in (0, 1):
            base = h * 2 * FEAT + side * FEAT
            for n, (i, j) in enumerate(PAIRS):
                maps[side, h, base + i, n] = 1.0
                maps[side, h, base + j, WIDE + n] = 1.0
            for i in range(FEAT):
                maps[side, h, base + i, len(PAIRS) + i] = 1.0
    for n, (i, j) in enumerate(PAIRS):
        rows[2, n] = (2.0 * FEAT) ** -0.5 * (1.0 if i == j else 2.0**0.5)
    rows[1, len(PAIRS) : len(PAIRS) + FEAT + 1] = 1.0
    rows[0, len(PAIRS) + FEAT] = 1.0
    rows[2, len(PAIRS) : len(PAIRS) + FEAT] = FEAT**-0.25
    rows[2, len(PAIRS) + FEAT] = 1.0
    return maps.astype(jnp.bfloat16), rows


def picks(heads):
    lanes = heads * 2 * FEAT
    maps = np.zeros((heads, lanes, 256), np.float32)
    for h in range(heads):
        for i in range(FEAT):
            maps[h, h * 2 * FEAT + i, i] = 1.0
            maps[h, h * 2 * FEAT + FEAT + i, 128 + i] = 1.0
    return maps.astype(jnp.bfloat16)


def phi(features, expand, rows):
    factors = jnp.dot(features, expand, preferred_element_type=F32)
    left = factors[:, :WIDE] + rows[0:1]
    right = factors[:, WIDE:] + rows[1:2]
    return (left * right * rows[2:3]).astype(BF16)


def chunk_sums(limits, start, features, values, expand, rows, heads):
    sums = []
    for n in range(features.shape[0] // CHUNK):
        here = slice(n * CHUNK, (n + 1) * CHUNK)
        at = lax.broadcasted_iota(jnp.int32, (CHUNK, HEAD_DIM), 0) + (start + n) * CHUNK
        good = at >= limits[start + n]
        one = []
        for h in range(heads):
            phi_key = phi(features[here], expand[h], rows[...])
            kept = jnp.where(good, values[here, h * HEAD_DIM : (h + 1) * HEAD_DIM].astype(F32), 0.0)
            one.append(
                lax.dot_general(
                    phi_key, kept.astype(BF16), (((0,), (0,)), ((), ())), preferred_element_type=F32
                )[:STATE]
            )
        sums.append(one)
    return sums


def high_sums_kernel(start, limits, features, values, expand, rows, out):
    heads = out.shape[1]
    for n, one in enumerate(chunk_sums(limits, start, features, values, expand, rows, heads)):
        for h in range(heads):
            out[n, h] = one[h]


def low_sums_kernel(limits, features, values, expand, rows, high, prefix, end):
    mark = lax.broadcasted_iota(jnp.int32, (STATE, HEAD_DIM), 0) == STATE - 1
    heads = high.shape[1]
    low = chunk_sums(limits, 0, features, values, expand, rows, heads)
    for h in range(heads):
        state = jnp.zeros((STATE, HEAD_DIM), F32)
        for n in range(len(low) + high.shape[0]):
            prefix[n, h] = state
            chunk = low[n][h] if n < len(low) else high[n - len(low), h]
            state = chunk + jnp.where(limits[n] <= n * CHUNK, state, 0.0)
        end[h] = jnp.where(mark, (limits[2 * len(low)] + 1).astype(F32), state).astype(BF16)


def sums(limits, features, values, expand, rows, high=None):
    count, columns = values.shape
    heads = columns // HEAD_DIM
    chunks = count // CHUNK
    shape = jax.ShapeDtypeStruct((chunks, heads, STATE, HEAD_DIM), F32)
    vmem = pl.BlockSpec(memory_space=pltpu.VMEM)
    smem = pl.BlockSpec(memory_space=pltpu.SMEM)
    if high is None:
        return pl.pallas_call(
            functools.partial(high_sums_kernel, chunks),
            in_specs=[smem] + [vmem] * 4,
            out_specs=vmem,
            out_shape=shape,
            compiler_params=pltpu.CompilerParams(vmem_limit_bytes=VMEM),
        )(limits, features, values, expand, rows)
    return pl.pallas_call(
        low_sums_kernel,
        in_specs=[smem] + [vmem] * 5,
        out_specs=[vmem, vmem],
        out_shape=[
            jax.ShapeDtypeStruct((2 * chunks, heads, STATE, HEAD_DIM), F32),
            jax.ShapeDtypeStruct((heads, STATE, HEAD_DIM), BF16),
        ],
        compiler_params=pltpu.CompilerParams(vmem_limit_bytes=VMEM),
    )(limits, features, values, expand, rows, high)


TILE = 128


def windows(tiles):
    wide = TILE + WIN
    logits = jnp.concatenate(
        [
            lax.dot_general(q, k, (((1,), (1,)), ((), ())), preferred_element_type=F32)
            for q, k, _, _, _ in tiles
        ],
        0,
    )
    at = lax.broadcasted_iota(jnp.int32, (TILE, wide), 1)
    row = lax.broadcasted_iota(jnp.int32, (TILE, wide), 0)
    near = (at <= row + WIN) & (at > row)
    good = jnp.concatenate([near & (at >= first - start) for _, _, _, first, start in tiles], 0)
    logits = jnp.where(good, logits * HEAD_DIM**-0.5, -1e30)
    top = jnp.max(logits, 1, keepdims=True)
    weight = jnp.where(good, jnp.exp(logits - top), 0.0)
    probs = (weight / jnp.sum(weight, 1, keepdims=True)).astype(BF16)
    return [
        jnp.dot(probs[n * TILE : (n + 1) * TILE], tile[2], preferred_element_type=F32)
        for n, tile in enumerate(tiles)
    ]


def local_kernel(low, features, values, window, bounds, pick, expand, rows, *refs):
    if low:
        tail, tail_docs, first_doc, next_values, next_window = refs[:5]
        inner, windowed, phi_query, next_windowed = refs[5:]
        same = jnp.where(tail_docs[...].astype(F32) == first_doc[0:1, 0:1] + 1.0, 1.0, 0.0)
        in_tail = jnp.sum(same, 0, keepdims=True)[:, 0:1].astype(jnp.int32)
    else:
        inner, windowed, phi_query = refs
    half = features.shape[0]
    base = 0 if low else half
    chunks = half // CHUNK
    at = lax.broadcasted_iota(jnp.int32, (CHUNK, CHUNK), 1)
    row = lax.broadcasted_iota(jnp.int32, (CHUNK, CHUNK), 0)
    good = jnp.concatenate(
        [
            (at <= row) & (at >= bounds[base + n * CHUNK : base + (n + 1) * CHUNK] - (base + n * CHUNK))
            for n in range(chunks)
        ],
        0,
    )
    heads = values.shape[1] // HEAD_DIM
    for h in range(heads):
        column = slice(h * HEAD_DIM, (h + 1) * HEAD_DIM)
        query = slice(2 * h * HEAD_DIM, (2 * h + 1) * HEAD_DIM)
        key = slice((2 * h + 1) * HEAD_DIM, (2 * h + 2) * HEAD_DIM)
        both = jnp.dot(features[...], pick[h], preferred_element_type=F32).astype(BF16)
        dots = jnp.concatenate(
            [
                lax.dot_general(
                    both[n * CHUNK : (n + 1) * CHUNK, :128], both[n * CHUNK : (n + 1) * CHUNK, 128:],
                    (((1,), (1,)), ((), ())), preferred_element_type=F32,
                )
                for n in range(chunks)
            ],
            0,
        )
        tiles, targets = [], []
        for n in range(half // TILE):
            here = slice(n * TILE, (n + 1) * TILE)
            near = slice(n * TILE - WIN, (n + 1) * TILE)
            start = base + n * TILE - WIN
            first = bounds[base + n * TILE : base + (n + 1) * TILE]
            if n:
                keys, vals = window[near, key], values[near, column]
            elif low:
                skip = 2 * heads * HEAD_DIM
                keys = jnp.concatenate([tail[:, key], window[:TILE, key]], 0)
                vals = jnp.concatenate(
                    [tail[:, skip + h * HEAD_DIM : skip + (h + 1) * HEAD_DIM], values[:TILE, column]], 0
                )
                first = jnp.where(first == 0, -in_tail, first)
            else:
                continue
            tiles.append((window[here, query], keys, vals, first, start))
            targets.append((windowed, here))
        if low:
            keys = jnp.concatenate([window[half - WIN :, key], next_window[:, key]], 0)
            vals = jnp.concatenate([values[half - WIN :, column], next_values[:, column]], 0)
            first = bounds[half : half + TILE]
            tiles.append((next_window[:, query], keys, vals, first, half - WIN))
            targets.append((next_windowed, slice(0, TILE)))
        results = windows(tiles)
        score = dots * (dots * (0.5 / FEAT) + FEAT**-0.5) + 1.0
        score = jnp.where(good, score, 0.0).astype(BF16)
        phi_query[:, h * WIDE : (h + 1) * WIDE] = phi(features[...], expand[h], rows[...])
        for n in range(chunks):
            here = slice(n * CHUNK, (n + 1) * CHUNK)
            inner[here, column] = jnp.dot(
                score[here], values[here, column], preferred_element_type=F32
            )
        for (ref, here), result in zip(targets, results):
            ref[here, column] = result


def local(low, features, values, window, bounds, pick, expand, rows, tails=(), after=()):
    half, columns = values.shape
    heads = columns // HEAD_DIM
    group = min(GROUP, heads)

    def full(a):
        return pl.BlockSpec(a.shape, lambda g: (0,) * a.ndim)

    def some(count, width):
        return pl.BlockSpec((count, group * width), lambda g: (0, g))

    def per_head(a):
        return pl.BlockSpec((group,) + a.shape[1:], lambda g: (g, 0, 0))

    specs = [
        full(features), some(half, HEAD_DIM), some(half, 2 * HEAD_DIM), full(bounds),
        per_head(pick), per_head(expand), full(rows),
    ]
    out_specs = [some(half, HEAD_DIM), some(half, HEAD_DIM), some(half, WIDE)]
    shapes = [
        jax.ShapeDtypeStruct((half, columns), F32),
        jax.ShapeDtypeStruct((half, columns), F32),
        jax.ShapeDtypeStruct((half, heads * WIDE), BF16),
    ]
    if low:
        specs += [
            some(WIN, 3 * HEAD_DIM),
            pl.BlockSpec((WIN, HEAD_DIM), lambda g: (0, 3 * heads)),
            full(tails[-1]),
            some(TILE, HEAD_DIM), some(TILE, 2 * HEAD_DIM),
        ]
        out_specs.append(some(TILE, HEAD_DIM))
        shapes.append(jax.ShapeDtypeStruct((TILE, columns), F32))
    return pl.pallas_call(
        functools.partial(local_kernel, low),
        grid=(heads // group,),
        in_specs=specs,
        out_specs=out_specs,
        out_shape=shapes,
        compiler_params=params(),
    )(features, values, window, bounds, pick, expand, rows, *tails, *after)


def finish_kernel(start, shifts, limits, first_doc, phi_query, bounds, inner, windowed, prefix, *refs):
    states, out = refs[:shifts], refs[-1]
    head_first = refs[shifts] if len(refs) == shifts + 2 else None
    unmarked = lax.broadcasted_iota(jnp.int32, (STATE, HEAD_DIM), 0) < STATE - 1
    for h in range(inner.shape[1] // HEAD_DIM):
        column = slice(h * HEAD_DIM, (h + 1) * HEAD_DIM)
        incoming = jnp.zeros((STATE, HEAD_DIM), F32)
        for k in range(shifts):
            sent = states[k][h].astype(F32)
            wanted = (sent[STATE - 1 :] == first_doc[0:1, :] + 1.0) & unmarked
            incoming += jnp.where(wanted, sent, 0.0)
        for n in range(inner.shape[0] // CHUNK):
            here = slice(n * CHUNK, (n + 1) * CHUNK)
            chunk = start + n
            state = incoming
            if chunk:
                state = jnp.where(limits[chunk - 1] <= 0, incoming, 0.0) + prefix[n, h]
            state = jnp.concatenate([state, jnp.zeros((WIDE - STATE, HEAD_DIM), F32)], 0)
            carried = jnp.dot(
                phi_query[here, h * WIDE : (h + 1) * WIDE], state.astype(BF16),
                preferred_element_type=F32,
            )
            first = bounds[chunk * CHUNK : (chunk + 1) * CHUNK, 0:1]
            linear = inner[here, column] + jnp.where(first <= chunk * CHUNK, carried, 0.0)
            mean = jnp.mean(linear * linear, 1, keepdims=True)
            normed = linear * lax.rsqrt(mean + 1e-5)
            if n == 0 and head_first is not None:
                out[:TILE, column] = (normed[:TILE] + head_first[:, column]).astype(BF16)
                out[TILE:CHUNK, column] = (normed[TILE:] + windowed[TILE:CHUNK, column]).astype(BF16)
            else:
                out[here, column] = (normed + windowed[here, column]).astype(BF16)


def finish(start, limits, first_doc, phi_query, bounds, inner, windowed, prefix, states, head_first=None):
    half, columns = inner.shape
    heads = columns // HEAD_DIM
    group = min(GROUP, heads)
    chunks = half // CHUNK

    def some(count, width):
        return pl.BlockSpec((count, group * width), lambda g, *_: (0, g))

    specs = [
        pl.BlockSpec(first_doc.shape, lambda g, *_: (0, 0)),
        some(half, WIDE), pl.BlockSpec(bounds.shape, lambda g, *_: (0, 0)),
        some(half, HEAD_DIM), some(half, HEAD_DIM),
        pl.BlockSpec((chunks, group, STATE, HEAD_DIM), lambda g, *_: (start // chunks, g, 0, 0)),
    ]
    specs += [pl.BlockSpec((group, STATE, HEAD_DIM), lambda g, *_: (g, 0, 0))] * len(states)
    args = [first_doc, phi_query, bounds, inner, windowed, prefix, *states]
    if head_first is not None:
        specs.append(some(TILE, HEAD_DIM))
        args.append(head_first)
    return pl.pallas_call(
        functools.partial(finish_kernel, start, len(states)),
        grid_spec=pltpu.PrefetchScalarGridSpec(
            num_scalar_prefetch=1,
            grid=(heads // group,),
            in_specs=specs,
            out_specs=some(half, HEAD_DIM),
        ),
        out_shape=jax.ShapeDtypeStruct((half, columns), BF16),
        compiler_params=params(),
    )(limits, *args)


def after(x, *others):
    return lax.optimization_barrier((x, *others))[0]


def shards(tokens, doc_ids, w_feat, w_value, w_window, w_out):
    rows = tokens.shape[0]
    half = rows // 2
    chunks = rows // CHUNK
    heads = w_value.shape[1] // HEAD_DIM
    count = lax.axis_size("head") // 2
    blocks = lax.axis_size("ctx")
    me = lax.axis_index("head")
    z, c = me // 2, me % 2
    place = jnp.stack([z, c]).astype(jnp.int32)

    def hop(x, step, sources):
        return lax.ppermute(x, "head", line(count, step, sources))

    def near(x):
        return hop(x, 1, range(count)), hop(x, -1, range(count))

    def far(x):
        return hop(x, count - 1, [0]), hop(x, 1 - count, [count - 1])

    def chain(up, down):
        ups, downs = [up], [down]
        for s in range(2, count - 1):
            ups.append(hop(ups[-1], 1, range(s - 1, count)))
            downs.append(hop(downs[-1], -1, range(0, count - s + 1)))
        return ups, downs

    def early_pieces(x, up, down, far_up, far_down):
        mine = jnp.concatenate([x, down + far_up, far_down + up], 1)
        return mine, swap(mine, count)

    def late_pieces(ups, downs):
        mine = jnp.concatenate(
            [downs[s - 1] + ups[count - s - 1] for s in range(2, count - 1)], 1
        )
        return mine, swap(mine, count)

    high, low = tokens[half:], tokens[:half]
    high_near = near(high)
    high_far = far(high)

    docs = doc_ids.astype(F32)
    ends = jnp.concatenate([docs[CHUNK::CHUNK], docs[rows - 1 :]])
    limits = jnp.sum((docs[None, :] < ends[:, None]).astype(F32), 1).astype(jnp.int32)
    limits = jnp.concatenate([limits, doc_ids[rows - 1 :]])
    first = jnp.sum((docs[None, :] < docs[:, None]).astype(F32), 1, keepdims=True)
    bounds = first.astype(jnp.int32)
    first_doc = jnp.broadcast_to(docs[:1], (8, HEAD_DIM))
    tail_docs = jnp.broadcast_to((docs[rows - WIN :] + 1.0).astype(BF16)[:, None], (WIN, HEAD_DIM))

    maps, scale_rows = expansions(heads)
    query_map, key_map = jnp.asarray(maps[0]), jnp.asarray(maps[1])
    scale_rows = jnp.asarray(scale_rows)
    pick = jnp.asarray(picks(heads))

    depth, columns = w_out.shape
    width = columns // (2 * count)

    def cut(rows_out, chip, core):
        return lax.dynamic_slice(rows_out, (0, (2 * chip + core) * width), (depth, width))

    ready = lax.optimization_barrier((*high_near, *high_far, limits, bounds, first_doc, tail_docs))
    high_near, high_far = ready[:2], ready[2:4]
    limits, bounds, first_doc, tail_docs = ready[4:]
    rows_out = after(w_out, *high_near)
    other_rows = jnp.stack([cut(rows_out, chip, 1 - c) for chip in range(count)])

    fv_weights = (w_value, w_feat)
    high_ups, high_downs = chain(*high_near)
    low_far = far(after(low, *high_near))
    *pieces, other_rows = lax.optimization_barrier((*high_near, *high_far, other_rows))
    high_early = early_pieces(high, *pieces)
    other_rows = swap(other_rows, count)
    high_ups[-1], high_downs[-1] = lax.optimization_barrier(
        (high_ups[-1], high_downs[-1], *high_early)
    )[:2]
    low_near = near(after(low, high_ups[-1], high_downs[-1]))
    high_late = late_pieces(high_ups, high_downs)
    value_high, feat_high, win_high = project(place, high_early, high_late, fv_weights + (w_window,))

    group = min(GROUP, heads)
    parts = []
    for g in range(0, heads, group):
        parts.append(win_high[half - WIN :, 2 * g * HEAD_DIM : 2 * (g + group) * HEAD_DIM])
        parts.append(value_high[half - WIN :, g * HEAD_DIM : (g + group) * HEAD_DIM])
    tail = lax.ppermute(
        jnp.concatenate(parts + [tail_docs], 1), "ctx", [(i, i + 1) for i in range(blocks - 1)]
    )
    high_sums = sums(limits, feat_high, value_high, key_map, scale_rows)
    inner_high, windowed_high, phi_high = local(
        False, feat_high, value_high, win_high, bounds, pick, query_map, scale_rows
    )

    *low_near, far_up, far_down, tail, other_rows = lax.optimization_barrier(
        (*low_near, *low_far, tail, other_rows, inner_high, high_sums)
    )[:6]
    low_ups, low_downs = chain(*low_near)
    rows_out = after(w_out, *low_near)

    def out_for(chip):
        chip = jnp.clip(chip, 0, count - 1)
        return jnp.concatenate(
            [cut(rows_out, chip, c), lax.dynamic_index_in_dim(other_rows, chip, 0, keepdims=False)], 0
        )

    out_up = [out_for(z + count - s) for s in range(1, count)]
    out_down = [out_for(z - count + s) for s in range(1, count)]
    *pieces, out_up[0], out_down[0] = lax.optimization_barrier(
        (*low_near, far_up, far_down, out_up[0], out_down[0])
    )
    low_early = early_pieces(low, *pieces)
    ready = lax.optimization_barrier((low_ups[-1], low_downs[-1], out_for(z), *out_up, *out_down))
    low_ups[-1], low_downs[-1], out_here = ready[:3]
    out_up, out_down = ready[3 : 2 + count], ready[2 + count :]
    low_late = late_pieces(low_ups, low_downs)
    value_low, feat_low = project(place, low_early, low_late, fv_weights)
    prefix, state = sums(limits, feat_low, value_low, key_map, scale_rows, high_sums)
    states = [
        lax.ppermute(state, "ctx", [(i, i + k) for i in range(blocks - k)])
        for k in range(1, blocks)
    ]
    (win_low,) = project(place, low_early, (after(low_late[0], state), low_late[1]), (w_window,))
    inner_low, windowed_low, phi_low, windowed_next = local(
        True, feat_low, value_low, win_low, bounds, pick, query_map, scale_rows,
        (tail, tail, first_doc), (value_high, win_high),
    )
    mixed_low = finish(
        0, limits, first_doc, phi_low, bounds, inner_low, windowed_low, prefix, states
    )
    mixed_high = finish(
        chunks // 2, limits, first_doc, phi_high, bounds, inner_high, windowed_high, prefix, states,
        windowed_next,
    )

    outs = []
    for mixed in (mixed_low, mixed_high):
        chip = jnp.concatenate([mixed, swap(mixed, count)], 1)

        def partial(weight, *received):
            total = jnp.dot(chip, weight, preferred_element_type=F32)
            for r in received:
                total += r.astype(F32)
            return total.astype(BF16)

        up, down = (), ()
        for s in range(1, count):
            up = (hop(partial(out_up[s - 1], *up), 1, range(0, s)),)
            down = (hop(partial(out_down[s - 1], *down), -1, range(count - s, count)),)
        outs.append(partial(out_here, *up, *down))
    return jnp.concatenate(outs, 0)


def solution(mesh):
    return jax.shard_map(
        shards,
        mesh=mesh,
        in_specs=(
            P("ctx", "head"),
            P("ctx"),
            P(None, "head"),
            P(None, "head"),
            P(None, "head"),
            P("head", None),
        ),
        out_specs=P("ctx", "head"),
        check_vma=False,
    )
```

time: 287 us -> 258 us (0.90)
  Pallas kernels: 133 us -> 65 us
  waiting for transfers between devices: 26.7 us -> 77.8 us
  matrix products: 0 us -> 9.93 us
  other arithmetic: 23.2 us -> 14.8 us
  local copies, waits for them, and re-layouts: 22.6 us -> 16.9 us
  starting transfers between devices: 75.3 us -> 71.6 us
  between operations: 3.99 us -> 0.94 us
    pallas_call x19 -> x3, Pallas kernels: 94.2 us -> 32.2 us  [project(): pl.pallas_call(functools.partial(project_kernel, len(weights)), grid_spec...]
    ppermute x24, waiting for transfers between devices: 24.4 us -> 75.9 us  [hop(): return lax.ppermute(x, 'head', line(count, step, sources))]
    dot_general x0 -> x14, matrix products: none -> 9.93 us  [partial(): total = jnp.dot(chip, weight, preferred_element_type=F32)]
    ppermute x5 -> x1, starting transfers between devices: 12.4 us -> 3.95 us  [shards(): lax.ppermute(jnp.concatenate(parts + [tail_docs], 1), 'ctx', [(i, i + 1)...]
    concatenate x0 -> x6, other arithmetic: none -> 7.55 us  [the longest x4 5.6 us: out_for(): jnp.concatenate([cut(rows_out, chip, c), lax.dynamic_index_in_dim(other_r...]
    another operation x10 -> x1, other arithmetic: 8.97 us -> 1.59 us  [shards(): jnp.stack([cut(rows_out, chip, 1 - c) for chip in range(count)])]
    pallas_call x2, Pallas kernels: 20.4 us -> 14.3 us  [local(): pl.pallas_call(functools.partial(local_kernel, low), grid=(heads // group...]
    unnamed x56 -> x66, local copies, waits for them, and re-layouts: 14 us -> 9.64 us
  transfers between devices with their start and end apart: 39 -> 35, of which waited for: 7 -> 13; matrix products, arithmetic and copies ran while one was open for 8% -> 9% of each run, Pallas kernels for 40% -> 18%
where the time goes in v3:
time: 258 us; the launch traced here: 257 us
  waiting for transfers between devices  77.8 us (30%)
  starting transfers between devices  71.6 us (28%)
  Pallas kernels  65 us (25%)
  local copies, waits for them, and re-layouts  16.9 us (7%)
  other arithmetic  14.8 us (6%)
  matrix products  9.93 us (4%)
    ppermute x24, waiting for transfers between devices, hop(): return lax.ppermute(x, 'head', line(count, step, sources))  75.9 us
    ppermute x24, starting transfers between devices, hop(): return lax.ppermute(x, 'head', line(count, step, sources))  60.6 us
    pallas_call x3, Pallas kernels, project(): pl.pallas_call(functools.partial(project_kernel, len(weights)), grid_spec...  32.2 us
    pallas_call x2, Pallas kernels, local(): pl.pallas_call(functools.partial(local_kernel, low), grid=(heads // group...  14.3 us
    dot_general x14, matrix products, partial(): total = jnp.dot(chip, weight, preferred_element_type=F32)  9.93 us
    unnamed x66, local copies, waits for them, and re-layouts  9.64 us
    pallas_call x2, Pallas kernels, finish(): pl.pallas_call(functools.partial(finish_kernel, start, len(states)), grid...  8.96 us
    ppermute x3, starting transfers between devices, shards(): lax.ppermute(state, 'ctx', [(i, i + k) for i in range(blocks - k)])  6 us
  transfers between devices with their start and end apart: 35, of which 13 were waited for; matrix products, arithmetic and copies ran while one was open for 9% of the time, Pallas kernels for 18%

profile of v3, /device:TPU:0, one launch (start us, length us, event | category | flops | bytes accessed | tf_op | source)
XLA Modules:
  0.0 257.0 jit_solution(17140427503830624651)
XLA Ops:
  2.6 7.0 %collective-permute-start.2 = (bf16[512,512]{1,0:T(8,128)(2,1)S(1)}, bf16[512,512]{1,0:T(8,128)(2,1)S(1)}, u32[]{:S(2)}, u32[]{:S(2)}) collective-permute-start(bf16[512,512]{1,0:T(8,128)(2,1)S(1)} %get-tuple-element.133), channel_id=1, source_target_pairs={{0,6},{1,7},{8,14},{9,15},{16,22},{17,23},{24,30},{25,31}} | collective-permute-start | bytes 1572872 | tf_op jit(solution)/shard_map/ppermute | solution.py:427
  10.9 4.6 %collective-permute-start = (bf16[512,512]{1,0:T(8,128)(2,1)S(1)}, bf16[512,512]{1,0:T(8,128)(2,1)S(1)}, u32[]{:S(2)}, u32[]{:S(2)}) collective-permute-start(bf16[512,512]{1,0:T(8,128)(2,1)S(1)} %get-tuple-element.133), channel_id=1, source_target_pairs={{0,2},{1,3},{2,4},{3,5},{4,6},{5,7},{8,10},{9,11},{10,12},{11,13},... | collective-permute-start | bytes 1572872 | tf_op jit(solution)/shard_map/ppermute | solution.py:427
  22.0 8.9 %collective-permute-done.1 = bf16[512,512]{1,0:T(8,128)(2,1)S(1)} collective-permute-done((bf16[512,512]{1,0:T(8,128)(2,1)S(1)}, bf16[512,512]{1,0:T(8,128)(2,1)S(1)}, u32[]{:S(2)}, u32[]{:S(2)}) %collective-permute-start.1) | collective-permute-done | bytes 524320 | tf_op jit(solution)/shard_map/ppermute | solution.py:427
  40.2 17.5 %collective-permute-done.5 = bf16[512,512]{1,0:T(8,128)(2,1)S(1)} collective-permute-done((bf16[512,512]{1,0:T(8,128)(2,1)S(1)}, bf16[512,512]{1,0:T(8,128)(2,1)S(1)}, u32[]{:S(2)}, u32[]{:S(2)}) %collective-permute-start.5) | collective-permute-done | bytes 524320 | tf_op jit(solution)/shard_map/ppermute | solution.py:427
  59.8 7.2 %collective-permute-start.9 = (bf16[512,512]{1,0:T(8,128)(2,1)S(1)}, bf16[512,512]{1,0:T(8,128)(2,1)}, u32[]{:S(2)}, u32[]{:S(2)}) collective-permute-start(bf16[512,512]{1,0:T(8,128)(2,1)S(1)} %get-tuple-element.74), channel_id=1, source_target_pairs={{0,6},{1,7},{8,14},{9,15},{16,22},{17,23},{24,30},{25,31}} | collective-permute-start | bytes 1572872 | tf_op jit(solution)/shard_map/ppermute | solution.py:427
  68.3 5.3 %collective-permute-start.7 = (bf16[512,512]{1,0:T(8,128)(2,1)S(1)}, bf16[512,512]{1,0:T(8,128)(2,1)}, u32[]{:S(2)}, u32[]{:S(2)}) collective-permute-start(bf16[512,512]{1,0:T(8,128)(2,1)S(1)} %get-tuple-element.74), channel_id=1, source_target_pairs={{0,2},{1,3},{2,4},{3,5},{4,6},{5,7},{8,10},{9,11},{10,12},{11,13},... | collective-permute-start | bytes 1572872 | tf_op jit(solution)/shard_map/ppermute | solution.py:427
  73.6 13.7 %shard_map.100 = (bf16[512,512]{1,0:T(8,128)(2,1)}, bf16[512,128]{1,0:T(8,128)(2,1)}, bf16[512,1024]{1,0:T(8,128)(2,1)}) custom-call(s32[2]{0:T(128)} %pad_add_fusion.1.place, bf16[512,1536]{1,0:T(8,128)(2,1)} %copy-done.2, bf16[512,1536]{1,0:T(8,128)(2,1)} %collective-permute-done.6.theirs, bf16[512,512]{1,0:T(8,128)(2,1)} %copy-done.5, ...), custom_call_target="tpu_custom_call" | custom-call | tf_op jit(solution)/shard_map/pallas_call | solution.py:82
  91.3 4.0 %collective-permute-start.12 = (bf16[64,1664]{1,0:T(8,128)(2,1)S(1)}, bf16[64,1664]{1,0:T(8,128)(2,1)S(1)}, u32[]{:S(2)}, u32[]{:S(2)}) collective-permute-start(bf16[64,1664]{1,0:T(8,128)(2,1)S(1)} %constant_dynamic-update-slice_fusion), channel_id=1, source_target_pairs={{0,8},{8,16},{16,24},{1,9},{9,17},{17,25},{2,10},{10,18},{18,26},{... | collective-permute-start | bytes 638984 | tf_op jit(solution)/shard_map/ppermute | solution.py:500
  96.4 4.6 %shard_map.102.high = f32[2,4,160,128]{3,2,1,0:T(8,128)} custom-call(s32[5]{0:T(128)} %pad_add_fusion.limits, bf16[512,128]{1,0:T(8,128)(2,1)} %get-tuple-element.79.features, bf16[512,512]{1,0:T(8,128)(2,1)} %get-tuple-element.76.values.refs_3_, bf16[4,128,512]{2,1,0:T(8,128)(2,1)} %constant.91.clone.expand, f32[3,256]{1,0:T(4,128)} %constant.92.clone.rows), custom_call_target="tpu_custom_call" | custom-call | tf_op jit(solution)/shard_map/pallas_call | solution.py:183
  100.9 6.9 %shard_map.101 = (f32[512,512]{1,0:T(8,128)}, f32[512,512]{1,0:T(8,128)}, bf16[512,1024]{1,0:T(8,128)(2,1)}) custom-call(bf16[512,128]{1,0:T(8,128)(2,1)} %get-tuple-element.79.features, bf16[512,512]{1,0:T(8,128)(2,1)} %get-tuple-element.76.values.refs_3_, bf16[512,1024]{1,0:T(8,128)(2,1)} %get-tuple-element.75.window.refs_4_, s32[1024,1]{1,0:T(8,128)} %copy.15.bounds, ...), custom_call_target="tpu_custom_call" | custom-call | tf_op jit(solution)/shard_map/pallas_call | solution.py:335
  121.1 11.1 %collective-permute-done.16 = bf16[512,512]{1,0:T(8,128)(2,1)S(1)} collective-permute-done((bf16[512,512]{1,0:T(8,128)(2,1)}, bf16[512,512]{1,0:T(8,128)(2,1)S(1)}, u32[]{:S(2)}, u32[]{:S(2)}) %collective-permute-start.16) | collective-permute-done | bytes 524320 | tf_op jit(solution)/shard_map/ppermute | solution.py:427
  132.4 1.9 collective-permute-done.17.theirs_late
  136.3 8.4 %shard_map.103 = (bf16[512,512]{1,0:T(8,128)(2,1)}, bf16[512,128]{1,0:T(8,128)(2,1)}) custom-call(s32[2]{0:T(128)} %pad_add_fusion.1.place, bf16[512,1536]{1,0:T(8,128)(2,1)} %copy-done, bf16[512,1536]{1,0:T(8,128)(2,1)} %copy-done.3, bf16[512,512]{1,0:T(8,128)(2,1)} %copy-done.4, bf16[512,512]{1,0:T(8,128)(2,1)} %copy-done.6, bf16[4096,512]{1,0:T(8,128)(2,1)} %refs_0_.4, ...), custom_call_target="tpu_custom_call" | custom-call | tf_op jit(solution)/shard_map/pallas_call | solution.py:82
  144.7 5.1 %shard_map.104 = (f32[4,4,160,128]{3,2,1,0:T(8,128)}, bf16[4,160,128]{2,1,0:T(8,128)(2,1)}) custom-call(s32[5]{0:T(128)} %pad_add_fusion.limits, bf16[512,128]{1,0:T(8,128)(2,1)} %get-tuple-element.96.features, bf16[512,512]{1,0:T(8,128)(2,1)} %get-tuple-element.97.values, bf16[4,128,512]{2,1,0:T(8,128)(2,1)} %constant.91.clone.expand, ...), custom_call_target="tpu_custom_call" | custom-call | tf_op jit(solution)/shard_map/pallas_call | solution.py:190
  149.8 2.2 collective-permute-start.20
  152.0 1.9 collective-permute-start.19
  153.9 1.9 collective-permute-start.18
  155.8 10.1 %shard_map.105.window = bf16[512,1024]{1,0:T(8,128)(2,1)} custom-call(s32[2]{0:T(128)} %pad_add_fusion.1.place, bf16[512,1536]{1,0:T(8,128)(2,1)} %copy-done, bf16[512,1536]{1,0:T(8,128)(2,1)} %copy-done.3, bf16[512,512]{1,0:T(8,128)(2,1)} %copy-done.4, bf16[512,512]{1,0:T(8,128)(2,1)} %copy-done.6, bf16[4096,1024]{1,0:T(8,128)(2,1)} %refs_0_.5), custom_call_target="tpu_custom_call" | custom-call | tf_op jit(solution)/shard_map/pallas_call | solution.py:82
  165.9 7.4 %shard_map.106 = (f32[512,512]{1,0:T(8,128)}, f32[512,512]{1,0:T(8,128)}, bf16[512,1024]{1,0:T(8,128)(2,1)}, f32[128,512]{1,0:T(8,128)}) custom-call(bf16[512,128]{1,0:T(8,128)(2,1)} %get-tuple-element.96.features, bf16[512,512]{1,0:T(8,128)(2,1)} %get-tuple-element.97.values, bf16[512,1024]{1,0:T(8,128)(2,1)} %shard_map.105.window, s32[1024,1]{1,0:T(8,128)} %copy.15.bounds, ...), custom_call_target="tpu_custom_call" | custom-call | tf_op jit(solution)/shard_map/pallas_call | solution.py:335
  174.1 4.4 %shard_map.107 = bf16[512,512]{1,0:T(8,128)(2,1)} custom-call(s32[5]{0:T(128)} %pad_add_fusion.limits, f32[8,128]{1,0:T(8,128)} %broadcast_in_dim.4.refs_2_.first_doc, bf16[512,1024]{1,0:T(8,128)(2,1)} %get-tuple-element.101.phi_query, s32[1024,1]{1,0:T(8,128)} %copy.15.bounds, f32[512,512]{1,0:T(8,128)} %get-tuple-element.102.inner, ...), custom_call_target="tpu_custom_call" | custom-call | tf_op jit(solution)/shard_map/pallas_call | solution.py:398
  178.4 4.6 %shard_map.108 = bf16[512,512]{1,0:T(8,128)(2,1)} custom-call(s32[5]{0:T(128)} %pad_add_fusion.limits, f32[8,128]{1,0:T(8,128)} %broadcast_in_dim.4.refs_2_.first_doc, bf16[512,1024]{1,0:T(8,128)(2,1)} %get-tuple-element.112.phi_query, s32[1024,1]{1,0:T(8,128)} %copy.15.bounds, f32[512,512]{1,0:T(8,128)} %get-tuple-element.81.inner, ...), custom_call_target="tpu_custom_call" | custom-call | tf_op jit(solution)/shard_map/pallas_call | solution.py:398
  185.9 1.8 collective-permute-start.22
  193.1 6.8 %collective-permute-done.22 = bf16[512,512]{1,0:T(8,128)(2,1)S(1)} collective-permute-done((bf16[512,512]{1,0:T(8,128)(2,1)S(1)}, bf16[512,512]{1,0:T(8,128)(2,1)S(1)}, u32[]{:S(2)}, u32[]{:S(2)}) %collective-permute-start.22) | collective-permute-done | bytes 524320 | tf_op jit(solution)/shard_map/ppermute | solution.py:427
  200.7 4.4 %collective-permute-start.23 = (bf16[512,512]{1,0:T(8,128)(2,1)S(1)}, bf16[512,512]{1,0:T(8,128)(2,1)S(1)}, u32[]{:S(2)}, u32[]{:S(2)}) collective-permute-start(bf16[512,512]{1,0:T(8,128)(2,1)S(1)} %fusion.3), channel_id=1, source_target_pairs={{0,2},{1,3},{2,4},{3,5},{8,10},{9,11},{10,12},{11,13},{16,18},{17,... | collective-permute-start | bytes 1572872 | tf_op jit(solution)/shard_map/ppermute | solution.py:427
  206.6 4.5 %collective-permute-done.29 = bf16[512,512]{1,0:T(8,128)(2,1)S(1)} collective-permute-done((bf16[512,512]{1,0:T(8,128)(2,1)S(1)}, bf16[512,512]{1,0:T(8,128)(2,1)S(1)}, u32[]{:S(2)}, u32[]{:S(2)}) %collective-permute-start.29) | collective-permute-done | bytes 524320 | tf_op jit(solution)/shard_map/ppermute | solution.py:427
  211.9 4.5 %collective-permute-start.30 = (bf16[512,512]{1,0:T(8,128)(2,1)S(1)}, bf16[512,512]{1,0:T(8,128)(2,1)S(1)}, u32[]{:S(2)}, u32[]{:S(2)}) collective-permute-start(bf16[512,512]{1,0:T(8,128)(2,1)S(1)} %fusion.7), channel_id=1, source_target_pairs={{0,2},{1,3},{2,4},{3,5},{8,10},{9,11},{10,12},{11,13},{16,18},{17,... | collective-permute-start | bytes 1572872 | tf_op jit(solution)/shard_map/ppermute | solution.py:427
  218.5 3.9 %collective-permute-done.23 = bf16[512,512]{1,0:T(8,128)(2,1)S(1)} collective-permute-done((bf16[512,512]{1,0:T(8,128)(2,1)S(1)}, bf16[512,512]{1,0:T(8,128)(2,1)S(1)}, u32[]{:S(2)}, u32[]{:S(2)}) %collective-permute-start.23) | collective-permute-done | bytes 524320 | tf_op jit(solution)/shard_map/ppermute | solution.py:427
  223.1 4.4 %collective-permute-start.24 = (bf16[512,512]{1,0:T(8,128)(2,1)S(1)}, bf16[512,512]{1,0:T(8,128)(2,1)S(1)}, u32[]{:S(2)}, u32[]{:S(2)}) collective-permute-start(bf16[512,512]{1,0:T(8,128)(2,1)S(1)} %fusion.2), channel_id=1, source_target_pairs={{0,2},{1,3},{2,4},{3,5},{4,6},{5,7},{8,10},{9,11},{10,12},{11,13},... | collective-permute-start | bytes 1572872 | tf_op jit(solution)/shard_map/ppermute | solution.py:427
  229.7 3.9 %collective-permute-done.30 = bf16[512,512]{1,0:T(8,128)(2,1)S(1)} collective-permute-done((bf16[512,512]{1,0:T(8,128)(2,1)S(1)}, bf16[512,512]{1,0:T(8,128)(2,1)S(1)}, u32[]{:S(2)}, u32[]{:S(2)}) %collective-permute-start.30) | collective-permute-done | bytes 524320 | tf_op jit(solution)/shard_map/ppermute | solution.py:427
  234.4 4.4 %collective-permute-start.31 = (bf16[512,512]{1,0:T(8,128)(2,1)S(1)}, bf16[512,512]{1,0:T(8,128)(2,1)S(1)}, u32[]{:S(2)}, u32[]{:S(2)}) collective-permute-start(bf16[512,512]{1,0:T(8,128)(2,1)S(1)} %fusion.6), channel_id=1, source_target_pairs={{0,2},{1,3},{2,4},{3,5},{4,6},{5,7},{8,10},{9,11},{10,12},{11,13},... | collective-permute-start | bytes 1572872 | tf_op jit(solution)/shard_map/ppermute | solution.py:427
  238.8 6.1 %collective-permute-done.24 = bf16[512,512]{1,0:T(8,128)(2,1)S(1)} collective-permute-done((bf16[512,512]{1,0:T(8,128)(2,1)S(1)}, bf16[512,512]{1,0:T(8,128)(2,1)S(1)}, u32[]{:S(2)}, u32[]{:S(2)}) %collective-permute-start.24) | collective-permute-done | bytes 524320 | tf_op jit(solution)/shard_map/ppermute | solution.py:427
  245.6 9.6 %collective-permute-done.31 = bf16[512,512]{1,0:T(8,128)(2,1)S(1)} collective-permute-done((bf16[512,512]{1,0:T(8,128)(2,1)S(1)}, bf16[512,512]{1,0:T(8,128)(2,1)S(1)}, u32[]{:S(2)}, u32[]{:S(2)}) %collective-permute-start.31) | collective-permute-done | bytes 524320 | tf_op jit(solution)/shard_map/ppermute | solution.py:427
  (161 shorter events, 63.1 us)
Async XLA Ops:
  1.3 19.2 %collective-permute-start.3 = (bf16[512,512]{1,0:T(8,128)(2,1)S(1)}, bf16[512,512]{1,0:T(8,128)(2,1)S(1)}, u32[]{:S(2)}, u32[]{:S(2)}) collective-permute-start(bf16[512,512]{1,0:T(8,128)(2,1)S(1)} %get-tuple-element.133), channel_id=1, source_target_pairs={{6,0},{7,1},{14,8},{15,9},{22,16},{23,17},{30,24},{31,25}} | collective-permute-start | bytes 1572872 | tf_op jit(solution)/shard_map/ppermute | solution.py:427
  2.6 19.4 %collective-permute-start.2 = (bf16[512,512]{1,0:T(8,128)(2,1)S(1)}, bf16[512,512]{1,0:T(8,128)(2,1)S(1)}, u32[]{:S(2)}, u32[]{:S(2)}) collective-permute-start(bf16[512,512]{1,0:T(8,128)(2,1)S(1)} %get-tuple-element.133), channel_id=1, source_target_pairs={{0,6},{1,7},{8,14},{9,15},{16,22},{17,23},{24,30},{25,31}} | collective-permute-start | bytes 1572872 | tf_op jit(solution)/shard_map/ppermute | solution.py:427
  9.6 21.3 %collective-permute-start.1 = (bf16[512,512]{1,0:T(8,128)(2,1)S(1)}, bf16[512,512]{1,0:T(8,128)(2,1)S(1)}, u32[]{:S(2)}, u32[]{:S(2)}) collective-permute-start(bf16[512,512]{1,0:T(8,128)(2,1)S(1)} %get-tuple-element.133), channel_id=1, source_target_pairs={{2,0},{3,1},{4,2},{5,3},{6,4},{7,5},{10,8},{11,9},{12,10},{13,11},... | collective-permute-start | bytes 1572872 | tf_op jit(solution)/shard_map/ppermute | solution.py:427
  10.9 21.2 %collective-permute-start = (bf16[512,512]{1,0:T(8,128)(2,1)S(1)}, bf16[512,512]{1,0:T(8,128)(2,1)S(1)}, u32[]{:S(2)}, u32[]{:S(2)}) collective-permute-start(bf16[512,512]{1,0:T(8,128)(2,1)S(1)} %get-tuple-element.133), channel_id=1, source_target_pairs={{0,2},{1,3},{2,4},{3,5},{4,6},{5,7},{8,10},{9,11},{10,12},{11,13},... | collective-permute-start | bytes 1572872 | tf_op jit(solution)/shard_map/ppermute | solution.py:427
  37.6 20.1 %collective-permute-start.6 = (bf16[512,1536]{1,0:T(8,128)(2,1)S(1)}, bf16[512,1536]{1,0:T(8,128)(2,1)}, u32[]{:S(2)}, u32[]{:S(2)}) collective-permute-start(bf16[512,1536]{1,0:T(8,128)(2,1)S(1)} %pad_maximum_fusion.1.mine), channel_id=1, source_target_pairs={{0,1},{1,0},{2,3},{3,2},{4,5},{5,4},{6,7},{7,6},{8,9},{9,8},{10,11... | collective-permute-start | bytes 4718600 | tf_op jit(solution)/shard_map/ppermute | solution.py:33
  38.7 19.0 %collective-permute-start.5 = (bf16[512,512]{1,0:T(8,128)(2,1)S(1)}, bf16[512,512]{1,0:T(8,128)(2,1)S(1)}, u32[]{:S(2)}, u32[]{:S(2)}) collective-permute-start(bf16[512,512]{1,0:T(8,128)(2,1)S(1)} %copy-done.21), channel_id=1, source_target_pairs={{2,0},{3,1},{4,2},{5,3},{10,8},{11,9},{12,10},{13,11},{18,16},{19,... | collective-permute-start | bytes 1572872 | tf_op jit(solution)/shard_map/ppermute | solution.py:427
  40.0 67.9 %collective-permute-start.13 = (bf16[4,512,512]{2,1,0:T(8,128)(2,1)}, bf16[4,512,512]{2,1,0:T(8,128)(2,1)S(1)}, u32[]{:S(2)}, u32[]{:S(2)}) collective-permute-start(bf16[4,512,512]{2,1,0:T(8,128)(2,1)} %pad_maximum_fusion), channel_id=1, source_target_pairs={{0,1},{1,0},{2,3},{3,2},{4,5},{5,4},{6,7},{7,6},{8,9},{9,8},{10,11... | collective-permute-start | bytes 6291464 | tf_op jit(solution)/shard_map/ppermute | solution.py:33
  57.8 10.4 %collective-permute-start.11 = (bf16[512,512]{1,0:T(8,128)(2,1)S(1)}, bf16[512,512]{1,0:T(8,128)(2,1)}, u32[]{:S(2)}, u32[]{:S(2)}) collective-permute-start(bf16[512,512]{1,0:T(8,128)(2,1)S(1)} %add.175.mine_late), channel_id=1, source_target_pairs={{0,1},{1,0},{2,3},{3,2},{4,5},{5,4},{6,7},{7,6},{8,9},{9,8},{10,11... | collective-permute-start | bytes 1572872 | tf_op jit(solution)/shard_map/ppermute | solution.py:33
  58.5 32.0 %collective-permute-start.10 = (bf16[512,512]{1,0:T(8,128)(2,1)S(1)}, bf16[512,512]{1,0:T(8,128)(2,1)S(1)}, u32[]{:S(2)}, u32[]{:S(2)}) collective-permute-start(bf16[512,512]{1,0:T(8,128)(2,1)S(1)} %get-tuple-element.74), channel_id=1, source_target_pairs={{6,0},{7,1},{14,8},{15,9},{22,16},{23,17},{30,24},{31,25}} | collective-permute-start | bytes 1572872 | tf_op jit(solution)/shard_map/ppermute | solution.py:427
  59.8 48.1 %collective-permute-start.9 = (bf16[512,512]{1,0:T(8,128)(2,1)S(1)}, bf16[512,512]{1,0:T(8,128)(2,1)}, u32[]{:S(2)}, u32[]{:S(2)}) collective-permute-start(bf16[512,512]{1,0:T(8,128)(2,1)S(1)} %get-tuple-element.74), channel_id=1, source_target_pairs={{0,6},{1,7},{8,14},{9,15},{16,22},{17,23},{24,30},{25,31}} | collective-permute-start | bytes 1572872 | tf_op jit(solution)/shard_map/ppermute | solution.py:427
  67.0 40.9 %collective-permute-start.8 = (bf16[512,512]{1,0:T(8,128)(2,1)S(1)}, bf16[512,512]{1,0:T(8,128)(2,1)}, u32[]{:S(2)}, u32[]{:S(2)}) collective-permute-start(bf16[512,512]{1,0:T(8,128)(2,1)S(1)} %get-tuple-element.74), channel_id=1, source_target_pairs={{2,0},{3,1},{4,2},{5,3},{6,4},{7,5},{10,8},{11,9},{12,10},{13,11},... | collective-permute-start | bytes 1572872 | tf_op jit(solution)/shard_map/ppermute | solution.py:427
  68.3 39.6 %collective-permute-start.7 = (bf16[512,512]{1,0:T(8,128)(2,1)S(1)}, bf16[512,512]{1,0:T(8,128)(2,1)}, u32[]{:S(2)}, u32[]{:S(2)}) collective-permute-start(bf16[512,512]{1,0:T(8,128)(2,1)S(1)} %get-tuple-element.74), channel_id=1, source_target_pairs={{0,2},{1,3},{2,4},{3,5},{4,6},{5,7},{8,10},{9,11},{10,12},{11,13},... | collective-permute-start | bytes 1572872 | tf_op jit(solution)/shard_map/ppermute | solution.py:427
  91.3 16.6 %collective-permute-start.12 = (bf16[64,1664]{1,0:T(8,128)(2,1)S(1)}, bf16[64,1664]{1,0:T(8,128)(2,1)S(1)}, u32[]{:S(2)}, u32[]{:S(2)}) collective-permute-start(bf16[64,1664]{1,0:T(8,128)(2,1)S(1)} %constant_dynamic-update-slice_fusion), channel_id=1, source_target_pairs={{0,8},{8,16},{16,24},{1,9},{9,17},{17,25},{2,10},{10,18},{18,26},{... | collective-permute-start | bytes 638984 | tf_op jit(solution)/shard_map/ppermute | solution.py:500
  114.8 19.5 %collective-permute-start.14 = (bf16[512,1536]{1,0:T(8,128)(2,1)S(1)}, bf16[512,1536]{1,0:T(8,128)(2,1)S(1)}, u32[]{:S(2)}, u32[]{:S(2)}) collective-permute-start(bf16[512,1536]{1,0:T(8,128)(2,1)S(1)} %pad_maximum_fusion.2.mine), channel_id=1, source_target_pairs={{0,1},{1,0},{2,3},{3,2},{4,5},{5,4},{6,7},{7,6},{8,9},{9,8},{10,11... | collective-permute-start | bytes 4718600 | tf_op jit(solution)/shard_map/ppermute | solution.py:33
  114.9 6.2 %collective-permute-start.15 = (bf16[512,512]{1,0:T(8,128)(2,1)}, bf16[512,512]{1,0:T(8,128)(2,1)S(1)}, u32[]{:S(2)}, u32[]{:S(2)}) collective-permute-start(bf16[512,512]{1,0:T(8,128)(2,1)} %collective-permute-done.7), channel_id=1, source_target_pairs={{2,4},{3,5},{4,6},{5,7},{10,12},{11,13},{12,14},{13,15},{18,20},{1... | collective-permute-start | bytes 1572872 | tf_op jit(solution)/shard_map/ppermute | solution.py:427
  115.8 16.4 %collective-permute-start.16 = (bf16[512,512]{1,0:T(8,128)(2,1)}, bf16[512,512]{1,0:T(8,128)(2,1)S(1)}, u32[]{:S(2)}, u32[]{:S(2)}) collective-permute-start(bf16[512,512]{1,0:T(8,128)(2,1)} %collective-permute-done.8), channel_id=1, source_target_pairs={{2,0},{3,1},{4,2},{5,3},{10,8},{11,9},{12,10},{13,11},{18,16},{19,... | collective-permute-start | bytes 1572872 | tf_op jit(solution)/shard_map/ppermute | solution.py:427
  149.8 23.5 %collective-permute-start.20 = (bf16[4,160,128]{2,1,0:T(8,128)(2,1)}, bf16[4,160,128]{2,1,0:T(8,128)(2,1)S(1)}, u32[]{:S(2)}, u32[]{:S(2)}) collective-permute-start(bf16[4,160,128]{2,1,0:T(8,128)(2,1)} %get-tuple-element.98), channel_id=1, source_target_pairs={{0,24},{1,25},{2,26},{3,27},{4,28},{5,29},{6,30},{7,31}} | collective-permute-start | bytes 491528 | tf_op jit(solution)/shard_map/ppermute | solution.py:533
  152.0 21.3 %collective-permute-start.19 = (bf16[4,160,128]{2,1,0:T(8,128)(2,1)}, bf16[4,160,128]{2,1,0:T(8,128)(2,1)S(1)}, u32[]{:S(2)}, u32[]{:S(2)}) collective-permute-start(bf16[4,160,128]{2,1,0:T(8,128)(2,1)} %get-tuple-element.98), channel_id=1, source_target_pairs={{0,16},{8,24},{1,17},{9,25},{2,18},{10,26},{3,19},{11,27},{4,20},{... | collective-permute-start | bytes 491528 | tf_op jit(solution)/shard_map/ppermute | solution.py:533
  153.9 19.4 %collective-permute-start.18 = (bf16[4,160,128]{2,1,0:T(8,128)(2,1)}, bf16[4,160,128]{2,1,0:T(8,128)(2,1)S(1)}, u32[]{:S(2)}, u32[]{:S(2)}) collective-permute-start(bf16[4,160,128]{2,1,0:T(8,128)(2,1)} %get-tuple-element.98), channel_id=1, source_target_pairs={{0,8},{8,16},{16,24},{1,9},{9,17},{17,25},{2,10},{10,18},{18,26},{... | collective-permute-start | bytes 491528 | tf_op jit(solution)/shard_map/ppermute | solution.py:533
  178.4 5.2 %collective-permute-start.21 = (bf16[512,512]{1,0:T(8,128)(2,1)}, bf16[512,512]{1,0:T(8,128)(2,1)S(1)}, u32[]{:S(2)}, u32[]{:S(2)}) collective-permute-start(bf16[512,512]{1,0:T(8,128)(2,1)} %shard_map.107), channel_id=1, source_target_pairs={{0,1},{1,0},{2,3},{3,2},{4,5},{5,4},{6,7},{7,6},{8,9},{9,8},{10,11... | collective-permute-start | bytes 1572872 | tf_op jit(solution)/shard_map/ppermute | solution.py:33
  184.3 7.3 %collective-permute-start.25 = (bf16[512,512]{1,0:T(8,128)(2,1)S(1)}, bf16[512,512]{1,0:T(8,128)(2,1)S(1)}, u32[]{:S(2)}, u32[]{:S(2)}) collective-permute-start(bf16[512,512]{1,0:T(8,128)(2,1)S(1)} %convolution_convert_fusion.2), channel_id=1, source_target_pairs={{6,4},{7,5},{14,12},{15,13},{22,20},{23,21},{30,28},{31,29}} | collective-permute-start | bytes 1572872 | tf_op jit(solution)/shard_map/ppermute | solution.py:427
  185.9 14.1 %collective-permute-start.22 = (bf16[512,512]{1,0:T(8,128)(2,1)S(1)}, bf16[512,512]{1,0:T(8,128)(2,1)S(1)}, u32[]{:S(2)}, u32[]{:S(2)}) collective-permute-start(bf16[512,512]{1,0:T(8,128)(2,1)S(1)} %convolution_convert_fusion.3), channel_id=1, source_target_pairs={{0,2},{1,3},{8,10},{9,11},{16,18},{17,19},{24,26},{25,27}} | collective-permute-start | bytes 1572872 | tf_op jit(solution)/shard_map/ppermute | solution.py:427
  188.4 16.7 %collective-permute-start.32 = (bf16[512,512]{1,0:T(8,128)(2,1)S(1)}, bf16[512,512]{1,0:T(8,128)(2,1)S(1)}, u32[]{:S(2)}, u32[]{:S(2)}) collective-permute-start(bf16[512,512]{1,0:T(8,128)(2,1)S(1)} %convolution_convert_fusion), channel_id=1, source_target_pairs={{6,4},{7,5},{14,12},{15,13},{22,20},{23,21},{30,28},{31,29}} | collective-permute-start | bytes 1572872 | tf_op jit(solution)/shard_map/ppermute | solution.py:427
  190.0 21.2 %collective-permute-start.29 = (bf16[512,512]{1,0:T(8,128)(2,1)S(1)}, bf16[512,512]{1,0:T(8,128)(2,1)S(1)}, u32[]{:S(2)}, u32[]{:S(2)}) collective-permute-start(bf16[512,512]{1,0:T(8,128)(2,1)S(1)} %convolution_convert_fusion.1), channel_id=1, source_target_pairs={{0,2},{1,3},{8,10},{9,11},{16,18},{17,19},{24,26},{25,27}} | collective-permute-start | bytes 1572872 | tf_op jit(solution)/shard_map/ppermute | solution.py:427
  192.4 24.1 %collective-permute-start.26 = (bf16[512,512]{1,0:T(8,128)(2,1)S(1)}, bf16[512,512]{1,0:T(8,128)(2,1)S(1)}, u32[]{:S(2)}, u32[]{:S(2)}) collective-permute-start(bf16[512,512]{1,0:T(8,128)(2,1)S(1)} %fusion.5), channel_id=1, source_target_pairs={{4,2},{5,3},{6,4},{7,5},{12,10},{13,11},{14,12},{15,13},{20,18},{2... | collective-permute-start | bytes 1572872 | tf_op jit(solution)/shard_map/ppermute | solution.py:427
  200.7 21.8 %collective-permute-start.23 = (bf16[512,512]{1,0:T(8,128)(2,1)S(1)}, bf16[512,512]{1,0:T(8,128)(2,1)S(1)}, u32[]{:S(2)}, u32[]{:S(2)}) collective-permute-start(bf16[512,512]{1,0:T(8,128)(2,1)S(1)} %fusion.3), channel_id=1, source_target_pairs={{0,2},{1,3},{2,4},{3,5},{8,10},{9,11},{10,12},{11,13},{16,18},{17,... | collective-permute-start | bytes 1572872 | tf_op jit(solution)/shard_map/ppermute | solution.py:427
  205.8 21.7 %collective-permute-start.33 = (bf16[512,512]{1,0:T(8,128)(2,1)S(1)}, bf16[512,512]{1,0:T(8,128)(2,1)S(1)}, u32[]{:S(2)}, u32[]{:S(2)}) collective-permute-start(bf16[512,512]{1,0:T(8,128)(2,1)S(1)} %fusion.9), channel_id=1, source_target_pairs={{4,2},{5,3},{6,4},{7,5},{12,10},{13,11},{14,12},{15,13},{20,18},{2... | collective-permute-start | bytes 1572872 | tf_op jit(solution)/shard_map/ppermute | solution.py:427
  211.9 21.8 %collective-permute-start.30 = (bf16[512,512]{1,0:T(8,128)(2,1)S(1)}, bf16[512,512]{1,0:T(8,128)(2,1)S(1)}, u32[]{:S(2)}, u32[]{:S(2)}) collective-permute-start(bf16[512,512]{1,0:T(8,128)(2,1)S(1)} %fusion.7), channel_id=1, source_target_pairs={{0,2},{1,3},{2,4},{3,5},{8,10},{9,11},{10,12},{11,13},{16,18},{17,... | collective-permute-start | bytes 1572872 | tf_op jit(solution)/shard_map/ppermute | solution.py:427
  217.2 21.6 %collective-permute-start.27 = (bf16[512,512]{1,0:T(8,128)(2,1)S(1)}, bf16[512,512]{1,0:T(8,128)(2,1)S(1)}, u32[]{:S(2)}, u32[]{:S(2)}) collective-permute-start(bf16[512,512]{1,0:T(8,128)(2,1)S(1)} %fusion.4), channel_id=1, source_target_pairs={{2,0},{3,1},{4,2},{5,3},{6,4},{7,5},{10,8},{11,9},{12,10},{13,11},... | collective-permute-start | bytes 1572872 | tf_op jit(solution)/shard_map/ppermute | solution.py:427
  223.1 21.8 %collective-permute-start.24 = (bf16[512,512]{1,0:T(8,128)(2,1)S(1)}, bf16[512,512]{1,0:T(8,128)(2,1)S(1)}, u32[]{:S(2)}, u32[]{:S(2)}) collective-permute-start(bf16[512,512]{1,0:T(8,128)(2,1)S(1)} %fusion.2), channel_id=1, source_target_pairs={{0,2},{1,3},{2,4},{3,5},{4,6},{5,7},{8,10},{9,11},{10,12},{11,13},... | collective-permute-start | bytes 1572872 | tf_op jit(solution)/shard_map/ppermute | solution.py:427
  228.3 17.3 %collective-permute-start.34 = (bf16[512,512]{1,0:T(8,128)(2,1)S(1)}, bf16[512,512]{1,0:T(8,128)(2,1)S(1)}, u32[]{:S(2)}, u32[]{:S(2)}) collective-permute-start(bf16[512,512]{1,0:T(8,128)(2,1)S(1)} %fusion.8), channel_id=1, source_target_pairs={{2,0},{3,1},{4,2},{5,3},{6,4},{7,5},{10,8},{11,9},{12,10},{13,11},... | collective-permute-start | bytes 1572872 | tf_op jit(solution)/shard_map/ppermute | solution.py:427
  234.4 20.8 %collective-permute-start.31 = (bf16[512,512]{1,0:T(8,128)(2,1)S(1)}, bf16[512,512]{1,0:T(8,128)(2,1)S(1)}, u32[]{:S(2)}, u32[]{:S(2)}) collective-permute-start(bf16[512,512]{1,0:T(8,128)(2,1)S(1)} %fusion.6), channel_id=1, source_target_pairs={{0,2},{1,3},{2,4},{3,5},{4,6},{5,7},{8,10},{9,11},{10,12},{11,13},... | collective-permute-start | bytes 1572872 | tf_op jit(solution)/shard_map/ppermute | solution.py:427
  (34 other events, 161.1 us)

commit v4 on v0

v4 whole, which is shorter than its diff:
```python
import functools

import jax
import jax.numpy as jnp
import numpy as np
from jax import lax
from jax.experimental import pallas as pl
from jax.experimental.pallas import tpu as pltpu
from jax.sharding import PartitionSpec as P

HEAD_DIM = 128
FEAT = 16
WIN = 64
PAIRS = [(i, j) for i in range(FEAT) for j in range(i, FEAT)]
WIDE = 256
CHUNK = 256
GROUP = 2
STATE = -(-(len(PAIRS) + FEAT + 1) // 16) * 16
VMEM = 40 * 1024 * 1024
TILE = 128
LANES = 128
F32 = jnp.float32
BF16 = jnp.bfloat16


def params():
    return pltpu.CompilerParams(vmem_limit_bytes=VMEM, dimension_semantics=("arbitrary",))


def line(count, step, sources):
    return [(2 * z + c, 2 * (z + step) + c) for z in sources for c in (0, 1) if 0 <= z + step < count]


def swap(x, count):
    return lax.ppermute(x, "head", [(h, h ^ 1) for h in range(2 * count)])


def project_kernel(chips, has_before, place, mine, theirs, *refs):
    weights, out, both = refs[:chips], refs[-2], refs[-1]
    width = mine.shape[1] // chips
    c = place[1]

    @pl.when(pl.program_id(0) == 0)
    def _():
        for n in range(chips):
            piece = slice(n * width, (n + 1) * width)
            own = pl.multiple_of((2 * n + c) * width, width)
            other = pl.multiple_of((2 * n + 1 - c) * width, width)
            both[:, pl.ds(own, width)] = mine[:, piece]
            both[:, pl.ds(other, width)] = theirs[:, piece]

    total = refs[chips][...] if has_before else None
    for n in range(chips):
        rows = both[:, 2 * n * width : 2 * (n + 1) * width]
        part = jnp.dot(rows, weights[n][...], preferred_element_type=F32)
        total = part if total is None else total + part
    out[...] = total.astype(out.dtype)


def project(place, chips, mine, theirs, weight, first, columns, before=None, dtype=F32):
    rows = mine.shape[0]
    width = mine.shape[1] // len(chips)
    count = weight.shape[0] // (2 * width)
    tile = 256
    start = first // tile
    whole = pl.BlockSpec(mine.shape, lambda j, p: (0, 0))
    specs = [whole, whole]
    for n in chips:
        specs.append(
            pl.BlockSpec(
                (2 * width, tile), lambda j, p, n=n: (lax.rem(p[0] + n, count), start + j)
            )
        )
    args = [mine, theirs] + [weight] * len(chips)
    if before is not None:
        specs.append(pl.BlockSpec((rows, tile), lambda j, p: (0, start + j)))
        args.append(before)
    return pl.pallas_call(
        functools.partial(project_kernel, len(chips), before is not None),
        grid_spec=pltpu.PrefetchScalarGridSpec(
            num_scalar_prefetch=1,
            grid=(columns // tile,),
            in_specs=specs,
            out_specs=pl.BlockSpec((rows, tile), lambda j, p: (0, j)),
            scratch_shapes=[pltpu.VMEM((rows, 2 * mine.shape[1]), BF16)],
        ),
        out_shape=jax.ShapeDtypeStruct((rows, columns), dtype),
        compiler_params=params(),
    )(place, *args)


def expansions(heads):
    lanes = -(-heads * 2 * FEAT // LANES) * LANES
    maps = np.zeros((2, heads, lanes, 2 * WIDE), np.float32)
    rows = np.zeros((3, WIDE), np.float32)
    for h in range(heads):
        for side in (0, 1):
            base = h * 2 * FEAT + side * FEAT
            for n, (i, j) in enumerate(PAIRS):
                maps[side, h, base + i, n] = 1.0
                maps[side, h, base + j, WIDE + n] = 1.0
            for i in range(FEAT):
                maps[side, h, base + i, len(PAIRS) + i] = 1.0
    for n, (i, j) in enumerate(PAIRS):
        rows[2, n] = (2.0 * FEAT) ** -0.5 * (1.0 if i == j else 2.0**0.5)
    rows[1, len(PAIRS) : len(PAIRS) + FEAT + 1] = 1.0
    rows[0, len(PAIRS) + FEAT] = 1.0
    rows[2, len(PAIRS) : len(PAIRS) + FEAT] = FEAT**-0.25
    rows[2, len(PAIRS) + FEAT] = 1.0
    return maps.astype(jnp.bfloat16), rows


def picks(heads):
    lanes = -(-heads * 2 * FEAT // LANES) * LANES
    maps = np.zeros((heads, lanes, 256), np.float32)
    for h in range(heads):
        for i in range(FEAT):
            maps[h, h * 2 * FEAT + i, i] = 1.0
            maps[h, h * 2 * FEAT + FEAT + i, 128 + i] = 1.0
    return maps.astype(jnp.bfloat16)


def phi(features, expand, rows):
    factors = jnp.dot(features, expand, preferred_element_type=F32)
    left = factors[:, :WIDE] + rows[0:1]
    right = factors[:, WIDE:] + rows[1:2]
    return (left * right * rows[2:3]).astype(BF16)


def sums_kernel(limits, values, features, expand, rows, prefix, end):
    chunks, heads = prefix.shape[:2]
    mark = lax.broadcasted_iota(jnp.int32, (STATE, HEAD_DIM), 0) == STATE - 1
    at = lax.broadcasted_iota(jnp.int32, (CHUNK, HEAD_DIM), 0)
    for h in range(heads):
        column = slice(h * HEAD_DIM, (h + 1) * HEAD_DIM)
        phi_key = phi(features[...], expand[h], rows[...])
        parts = []
        for n in range(chunks):
            here = slice(n * CHUNK, (n + 1) * CHUNK)
            kept = jnp.where(at + n * CHUNK >= limits[n], values[here, column].astype(F32), 0.0)
            parts.append(
                lax.dot_general(
                    phi_key[here], kept.astype(BF16), (((0,), (0,)), ((), ())),
                    preferred_element_type=F32,
                )[:STATE]
            )
        state = jnp.zeros((STATE, HEAD_DIM), F32)
        for n in range(chunks):
            prefix[n, h] = state
            state = parts[n] + jnp.where(limits[n] <= n * CHUNK, state, 0.0)
        end[h] = jnp.where(mark, (limits[chunks] + 1).astype(F32), state).astype(BF16)


def sums(limits, both, heads, expand, rows):
    chunks = both.shape[0] // CHUNK
    group = min(GROUP, heads)
    count = both.shape[0]
    return pl.pallas_call(
        sums_kernel,
        grid_spec=pltpu.PrefetchScalarGridSpec(
            num_scalar_prefetch=1,
            grid=(heads // group,),
            in_specs=[
                pl.BlockSpec((count, group * HEAD_DIM), lambda g, _: (0, g)),
                pl.BlockSpec((count, LANES), lambda g, _: (0, heads)),
                pl.BlockSpec((group,) + expand.shape[1:], lambda g, _: (g, 0, 0)),
                pl.BlockSpec(rows.shape, lambda g, _: (0, 0)),
            ],
            out_specs=[
                pl.BlockSpec((chunks, group, STATE, HEAD_DIM), lambda g, _: (0, g, 0, 0)),
                pl.BlockSpec((group, STATE, HEAD_DIM), lambda g, _: (g, 0, 0)),
            ],
        ),
        out_shape=[
            jax.ShapeDtypeStruct((chunks, heads, STATE, HEAD_DIM), F32),
            jax.ShapeDtypeStruct((heads, STATE, HEAD_DIM), BF16),
        ],
        compiler_params=params(),
    )(limits, both, both, expand, rows)


def windows(tiles):
    wide = TILE + WIN
    logits = jnp.concatenate(
        [
            lax.dot_general(q, k, (((1,), (1,)), ((), ())), preferred_element_type=F32)
            for q, k, _, _, _ in tiles
        ],
        0,
    )
    at = lax.broadcasted_iota(jnp.int32, (TILE, wide), 1)
    row = lax.broadcasted_iota(jnp.int32, (TILE, wide), 0)
    near = (at <= row + WIN) & (at > row)
    good = jnp.concatenate([near & (at >= first - start) for _, _, _, first, start in tiles], 0)
    logits = jnp.where(good, logits * HEAD_DIM**-0.5, -1e30)
    top = jnp.max(logits, 1, keepdims=True)
    weight = jnp.where(good, jnp.exp(logits - top), 0.0)
    probs = (weight / jnp.sum(weight, 1, keepdims=True)).astype(BF16)
    return [
        jnp.dot(probs[n * TILE : (n + 1) * TILE], tile[2], preferred_element_type=F32)
        for n, tile in enumerate(tiles)
    ]


def local_kernel(part, features, values, window, old_values, old_window, bounds, pick, expand, rows, *refs):
    inner, windowed, phi_query = refs[-3:]
    half = features.shape[0]
    base = part * half
    chunks = half // CHUNK
    if part == 0:
        tail_docs, first_doc = refs[:2]
        same = jnp.where(tail_docs[...].astype(F32) == first_doc[0:1, :] + 1.0, 1.0, 0.0)
        in_tail = jnp.sum(same, 0, keepdims=True)[:, 0:1].astype(jnp.int32)
    at = lax.broadcasted_iota(jnp.int32, (CHUNK, CHUNK), 1)
    row = lax.broadcasted_iota(jnp.int32, (CHUNK, CHUNK), 0)
    good = jnp.concatenate(
        [
            (at <= row) & (at >= bounds[n * CHUNK : (n + 1) * CHUNK] - (base + n * CHUNK))
            for n in range(chunks)
        ],
        0,
    )
    for h in range(values.shape[1] // HEAD_DIM):
        column = slice(h * HEAD_DIM, (h + 1) * HEAD_DIM)
        query = slice(2 * h * HEAD_DIM, (2 * h + 1) * HEAD_DIM)
        key = slice((2 * h + 1) * HEAD_DIM, (2 * h + 2) * HEAD_DIM)
        both = jnp.dot(features[...], pick[h], preferred_element_type=F32).astype(BF16)
        dots = jnp.concatenate(
            [
                lax.dot_general(
                    both[n * CHUNK : (n + 1) * CHUNK, :128], both[n * CHUNK : (n + 1) * CHUNK, 128:],
                    (((1,), (1,)), ((), ())), preferred_element_type=F32,
                )
                for n in range(chunks)
            ],
            0,
        )
        tiles = []
        for n in range(half // TILE):
            near = slice(n * TILE - WIN, (n + 1) * TILE)
            first = bounds[n * TILE : (n + 1) * TILE]
            if n:
                keys, vals = window[near, key], values[near, column]
            else:
                keys = jnp.concatenate([old_window[:, key], window[:TILE, key]], 0)
                vals = jnp.concatenate([old_values[:, column], values[:TILE, column]], 0)
                if part == 0:
                    first = jnp.where(first == 0, -in_tail, first)
            tiles.append(
                (window[n * TILE : (n + 1) * TILE, query], keys, vals, first, base + n * TILE - WIN)
            )
        results = windows(tiles)
        score = dots * (dots * (0.5 / FEAT) + FEAT**-0.5) + 1.0
        score = jnp.where(good, score, 0.0).astype(BF16)
        phi_query[:, h * WIDE : (h + 1) * WIDE] = phi(features[...], expand[h], rows[...])
        for n in range(chunks):
            here = slice(n * CHUNK, (n + 1) * CHUNK)
            inner[here, column] = jnp.dot(
                score[here], values[here, column], preferred_element_type=F32
            )
        for n, result in enumerate(results):
            windowed[n * TILE : (n + 1) * TILE, column] = result


def local(part, both, window, bounds, pick, expand, rows, heads, old=None, docs=()):
    half = both.shape[0] // 2
    group = min(GROUP, heads)

    def full(a):
        return pl.BlockSpec(a.shape, lambda g: (0,) * a.ndim)

    def some(count, width, at=0):
        return pl.BlockSpec((count, group * width), lambda g: (at, g))

    def per_head(a):
        return pl.BlockSpec((group,) + a.shape[1:], lambda g: (g, 0, 0))

    at = half // WIN - 1 if old is None else 0
    return pl.pallas_call(
        functools.partial(local_kernel, part),
        grid=(heads // group,),
        in_specs=[
            pl.BlockSpec((half, LANES), lambda g: (part, heads)),
            some(half, HEAD_DIM, part), some(half, 2 * HEAD_DIM, part),
            some(WIN, HEAD_DIM, at), some(WIN, 2 * HEAD_DIM, at),
            pl.BlockSpec((half, 1), lambda g: (part, 0)),
            per_head(pick), per_head(expand), full(rows),
        ]
        + [full(a) for a in docs],
        out_specs=[some(half, HEAD_DIM), some(half, HEAD_DIM), some(half, WIDE)],
        out_shape=[
            jax.ShapeDtypeStruct((half, heads * HEAD_DIM), F32),
            jax.ShapeDtypeStruct((half, heads * HEAD_DIM), F32),
            jax.ShapeDtypeStruct((half, heads * WIDE), BF16),
        ],
        compiler_params=params(),
    )(both, both, window, *(old or (both, window)), bounds, pick, expand, rows, *docs)


def finish_kernel(part, shifts, limits, first_doc, phi_query, bounds, inner, windowed, prefix, *refs):
    states, out = refs[:shifts], refs[-1]
    unmarked = lax.broadcasted_iota(jnp.int32, (STATE, HEAD_DIM), 0) < STATE - 1
    chunks = inner.shape[0] // CHUNK
    for h in range(inner.shape[1] // HEAD_DIM):
        column = slice(h * HEAD_DIM, (h + 1) * HEAD_DIM)
        incoming = jnp.zeros((STATE, HEAD_DIM), F32)
        for k in range(shifts):
            sent = states[k][h].astype(F32)
            wanted = (sent[STATE - 1 :] == first_doc[0:1, :] + 1.0) & unmarked
            incoming += jnp.where(wanted, sent, 0.0)
        carried = []
        for n in range(chunks):
            chunk = part * chunks + n
            state = incoming
            if chunk:
                state = jnp.where(limits[chunk - 1] <= 0, incoming, 0.0) + prefix[n, h]
            state = jnp.concatenate([state, jnp.zeros((WIDE - STATE, HEAD_DIM), F32)], 0)
            here = slice(n * CHUNK, (n + 1) * CHUNK)
            one = jnp.dot(
                phi_query[here, h * WIDE : (h + 1) * WIDE], state.astype(BF16),
                preferred_element_type=F32,
            )
            carried.append(jnp.where(bounds[here] <= chunk * CHUNK, one, 0.0))
        linear = inner[:, column] + jnp.concatenate(carried, 0)
        mean = jnp.mean(linear * linear, 1, keepdims=True)
        out[:, column] = (linear * lax.rsqrt(mean + 1e-5) + windowed[:, column]).astype(BF16)


def finish(part, limits, first_doc, bounds, prefix, parts, states):
    inner, windowed, phi_query = parts
    half, columns = inner.shape
    heads = columns // HEAD_DIM
    group = min(GROUP, heads)

    def some(count, width):
        return pl.BlockSpec((count, group * width), lambda g, *_: (0, g))

    return pl.pallas_call(
        functools.partial(finish_kernel, part, len(states)),
        grid_spec=pltpu.PrefetchScalarGridSpec(
            num_scalar_prefetch=1,
            grid=(heads // group,),
            in_specs=[
                pl.BlockSpec(first_doc.shape, lambda g, *_: (0, 0)),
                some(half, WIDE), pl.BlockSpec((half, 1), lambda g, *_: (part, 0)),
                some(half, HEAD_DIM), some(half, HEAD_DIM),
                pl.BlockSpec(
                    (prefix.shape[0] // 2, group, STATE, HEAD_DIM), lambda g, *_: (part, g, 0, 0)
                ),
            ]
            + [pl.BlockSpec((group, STATE, HEAD_DIM), lambda g, *_: (g, 0, 0))] * len(states),
            out_specs=some(half, HEAD_DIM),
        ),
        out_shape=jax.ShapeDtypeStruct((half, columns), BF16),
        compiler_params=params(),
    )(limits, first_doc, phi_query, bounds, inner, windowed, prefix, *states)


def after(x, *others):
    return lax.optimization_barrier((x, *others))[0]


def shards(tokens, doc_ids, w_feat, w_value, w_window, w_out):
    rows = tokens.shape[0]
    chunks = rows // CHUNK
    value_columns = w_value.shape[1]
    heads = value_columns // HEAD_DIM
    count = lax.axis_size("head") // 2
    blocks = lax.axis_size("ctx")
    me = lax.axis_index("head")
    z, c = me // 2, me % 2
    place = jnp.stack([z, c]).astype(jnp.int32)

    def hop(x, step, sources):
        return lax.ppermute(x, "head", line(count, step, sources))

    up, down = hop(tokens, 1, range(count)), hop(tokens, -1, range(count))
    far_up, far_down = hop(tokens, count - 1, [0]), hop(tokens, 1 - count, [count - 1])
    tokens_there = swap(tokens, count)

    docs = doc_ids.astype(F32)
    ends = jnp.concatenate([docs[CHUNK::CHUNK], docs[rows - 1 :]])
    limits = jnp.sum((docs[None, :] < ends[:, None]).astype(F32), 1).astype(jnp.int32)
    limits = jnp.concatenate([limits, doc_ids[rows - 1 :]])
    first = jnp.sum((docs[None, :] < docs[:, None]).astype(F32), 1, keepdims=True)
    bounds = first.astype(jnp.int32)
    first_doc = jnp.broadcast_to(docs[:1], (8, HEAD_DIM))
    tail_docs = jnp.broadcast_to((docs[rows - WIN :] + 1.0).astype(BF16)[:, None], (WIN, HEAD_DIM))
    onward = [(i, i + 1) for i in range(blocks - 1)]
    tail_docs = lax.ppermute(tail_docs, "ctx", onward)

    maps, scale_rows = expansions(heads)
    query_map, key_map = jnp.asarray(maps[0]), jnp.asarray(maps[1])
    scale_rows = jnp.asarray(scale_rows)
    pick = jnp.asarray(picks(heads))

    depth, columns = w_out.shape
    width = columns // (2 * count)

    def cut(chip, core):
        return lax.dynamic_slice(w_out, (0, (2 * chip + core) * width), (depth, width))

    other_rows = swap(jnp.stack([cut(chip, 1 - c) for chip in range(count)]), count)

    def out_for(chip):
        chip = jnp.clip(chip, 0, count - 1)
        return jnp.concatenate(
            [cut(chip, c), lax.dynamic_index_in_dim(other_rows, chip, 0, keepdims=False)], 0
        )

    out_up = [out_for(z + count - s) for s in range(1, count)]
    out_down = [out_for(z - count + s) for s in range(1, count)]
    out_here = out_for(z)

    used = value_columns + w_feat.shape[1]
    fv_columns = -(-used // 256) * 256
    weight = jnp.concatenate(
        [w_value, w_feat, jnp.zeros((w_value.shape[0], fv_columns - used), BF16), w_window], 1
    )
    all_columns = weight.shape[1]
    part = project(place, (0,), tokens, tokens_there, weight, 0, all_columns)

    ready = lax.optimization_barrier(
        (up, down, far_up, far_down, limits, bounds, first_doc, tail_docs, part, out_here, *out_up, *out_down)
    )
    up, down, far_up, far_down, limits, bounds, first_doc, tail_docs, part, out_here = ready[:10]
    out_up, out_down = ready[10 : 9 + count], ready[9 + count :]

    ups, downs = [up], [down]
    for s in range(2, count - 1):
        ups.append(hop(ups[-1], 1, range(s - 1, count)))
        downs.append(hop(downs[-1], -1, range(0, count - s + 1)))
    mine = jnp.concatenate([down + far_up, far_down + up], 1)
    part = project(
        place, (1, count - 1), mine, swap(mine, count), weight, 0, all_columns, part
    )
    ups[-1], downs[-1], part = lax.optimization_barrier((ups[-1], downs[-1], part))
    mine = jnp.concatenate([downs[s - 1] + ups[count - s - 1] for s in range(2, count - 1)], 1)
    late = tuple(range(2, count - 1))
    theirs = swap(mine, count)
    both = project(place, late, mine, theirs, weight, 0, fv_columns, part, BF16)
    prefix, state = sums(limits, both, heads, key_map, scale_rows)
    states = [
        lax.ppermute(state, "ctx", [(i, i + k) for i in range(blocks - k)])
        for k in range(1, blocks)
    ]
    window = project(
        place, late, after(mine, state), theirs, weight, fv_columns, all_columns - fv_columns, part,
        BF16,
    )
    local_high = local(1, both, window, bounds, pick, query_map, scale_rows, heads)
    tail = [
        lax.ppermute(a, "ctx", onward)
        for a in (after(both, window)[rows - WIN :, :value_columns], window[rows - WIN :])
    ]
    high = finish(1, limits, first_doc, bounds, prefix, local_high, states)
    def partial(chip, weight, *received):
        total = jnp.dot(chip, weight, preferred_element_type=F32)
        for r in received:
            total += r.astype(F32)
        return total.astype(BF16)

    def first_parts(mixed):
        chip = jnp.concatenate([mixed, swap(mixed, count)], 1)
        return chip, partial(chip, out_up[0]), partial(chip, out_down[0])

    def scattered(chip, up, down):
        for s in range(1, count):
            if s > 1:
                up, down = partial(chip, out_up[s - 1], up), partial(chip, out_down[s - 1], down)
            up = hop(up, 1, range(0, s))
            down = hop(down, -1, range(count - s, count))
        return partial(chip, out_here, up, down)

    high_parts = first_parts(high)
    local_low = local(
        0, after(both, *high_parts[1:]), window, bounds, pick, query_map, scale_rows, heads, tail,
        (tail_docs, first_doc),
    )
    low = finish(0, limits, first_doc, bounds, prefix, local_low, states)

    high_out = scattered(*high_parts)
    low_out = scattered(*first_parts(low))
    return jnp.concatenate([low_out, high_out], 0)


def solution(mesh):
    return jax.shard_map(
        shards,
        mesh=mesh,
        in_specs=(
            P("ctx", "head"),
            P("ctx"),
            P(None, "head"),
            P(None, "head"),
            P(None, "head"),
            P("head", None),
        ),
        out_specs=P("ctx", "head"),
        check_vma=False,
    )
```

time: 281 us -> 221 us (0.79)
  waiting for transfers between devices: 148 us -> 59.9 us
  matrix products: 75.5 us -> 9.95 us
  starting transfers between devices: 11.8 us -> 61.6 us
  Pallas kernels: 0 us -> 47.8 us
  between operations: 13.3 us -> 0.79 us
  other arithmetic: 10.1 us -> 21.6 us
  blocking collectives: 8.97 us -> 0 us
  local copies, waits for them, and re-layouts: 12.5 us -> 17.7 us
    reduce_scatter x1 -> x0, waiting for transfers between devices: 87.4 us -> none  [shards(): lax.psum_scatter(lax.dot_general(w_out, mixed, (((0,), (1,)), ((), ())),...]
    all_gather x2 -> x0, waiting for transfers between devices: 60 us -> none  [the longest x1 60 us: shards(): column_piece = lax.all_gather(tokens, 'head', axis=1, tiled=True)]
    ppermute x3 -> x30, waiting for transfers between devices: 0.01 us -> 59.9 us  [the longest x18 53.5 us: hop(): return lax.ppermute(x, 'head', line(count, step, sources))]
    dot_general x9 -> x14, matrix products: 60.3 us -> 9.95 us  [partial(): total = jnp.dot(chip, weight, preferred_element_type=F32)]
    ppermute x3 -> x30, starting transfers between devices: 11.5 us -> 61.6 us  [the longest x18 44.3 us: hop(): return lax.ppermute(x, 'head', line(count, step, sources))]
    pallas_call x0 -> x9, Pallas kernels: none -> 47.8 us  [the longest x4 30.2 us: project(): pl.pallas_call(functools.partial(project_kernel, len(chips), before is no...]
    concatenate x1 -> x9, other arithmetic: 0.07 us -> 15.5 us  [the longest x1 7.32 us: shards(): jnp.concatenate([w_value, w_feat, jnp.zeros((w_value.shape[0], fv_columns...]
    sub x1 -> x0, matrix products: 15.2 us -> none  [shards(): weights = jnp.exp(logits - top_logit) * within[None].astype(jnp.float32)]
  transfers between devices with their start and end apart: 6 -> 30, of which waited for: 2 -> 11; matrix products, arithmetic and copies ran while one was open for 23% -> 16% of each run, Pallas kernels for 0% -> 14%
where the time goes in v4:
time: 221 us; the launch traced here: 219 us
  starting transfers between devices  61.6 us (28%)
  waiting for transfers between devices  59.9 us (27%)
  Pallas kernels  47.8 us (22%)
  other arithmetic  21.6 us (10%)
  local copies, waits for them, and re-layouts  17.7 us (8%)
  matrix products  9.95 us (5%)
    ppermute x18, waiting for transfers between devices, hop(): return lax.ppermute(x, 'head', line(count, step, sources))  53.5 us
    ppermute x18, starting transfers between devices, hop(): return lax.ppermute(x, 'head', line(count, step, sources))  44.3 us
    pallas_call x4, Pallas kernels, project(): pl.pallas_call(functools.partial(project_kernel, len(chips), before is no...  30.2 us
    dot_general x14, matrix products, partial(): total = jnp.dot(chip, weight, preferred_element_type=F32)  9.95 us
    ppermute x3, starting transfers between devices, shards(): lax.ppermute(state, 'ctx', [(i, i + k) for i in range(blocks - k)])  8.78 us
    pallas_call x2, Pallas kernels, local(): pl.pallas_call(functools.partial(local_kernel, part), grid=(heads // grou...  8.71 us
    unnamed x58, local copies, waits for them, and re-layouts  8.13 us
    concatenate x1, other arithmetic, shards(): jnp.concatenate([w_value, w_feat, jnp.zeros((w_value.shape[0], fv_columns...  7.32 us
  transfers between devices with their start and end apart: 30, of which 11 were waited for; matrix products, arithmetic and copies ran while one was open for 16% of the time, Pallas kernels for 14%

profile of v4, /device:TPU:0, one launch (start us, length us, event | category | flops | bytes accessed | tf_op | source)
XLA Modules:
  0.0 219.4 jit_solution(15927219460866236969)
XLA Ops:
  0.5 5.5 %collective-permute-start = (bf16[1024,512]{1,0:T(8,128)(2,1)}, bf16[1024,512]{1,0:T(8,128)(2,1)}, u32[]{:S(2)}, u32[]{:S(2)}) collective-permute-start(bf16[1024,512]{1,0:T(8,128)(2,1)} %mine.1), channel_id=1, source_target_pairs={{0,2},{1,3},{2,4},{3,5},{4,6},{5,7},{8,10},{9,11},{10,12},{11,13},... | collective-permute-start | bytes 3145736 | tf_op jit(solution)/shard_map/ppermute | solution.py:375
  7.2 7.7 %collective-permute-start.2 = (bf16[1024,512]{1,0:T(8,128)(2,1)}, bf16[1024,512]{1,0:T(8,128)(2,1)}, u32[]{:S(2)}, u32[]{:S(2)}) collective-permute-start(bf16[1024,512]{1,0:T(8,128)(2,1)} %mine.1), channel_id=1, source_target_pairs={{0,6},{1,7},{8,14},{9,15},{16,22},{17,23},{24,30},{25,31}} | collective-permute-start | bytes 3145736 | tf_op jit(solution)/shard_map/ppermute | solution.py:375
  14.9 4.7 %constant_dynamic-slice_fusion = (bf16[512,512]{1,0:T(8,128)(2,1)S(1)}, bf16[512,512]{1,0:T(8,128)(2,1)}, bf16[512,512]{1,0:T(8,128)(2,1)}, bf16[512,512]{1,0:T(...) fusion(bf16[512,4096]{1,0:T(8,128)(2,1)} %param.15, ...), kind=kLoop, calls=%fused_computation.52 | loop fusion | bytes 11534380 | tf_op jit(solution)/shard_map/dynamic_slice | solution.py:401
  23.6 7.3 %pad_maximum_fusion.refs_0_.refs_1_ = bf16[4096,1792]{1,0:T(8,128)(2,1)} fusion(bf16[4096,1024]{1,0:T(8,128)(2,1)S(1)} %copy-done.12, bf16[4096,128]{1,0:T(8,128)(2,1)S(1)} %copy-done.27, bf16[4096,512]{1,0:T(8,128)(2,1)S(1)} %copy-done.13, bf16[1792]{0:T(1024)(128)(2,1)S(1)} %pad.28.clone), kind=kLoop, calls=%fused_computation | loop fusion | flops 58720256 | bytes 28315136 | tf_op jit(solution)/shard_map/concatenate | solution.py:417
  35.8 8.0 %shard_map.100.refs_2_ = f32[1024,1792]{1,0:T(8,128)S(1)} custom-call(s32[2]{0:T(128)S(1)} %pad_add_fusion.1.place, bf16[1024,512]{1,0:T(8,128)(2,1)S(1)} %copy-done.9, bf16[1024,512]{1,0:T(8,128)(2,1)S(1)} %collective-permute-done.5.theirs, bf16[4096,1792]{1,0:T(8,128)(2,1)} %pad_maximum_fusion.refs_0_.refs_1_), custom_call_target="tpu_custom_call" | custom-call | tf_op jit(solution)/shard_map/pallas_call | solution.py:78
  43.9 3.7 %collective-permute-start.4 = (bf16[64,128]{1,0:T(8,128)(2,1)S(1)}, bf16[64,128]{1,0:T(8,128)(2,1)S(1)}, u32[]{:S(2)}, u32[]{:S(2)}) collective-permute-start(bf16[64,128]{1,0:T(8,128)(2,1)S(1)} %broadcast_in_dim.7), channel_id=1, source_target_pairs={{0,8},{8,16},{16,24},{1,9},{9,17},{17,25},{2,10},{10,18},{18,26},{... | collective-permute-start | bytes 49160 | tf_op jit(solution)/shard_map/ppermute | solution.py:390
  47.6 2.6 %dynamic-slice_bitcast_fusion = (bf16[512,512]{1,0:T(8,128)(2,1)S(1)}, bf16[512,512]{1,0:T(8,128)(2,1)S(1)}, bf16[512,512]{1,0:T(8,128)(2,1)S(1)}, bf16[512,512]...) fusion(bf16[4,512,512]{2,1,0:T(8,128)(2,1)} %collective-permute-, ...), kind=kLoop, calls=%fused_computation.40 | loop fusion | bytes 7340060 | tf_op jit(solution)/shard_map/jit(dynamic_index_in_dim)/squeeze | solution.py:408
  56.0 6.9 %collective-permute-done.3 = bf16[1024,512]{1,0:T(8,128)(2,1)S(1)} collective-permute-done((bf16[1024,512]{1,0:T(8,128)(2,1)S(1)}, bf16[1024,512]{1,0:T(8,128)(2,1)S(1)}, u32[]{:S(2)}, u32[]{:S(2)}) %collective-permute-start.3) | collective-permute-done | bytes 1048608 | tf_op jit(solution)/shard_map/ppermute | solution.py:375
  71.4 12.5 %shard_map.101.refs_1_ = f32[1024,1792]{1,0:T(8,128)S(1)} custom-call(s32[2]{0:T(128)S(1)} %pad_add_fusion.1.place, bf16[1024,1024]{1,0:T(8,128)(2,1)S(1)} %pad_maximum_fusion.2.mine, bf16[1024,1024]{1,0:T(8,128)(2,1)S(1)} %collective-permute-done.9.theirs, bf16[4096,1792]{1,0:T(8,128)(2,1)} %pad_maximum_fusion.refs_0_.refs_1_, ...), custom_call_target="tpu_custom_call" | custom-call | tf_op jit(solution)/shard_map/pallas_call | solution.py:78
  84.0 11.7 %collective-permute-done.8 = bf16[1024,512]{1,0:T(8,128)(2,1)S(1)} collective-permute-done((bf16[1024,512]{1,0:T(8,128)(2,1)}, bf16[1024,512]{1,0:T(8,128)(2,1)S(1)}, u32[]{:S(2)}, u32[]{:S(2)}) %collective-permute-start.8) | collective-permute-done | bytes 1048608 | tf_op jit(solution)/shard_map/ppermute | solution.py:375
  96.1 2.6 %collective-permute-done.10.theirs = bf16[1024,512]{1,0:T(8,128)(2,1)S(1)} collective-permute-done((bf16[1024,512]{1,0:T(8,128)(2,1)S(1)}, bf16[1024,512]{1,0:T(8,128)(2,1)S(1)}, u32[]{:S(2)}, u32[]{:S(2)}) %collective-permute-start.10) | collective-permute-done | bytes 1048608 | tf_op jit(solution)/shard_map/ppermute | solution.py:35
  98.7 4.3 %shard_map.102.values.features.old_values = bf16[1024,768]{1,0:T(8,128)(2,1)S(1)} custom-call(s32[2]{0:T(128)S(1)} %pad_add_fusion.1.place, bf16[1024,512]{1,0:T(8,128)(2,1)S(1)} %add.183.mine, bf16[1024,512]{1,0:T(8,128)(2,1)S(1)} %collective-permute-done.10.theirs, bf16[4096,1792]{1,0:T(8,128)(2,1)} %pad_maximum_fusion.refs_0_.refs_1_, ...), custom_call_target="tpu_custom_call" | custom-call | tf_op jit(solution)/shard_map/pallas_call | solution.py:78
  103.1 3.8 %shard_map.103 = (f32[4,4,160,128]{3,2,1,0:T(8,128)S(1)}, bf16[4,160,128]{2,1,0:T(8,128)(2,1)}) custom-call(s32[5]{0:T(128)S(1)} %pad_add_fusion.limits, bf16[1024,768]{1,0:T(8,128)(2,1)S(1)} %shard_map.102.values.features.old_values, bf16[1024,768]{1,0:T(8,128)(2,1)S(1)} %shard_map.102.values.features.old_values, bf16[4,128,512]{2,1,0:T(8,128)(2,1)S(1)} %copy-done.10, ...), custom_call_target="tpu_custom_call" | custom-call | tf_op jit(solution)/shard_map/pallas_call | solution.py:158
  108.0 3.4 %collective-permute-start.11 = (bf16[4,160,128]{2,1,0:T(8,128)(2,1)}, bf16[4,160,128]{2,1,0:T(8,128)(2,1)S(1)}, u32[]{:S(2)}, u32[]{:S(2)}) collective-permute-start(bf16[4,160,128]{2,1,0:T(8,128)(2,1)} %get-tuple-element.45), channel_id=1, source_target_pairs={{0,8},{8,16},{16,24},{1,9},{9,17},{17,25},{2,10},{10,18},{18,26},{... | collective-permute-start | bytes 491528 | tf_op jit(solution)/shard_map/ppermute | solution.py:444
  111.4 3.4 %collective-permute-start.12 = (bf16[4,160,128]{2,1,0:T(8,128)(2,1)}, bf16[4,160,128]{2,1,0:T(8,128)(2,1)S(1)}, u32[]{:S(2)}, u32[]{:S(2)}) collective-permute-start(bf16[4,160,128]{2,1,0:T(8,128)(2,1)} %get-tuple-element.45), channel_id=1, source_target_pairs={{0,16},{8,24},{1,17},{9,25},{2,18},{10,26},{3,19},{11,27},{4,20},{... | collective-permute-start | bytes 491528 | tf_op jit(solution)/shard_map/ppermute | solution.py:444
  117.0 3.1 %copy-done.1 = f32[1024,1792]{1,0:T(8,128)S(1)} copy-done((f32[1024,1792]{1,0:T(8,128)S(1)}, f32[1024,1792]{1,0:T(8,128)}, u32[]{:S(2)}) %copy-start.1) | copy-done | bytes 7340056
  121.3 5.3 %shard_map.104.window.old_window = bf16[1024,1024]{1,0:T(8,128)(2,1)S(1)} custom-call(s32[2]{0:T(128)S(1)} %pad_add_fusion.1.place, bf16[1024,512]{1,0:T(8,128)(2,1)S(1)} %add.183.mine, bf16[1024,512]{1,0:T(8,128)(2,1)S(1)} %copy-done.6, bf16[4096,1792]{1,0:T(8,128)(2,1)} %pad_maximum_fusion.refs_0_.refs_1_, f32[1024,1792]{1,0:T(8,128)S(1)} %copy-done.1), custom_call_target="tpu_custom_call" | custom-call | tf_op jit(solution)/shard_map/pallas_call | solution.py:78
  126.7 4.4 %shard_map.105 = (f32[512,512]{1,0:T(8,128)S(1)}, f32[512,512]{1,0:T(8,128)S(1)}, bf16[512,1024]{1,0:T(8,128)(2,1)S(1)}) custom-call(bf16[1024,768]{1,0:T(8,128)(2,1)S(1)} %shard_map.102.values.features.old_values, bf16[1024,768]{1,0:T(8,128)(2,1)S(1)} %shard_map.102.values.features.old_values, bf16[1024,1024]{1,0:T(8,128)(2,1)S(1)} %shard_map.104.window.old_window, ...), custom_call_target="tpu_custom_call" | custom-call | tf_op jit(solution)/shard_map/pallas_call | solution.py:279
  131.1 2.5 %shard_map.106 = bf16[512,512]{1,0:T(8,128)(2,1)S(1)} custom-call(s32[5]{0:T(128)S(1)} %pad_add_fusion.limits, f32[8,128]{1,0:T(8,128)S(1)} %broadcast_in_dim.6.first_doc.refs_1_, bf16[512,1024]{1,0:T(8,128)(2,1)S(1)} %get-tuple-element.48.phi_query, s32[1024,1]{1,0:T(8,128)S(1)} %copy.15.bounds, f32[512,512]{1,0:T(8,128)S(1)} %get-tuple-element.49.inner, ...), custom_call_target="tpu_custom_call" | custom-call | tf_op jit(solution)/shard_map/pallas_call | solution.py:338
  135.2 2.7 %collective-permute-start.16 = (bf16[64,1024]{1,0:T(8,128)(2,1)S(1)}, bf16[64,1024]{1,0:T(8,128)(2,1)S(1)}, u32[]{:S(2)}, u32[]{:S(2)}) collective-permute-start(bf16[64,1024]{1,0:T(8,128)(2,1)S(1)} %slice.31), channel_id=1, source_target_pairs={{0,8},{8,16},{16,24},{1,9},{9,17},{17,25},{2,10},{10,18},{18,26},{... | collective-permute-start | bytes 393224 | tf_op jit(solution)/shard_map/ppermute | solution.py:453
  141.0 4.3 %shard_map.107 = (f32[512,512]{1,0:T(8,128)S(1)}, f32[512,512]{1,0:T(8,128)S(1)}, bf16[512,1024]{1,0:T(8,128)(2,1)S(1)}) custom-call(bf16[1024,768]{1,0:T(8,128)(2,1)S(1)} %shard_map.102.values.features.old_values, bf16[1024,768]{1,0:T(8,128)(2,1)S(1)} %shard_map.102.values.features.old_values, bf16[1024,1024]{1,0:T(8,128)(2,1)S(1)} %shard_map.104.window.old_window, ...), custom_call_target="tpu_custom_call" | custom-call | tf_op jit(solution)/shard_map/pallas_call | solution.py:279
  145.4 2.6 %shard_map.108 = bf16[512,512]{1,0:T(8,128)(2,1)S(1)} custom-call(s32[5]{0:T(128)S(1)} %pad_add_fusion.limits, f32[8,128]{1,0:T(8,128)S(1)} %broadcast_in_dim.6.first_doc.refs_1_, bf16[512,1024]{1,0:T(8,128)(2,1)S(1)} %get-tuple-element.57.phi_query, s32[1024,1]{1,0:T(8,128)S(1)} %copy.15.bounds, f32[512,512]{1,0:T(8,128)S(1)} %get-tuple-element.58.inner, ...), custom_call_target="tpu_custom_call" | custom-call | tf_op jit(solution)/shard_map/pallas_call | solution.py:338
  154.1 7.7 %collective-permute-done.24 = bf16[512,512]{1,0:T(8,128)(2,1)S(1)} collective-permute-done((bf16[512,512]{1,0:T(8,128)(2,1)S(1)}, bf16[512,512]{1,0:T(8,128)(2,1)S(1)}, u32[]{:S(2)}, u32[]{:S(2)}) %collective-permute-start.24) | collective-permute-done | bytes 524320 | tf_op jit(solution)/shard_map/ppermute | solution.py:375
  162.6 4.4 %collective-permute-start.25 = (bf16[512,512]{1,0:T(8,128)(2,1)S(1)}, bf16[512,512]{1,0:T(8,128)(2,1)S(1)}, u32[]{:S(2)}, u32[]{:S(2)}) collective-permute-start(bf16[512,512]{1,0:T(8,128)(2,1)S(1)} %fusion.7), channel_id=1, source_target_pairs={{0,2},{1,3},{2,4},{3,5},{8,10},{9,11},{10,12},{11,13},{16,18},{17,... | collective-permute-start | bytes 1572872 | tf_op jit(solution)/shard_map/ppermute | solution.py:375
  168.4 4.7 %collective-permute-done.18 = bf16[512,512]{1,0:T(8,128)(2,1)S(1)} collective-permute-done((bf16[512,512]{1,0:T(8,128)(2,1)S(1)}, bf16[512,512]{1,0:T(8,128)(2,1)S(1)}, u32[]{:S(2)}, u32[]{:S(2)}) %collective-permute-start.18) | collective-permute-done | bytes 524320 | tf_op jit(solution)/shard_map/ppermute | solution.py:375
  173.8 4.5 %collective-permute-start.19 = (bf16[512,512]{1,0:T(8,128)(2,1)S(1)}, bf16[512,512]{1,0:T(8,128)(2,1)S(1)}, u32[]{:S(2)}, u32[]{:S(2)}) collective-permute-start(bf16[512,512]{1,0:T(8,128)(2,1)S(1)} %fusion.3), channel_id=1, source_target_pairs={{0,2},{1,3},{2,4},{3,5},{8,10},{9,11},{10,12},{11,13},{16,18},{17,... | collective-permute-start | bytes 1572872 | tf_op jit(solution)/shard_map/ppermute | solution.py:375
  179.9 4.4 %collective-permute-done.25 = bf16[512,512]{1,0:T(8,128)(2,1)S(1)} collective-permute-done((bf16[512,512]{1,0:T(8,128)(2,1)S(1)}, bf16[512,512]{1,0:T(8,128)(2,1)S(1)}, u32[]{:S(2)}, u32[]{:S(2)}) %collective-permute-start.25) | collective-permute-done | bytes 524320 | tf_op jit(solution)/shard_map/ppermute | solution.py:375
  185.0 4.4 %collective-permute-start.26 = (bf16[512,512]{1,0:T(8,128)(2,1)S(1)}, bf16[512,512]{1,0:T(8,128)(2,1)S(1)}, u32[]{:S(2)}, u32[]{:S(2)}) collective-permute-start(bf16[512,512]{1,0:T(8,128)(2,1)S(1)} %fusion.6), channel_id=1, source_target_pairs={{0,2},{1,3},{2,4},{3,5},{4,6},{5,7},{8,10},{9,11},{10,12},{11,13},... | collective-permute-start | bytes 1572872 | tf_op jit(solution)/shard_map/ppermute | solution.py:375
  191.5 4.1 %collective-permute-done.19 = bf16[512,512]{1,0:T(8,128)(2,1)S(1)} collective-permute-done((bf16[512,512]{1,0:T(8,128)(2,1)S(1)}, bf16[512,512]{1,0:T(8,128)(2,1)S(1)}, u32[]{:S(2)}, u32[]{:S(2)}) %collective-permute-start.19) | collective-permute-done | bytes 524320 | tf_op jit(solution)/shard_map/ppermute | solution.py:375
  196.3 4.6 %collective-permute-start.20 = (bf16[512,512]{1,0:T(8,128)(2,1)S(1)}, bf16[512,512]{1,0:T(8,128)(2,1)S(1)}, u32[]{:S(2)}, u32[]{:S(2)}) collective-permute-start(bf16[512,512]{1,0:T(8,128)(2,1)S(1)} %fusion.2), channel_id=1, source_target_pairs={{0,2},{1,3},{2,4},{3,5},{4,6},{5,7},{8,10},{9,11},{10,12},{11,13},... | collective-permute-start | bytes 1572872 | tf_op jit(solution)/shard_map/ppermute | solution.py:375
  202.9 3.9 %collective-permute-done.26 = bf16[512,512]{1,0:T(8,128)(2,1)S(1)} collective-permute-done((bf16[512,512]{1,0:T(8,128)(2,1)S(1)}, bf16[512,512]{1,0:T(8,128)(2,1)S(1)}, u32[]{:S(2)}, u32[]{:S(2)}) %collective-permute-start.26) | collective-permute-done | bytes 524320 | tf_op jit(solution)/shard_map/ppermute | solution.py:375
  207.5 10.1 %collective-permute-done.20 = bf16[512,512]{1,0:T(8,128)(2,1)S(1)} collective-permute-done((bf16[512,512]{1,0:T(8,128)(2,1)S(1)}, bf16[512,512]{1,0:T(8,128)(2,1)S(1)}, u32[]{:S(2)}, u32[]{:S(2)}) %collective-permute-start.20) | collective-permute-done | bytes 524320 | tf_op jit(solution)/shard_map/ppermute | solution.py:375
  (141 shorter events, 52.8 us)
Async XLA Ops:
  0.0 34.5 %collective-permute-start.5 = (bf16[1024,512]{1,0:T(8,128)(2,1)}, bf16[1024,512]{1,0:T(8,128)(2,1)S(1)}, u32[]{:S(2)}, u32[]{:S(2)}) collective-permute-start(bf16[1024,512]{1,0:T(8,128)(2,1)} %mine.1), channel_id=1, source_target_pairs={{0,1},{1,0},{2,3},{3,2},{4,5},{5,4},{6,7},{7,6},{8,9},{9,8},{10,11... | collective-permute-start | bytes 3145736 | tf_op jit(solution)/shard_map/ppermute | solution.py:35
  0.5 55.5 %collective-permute-start = (bf16[1024,512]{1,0:T(8,128)(2,1)}, bf16[1024,512]{1,0:T(8,128)(2,1)}, u32[]{:S(2)}, u32[]{:S(2)}) collective-permute-start(bf16[1024,512]{1,0:T(8,128)(2,1)} %mine.1), channel_id=1, source_target_pairs={{0,2},{1,3},{2,4},{3,5},{4,6},{5,7},{8,10},{9,11},{10,12},{11,13},... | collective-permute-start | bytes 3145736 | tf_op jit(solution)/shard_map/ppermute | solution.py:375
  5.9 50.1 %collective-permute-start.1 = (bf16[1024,512]{1,0:T(8,128)(2,1)}, bf16[1024,512]{1,0:T(8,128)(2,1)}, u32[]{:S(2)}, u32[]{:S(2)}) collective-permute-start(bf16[1024,512]{1,0:T(8,128)(2,1)} %mine.1), channel_id=1, source_target_pairs={{2,0},{3,1},{4,2},{5,3},{6,4},{7,5},{10,8},{11,9},{12,10},{13,11},... | collective-permute-start | bytes 3145736 | tf_op jit(solution)/shard_map/ppermute | solution.py:375
  7.2 48.8 %collective-permute-start.2 = (bf16[1024,512]{1,0:T(8,128)(2,1)}, bf16[1024,512]{1,0:T(8,128)(2,1)}, u32[]{:S(2)}, u32[]{:S(2)}) collective-permute-start(bf16[1024,512]{1,0:T(8,128)(2,1)} %mine.1), channel_id=1, source_target_pairs={{0,6},{1,7},{8,14},{9,15},{16,22},{17,23},{24,30},{25,31}} | collective-permute-start | bytes 3145736 | tf_op jit(solution)/shard_map/ppermute | solution.py:375
  21.2 22.7 %collective-permute-start.6 = (bf16[4,512,512]{2,1,0:T(8,128)(2,1)}, bf16[4,512,512]{2,1,0:T(8,128)(2,1)}, u32[]{:S(2)}, u32[]{:S(2)}) collective-permute-start(bf16[4,512,512]{2,1,0:T(8,128)(2,1)} %pad_maximum_fusion.1), channel_id=1, source_target_pairs={{0,1},{1,0},{2,3},{3,2},{4,5},{5,4},{6,7},{7,6},{8,9},{9,8},{10,11... | collective-permute-start | bytes 6291464 | tf_op jit(solution)/shard_map/ppermute | solution.py:35
  34.5 28.4 %collective-permute-start.3 = (bf16[1024,512]{1,0:T(8,128)(2,1)S(1)}, bf16[1024,512]{1,0:T(8,128)(2,1)S(1)}, u32[]{:S(2)}, u32[]{:S(2)}) collective-permute-start(bf16[1024,512]{1,0:T(8,128)(2,1)S(1)} %copy-done.9), channel_id=1, source_target_pairs={{6,0},{7,1},{14,8},{15,9},{22,16},{23,17},{30,24},{31,25}} | collective-permute-start | bytes 3145736 | tf_op jit(solution)/shard_map/ppermute | solution.py:375
  43.9 12.0 %collective-permute-start.4 = (bf16[64,128]{1,0:T(8,128)(2,1)S(1)}, bf16[64,128]{1,0:T(8,128)(2,1)S(1)}, u32[]{:S(2)}, u32[]{:S(2)}) collective-permute-start(bf16[64,128]{1,0:T(8,128)(2,1)S(1)} %broadcast_in_dim.7), channel_id=1, source_target_pairs={{0,8},{8,16},{16,24},{1,9},{9,17},{17,25},{2,10},{10,18},{18,26},{... | collective-permute-start | bytes 49160 | tf_op jit(solution)/shard_map/ppermute | solution.py:390
  67.2 4.2 %collective-permute-start.9 = (bf16[1024,1024]{1,0:T(8,128)(2,1)S(1)}, bf16[1024,1024]{1,0:T(8,128)(2,1)S(1)}, u32[]{:S(2)}, u32[]{:S(2)}) collective-permute-start(bf16[1024,1024]{1,0:T(8,128)(2,1)S(1)} %pad_maximum_fusion.2.mine), channel_id=1, source_target_pairs={{0,1},{1,0},{2,3},{3,2},{4,5},{5,4},{6,7},{7,6},{8,9},{9,8},{10,11... | collective-permute-start | bytes 6291464 | tf_op jit(solution)/shard_map/ppermute | solution.py:35
  67.2 16.7 %collective-permute-start.7 = (bf16[1024,512]{1,0:T(8,128)(2,1)}, bf16[1024,512]{1,0:T(8,128)(2,1)S(1)}, u32[]{:S(2)}, u32[]{:S(2)}) collective-permute-start(bf16[1024,512]{1,0:T(8,128)(2,1)} %collective-permute-done), channel_id=1, source_target_pairs={{2,4},{3,5},{4,6},{5,7},{10,12},{11,13},{12,14},{13,15},{18,20},{1... | collective-permute-start | bytes 3145736 | tf_op jit(solution)/shard_map/ppermute | solution.py:375
  68.0 27.7 %collective-permute-start.8 = (bf16[1024,512]{1,0:T(8,128)(2,1)}, bf16[1024,512]{1,0:T(8,128)(2,1)S(1)}, u32[]{:S(2)}, u32[]{:S(2)}) collective-permute-start(bf16[1024,512]{1,0:T(8,128)(2,1)} %collective-permute-done.1), channel_id=1, source_target_pairs={{2,0},{3,1},{4,2},{5,3},{10,8},{11,9},{12,10},{13,11},{18,16},{19,... | collective-permute-start | bytes 3145736 | tf_op jit(solution)/shard_map/ppermute | solution.py:375
  83.9 19.1 %copy-start = (f32[1024,1792]{1,0:T(8,128)}, f32[1024,1792]{1,0:T(8,128)S(1)}, u32[]{:S(2)}) copy-start(f32[1024,1792]{1,0:T(8,128)S(1)} %shard_map.101.refs_1_) | copy-start | bytes 22020100
  96.0 2.7 %collective-permute-start.10 = (bf16[1024,512]{1,0:T(8,128)(2,1)S(1)}, bf16[1024,512]{1,0:T(8,128)(2,1)S(1)}, u32[]{:S(2)}, u32[]{:S(2)}) collective-permute-start(bf16[1024,512]{1,0:T(8,128)(2,1)S(1)} %add.183.mine), channel_id=1, source_target_pairs={{0,1},{1,0},{2,3},{3,2},{4,5},{5,4},{6,7},{7,6},{8,9},{9,8},{10,11... | collective-permute-start | bytes 3145736 | tf_op jit(solution)/shard_map/ppermute | solution.py:35
  108.0 23.0 %collective-permute-start.11 = (bf16[4,160,128]{2,1,0:T(8,128)(2,1)}, bf16[4,160,128]{2,1,0:T(8,128)(2,1)S(1)}, u32[]{:S(2)}, u32[]{:S(2)}) collective-permute-start(bf16[4,160,128]{2,1,0:T(8,128)(2,1)} %get-tuple-element.45), channel_id=1, source_target_pairs={{0,8},{8,16},{16,24},{1,9},{9,17},{17,25},{2,10},{10,18},{18,26},{... | collective-permute-start | bytes 491528 | tf_op jit(solution)/shard_map/ppermute | solution.py:444
  111.4 19.7 %collective-permute-start.12 = (bf16[4,160,128]{2,1,0:T(8,128)(2,1)}, bf16[4,160,128]{2,1,0:T(8,128)(2,1)S(1)}, u32[]{:S(2)}, u32[]{:S(2)}) collective-permute-start(bf16[4,160,128]{2,1,0:T(8,128)(2,1)} %get-tuple-element.45), channel_id=1, source_target_pairs={{0,16},{8,24},{1,17},{9,25},{2,18},{10,26},{3,19},{11,27},{4,20},{... | collective-permute-start | bytes 491528 | tf_op jit(solution)/shard_map/ppermute | solution.py:444
  114.8 16.2 %collective-permute-start.13 = (bf16[4,160,128]{2,1,0:T(8,128)(2,1)}, bf16[4,160,128]{2,1,0:T(8,128)(2,1)}, u32[]{:S(2)}, u32[]{:S(2)}) collective-permute-start(bf16[4,160,128]{2,1,0:T(8,128)(2,1)} %get-tuple-element.45), channel_id=1, source_target_pairs={{0,24},{1,25},{2,26},{3,27},{4,28},{5,29},{6,30},{7,31}} | collective-permute-start | bytes 491528 | tf_op jit(solution)/shard_map/ppermute | solution.py:444
  133.6 4.3 %collective-permute-start.14 = (bf16[512,512]{1,0:T(8,128)(2,1)S(1)}, bf16[512,512]{1,0:T(8,128)(2,1)S(1)}, u32[]{:S(2)}, u32[]{:S(2)}) collective-permute-start(bf16[512,512]{1,0:T(8,128)(2,1)S(1)} %shard_map.106), channel_id=1, source_target_pairs={{0,1},{1,0},{2,3},{3,2},{4,5},{5,4},{6,7},{7,6},{8,9},{9,8},{10,11... | collective-permute-start | bytes 1572872 | tf_op jit(solution)/shard_map/ppermute | solution.py:35
  133.7 5.6 %collective-permute-start.15 = (bf16[64,512]{1,0:T(8,128)(2,1)S(1)}, bf16[64,512]{1,0:T(8,128)(2,1)S(1)}, u32[]{:S(2)}, u32[]{:S(2)}) collective-permute-start(bf16[64,512]{1,0:T(8,128)(2,1)S(1)} %slice.29), channel_id=1, source_target_pairs={{0,8},{8,16},{16,24},{1,9},{9,17},{17,25},{2,10},{10,18},{18,26},{... | collective-permute-start | bytes 196616 | tf_op jit(solution)/shard_map/ppermute | solution.py:453
  135.2 5.8 %collective-permute-start.16 = (bf16[64,1024]{1,0:T(8,128)(2,1)S(1)}, bf16[64,1024]{1,0:T(8,128)(2,1)S(1)}, u32[]{:S(2)}, u32[]{:S(2)}) collective-permute-start(bf16[64,1024]{1,0:T(8,128)(2,1)S(1)} %slice.31), channel_id=1, source_target_pairs={{0,8},{8,16},{16,24},{1,9},{9,17},{17,25},{2,10},{10,18},{18,26},{... | collective-permute-start | bytes 393224 | tf_op jit(solution)/shard_map/ppermute | solution.py:453
  148.0 2.4 %collective-permute-start.17 = (bf16[512,512]{1,0:T(8,128)(2,1)S(1)}, bf16[512,512]{1,0:T(8,128)(2,1)S(1)}, u32[]{:S(2)}, u32[]{:S(2)}) collective-permute-start(bf16[512,512]{1,0:T(8,128)(2,1)S(1)} %shard_map.108), channel_id=1, source_target_pairs={{0,1},{1,0},{2,3},{3,2},{4,5},{5,4},{6,7},{7,6},{8,9},{9,8},{10,11... | collective-permute-start | bytes 1572872 | tf_op jit(solution)/shard_map/ppermute | solution.py:35
  148.1 13.8 %collective-permute-start.24 = (bf16[512,512]{1,0:T(8,128)(2,1)S(1)}, bf16[512,512]{1,0:T(8,128)(2,1)S(1)}, u32[]{:S(2)}, u32[]{:S(2)}) collective-permute-start(bf16[512,512]{1,0:T(8,128)(2,1)S(1)} %convolution_convert_fusion.3), channel_id=1, source_target_pairs={{0,2},{1,3},{8,10},{9,11},{16,18},{17,19},{24,26},{25,27}} | collective-permute-start | bytes 1572872 | tf_op jit(solution)/shard_map/ppermute | solution.py:375
  149.7 17.3 %collective-permute-start.27 = (bf16[512,512]{1,0:T(8,128)(2,1)S(1)}, bf16[512,512]{1,0:T(8,128)(2,1)S(1)}, u32[]{:S(2)}, u32[]{:S(2)}) collective-permute-start(bf16[512,512]{1,0:T(8,128)(2,1)S(1)} %convolution_convert_fusion.2), channel_id=1, source_target_pairs={{6,4},{7,5},{14,12},{15,13},{22,20},{23,21},{30,28},{31,29}} | collective-permute-start | bytes 1572872 | tf_op jit(solution)/shard_map/ppermute | solution.py:375
  151.1 22.0 %collective-permute-start.18 = (bf16[512,512]{1,0:T(8,128)(2,1)S(1)}, bf16[512,512]{1,0:T(8,128)(2,1)S(1)}, u32[]{:S(2)}, u32[]{:S(2)}) collective-permute-start(bf16[512,512]{1,0:T(8,128)(2,1)S(1)} %convolution_convert_fusion.1), channel_id=1, source_target_pairs={{0,2},{1,3},{8,10},{9,11},{16,18},{17,19},{24,26},{25,27}} | collective-permute-start | bytes 1572872 | tf_op jit(solution)/shard_map/ppermute | solution.py:375
  153.3 13.7 %copy-start.23 = (bf16[1024,512]{1,0:T(8,128)(2,1)S(1)}, bf16[1024,512]{1,0:T(8,128)(2,1)}, u32[]{:S(2)}) copy-start(bf16[1024,512]{1,0:T(8,128)(2,1)} %get-tuple-element.64) | copy-start | bytes 3145732
  153.3 25.1 %collective-permute-start.21 = (bf16[512,512]{1,0:T(8,128)(2,1)S(1)}, bf16[512,512]{1,0:T(8,128)(2,1)S(1)}, u32[]{:S(2)}, u32[]{:S(2)}) collective-permute-start(bf16[512,512]{1,0:T(8,128)(2,1)S(1)} %convolution_convert_fusion), channel_id=1, source_target_pairs={{6,4},{7,5},{14,12},{15,13},{22,20},{23,21},{30,28},{31,29}} | collective-permute-start | bytes 1572872 | tf_op jit(solution)/shard_map/ppermute | solution.py:375
  162.6 21.8 %collective-permute-start.25 = (bf16[512,512]{1,0:T(8,128)(2,1)S(1)}, bf16[512,512]{1,0:T(8,128)(2,1)S(1)}, u32[]{:S(2)}, u32[]{:S(2)}) collective-permute-start(bf16[512,512]{1,0:T(8,128)(2,1)S(1)} %fusion.7), channel_id=1, source_target_pairs={{0,2},{1,3},{2,4},{3,5},{8,10},{9,11},{10,12},{11,13},{16,18},{17,... | collective-permute-start | bytes 1572872 | tf_op jit(solution)/shard_map/ppermute | solution.py:375
  167.7 21.7 %collective-permute-start.28 = (bf16[512,512]{1,0:T(8,128)(2,1)S(1)}, bf16[512,512]{1,0:T(8,128)(2,1)S(1)}, u32[]{:S(2)}, u32[]{:S(2)}) collective-permute-start(bf16[512,512]{1,0:T(8,128)(2,1)S(1)} %fusion.9), channel_id=1, source_target_pairs={{4,2},{5,3},{6,4},{7,5},{12,10},{13,11},{14,12},{15,13},{20,18},{2... | collective-permute-start | bytes 1572872 | tf_op jit(solution)/shard_map/ppermute | solution.py:375
  173.8 21.7 %collective-permute-start.19 = (bf16[512,512]{1,0:T(8,128)(2,1)S(1)}, bf16[512,512]{1,0:T(8,128)(2,1)S(1)}, u32[]{:S(2)}, u32[]{:S(2)}) collective-permute-start(bf16[512,512]{1,0:T(8,128)(2,1)S(1)} %fusion.3), channel_id=1, source_target_pairs={{0,2},{1,3},{2,4},{3,5},{8,10},{9,11},{10,12},{11,13},{16,18},{17,... | collective-permute-start | bytes 1572872 | tf_op jit(solution)/shard_map/ppermute | solution.py:375
  179.1 21.7 %collective-permute-start.22 = (bf16[512,512]{1,0:T(8,128)(2,1)S(1)}, bf16[512,512]{1,0:T(8,128)(2,1)S(1)}, u32[]{:S(2)}, u32[]{:S(2)}) collective-permute-start(bf16[512,512]{1,0:T(8,128)(2,1)S(1)} %fusion.5), channel_id=1, source_target_pairs={{4,2},{5,3},{6,4},{7,5},{12,10},{13,11},{14,12},{15,13},{20,18},{2... | collective-permute-start | bytes 1572872 | tf_op jit(solution)/shard_map/ppermute | solution.py:375
  185.0 21.8 %collective-permute-start.26 = (bf16[512,512]{1,0:T(8,128)(2,1)S(1)}, bf16[512,512]{1,0:T(8,128)(2,1)S(1)}, u32[]{:S(2)}, u32[]{:S(2)}) collective-permute-start(bf16[512,512]{1,0:T(8,128)(2,1)S(1)} %fusion.6), channel_id=1, source_target_pairs={{0,2},{1,3},{2,4},{3,5},{4,6},{5,7},{8,10},{9,11},{10,12},{11,13},... | collective-permute-start | bytes 1572872 | tf_op jit(solution)/shard_map/ppermute | solution.py:375
  190.2 16.6 %collective-permute-start.29 = (bf16[512,512]{1,0:T(8,128)(2,1)S(1)}, bf16[512,512]{1,0:T(8,128)(2,1)S(1)}, u32[]{:S(2)}, u32[]{:S(2)}) collective-permute-start(bf16[512,512]{1,0:T(8,128)(2,1)S(1)} %fusion.8), channel_id=1, source_target_pairs={{2,0},{3,1},{4,2},{5,3},{6,4},{7,5},{10,8},{11,9},{12,10},{13,11},... | collective-permute-start | bytes 1572872 | tf_op jit(solution)/shard_map/ppermute | solution.py:375
  196.3 21.4 %collective-permute-start.20 = (bf16[512,512]{1,0:T(8,128)(2,1)S(1)}, bf16[512,512]{1,0:T(8,128)(2,1)S(1)}, u32[]{:S(2)}, u32[]{:S(2)}) collective-permute-start(bf16[512,512]{1,0:T(8,128)(2,1)S(1)} %fusion.2), channel_id=1, source_target_pairs={{0,2},{1,3},{2,4},{3,5},{4,6},{5,7},{8,10},{9,11},{10,12},{11,13},... | collective-permute-start | bytes 1572872 | tf_op jit(solution)/shard_map/ppermute | solution.py:375
  201.6 16.1 %collective-permute-start.23 = (bf16[512,512]{1,0:T(8,128)(2,1)S(1)}, bf16[512,512]{1,0:T(8,128)(2,1)S(1)}, u32[]{:S(2)}, u32[]{:S(2)}) collective-permute-start(bf16[512,512]{1,0:T(8,128)(2,1)S(1)} %fusion.4), channel_id=1, source_target_pairs={{2,0},{3,1},{4,2},{5,3},{6,4},{7,5},{10,8},{11,9},{12,10},{13,11},... | collective-permute-start | bytes 1572872 | tf_op jit(solution)/shard_map/ppermute | solution.py:375
  (27 other events, 154.6 us)

commit v5 on v4

--- a/solution.py
+++ b/solution.py
@@ -23,33 +23,35 @@
 BF16 = jnp.bfloat16
 
 
-def params():
-    return pltpu.CompilerParams(vmem_limit_bytes=VMEM, dimension_semantics=("arbitrary",))
-
-
-def line(count, step, sources):
-    return [(2 * z + c, 2 * (z + step) + c) for z in sources for c in (0, 1) if 0 <= z + step < count]
+def params(limit=VMEM):
+    return pltpu.CompilerParams(vmem_limit_bytes=limit, dimension_semantics=("arbitrary",))
+
+
+def ring(x, step, count):
+    return lax.ppermute(
+        x, "head", [(2 * z + c, 2 * ((z + step) % count) + c) for z in range(count) for c in (0, 1)]
+    )
 
 
 def swap(x, count):
     return lax.ppermute(x, "head", [(h, h ^ 1) for h in range(2 * count)])
 
 
-def project_kernel(chips, has_before, place, mine, theirs, *refs):
-    weights, out, both = refs[:chips], refs[-2], refs[-1]
-    width = mine.shape[1] // chips
+def project_kernel(chips, has_before, place, *refs):
+    mine, theirs, weights = refs[:chips], refs[chips : 2 * chips], refs[2 * chips : 3 * chips]
+    out, both = refs[-2], refs[-1]
+    width = mine[0].shape[1]
     c = place[1]
 
     @pl.when(pl.program_id(0) == 0)
     def _():
         for n in range(chips):
-            piece = slice(n * width, (n + 1) * width)
             own = pl.multiple_of((2 * n + c) * width, width)
             other = pl.multiple_of((2 * n + 1 - c) * width, width)
-            both[:, pl.ds(own, width)] = mine[:, piece]
-            both[:, pl.ds(other, width)] = theirs[:, piece]
-
-    total = refs[chips][...] if has_before else None
+            both[:, pl.ds(own, width)] = mine[n][...]
+            both[:, pl.ds(other, width)] = theirs[n][...]
+
+    total = refs[3 * chips][...] if has_before else None
     for n in range(chips):
         rows = both[:, 2 * n * width : 2 * (n + 1) * width]
         part = jnp.dot(rows, weights[n][...], preferred_element_type=F32)
@@ -58,20 +60,18 @@
 
 
 def project(place, chips, mine, theirs, weight, first, columns, before=None, dtype=F32):
-    rows = mine.shape[0]
-    width = mine.shape[1] // len(chips)
+    rows, width = mine[0].shape
     count = weight.shape[0] // (2 * width)
     tile = 256
     start = first // tile
-    whole = pl.BlockSpec(mine.shape, lambda j, p: (0, 0))
-    specs = [whole, whole]
+    specs = [pl.BlockSpec((rows, width), lambda j, p: (0, 0))] * (2 * len(chips))
     for n in chips:
         specs.append(
             pl.BlockSpec(
                 (2 * width, tile), lambda j, p, n=n: (lax.rem(p[0] + n, count), start + j)
             )
         )
-    args = [mine, theirs] + [weight] * len(chips)
+    args = [*mine, *theirs] + [weight] * len(chips)
     if before is not None:
         specs.append(pl.BlockSpec((rows, tile), lambda j, p: (0, start + j)))
         args.append(before)
@@ -82,10 +82,10 @@
             grid=(columns // tile,),
             in_specs=specs,
             out_specs=pl.BlockSpec((rows, tile), lambda j, p: (0, j)),
-            scratch_shapes=[pltpu.VMEM((rows, 2 * mine.shape[1]), BF16)],
+            scratch_shapes=[pltpu.VMEM((rows, 2 * width * len(chips)), BF16)],
         ),
         out_shape=jax.ShapeDtypeStruct((rows, columns), dtype),
-        compiler_params=params(),
+        compiler_params=params(60 * 1024 * 1024),
     )(place, *args)
 
 
@@ -371,11 +371,7 @@
     z, c = me // 2, me % 2
     place = jnp.stack([z, c]).astype(jnp.int32)
 
-    def hop(x, step, sources):
-        return lax.ppermute(x, "head", line(count, step, sources))
-
-    up, down = hop(tokens, 1, range(count)), hop(tokens, -1, range(count))
-    far_up, far_down = hop(tokens, count - 1, [0]), hop(tokens, 1 - count, [count - 1])
+    pieces = {0: tokens, 1: ring(tokens, -1, count), count - 1: ring(tokens, 1, count)}
     tokens_there = swap(tokens, count)
 
     docs = doc_ids.astype(F32)
@@ -397,20 +393,17 @@
     depth, columns = w_out.shape
     width = columns // (2 * count)
 
+    rows_out = after(w_out, tokens_there)
+
     def cut(chip, core):
-        return lax.dynamic_slice(w_out, (0, (2 * chip + core) * width), (depth, width))
+        return lax.dynamic_slice(rows_out, (0, (2 * chip + core) * width), (depth, width))
 
     other_rows = swap(jnp.stack([cut(chip, 1 - c) for chip in range(count)]), count)
-
-    def out_for(chip):
-        chip = jnp.clip(chip, 0, count - 1)
-        return jnp.concatenate(
-            [cut(chip, c), lax.dynamic_index_in_dim(other_rows, chip, 0, keepdims=False)], 0
-        )
-
-    out_up = [out_for(z + count - s) for s in range(1, count)]
-    out_down = [out_for(z - count + s) for s in range(1, count)]
-    out_here = out_for(z)
+    out_rows = []
+    for n in range(count):
+        chip = lax.rem(z + n, count)
+        theirs = lax.dynamic_index_in_dim(other_rows, chip, 0, keepdims=False)
+        out_rows.append(jnp.concatenate([cut(chip, c), theirs], 0))
 
     used = value_columns + w_feat.shape[1]
     fv_columns = -(-used // 256) * 256
@@ -418,26 +411,26 @@
         [w_value, w_feat, jnp.zeros((w_value.shape[0], fv_columns - used), BF16), w_window], 1
     )
     all_columns = weight.shape[1]
-    part = project(place, (0,), tokens, tokens_there, weight, 0, all_columns)
+    part = project(place, (0,), [tokens], [tokens_there], weight, 0, all_columns)
 
     ready = lax.optimization_barrier(
-        (up, down, far_up, far_down, limits, bounds, first_doc, tail_docs, part, out_here, *out_up, *out_down)
-    )
-    up, down, far_up, far_down, limits, bounds, first_doc, tail_docs, part, out_here = ready[:10]
-    out_up, out_down = ready[10 : 9 + count], ready[9 + count :]
-
-    ups, downs = [up], [down]
-    for s in range(2, count - 1):
-        ups.append(hop(ups[-1], 1, range(s - 1, count)))
-        downs.append(hop(downs[-1], -1, range(0, count - s + 1)))
-    mine = jnp.concatenate([down + far_up, far_down + up], 1)
+        (pieces[1], pieces[count - 1], limits, bounds, first_doc, tail_docs, part, *out_rows)
+    )
+    pieces[1], pieces[count - 1], limits, bounds, first_doc, tail_docs, part = ready[:7]
+    out_rows = ready[7:]
+
+    for n in range(2, count // 2 + 1):
+        pieces[n] = ring(pieces[n - 1], -1, count)
+    for n in range(count - 2, count // 2, -1):
+        pieces[n] = ring(pieces[n + 1], 1, count)
+    near = (1, count - 1)
+    mine = [pieces[n] for n in near]
     part = project(
-        place, (1, count - 1), mine, swap(mine, count), weight, 0, all_columns, part
-    )
-    ups[-1], downs[-1], part = lax.optimization_barrier((ups[-1], downs[-1], part))
-    mine = jnp.concatenate([downs[s - 1] + ups[count - s - 1] for s in range(2, count - 1)], 1)
+        place, near, mine, [swap(p, count) for p in mine], weight, 0, all_columns, part
+    )
     late = tuple(range(2, count - 1))
-    theirs = swap(mine, count)
+    *mine, part = lax.optimization_barrier((*[pieces[n] for n in late], part))
+    theirs = [swap(p, count) for p in mine]
     both = project(place, late, mine, theirs, weight, 0, fv_columns, part, BF16)
     prefix, state = sums(limits, both, heads, key_map, scale_rows)
     states = [
@@ -445,7 +438,7 @@
         for k in range(1, blocks)
     ]
     window = project(
-        place, late, after(mine, state), theirs, weight, fv_columns, all_columns - fv_columns, part,
+        place, late, [after(mine[0], state), *mine[1:]], theirs, weight, fv_columns, all_columns - fv_columns, part,
         BF16,
     )
     local_high = local(1, both, window, bounds, pick, query_map, scale_rows, heads)
@@ -460,27 +453,23 @@
             total += r.astype(F32)
         return total.astype(BF16)
 
-    def first_parts(mixed):
+    def first_part(mixed, step):
         chip = jnp.concatenate([mixed, swap(mixed, count)], 1)
-        return chip, partial(chip, out_up[0]), partial(chip, out_down[0])
-
-    def scattered(chip, up, down):
-        for s in range(1, count):
-            if s > 1:
-                up, down = partial(chip, out_up[s - 1], up), partial(chip, out_down[s - 1], down)
-            up = hop(up, 1, range(0, s))
-            down = hop(down, -1, range(count - s, count))
-        return partial(chip, out_here, up, down)
-
-    high_parts = first_parts(high)
+        return chip, partial(chip, out_rows[-step % count])
+
+    def scattered(chip, sent, step):
+        for n in range(2, count + 1):
+            sent = partial(chip, out_rows[-step * n % count], ring(sent, step, count))
+        return sent
+
+    high_parts = first_part(high, -1)
     local_low = local(
-        0, after(both, *high_parts[1:]), window, bounds, pick, query_map, scale_rows, heads, tail,
+        0, after(both, high_parts[1]), window, bounds, pick, query_map, scale_rows, heads, tail,
         (tail_docs, first_doc),
     )
     low = finish(0, limits, first_doc, bounds, prefix, local_low, states)
-
-    high_out = scattered(*high_parts)
-    low_out = scattered(*first_parts(low))
+    high_out = scattered(*high_parts, -1)
+    low_out = scattered(*first_part(low, 1), 1)
     return jnp.concatenate([low_out, high_out], 0)
 
 

time: 221 us -> 210 us (0.950)
  starting transfers between devices: 61.6 us -> 40.2 us
  Pallas kernels: 47.8 us -> 59.2 us
  waiting for transfers between devices: 59.9 us -> 70.5 us
  other arithmetic: 21.6 us -> 16 us
  matrix products: 9.95 us -> 5.64 us
    ppermute x18 -> x9, starting transfers between devices: 44.3 us -> 22.5 us  [ring(): lax.ppermute(x, 'head', [(2 * z + c, 2 * ((z + step) % count) + c) for z...]
    pallas_call x4, Pallas kernels: 30.2 us -> 41.2 us  [project(): pl.pallas_call(functools.partial(project_kernel, len(chips), before is no...]
    ppermute x18 -> x9, waiting for transfers between devices: 53.5 us -> 63.6 us  [ring(): lax.ppermute(x, 'head', [(2 * z + c, 2 * ((z + step) % count) + c) for z...]
    dot_general x14 -> x8, matrix products: 9.95 us -> 5.64 us  [partial(): total = jnp.dot(chip, weight, preferred_element_type=F32)]
    add x3 -> x0, other arithmetic: 3.65 us -> none  [the longest x2 3.34 us: shards(): mine = jnp.concatenate([down + far_up, far_down + up], 1)]
    concatenate x5 -> x2, other arithmetic: 5.78 us -> 2.91 us  [shards(): out_rows.append(jnp.concatenate([cut(chip, c), theirs], 0))]
    unnamed x58 -> x44, local copies, waits for them, and re-layouts: 8.13 us -> 8.55 us
    ppermute x6 -> x7, waiting for transfers between devices: 4.77 us -> 4.78 us  [swap(): return lax.ppermute(x, 'head', [(h, h ^ 1) for h in range(2 * count)])]
  transfers between devices with their start and end apart: 30 -> 22, of which waited for: 11 -> 12; matrix products, arithmetic and copies ran while one was open for 16% -> 13% of each run, Pallas kernels for 14% -> 19%
where the time goes in v5:
time: 210 us; the launch traced here: 209 us
  waiting for transfers between devices  70.5 us (34%)
  Pallas kernels  59.2 us (28%)
  starting transfers between devices  40.2 us (19%)
  local copies, waits for them, and re-layouts  17.1 us (8%)
  other arithmetic  16 us (8%)
  matrix products  5.64 us (3%)
    ppermute x9, waiting for transfers between devices, ring(): lax.ppermute(x, 'head', [(2 * z + c, 2 * ((z + step) % count) + c) for z...  63.6 us
    pallas_call x4, Pallas kernels, project(): pl.pallas_call(functools.partial(project_kernel, len(chips), before is no...  41.2 us
    ppermute x9, starting transfers between devices, ring(): lax.ppermute(x, 'head', [(2 * z + c, 2 * ((z + step) % count) + c) for z...  22.5 us
    ppermute x3, starting transfers between devices, shards(): lax.ppermute(state, 'ctx', [(i, i + k) for i in range(blocks - k)])  8.82 us
    pallas_call x2, Pallas kernels, local(): pl.pallas_call(functools.partial(local_kernel, part), grid=(heads // grou...  8.68 us
    unnamed x44, local copies, waits for them, and re-layouts  8.55 us
    concatenate x1, other arithmetic, shards(): jnp.concatenate([w_value, w_feat, jnp.zeros((w_value.shape[0], fv_columns...  8.38 us
    dot_general x8, matrix products, partial(): total = jnp.dot(chip, weight, preferred_element_type=F32)  5.64 us
  transfers between devices with their start and end apart: 22, of which 12 were waited for; matrix products, arithmetic and copies ran while one was open for 13% of the time, Pallas kernels for 19%

profile of v5, /device:TPU:0, one launch (start us, length us, event | category | flops | bytes accessed | tf_op | source)
XLA Modules:
  0.0 209.2 jit_solution(12831737525193922761)
XLA Ops:
  0.5 4.6 %collective-permute-start = (bf16[1024,512]{1,0:T(8,128)(2,1)}, bf16[1024,512]{1,0:T(8,128)(2,1)}, u32[]{:S(2)}, u32[]{:S(2)}) collective-permute-start(bf16[1024,512]{1,0:T(8,128)(2,1)} %refs_0_.1), channel_id=1, source_target_pairs={{0,6},{1,7},{2,0},{3,1},{4,2},{5,3},{6,4},{7,5},{8,14},{9,15},{10,... | collective-permute-start | bytes 3145736 | tf_op jit(solution)/shard_map/ppermute | solution.py:31
  5.9 3.4 %collective-permute-start.2 = (bf16[64,128]{1,0:T(8,128)(2,1)S(1)}, bf16[64,128]{1,0:T(8,128)(2,1)S(1)}, u32[]{:S(2)}, u32[]{:S(2)}) collective-permute-start(bf16[64,128]{1,0:T(8,128)(2,1)S(1)} %broadcast_in_dim.7), channel_id=1, source_target_pairs={{0,8},{8,16},{16,24},{1,9},{9,17},{17,25},{2,10},{10,18},{18,26},{... | collective-permute-start | bytes 49160 | tf_op jit(solution)/shard_map/ppermute | solution.py:386
  10.1 4.0 %constant_dynamic-slice_fusion = (bf16[512,512]{1,0:T(8,128)(2,1)}, bf16[512,512]{1,0:T(8,128)(2,1)}, bf16[512,512]{1,0:T(8,128)(2,1)S(1)}, bf16[1,512,512]{2,1,...) fusion(bf16[512,4096]{1,0:T(8,128)(2,1)} %param.15, ...), kind=kLoop, calls=%fused_computation.33 | loop fusion | bytes 8388640 | tf_op jit(solution)/shard_map/dynamic_slice | solution.py:399
  17.0 8.4 %pad_maximum_fusion.refs_2_.refs_4_.refs_5_ = bf16[4096,1792]{1,0:T(8,128)(2,1)} fusion(bf16[4096,1024]{1,0:T(8,128)(2,1)S(1)} %copy-done.9, bf16[4096,128]{1,0:T(8,128)(2,1)} %param.12, bf16[4096,512]{1,0:T(8,128)(2,1)S(1)} %copy-done.12, bf16[1792]{0:T(1024)(128)(2,1)S(1)} %pad.20.clone), kind=kLoop, calls=%fused_computation | loop fusion | flops 58720256 | bytes 28315136 | tf_op jit(solution)/shard_map/concatenate | solution.py:410
  29.3 10.8 %shard_map.100.refs_6_ = f32[1024,1792]{1,0:T(8,128)} custom-call(s32[2]{0:T(128)} %pad_add_fusion.1.place, bf16[1024,512]{1,0:T(8,128)(2,1)} %refs_0_.1, bf16[1024,512]{1,0:T(8,128)(2,1)} %copy-done.21, bf16[4096,1792]{1,0:T(8,128)(2,1)} %pad_maximum_fusion.refs_2_.refs_4_.refs_5_), custom_call_target="tpu_custom_call" | custom-call | tf_op jit(solution)/shard_map/pallas_call | solution.py:78
  44.8 7.0 %collective-permute-done.1.refs_1_ = bf16[1024,512]{1,0:T(8,128)(2,1)} collective-permute-done((bf16[1024,512]{1,0:T(8,128)(2,1)}, bf16[1024,512]{1,0:T(8,128)(2,1)}, u32[]{:S(2)}, u32[]{:S(2)}) %collective-permute-start.1) | collective-permute-done | bytes 1048608 | tf_op jit(solution)/shard_map/ppermute | solution.py:31
  57.8 15.9 %shard_map.101.refs_3_ = f32[1024,1792]{1,0:T(8,128)} custom-call(s32[2]{0:T(128)} %pad_add_fusion.1.place, bf16[1024,512]{1,0:T(8,128)(2,1)} %collective-permute-done.refs_0_, bf16[1024,512]{1,0:T(8,128)(2,1)} %collective-permute-done.1.refs_1_, bf16[1024,512]{1,0:T(8,128)(2,1)} %copy-done.15, bf16[1024,512]{1,0:T(8,128)(2,1)} %copy-done.16, ...), custom_call_target="tpu_custom_call" | custom-call | tf_op jit(solution)/shard_map/pallas_call | solution.py:78
  73.8 4.5 %collective-permute-done.5.refs_0_ = bf16[1024,512]{1,0:T(8,128)(2,1)S(1)} collective-permute-done((bf16[1024,512]{1,0:T(8,128)(2,1)}, bf16[1024,512]{1,0:T(8,128)(2,1)S(1)}, u32[]{:S(2)}, u32[]{:S(2)}) %collective-permute-start.5) | collective-permute-done | bytes 1048608 | tf_op jit(solution)/shard_map/ppermute | solution.py:31
  78.3 2.7 %collective-permute-done.8.refs_1_ = bf16[1024,512]{1,0:T(8,128)(2,1)S(1)} collective-permute-done((bf16[1024,512]{1,0:T(8,128)(2,1)S(1)}, bf16[1024,512]{1,0:T(8,128)(2,1)S(1)}, u32[]{:S(2)}, u32[]{:S(2)}) %collective-permute-start.8) | collective-permute-done | bytes 1048608 | tf_op jit(solution)/shard_map/ppermute | solution.py:37
  82.0 6.8 %shard_map.102.values.features.old_values = bf16[1024,768]{1,0:T(8,128)(2,1)} custom-call(s32[2]{0:T(128)} %pad_add_fusion.1.place, bf16[1024,512]{1,0:T(8,128)(2,1)} %copy-done.10, bf16[1024,512]{1,0:T(8,128)(2,1)} %copy-done.11, bf16[4096,1792]{1,0:T(8,128)(2,1)} %pad_maximum_fusion.refs_2_.refs_4_.refs_5_, f32[1024,1792]{1,0:T(8,128)} %shard_map.101.refs_3_), custom_call_target="tpu_custom_call" | custom-call | tf_op jit(solution)/shard_map/pallas_call | solution.py:78
  90.2 3.8 %shard_map.103 = (f32[4,4,160,128]{3,2,1,0:T(8,128)S(1)}, bf16[4,160,128]{2,1,0:T(8,128)(2,1)}) custom-call(s32[5]{0:T(128)S(1)} %pad_add_fusion.limits, bf16[1024,768]{1,0:T(8,128)(2,1)S(1)} %copy-done, bf16[1024,768]{1,0:T(8,128)(2,1)S(1)} %copy-done, bf16[4,128,512]{2,1,0:T(8,128)(2,1)S(1)} %copy-done.7, f32[3,256]{1,0:T(4,128)S(1)} %copy-done.8), custom_call_target="tpu_custom_call" | custom-call | tf_op jit(solution)/shard_map/pallas_call | solution.py:158
  93.9 3.4 %collective-permute-start.10 = (bf16[4,160,128]{2,1,0:T(8,128)(2,1)}, bf16[4,160,128]{2,1,0:T(8,128)(2,1)S(1)}, u32[]{:S(2)}, u32[]{:S(2)}) collective-permute-start(bf16[4,160,128]{2,1,0:T(8,128)(2,1)} %get-tuple-element.38), channel_id=1, source_target_pairs={{0,16},{8,24},{1,17},{9,25},{2,18},{10,26},{3,19},{11,27},{4,20},{... | collective-permute-start | bytes 491528 | tf_op jit(solution)/shard_map/ppermute | solution.py:437
  97.4 2.9 %collective-permute-start.11 = (bf16[4,160,128]{2,1,0:T(8,128)(2,1)}, bf16[4,160,128]{2,1,0:T(8,128)(2,1)}, u32[]{:S(2)}, u32[]{:S(2)}) collective-permute-start(bf16[4,160,128]{2,1,0:T(8,128)(2,1)} %get-tuple-element.38), channel_id=1, source_target_pairs={{0,24},{1,25},{2,26},{3,27},{4,28},{5,29},{6,30},{7,31}} | collective-permute-start | bytes 491528 | tf_op jit(solution)/shard_map/ppermute | solution.py:437
  100.3 2.5 %collective-permute-start.9 = (bf16[4,160,128]{2,1,0:T(8,128)(2,1)}, bf16[4,160,128]{2,1,0:T(8,128)(2,1)}, u32[]{:S(2)}, u32[]{:S(2)}) collective-permute-start(bf16[4,160,128]{2,1,0:T(8,128)(2,1)} %get-tuple-element.38), channel_id=1, source_target_pairs={{0,8},{8,16},{16,24},{1,9},{9,17},{17,25},{2,10},{10,18},{18,26},{... | collective-permute-start | bytes 491528 | tf_op jit(solution)/shard_map/ppermute | solution.py:437
  103.0 7.8 %shard_map.104.window.old_window = bf16[1024,1024]{1,0:T(8,128)(2,1)} custom-call(s32[2]{0:T(128)} %pad_add_fusion.1.place, bf16[1024,512]{1,0:T(8,128)(2,1)} %copy-done.10, bf16[1024,512]{1,0:T(8,128)(2,1)} %copy-done.11, bf16[4096,1792]{1,0:T(8,128)(2,1)} %pad_maximum_fusion.refs_2_.refs_4_.refs_5_, f32[1024,1792]{1,0:T(8,128)} %shard_map.101.refs_3_), custom_call_target="tpu_custom_call" | custom-call | tf_op jit(solution)/shard_map/pallas_call | solution.py:78
  113.3 4.3 %shard_map.105 = (f32[512,512]{1,0:T(8,128)S(1)}, f32[512,512]{1,0:T(8,128)S(1)}, bf16[512,1024]{1,0:T(8,128)(2,1)S(1)}) custom-call(bf16[1024,768]{1,0:T(8,128)(2,1)S(1)} %copy-done.1, bf16[1024,768]{1,0:T(8,128)(2,1)S(1)} %copy-done.1, bf16[1024,1024]{1,0:T(8,128)(2,1)S(1)} %copy-done.2, bf16[1024,768]{1,0:T(8,128)(2,1)S(1)} %copy-done.1, ...), custom_call_target="tpu_custom_call" | custom-call | tf_op jit(solution)/shard_map/pallas_call | solution.py:279
  117.7 2.8 %shard_map.106 = bf16[512,512]{1,0:T(8,128)(2,1)S(1)} custom-call(s32[5]{0:T(128)S(1)} %pad_add_fusion.limits, f32[8,128]{1,0:T(8,128)S(1)} %broadcast_in_dim.6.first_doc.refs_1_, bf16[512,1024]{1,0:T(8,128)(2,1)S(1)} %get-tuple-element.41.phi_query, s32[1024,1]{1,0:T(8,128)S(1)} %copy.15.bounds, f32[512,512]{1,0:T(8,128)S(1)} %get-tuple-element.42.inner, ...), custom_call_target="tpu_custom_call" | custom-call | tf_op jit(solution)/shard_map/pallas_call | solution.py:338
  122.1 2.9 %collective-permute-start.14 = (bf16[64,1024]{1,0:T(8,128)(2,1)S(1)}, bf16[64,1024]{1,0:T(8,128)(2,1)S(1)}, u32[]{:S(2)}, u32[]{:S(2)}) collective-permute-start(bf16[64,1024]{1,0:T(8,128)(2,1)S(1)} %slice.31), channel_id=1, source_target_pairs={{0,8},{8,16},{16,24},{1,9},{9,17},{17,25},{2,10},{10,18},{18,26},{... | collective-permute-start | bytes 393224 | tf_op jit(solution)/shard_map/ppermute | solution.py:446
  125.7 2.2 %collective-permute-done.14.old_window = bf16[64,1024]{1,0:T(8,128)(2,1)S(1)} collective-permute-done((bf16[64,1024]{1,0:T(8,128)(2,1)S(1)}, bf16[64,1024]{1,0:T(8,128)(2,1)S(1)}, u32[]{:S(2)}, u32[]{:S(2)}) %collective-permute-start.14) | collective-permute-done | bytes 131104 | tf_op jit(solution)/shard_map/ppermute | solution.py:446
  127.9 4.4 %shard_map.107 = (f32[512,512]{1,0:T(8,128)S(1)}, f32[512,512]{1,0:T(8,128)S(1)}, bf16[512,1024]{1,0:T(8,128)(2,1)S(1)}) custom-call(bf16[1024,768]{1,0:T(8,128)(2,1)S(1)} %copy-done.1, bf16[1024,768]{1,0:T(8,128)(2,1)S(1)} %copy-done.1, bf16[1024,1024]{1,0:T(8,128)(2,1)S(1)} %copy-done.3, bf16[64,512]{1,0:T(8,128)(2,1)S(1)} %collective-permute-done.13.old_values, ...), custom_call_target="tpu_custom_call" | custom-call | tf_op jit(solution)/shard_map/pallas_call | solution.py:279
  132.3 2.6 %shard_map.108 = bf16[512,512]{1,0:T(8,128)(2,1)S(1)} custom-call(s32[5]{0:T(128)S(1)} %pad_add_fusion.limits, f32[8,128]{1,0:T(8,128)S(1)} %broadcast_in_dim.6.first_doc.refs_1_, bf16[512,1024]{1,0:T(8,128)(2,1)S(1)} %get-tuple-element.49.phi_query, s32[1024,1]{1,0:T(8,128)S(1)} %copy.15.bounds, f32[512,512]{1,0:T(8,128)S(1)} %get-tuple-element.50.inner, ...), custom_call_target="tpu_custom_call" | custom-call | tf_op jit(solution)/shard_map/pallas_call | solution.py:338
  135.0 3.6 %collective-permute-start.19 = (bf16[512,512]{1,0:T(8,128)(2,1)S(1)}, bf16[512,512]{1,0:T(8,128)(2,1)S(1)}, u32[]{:S(2)}, u32[]{:S(2)}) collective-permute-start(bf16[512,512]{1,0:T(8,128)(2,1)S(1)} %convolution_convert_fusion.1), channel_id=1, source_target_pairs={{0,6},{1,7},{2,0},{3,1},{4,2},{5,3},{6,4},{7,5},{8,14},{9,15},{10,... | collective-permute-start | bytes 1572872 | tf_op jit(solution)/shard_map/ppermute | solution.py:31
  139.4 11.6 %collective-permute-done.19 = bf16[512,512]{1,0:T(8,128)(2,1)S(1)} collective-permute-done((bf16[512,512]{1,0:T(8,128)(2,1)S(1)}, bf16[512,512]{1,0:T(8,128)(2,1)S(1)}, u32[]{:S(2)}, u32[]{:S(2)}) %collective-permute-start.19) | collective-permute-done | bytes 524320 | tf_op jit(solution)/shard_map/ppermute | solution.py:31
  151.7 4.3 %collective-permute-start.20 = (bf16[512,512]{1,0:T(8,128)(2,1)S(1)}, bf16[512,512]{1,0:T(8,128)(2,1)S(1)}, u32[]{:S(2)}, u32[]{:S(2)}) collective-permute-start(bf16[512,512]{1,0:T(8,128)(2,1)S(1)} %fusion.5), channel_id=1, source_target_pairs={{0,6},{1,7},{2,0},{3,1},{4,2},{5,3},{6,4},{7,5},{8,14},{9,15},{10,... | collective-permute-start | bytes 1572872 | tf_op jit(solution)/shard_map/ppermute | solution.py:31
  156.0 6.7 %collective-permute-done.16 = bf16[512,512]{1,0:T(8,128)(2,1)S(1)} collective-permute-done((bf16[512,512]{1,0:T(8,128)(2,1)S(1)}, bf16[512,512]{1,0:T(8,128)(2,1)S(1)}, u32[]{:S(2)}, u32[]{:S(2)}) %collective-permute-start.16) | collective-permute-done | bytes 524320 | tf_op jit(solution)/shard_map/ppermute | solution.py:31
  163.4 2.0 collective-permute-start.17
  165.4 8.4 %collective-permute-done.20 = bf16[512,512]{1,0:T(8,128)(2,1)S(1)} collective-permute-done((bf16[512,512]{1,0:T(8,128)(2,1)S(1)}, bf16[512,512]{1,0:T(8,128)(2,1)S(1)}, u32[]{:S(2)}, u32[]{:S(2)}) %collective-permute-start.20) | collective-permute-done | bytes 524320 | tf_op jit(solution)/shard_map/ppermute | solution.py:31
  174.6 4.0 %collective-permute-start.21 = (bf16[512,512]{1,0:T(8,128)(2,1)S(1)}, bf16[512,512]{1,0:T(8,128)(2,1)S(1)}, u32[]{:S(2)}, u32[]{:S(2)}) collective-permute-start(bf16[512,512]{1,0:T(8,128)(2,1)S(1)} %fusion.4), channel_id=1, source_target_pairs={{0,6},{1,7},{2,0},{3,1},{4,2},{5,3},{6,4},{7,5},{8,14},{9,15},{10,... | collective-permute-start | bytes 1572872 | tf_op jit(solution)/shard_map/ppermute | solution.py:31
  178.6 6.6 %collective-permute-done.17 = bf16[512,512]{1,0:T(8,128)(2,1)S(1)} collective-permute-done((bf16[512,512]{1,0:T(8,128)(2,1)S(1)}, bf16[512,512]{1,0:T(8,128)(2,1)S(1)}, u32[]{:S(2)}, u32[]{:S(2)}) %collective-permute-start.17) | collective-permute-done | bytes 524320 | tf_op jit(solution)/shard_map/ppermute | solution.py:31
  185.9 2.1 collective-permute-start.18
  188.0 8.4 %collective-permute-done.21 = bf16[512,512]{1,0:T(8,128)(2,1)S(1)} collective-permute-done((bf16[512,512]{1,0:T(8,128)(2,1)S(1)}, bf16[512,512]{1,0:T(8,128)(2,1)S(1)}, u32[]{:S(2)}, u32[]{:S(2)}) %collective-permute-start.21) | collective-permute-done | bytes 524320 | tf_op jit(solution)/shard_map/ppermute | solution.py:31
  197.0 10.4 %collective-permute-done.18 = bf16[512,512]{1,0:T(8,128)(2,1)S(1)} collective-permute-done((bf16[512,512]{1,0:T(8,128)(2,1)S(1)}, bf16[512,512]{1,0:T(8,128)(2,1)S(1)}, u32[]{:S(2)}, u32[]{:S(2)}) %collective-permute-start.18) | collective-permute-done | bytes 524320 | tf_op jit(solution)/shard_map/ppermute | solution.py:31
  (99 shorter events, 33.0 us)
Async XLA Ops:
  0.0 10.1 %collective-permute-start.3 = (bf16[1024,512]{1,0:T(8,128)(2,1)}, bf16[1024,512]{1,0:T(8,128)(2,1)S(1)}, u32[]{:S(2)}, u32[]{:S(2)}) collective-permute-start(bf16[1024,512]{1,0:T(8,128)(2,1)} %refs_0_.1), channel_id=1, source_target_pairs={{0,1},{1,0},{2,3},{3,2},{4,5},{5,4},{6,7},{7,6},{8,9},{9,8},{10,11... | collective-permute-start | bytes 3145736 | tf_op jit(solution)/shard_map/ppermute | solution.py:37
  0.5 44.3 %collective-permute-start = (bf16[1024,512]{1,0:T(8,128)(2,1)}, bf16[1024,512]{1,0:T(8,128)(2,1)}, u32[]{:S(2)}, u32[]{:S(2)}) collective-permute-start(bf16[1024,512]{1,0:T(8,128)(2,1)} %refs_0_.1), channel_id=1, source_target_pairs={{0,6},{1,7},{2,0},{3,1},{4,2},{5,3},{6,4},{7,5},{8,14},{9,15},{10,... | collective-permute-start | bytes 3145736 | tf_op jit(solution)/shard_map/ppermute | solution.py:31
  5.1 46.8 %collective-permute-start.1 = (bf16[1024,512]{1,0:T(8,128)(2,1)}, bf16[1024,512]{1,0:T(8,128)(2,1)}, u32[]{:S(2)}, u32[]{:S(2)}) collective-permute-start(bf16[1024,512]{1,0:T(8,128)(2,1)} %refs_0_.1), channel_id=1, source_target_pairs={{0,2},{1,3},{2,4},{3,5},{4,6},{5,7},{6,0},{7,1},{8,10},{9,11},{10,... | collective-permute-start | bytes 3145736 | tf_op jit(solution)/shard_map/ppermute | solution.py:31
  5.9 38.9 %collective-permute-start.2 = (bf16[64,128]{1,0:T(8,128)(2,1)S(1)}, bf16[64,128]{1,0:T(8,128)(2,1)S(1)}, u32[]{:S(2)}, u32[]{:S(2)}) collective-permute-start(bf16[64,128]{1,0:T(8,128)(2,1)S(1)} %broadcast_in_dim.7), channel_id=1, source_target_pairs={{0,8},{8,16},{16,24},{1,9},{9,17},{17,25},{2,10},{10,18},{18,26},{... | collective-permute-start | bytes 49160 | tf_op jit(solution)/shard_map/ppermute | solution.py:386
  10.1 5.4 %copy-start.9 = (bf16[4096,1024]{1,0:T(8,128)(2,1)S(1)}, bf16[4096,1024]{1,0:T(8,128)(2,1)}, u32[]{:S(2)}) copy-start(bf16[4096,1024]{1,0:T(8,128)(2,1)} %param.14) | copy-start | bytes 25165828
  14.3 25.7 %collective-permute-start.4 = (bf16[4,512,512]{2,1,0:T(8,128)(2,1)S(1)}, bf16[4,512,512]{2,1,0:T(8,128)(2,1)}, u32[]{:S(2)}, u32[]{:S(2)}) collective-permute-start(bf16[4,512,512]{2,1,0:T(8,128)(2,1)S(1)} %pad_maximum_fusion.1), channel_id=1, source_target_pairs={{0,1},{1,0},{2,3},{3,2},{4,5},{5,4},{6,7},{7,6},{8,9},{9,8},{10,11... | collective-permute-start | bytes 6291464 | tf_op jit(solution)/shard_map/ppermute | solution.py:37
  52.4 2.9 %collective-permute-start.6 = (bf16[1024,512]{1,0:T(8,128)(2,1)}, bf16[1024,512]{1,0:T(8,128)(2,1)S(1)}, u32[]{:S(2)}, u32[]{:S(2)}) collective-permute-start(bf16[1024,512]{1,0:T(8,128)(2,1)} %collective-permute-done.refs_0_), channel_id=1, source_target_pairs={{0,1},{1,0},{2,3},{3,2},{4,5},{5,4},{6,7},{7,6},{8,9},{9,8},{10,11... | collective-permute-start | bytes 3145736 | tf_op jit(solution)/shard_map/ppermute | solution.py:37
  52.5 4.4 %collective-permute-start.7 = (bf16[1024,512]{1,0:T(8,128)(2,1)}, bf16[1024,512]{1,0:T(8,128)(2,1)S(1)}, u32[]{:S(2)}, u32[]{:S(2)}) collective-permute-start(bf16[1024,512]{1,0:T(8,128)(2,1)} %collective-permute-done.1.refs_1_), channel_id=1, source_target_pairs={{0,1},{1,0},{2,3},{3,2},{4,5},{5,4},{6,7},{7,6},{8,9},{9,8},{10,11... | collective-permute-start | bytes 3145736 | tf_op jit(solution)/shard_map/ppermute | solution.py:37
  53.0 25.4 %collective-permute-start.5 = (bf16[1024,512]{1,0:T(8,128)(2,1)}, bf16[1024,512]{1,0:T(8,128)(2,1)S(1)}, u32[]{:S(2)}, u32[]{:S(2)}) collective-permute-start(bf16[1024,512]{1,0:T(8,128)(2,1)} %collective-permute-done.refs_0_), channel_id=1, source_target_pairs={{0,6},{1,7},{2,0},{3,1},{4,2},{5,3},{6,4},{7,5},{8,14},{9,15},{10,... | collective-permute-start | bytes 3145736 | tf_op jit(solution)/shard_map/ppermute | solution.py:31
  73.8 15.0 %copy-start.7 = (bf16[4,128,512]{2,1,0:T(8,128)(2,1)S(1)}, bf16[4,128,512]{2,1,0:T(8,128)(2,1)}, u32[]{:S(2)}) copy-start(bf16[4,128,512]{2,1,0:T(8,128)(2,1)} %constant.77.clone.expand) | copy-start | bytes 1572868
  73.8 15.0 %copy-start.8 = (f32[3,256]{1,0:T(4,128)S(1)}, f32[3,256]{1,0:T(4,128)}, u32[]{:S(2)}) copy-start(f32[3,256]{1,0:T(4,128)} %constant.78.clone.rows) | copy-start | bytes 9220
  78.3 2.7 %collective-permute-start.8 = (bf16[1024,512]{1,0:T(8,128)(2,1)S(1)}, bf16[1024,512]{1,0:T(8,128)(2,1)S(1)}, u32[]{:S(2)}, u32[]{:S(2)}) collective-permute-start(bf16[1024,512]{1,0:T(8,128)(2,1)S(1)} %collective-permute-done.5.refs_0_), channel_id=1, source_target_pairs={{0,1},{1,0},{2,3},{3,2},{4,5},{5,4},{6,7},{7,6},{8,9},{9,8},{10,11... | collective-permute-start | bytes 3145736 | tf_op jit(solution)/shard_map/ppermute | solution.py:37
  93.9 23.7 %collective-permute-start.10 = (bf16[4,160,128]{2,1,0:T(8,128)(2,1)}, bf16[4,160,128]{2,1,0:T(8,128)(2,1)S(1)}, u32[]{:S(2)}, u32[]{:S(2)}) collective-permute-start(bf16[4,160,128]{2,1,0:T(8,128)(2,1)} %get-tuple-element.38), channel_id=1, source_target_pairs={{0,16},{8,24},{1,17},{9,25},{2,18},{10,26},{3,19},{11,27},{4,20},{... | collective-permute-start | bytes 491528 | tf_op jit(solution)/shard_map/ppermute | solution.py:437
  97.4 20.3 %collective-permute-start.11 = (bf16[4,160,128]{2,1,0:T(8,128)(2,1)}, bf16[4,160,128]{2,1,0:T(8,128)(2,1)}, u32[]{:S(2)}, u32[]{:S(2)}) collective-permute-start(bf16[4,160,128]{2,1,0:T(8,128)(2,1)} %get-tuple-element.38), channel_id=1, source_target_pairs={{0,24},{1,25},{2,26},{3,27},{4,28},{5,29},{6,30},{7,31}} | collective-permute-start | bytes 491528 | tf_op jit(solution)/shard_map/ppermute | solution.py:437
  100.3 17.4 %collective-permute-start.9 = (bf16[4,160,128]{2,1,0:T(8,128)(2,1)}, bf16[4,160,128]{2,1,0:T(8,128)(2,1)}, u32[]{:S(2)}, u32[]{:S(2)}) collective-permute-start(bf16[4,160,128]{2,1,0:T(8,128)(2,1)} %get-tuple-element.38), channel_id=1, source_target_pairs={{0,8},{8,16},{16,24},{1,9},{9,17},{17,25},{2,10},{10,18},{18,26},{... | collective-permute-start | bytes 491528 | tf_op jit(solution)/shard_map/ppermute | solution.py:437
  103.0 7.8 %copy-start.1 = (bf16[1024,768]{1,0:T(8,128)(2,1)S(1)}, bf16[1024,768]{1,0:T(8,128)(2,1)}, u32[]{:S(2)}) copy-start(bf16[1024,768]{1,0:T(8,128)(2,1)} %shard_map.102.values.features.old_values) | copy-start | bytes 4718596
  103.0 7.8 %copy-start.4 = (bf16[4,128,512]{2,1,0:T(8,128)(2,1)S(1)}, bf16[4,128,512]{2,1,0:T(8,128)(2,1)}, u32[]{:S(2)}) copy-start(bf16[4,128,512]{2,1,0:T(8,128)(2,1)} %constant.76.clone.expand) | copy-start | bytes 1572868
  117.7 7.3 %copy-start.18 = (bf16[1024,512]{1,0:T(8,128)(2,1)S(1)}, bf16[1024,512]{1,0:T(8,128)(2,1)}, u32[]{:S(2)}) copy-start(bf16[1024,512]{1,0:T(8,128)(2,1)} %get-tuple-element.45) | copy-start | bytes 3145732
  120.6 4.4 %collective-permute-start.12 = (bf16[512,512]{1,0:T(8,128)(2,1)S(1)}, bf16[512,512]{1,0:T(8,128)(2,1)S(1)}, u32[]{:S(2)}, u32[]{:S(2)}) collective-permute-start(bf16[512,512]{1,0:T(8,128)(2,1)S(1)} %shard_map.106), channel_id=1, source_target_pairs={{0,1},{1,0},{2,3},{3,2},{4,5},{5,4},{6,7},{7,6},{8,9},{9,8},{10,11... | collective-permute-start | bytes 1572872 | tf_op jit(solution)/shard_map/ppermute | solution.py:37
  120.7 7.3 %copy-start.6 = (bf16[4,128,256]{2,1,0:T(8,128)(2,1)S(1)}, bf16[4,128,256]{2,1,0:T(8,128)(2,1)}, u32[]{:S(2)}) copy-start(bf16[4,128,256]{2,1,0:T(8,128)(2,1)} %constant.79.clone.pick) | copy-start | bytes 786436
  120.7 5.0 %collective-permute-start.13 = (bf16[64,512]{1,0:T(8,128)(2,1)S(1)}, bf16[64,512]{1,0:T(8,128)(2,1)S(1)}, u32[]{:S(2)}, u32[]{:S(2)}) collective-permute-start(bf16[64,512]{1,0:T(8,128)(2,1)S(1)} %slice.29), channel_id=1, source_target_pairs={{0,8},{8,16},{16,24},{1,9},{9,17},{17,25},{2,10},{10,18},{18,26},{... | collective-permute-start | bytes 196616 | tf_op jit(solution)/shard_map/ppermute | solution.py:446
  122.1 5.8 %collective-permute-start.14 = (bf16[64,1024]{1,0:T(8,128)(2,1)S(1)}, bf16[64,1024]{1,0:T(8,128)(2,1)S(1)}, u32[]{:S(2)}, u32[]{:S(2)}) collective-permute-start(bf16[64,1024]{1,0:T(8,128)(2,1)S(1)} %slice.31), channel_id=1, source_target_pairs={{0,8},{8,16},{16,24},{1,9},{9,17},{17,25},{2,10},{10,18},{18,26},{... | collective-permute-start | bytes 393224 | tf_op jit(solution)/shard_map/ppermute | solution.py:446
  132.3 6.3 %copy-start.19 = (bf16[1024,512]{1,0:T(8,128)(2,1)S(1)}, bf16[1024,512]{1,0:T(8,128)(2,1)}, u32[]{:S(2)}) copy-start(bf16[1024,512]{1,0:T(8,128)(2,1)} %get-tuple-element.54) | copy-start | bytes 3145732
  134.9 16.0 %copy-start.20 = (bf16[1024,512]{1,0:T(8,128)(2,1)S(1)}, bf16[1024,512]{1,0:T(8,128)(2,1)}, u32[]{:S(2)}) copy-start(bf16[1024,512]{1,0:T(8,128)(2,1)} %get-tuple-element.53) | copy-start | bytes 3145732
  134.9 3.7 %collective-permute-start.15 = (bf16[512,512]{1,0:T(8,128)(2,1)S(1)}, bf16[512,512]{1,0:T(8,128)(2,1)S(1)}, u32[]{:S(2)}, u32[]{:S(2)}) collective-permute-start(bf16[512,512]{1,0:T(8,128)(2,1)S(1)} %shard_map.108), channel_id=1, source_target_pairs={{0,1},{1,0},{2,3},{3,2},{4,5},{5,4},{6,7},{7,6},{8,9},{9,8},{10,11... | collective-permute-start | bytes 1572872 | tf_op jit(solution)/shard_map/ppermute | solution.py:37
  135.0 15.9 %collective-permute-start.19 = (bf16[512,512]{1,0:T(8,128)(2,1)S(1)}, bf16[512,512]{1,0:T(8,128)(2,1)S(1)}, u32[]{:S(2)}, u32[]{:S(2)}) collective-permute-start(bf16[512,512]{1,0:T(8,128)(2,1)S(1)} %convolution_convert_fusion.1), channel_id=1, source_target_pairs={{0,6},{1,7},{2,0},{3,1},{4,2},{5,3},{6,4},{7,5},{8,14},{9,15},{10,... | collective-permute-start | bytes 1572872 | tf_op jit(solution)/shard_map/ppermute | solution.py:31
  139.3 23.3 %collective-permute-start.16 = (bf16[512,512]{1,0:T(8,128)(2,1)S(1)}, bf16[512,512]{1,0:T(8,128)(2,1)S(1)}, u32[]{:S(2)}, u32[]{:S(2)}) collective-permute-start(bf16[512,512]{1,0:T(8,128)(2,1)S(1)} %convolution_convert_fusion), channel_id=1, source_target_pairs={{0,2},{1,3},{2,4},{3,5},{4,6},{5,7},{6,0},{7,1},{8,10},{9,11},{10,... | collective-permute-start | bytes 1572872 | tf_op jit(solution)/shard_map/ppermute | solution.py:31
  151.7 22.2 %collective-permute-start.20 = (bf16[512,512]{1,0:T(8,128)(2,1)S(1)}, bf16[512,512]{1,0:T(8,128)(2,1)S(1)}, u32[]{:S(2)}, u32[]{:S(2)}) collective-permute-start(bf16[512,512]{1,0:T(8,128)(2,1)S(1)} %fusion.5), channel_id=1, source_target_pairs={{0,6},{1,7},{2,0},{3,1},{4,2},{5,3},{6,4},{7,5},{8,14},{9,15},{10,... | collective-permute-start | bytes 1572872 | tf_op jit(solution)/shard_map/ppermute | solution.py:31
  163.4 21.8 %collective-permute-start.17 = (bf16[512,512]{1,0:T(8,128)(2,1)S(1)}, bf16[512,512]{1,0:T(8,128)(2,1)S(1)}, u32[]{:S(2)}, u32[]{:S(2)}) collective-permute-start(bf16[512,512]{1,0:T(8,128)(2,1)S(1)} %fusion.2), channel_id=1, source_target_pairs={{0,2},{1,3},{2,4},{3,5},{4,6},{5,7},{6,0},{7,1},{8,10},{9,11},{10,... | collective-permute-start | bytes 1572872 | tf_op jit(solution)/shard_map/ppermute | solution.py:31
  174.5 21.8 %copy-start.17 = (bf16[1024,512]{1,0:T(8,128)(2,1)S(1)}, bf16[1024,512]{1,0:T(8,128)(2,1)}, u32[]{:S(2)}) copy-start(bf16[1024,512]{1,0:T(8,128)(2,1)} %get-tuple-element.52) | copy-start | bytes 3145732
  174.6 21.8 %collective-permute-start.21 = (bf16[512,512]{1,0:T(8,128)(2,1)S(1)}, bf16[512,512]{1,0:T(8,128)(2,1)S(1)}, u32[]{:S(2)}, u32[]{:S(2)}) collective-permute-start(bf16[512,512]{1,0:T(8,128)(2,1)S(1)} %fusion.4), channel_id=1, source_target_pairs={{0,6},{1,7},{2,0},{3,1},{4,2},{5,3},{6,4},{7,5},{8,14},{9,15},{10,... | collective-permute-start | bytes 1572872 | tf_op jit(solution)/shard_map/ppermute | solution.py:31
  185.9 21.5 %collective-permute-start.18 = (bf16[512,512]{1,0:T(8,128)(2,1)S(1)}, bf16[512,512]{1,0:T(8,128)(2,1)S(1)}, u32[]{:S(2)}, u32[]{:S(2)}) collective-permute-start(bf16[512,512]{1,0:T(8,128)(2,1)S(1)} %fusion.1), channel_id=1, source_target_pairs={{0,2},{1,3},{2,4},{3,5},{4,6},{5,7},{6,0},{7,1},{8,10},{9,11},{10,... | collective-permute-start | bytes 1572872 | tf_op jit(solution)/shard_map/ppermute | solution.py:31
  (12 other events, 23.5 us)

commit v6 on v5

--- a/solution.py
+++ b/solution.py
@@ -16,15 +16,15 @@
 CHUNK = 256
 GROUP = 2
 STATE = -(-(len(PAIRS) + FEAT + 1) // 16) * 16
-VMEM = 40 * 1024 * 1024
+VMEM = 24 * 1024 * 1024
 TILE = 128
 LANES = 128
 F32 = jnp.float32
 BF16 = jnp.bfloat16
 
 
-def params(limit=VMEM):
-    return pltpu.CompilerParams(vmem_limit_bytes=limit, dimension_semantics=("arbitrary",))
+def params():
+    return pltpu.CompilerParams(vmem_limit_bytes=VMEM, dimension_semantics=("arbitrary",))
 
 
 def ring(x, step, count):
@@ -37,13 +37,15 @@
     return lax.ppermute(x, "head", [(h, h ^ 1) for h in range(2 * count)])
 
 
-def project_kernel(chips, has_before, place, *refs):
+def project_kernel(chips, cuts, has_before, tailed, place, *refs):
     mine, theirs, weights = refs[:chips], refs[chips : 2 * chips], refs[2 * chips : 3 * chips]
-    out, both = refs[-2], refs[-1]
+    before = refs[3 * chips : 3 * chips + len(cuts)] if has_before else None
+    outs, both = refs[-1 - len(cuts) - tailed : -1], refs[-1]
     width = mine[0].shape[1]
     c = place[1]
-
-    @pl.when(pl.program_id(0) == 0)
+    step = pl.program_id(0)
+
+    @pl.when(step == 0)
     def _():
         for n in range(chips):
             own = pl.multiple_of((2 * n + c) * width, width)
@@ -51,41 +53,68 @@
             both[:, pl.ds(own, width)] = mine[n][...]
             both[:, pl.ds(other, width)] = theirs[n][...]
 
-    total = refs[3 * chips][...] if has_before else None
-    for n in range(chips):
-        rows = both[:, 2 * n * width : 2 * (n + 1) * width]
-        part = jnp.dot(rows, weights[n][...], preferred_element_type=F32)
-        total = part if total is None else total + part
-    out[...] = total.astype(out.dtype)
-
-
-def project(place, chips, mine, theirs, weight, first, columns, before=None, dtype=F32):
+    def tile(k):
+        total = before[k][...] if has_before else None
+        for n in range(chips):
+            rows = both[:, 2 * n * width : 2 * (n + 1) * width]
+            part = jnp.dot(rows, weights[n][...], preferred_element_type=F32)
+            total = part if total is None else total + part
+        outs[k][...] = total.astype(outs[k].dtype)
+        if tailed:
+            outs[-1][...] = total[total.shape[0] - WIN :].astype(outs[-1].dtype)
+
+    if len(cuts) == 1:
+        tile(0)
+    else:
+
+        @pl.when(step < cuts[0])
+        def _():
+            tile(0)
+
+        @pl.when(step >= cuts[0])
+        def _():
+            tile(1)
+
+
+def project(place, chips, mine, theirs, weight, first, columns, before=None, dtype=F32, tailed=False):
     rows, width = mine[0].shape
     count = weight.shape[0] // (2 * width)
-    tile = 256
-    start = first // tile
+    size = 256
+    start = first // size
+    cuts = [n // size for n in columns]
     specs = [pl.BlockSpec((rows, width), lambda j, p: (0, 0))] * (2 * len(chips))
     for n in chips:
         specs.append(
             pl.BlockSpec(
-                (2 * width, tile), lambda j, p, n=n: (lax.rem(p[0] + n, count), start + j)
+                (2 * width, size), lambda j, p, n=n: (lax.rem(p[0] + n, count), start + j)
             )
         )
+    results = [
+        pl.BlockSpec(
+            (rows, size),
+            lambda j, p, at=sum(cuts[:k]), n=cuts[k]: (0, jnp.clip(j - at, 0, n - 1)),
+        )
+        for k in range(len(cuts))
+    ]
     args = [*mine, *theirs] + [weight] * len(chips)
     if before is not None:
-        specs.append(pl.BlockSpec((rows, tile), lambda j, p: (0, start + j)))
-        args.append(before)
+        specs += results
+        args += before
+    shapes = [jax.ShapeDtypeStruct((rows, n), dtype) for n in columns]
+    if tailed:
+        results = results + [pl.BlockSpec((WIN, size), lambda j, p: (0, j))]
+        shapes.append(jax.ShapeDtypeStruct((WIN, columns[0]), dtype))
     return pl.pallas_call(
-        functools.partial(project_kernel, len(chips), before is not None),
+        functools.partial(project_kernel, len(chips), cuts, before is not None, tailed),
         grid_spec=pltpu.PrefetchScalarGridSpec(
             num_scalar_prefetch=1,
-            grid=(columns // tile,),
+            grid=(sum(cuts),),
             in_specs=specs,
-            out_specs=pl.BlockSpec((rows, tile), lambda j, p: (0, j)),
+            out_specs=results,
             scratch_shapes=[pltpu.VMEM((rows, 2 * width * len(chips)), BF16)],
         ),
-        out_shape=jax.ShapeDtypeStruct((rows, columns), dtype),
-        compiler_params=params(60 * 1024 * 1024),
+        out_shape=shapes,
+        compiler_params=params(),
     )(place, *args)
 
 
@@ -148,7 +177,8 @@
         for n in range(chunks):
             prefix[n, h] = state
             state = parts[n] + jnp.where(limits[n] <= n * CHUNK, state, 0.0)
-        end[h] = jnp.where(mark, (limits[chunks] + 1).astype(F32), state).astype(BF16)
+        end[h, :STATE] = jnp.where(mark, (limits[chunks] + 1).astype(F32), state).astype(BF16)
+        end[h, STATE:] = values[values.shape[0] - WIN :, column]
 
 
 def sums(limits, both, heads, expand, rows):
@@ -168,12 +198,12 @@
             ],
             out_specs=[
                 pl.BlockSpec((chunks, group, STATE, HEAD_DIM), lambda g, _: (0, g, 0, 0)),
-                pl.BlockSpec((group, STATE, HEAD_DIM), lambda g, _: (g, 0, 0)),
+                pl.BlockSpec((group, STATE + WIN, HEAD_DIM), lambda g, _: (g, 0, 0)),
             ],
         ),
         out_shape=[
             jax.ShapeDtypeStruct((chunks, heads, STATE, HEAD_DIM), F32),
-            jax.ShapeDtypeStruct((heads, STATE, HEAD_DIM), BF16),
+            jax.ShapeDtypeStruct((heads, STATE + WIN, HEAD_DIM), BF16),
         ],
         compiler_params=params(),
     )(limits, both, both, expand, rows)
@@ -243,7 +273,8 @@
                 keys, vals = window[near, key], values[near, column]
             else:
                 keys = jnp.concatenate([old_window[:, key], window[:TILE, key]], 0)
-                vals = jnp.concatenate([old_values[:, column], values[:TILE, column]], 0)
+                old = old_values[:, column] if part else old_values[h, STATE:]
+                vals = jnp.concatenate([old, values[:TILE, column]], 0)
                 if part == 0:
                     first = jnp.where(first == 0, -in_tail, first)
             tiles.append(
@@ -282,7 +313,10 @@
         in_specs=[
             pl.BlockSpec((half, LANES), lambda g: (part, heads)),
             some(half, HEAD_DIM, part), some(half, 2 * HEAD_DIM, part),
-            some(WIN, HEAD_DIM, at), some(WIN, 2 * HEAD_DIM, at),
+            some(WIN, HEAD_DIM, at)
+            if old is None
+            else pl.BlockSpec((group, STATE + WIN, HEAD_DIM), lambda g: (g, 0, 0)),
+            some(WIN, 2 * HEAD_DIM, at),
             pl.BlockSpec((half, 1), lambda g: (part, 0)),
             per_head(pick), per_head(expand), full(rows),
         ]
@@ -297,38 +331,39 @@
     )(both, both, window, *(old or (both, window)), bounds, pick, expand, rows, *docs)
 
 
-def finish_kernel(part, shifts, limits, first_doc, phi_query, bounds, inner, windowed, prefix, *refs):
-    states, out = refs[:shifts], refs[-1]
+def finish_kernel(shifts, limits, first_doc, bounds, prefix, *refs):
+    halves, states, outs = (refs[:3], refs[3:6]), refs[6 : 6 + shifts], refs[6 + shifts :]
     unmarked = lax.broadcasted_iota(jnp.int32, (STATE, HEAD_DIM), 0) < STATE - 1
-    chunks = inner.shape[0] // CHUNK
-    for h in range(inner.shape[1] // HEAD_DIM):
+    chunks = outs[0].shape[0] // CHUNK
+    for h in range(outs[0].shape[1] // HEAD_DIM):
         column = slice(h * HEAD_DIM, (h + 1) * HEAD_DIM)
         incoming = jnp.zeros((STATE, HEAD_DIM), F32)
         for k in range(shifts):
-            sent = states[k][h].astype(F32)
+            sent = states[k][h, :STATE].astype(F32)
             wanted = (sent[STATE - 1 :] == first_doc[0:1, :] + 1.0) & unmarked
             incoming += jnp.where(wanted, sent, 0.0)
-        carried = []
-        for n in range(chunks):
-            chunk = part * chunks + n
-            state = incoming
-            if chunk:
-                state = jnp.where(limits[chunk - 1] <= 0, incoming, 0.0) + prefix[n, h]
-            state = jnp.concatenate([state, jnp.zeros((WIDE - STATE, HEAD_DIM), F32)], 0)
-            here = slice(n * CHUNK, (n + 1) * CHUNK)
-            one = jnp.dot(
-                phi_query[here, h * WIDE : (h + 1) * WIDE], state.astype(BF16),
-                preferred_element_type=F32,
-            )
-            carried.append(jnp.where(bounds[here] <= chunk * CHUNK, one, 0.0))
-        linear = inner[:, column] + jnp.concatenate(carried, 0)
-        mean = jnp.mean(linear * linear, 1, keepdims=True)
-        out[:, column] = (linear * lax.rsqrt(mean + 1e-5) + windowed[:, column]).astype(BF16)
-
-
-def finish(part, limits, first_doc, bounds, prefix, parts, states):
-    inner, windowed, phi_query = parts
-    half, columns = inner.shape
+        for part, (inner, windowed, phi_query) in enumerate(halves):
+            carried = []
+            for n in range(chunks):
+                chunk = part * chunks + n
+                state = incoming
+                if chunk:
+                    state = jnp.where(limits[chunk - 1] <= 0, incoming, 0.0) + prefix[chunk, h]
+                state = jnp.concatenate([state, jnp.zeros((WIDE - STATE, HEAD_DIM), F32)], 0)
+                one = jnp.dot(
+                    phi_query[n * CHUNK : (n + 1) * CHUNK, h * WIDE : (h + 1) * WIDE],
+                    state.astype(BF16), preferred_element_type=F32,
+                )
+                first = bounds[chunk * CHUNK : (chunk + 1) * CHUNK]
+                carried.append(jnp.where(first <= chunk * CHUNK, one, 0.0))
+            linear = inner[:, column] + jnp.concatenate(carried, 0)
+            mean = jnp.mean(linear * linear, 1, keepdims=True)
+            normed = linear * lax.rsqrt(mean + 1e-5)
+            outs[part][:, column] = (normed + windowed[:, column]).astype(BF16)
+
+
+def finish(limits, first_doc, bounds, prefix, low, high, states):
+    half, columns = low[0].shape
     heads = columns // HEAD_DIM
     group = min(GROUP, heads)
 
@@ -336,24 +371,22 @@
         return pl.BlockSpec((count, group * width), lambda g, *_: (0, g))
 
     return pl.pallas_call(
-        functools.partial(finish_kernel, part, len(states)),
+        functools.partial(finish_kernel, len(states)),
         grid_spec=pltpu.PrefetchScalarGridSpec(
             num_scalar_prefetch=1,
             grid=(heads // group,),
             in_specs=[
                 pl.BlockSpec(first_doc.shape, lambda g, *_: (0, 0)),
-                some(half, WIDE), pl.BlockSpec((half, 1), lambda g, *_: (part, 0)),
-                some(half, HEAD_DIM), some(half, HEAD_DIM),
-                pl.BlockSpec(
-                    (prefix.shape[0] // 2, group, STATE, HEAD_DIM), lambda g, *_: (part, g, 0, 0)
-                ),
+                pl.BlockSpec(bounds.shape, lambda g, *_: (0, 0)),
+                pl.BlockSpec((prefix.shape[0], group, STATE, HEAD_DIM), lambda g, *_: (0, g, 0, 0)),
             ]
-            + [pl.BlockSpec((group, STATE, HEAD_DIM), lambda g, *_: (g, 0, 0))] * len(states),
-            out_specs=some(half, HEAD_DIM),
+            + [some(half, HEAD_DIM), some(half, HEAD_DIM), some(half, WIDE)] * 2
+            + [pl.BlockSpec((group, STATE + WIN, HEAD_DIM), lambda g, *_: (g, 0, 0))] * len(states),
+            out_specs=[some(half, HEAD_DIM)] * 2,
         ),
-        out_shape=jax.ShapeDtypeStruct((half, columns), BF16),
+        out_shape=[jax.ShapeDtypeStruct((half, columns), BF16)] * 2,
         compiler_params=params(),
-    )(limits, first_doc, phi_query, bounds, inner, windowed, prefix, *states)
+    )(limits, first_doc, bounds, prefix, *low, *high, *states)
 
 
 def after(x, *others):
@@ -403,7 +436,7 @@
     for n in range(count):
         chip = lax.rem(z + n, count)
         theirs = lax.dynamic_index_in_dim(other_rows, chip, 0, keepdims=False)
-        out_rows.append(jnp.concatenate([cut(chip, c), theirs], 0))
+        out_rows += [cut(chip, c), theirs]
 
     used = value_columns + w_feat.shape[1]
     fv_columns = -(-used // 256) * 256
@@ -411,13 +444,14 @@
         [w_value, w_feat, jnp.zeros((w_value.shape[0], fv_columns - used), BF16), w_window], 1
     )
     all_columns = weight.shape[1]
-    part = project(place, (0,), [tokens], [tokens_there], weight, 0, all_columns)
+    widths = (fv_columns, all_columns - fv_columns)
+    part = project(place, (0,), [tokens], [tokens_there], weight, 0, widths)
 
     ready = lax.optimization_barrier(
-        (pieces[1], pieces[count - 1], limits, bounds, first_doc, tail_docs, part, *out_rows)
-    )
-    pieces[1], pieces[count - 1], limits, bounds, first_doc, tail_docs, part = ready[:7]
-    out_rows = ready[7:]
+        (pieces[1], pieces[count - 1], limits, bounds, first_doc, tail_docs, *part, *out_rows)
+    )
+    pieces[1], pieces[count - 1], limits, bounds, first_doc, tail_docs = ready[:6]
+    part, out_rows = ready[6:8], ready[8:]
 
     for n in range(2, count // 2 + 1):
         pieces[n] = ring(pieces[n - 1], -1, count)
@@ -426,50 +460,43 @@
     near = (1, count - 1)
     mine = [pieces[n] for n in near]
     part = project(
-        place, near, mine, [swap(p, count) for p in mine], weight, 0, all_columns, part
+        place, near, mine, [swap(p, count) for p in mine], weight, 0, widths, part
     )
     late = tuple(range(2, count - 1))
-    *mine, part = lax.optimization_barrier((*[pieces[n] for n in late], part))
+    *mine, fv_part, win_part = lax.optimization_barrier((*[pieces[n] for n in late], *part))
     theirs = [swap(p, count) for p in mine]
-    both = project(place, late, mine, theirs, weight, 0, fv_columns, part, BF16)
+    (both,) = project(place, late, mine, theirs, weight, 0, widths[:1], [fv_part], BF16)
     prefix, state = sums(limits, both, heads, key_map, scale_rows)
     states = [
         lax.ppermute(state, "ctx", [(i, i + k) for i in range(blocks - k)])
         for k in range(1, blocks)
     ]
-    window = project(
-        place, late, [after(mine[0], state), *mine[1:]], theirs, weight, fv_columns, all_columns - fv_columns, part,
-        BF16,
-    )
-    local_high = local(1, both, window, bounds, pick, query_map, scale_rows, heads)
-    tail = [
-        lax.ppermute(a, "ctx", onward)
-        for a in (after(both, window)[rows - WIN :, :value_columns], window[rows - WIN :])
-    ]
-    high = finish(1, limits, first_doc, bounds, prefix, local_high, states)
-    def partial(chip, weight, *received):
-        total = jnp.dot(chip, weight, preferred_element_type=F32)
-        for r in received:
-            total += r.astype(F32)
-        return total.astype(BF16)
-
-    def first_part(mixed, step):
-        chip = jnp.concatenate([mixed, swap(mixed, count)], 1)
-        return chip, partial(chip, out_rows[-step % count])
-
-    def scattered(chip, sent, step):
-        for n in range(2, count + 1):
-            sent = partial(chip, out_rows[-step * n % count], ring(sent, step, count))
+    window, tail = project(
+        place, late, [after(mine[0], state), *mine[1:]], theirs, weight, fv_columns, widths[1:],
+        [win_part], BF16, True,
+    )
+    tail = lax.ppermute(tail, "ctx", onward)
+    common = (window, bounds, pick, query_map, scale_rows, heads)
+    local_high = local(1, both, *common)
+    local_low = local(
+        0, after(both, local_high[0]), *common, (states[0], tail), (tail_docs, first_doc)
+    )
+    low, high = finish(limits, first_doc, bounds, prefix, local_low, local_high, states)
+
+    def scattered(mixed, step):
+        swapped = swap(mixed, count)
+        sent = None
+        for n in range(1, count + 1):
+            at = 2 * (-step * n % count)
+            total = jnp.dot(mixed, out_rows[at], preferred_element_type=F32)
+            total += jnp.dot(swapped, out_rows[at + 1], preferred_element_type=F32)
+            if sent is not None:
+                total += ring(sent, step, count).astype(F32)
+            sent = total.astype(BF16)
         return sent
 
-    high_parts = first_part(high, -1)
-    local_low = local(
-        0, after(both, high_parts[1]), window, bounds, pick, query_map, scale_rows, heads, tail,
-        (tail_docs, first_doc),
-    )
-    low = finish(0, limits, first_doc, bounds, prefix, local_low, states)
-    high_out = scattered(*high_parts, -1)
-    low_out = scattered(*first_part(low, 1), 1)
+    high_out = scattered(high, -1)
+    low_out = scattered(low, 1)
     return jnp.concatenate([low_out, high_out], 0)
 
 

time: 210 us -> 198 us (0.943)
  Pallas kernels: 59.2 us -> 45.6 us
  local copies, waits for them, and re-layouts: 17.1 us -> 29.3 us
  starting transfers between devices: 40.2 us -> 30 us
    pallas_call x6 -> x5, Pallas kernels: 46.7 us -> 32.2 us  [the longest x4 28.3 us: project(): pl.pallas_call(functools.partial(project_kernel, len(chips), cuts, before...]
    unnamed x44 -> x60, local copies, waits for them, and re-layouts: 8.55 us -> 18.3 us
    ppermute x9, starting transfers between devices: 22.5 us -> 13.9 us  [ring(): lax.ppermute(x, 'head', [(2 * z + c, 2 * ((z + step) % count) + c) for z...]
    concatenate x2 -> x0, other arithmetic: 2.91 us -> none  [shards(): out_rows.append(jnp.concatenate([cut(chip, c), theirs], 0))]
    ppermute x2 -> x1, starting transfers between devices: 4.29 us -> 1.47 us  [shards(): tail = lax.ppermute(tail, 'ctx', onward)]
    squeeze x1, local copies, waits for them, and re-layouts: 1.75 us -> 4.11 us  [shards(): theirs = lax.dynamic_index_in_dim(other_rows, chip, 0, keepdims=False)]
    ppermute x2 -> x1, waiting for transfers between devices: 2.18 us -> 0.01 us  [shards(): tail = lax.ppermute(tail, 'ctx', onward)]
    dot_general x8 -> x16, matrix products: 5.64 us -> 6.99 us  [the longest x8 3.52 us: scattered(): total = jnp.dot(mixed, out_rows[at], preferred_element_type=F32)]
  transfers between devices with their start and end apart: 22 -> 21, of which waited for: 12 -> 12; matrix products, arithmetic and copies ran while one was open for 13% -> 15% of each run, Pallas kernels for 19% -> 17%
where the time goes in v6:
time: 198 us
  waiting for transfers between devices  71.2 us (36%)
  Pallas kernels  45.6 us (23%)
  starting transfers between devices  30 us (15%)
  local copies, waits for them, and re-layouts  29.3 us (15%)
  other arithmetic  14.1 us (7%)
  matrix products  6.99 us (4%)
    ppermute x9, waiting for transfers between devices, ring(): lax.ppermute(x, 'head', [(2 * z + c, 2 * ((z + step) % count) + c) for z...  65 us
    pallas_call x4, Pallas kernels, project(): pl.pallas_call(functools.partial(project_kernel, len(chips), cuts, before...  28.3 us
    unnamed x60, local copies, waits for them, and re-layouts  18.3 us
    ppermute x9, starting transfers between devices, ring(): lax.ppermute(x, 'head', [(2 * z + c, 2 * ((z + step) % count) + c) for z...  13.9 us
    ppermute x3, starting transfers between devices, shards(): lax.ppermute(state, 'ctx', [(i, i + k) for i in range(blocks - k)])  9.6 us
    pallas_call x2, Pallas kernels, local(): pl.pallas_call(functools.partial(local_kernel, part), grid=(heads // grou...  9.59 us
    concatenate x1, other arithmetic, shards(): jnp.concatenate([w_value, w_feat, jnp.zeros((w_value.shape[0], fv_columns...  8.41 us
    ppermute x7, waiting for transfers between devices, swap(): return lax.ppermute(x, 'head', [(h, h ^ 1) for h in range(2 * count)])  6.17 us
  transfers between devices with their start and end apart: 21, of which 12 were waited for; matrix products, arithmetic and copies ran while one was open for 15% of the time, Pallas kernels for 17%

profile of v6, /device:TPU:0, one launch (start us, length us, event | category | flops | bytes accessed | tf_op | source)
XLA Modules:
  0.0 197.8 jit_solution(11916170728541964453)
XLA Ops:
  0.5 4.6 %collective-permute-start = (bf16[1024,512]{1,0:T(8,128)(2,1)}, bf16[1024,512]{1,0:T(8,128)(2,1)}, u32[]{:S(2)}, u32[]{:S(2)}) collective-permute-start(bf16[1024,512]{1,0:T(8,128)(2,1)} %refs_0_.1), channel_id=1, source_target_pairs={{0,6},{1,7},{2,0},{3,1},{4,2},{5,3},{6,4},{7,5},{8,14},{9,15},{10,... | collective-permute-start | bytes 3145736 | tf_op jit(solution)/shard_map/ppermute | solution.py:31
  5.9 3.4 %collective-permute-start.2 = (bf16[64,128]{1,0:T(8,128)(2,1)S(1)}, bf16[64,128]{1,0:T(8,128)(2,1)S(1)}, u32[]{:S(2)}, u32[]{:S(2)}) collective-permute-start(bf16[64,128]{1,0:T(8,128)(2,1)S(1)} %broadcast_in_dim.7), channel_id=1, source_target_pairs={{0,8},{8,16},{16,24},{1,9},{9,17},{17,25},{2,10},{10,18},{18,26},{... | collective-permute-start | bytes 49160 | tf_op jit(solution)/shard_map/ppermute | solution.py:419
  9.4 3.9 %constant_dynamic-slice_fusion = (bf16[512,512]{1,0:T(8,128)(2,1)}, bf16[512,512]{1,0:T(8,128)(2,1)}, bf16[512,512]{1,0:T(8,128)(2,1)}, bf16[1,512,512]{2,1,0:T(...) fusion(bf16[512,4096]{1,0:T(8,128)(2,1)} %param.15, ...), kind=kLoop, calls=%fused_computation.35 | loop fusion | bytes 8388640 | tf_op jit(solution)/shard_map/dynamic_slice | solution.py:432
  17.1 8.4 %pad_maximum_fusion.refs_2_.refs_4_.refs_5_ = bf16[4096,1792]{1,0:T(8,128)(2,1)} fusion(bf16[4096,1024]{1,0:T(8,128)(2,1)S(1)} %copy-done.16, bf16[4096,128]{1,0:T(8,128)(2,1)} %param.12, bf16[4096,512]{1,0:T(8,128)(2,1)S(1)} %copy-done.25, bf16[1792]{0:T(1024)(128)(2,1)S(1)} %pad.8.clone), kind=kLoop, calls=%fused_computation | loop fusion | flops 58720256 | bytes 28315136 | tf_op jit(solution)/shard_map/concatenate | solution.py:443
  29.8 5.2 %copy-done = bf16[4096,1792]{1,0:T(8,128)(2,1)S(1)} copy-done((bf16[4096,1792]{1,0:T(8,128)(2,1)S(1)}, bf16[4096,1792]{1,0:T(8,128)(2,1)}, u32[]{:S(2)}) %copy-start) | copy-done | bytes 14680088
  35.0 6.8 %shard_map.100 = (f32[1024,768]{1,0:T(8,128)S(1)}, f32[1024,1024]{1,0:T(8,128)S(1)}) custom-call(s32[2]{0:T(128)S(1)} %pad_add_fusion.1.place, bf16[1024,512]{1,0:T(8,128)(2,1)S(1)} %copy-done.12, bf16[1024,512]{1,0:T(8,128)(2,1)S(1)} %collective-permute-done.3.refs_1_, bf16[4096,1792]{1,0:T(8,128)(2,1)S(1)} %copy-done), custom_call_target="tpu_custom_call" | custom-call | tf_op jit(solution)/shard_map/pallas_call | solution.py:107
  41.8 2.0 copy-done.5
  43.8 4.1 %dynamic-slice_bitcast_fusion = (bf16[512,512]{1,0:T(8,128)(2,1)}, bf16[512,512]{1,0:T(8,128)(2,1)}, bf16[512,512]{1,0:T(8,128)(2,1)}, bf16[512,512]{1,0:T(8,128)(2,1)}) fusion(bf16[4,512,512]{2,1,0:T(8,128)(2,1)} %collective-permute-done.4, s32[]{:T(128)S(6)} %select_n.61, s32[]{:T(128)S(6)} %select_n.59, s32[]{:T(128)S(6)} %select_n.57, s32[]{:T(128)S(6)} %select_n.55), kind=kLoop, calls=%fused_computation.26 | loop fusion | bytes 4194320 | tf_op jit(solution)/shard_map/jit(dynamic_index_in_dim)/squeeze | solution.py:438
  47.9 3.9 %collective-permute-done.1.refs_1_ = bf16[1024,512]{1,0:T(8,128)(2,1)} collective-permute-done((bf16[1024,512]{1,0:T(8,128)(2,1)}, bf16[1024,512]{1,0:T(8,128)(2,1)}, u32[]{:S(2)}, u32[]{:S(2)}) %collective-permute-start.1) | collective-permute-done | bytes 1048608 | tf_op jit(solution)/shard_map/ppermute | solution.py:31
  56.9 2.2 %copy-done.6 = f32[1024,1024]{1,0:T(8,128)S(1)} copy-done((f32[1024,1024]{1,0:T(8,128)S(1)}, f32[1024,1024]{1,0:T(8,128)}, u32[]{:S(2)}) %copy-start.6) | copy-done | bytes 4194328
  59.1 1.9 copy-done.8
  61.0 13.0 %shard_map.101 = (f32[1024,768]{1,0:T(8,128)S(1)}, f32[1024,1024]{1,0:T(8,128)S(1)}) custom-call(s32[2]{0:T(128)S(1)} %pad_add_fusion.1.place, bf16[1024,512]{1,0:T(8,128)(2,1)} %collective-permute-done.refs_0_, bf16[1024,512]{1,0:T(8,128)(2,1)} %collective-permute-done.1.refs_1_, bf16[1024,512]{1,0:T(8,128)(2,1)S(1)} %collective-permute-done.6.refs_2_, ...), custom_call_target="tpu_custom_call" | custom-call | tf_op jit(solution)/shard_map/pallas_call | solution.py:107
  74.0 2.0 copy-done.3
  76.0 2.4 %collective-permute-done.5.refs_0_ = bf16[1024,512]{1,0:T(8,128)(2,1)S(1)} collective-permute-done((bf16[1024,512]{1,0:T(8,128)(2,1)}, bf16[1024,512]{1,0:T(8,128)(2,1)S(1)}, u32[]{:S(2)}, u32[]{:S(2)}) %collective-permute-start.5) | collective-permute-done | bytes 1048608 | tf_op jit(solution)/shard_map/ppermute | solution.py:31
  78.4 2.7 %collective-permute-done.8.refs_1_ = bf16[1024,512]{1,0:T(8,128)(2,1)S(1)} collective-permute-done((bf16[1024,512]{1,0:T(8,128)(2,1)S(1)}, bf16[1024,512]{1,0:T(8,128)(2,1)S(1)}, u32[]{:S(2)}, u32[]{:S(2)}) %collective-permute-start.8) | collective-permute-done | bytes 1048608 | tf_op jit(solution)/shard_map/ppermute | solution.py:37
  81.1 3.4 %shard_map.102.values.features.old_values = bf16[1024,768]{1,0:T(8,128)(2,1)S(1)} custom-call(s32[2]{0:T(128)S(1)} %pad_add_fusion.1.place, bf16[1024,512]{1,0:T(8,128)(2,1)S(1)} %collective-permute-done.5.refs_0_, bf16[1024,512]{1,0:T(8,128)(2,1)S(1)} %collective-permute-done.8.refs_1_, bf16[4096,1792]{1,0:T(8,128)(2,1)S(1)} %bitcast.53, ...), custom_call_target="tpu_custom_call" | custom-call | tf_op jit(solution)/shard_map/pallas_call | solution.py:107
  84.5 3.8 %shard_map.103 = (f32[4,4,160,128]{3,2,1,0:T(8,128)S(1)}, bf16[4,224,128]{2,1,0:T(8,128)(2,1)}) custom-call(s32[5]{0:T(128)S(1)} %pad_add_fusion.limits, bf16[1024,768]{1,0:T(8,128)(2,1)S(1)} %shard_map.102.values.features.old_values, bf16[1024,768]{1,0:T(8,128)(2,1)S(1)} %shard_map.102.values.features.old_values, bf16[4,128,512]{2,1,0:T(8,128)(2,1)S(1)} %copy-done.14, ...), custom_call_target="tpu_custom_call" | custom-call | tf_op jit(solution)/shard_map/pallas_call | solution.py:188
  88.4 4.2 %collective-permute-start.9 = (bf16[4,224,128]{2,1,0:T(8,128)(2,1)}, bf16[4,224,128]{2,1,0:T(8,128)(2,1)}, u32[]{:S(2)}, u32[]{:S(2)}) collective-permute-start(bf16[4,224,128]{2,1,0:T(8,128)(2,1)} %get-tuple-element.58), channel_id=1, source_target_pairs={{0,8},{8,16},{16,24},{1,9},{9,17},{17,25},{2,10},{10,18},{18,26},{... | collective-permute-start | bytes 688136 | tf_op jit(solution)/shard_map/ppermute | solution.py:471
  92.6 3.4 %collective-permute-start.11 = (bf16[4,224,128]{2,1,0:T(8,128)(2,1)}, bf16[4,224,128]{2,1,0:T(8,128)(2,1)}, u32[]{:S(2)}, u32[]{:S(2)}) collective-permute-start(bf16[4,224,128]{2,1,0:T(8,128)(2,1)} %get-tuple-element.58), channel_id=1, source_target_pairs={{0,16},{8,24},{1,17},{9,25},{2,18},{10,26},{3,19},{11,27},{4,20},{... | collective-permute-start | bytes 688136 | tf_op jit(solution)/shard_map/ppermute | solution.py:471
  96.0 2.0 collective-permute-start.12
  98.0 5.1 %shard_map.104 = (bf16[1024,1024]{1,0:T(8,128)(2,1)S(1)}, bf16[64,1024]{1,0:T(8,128)(2,1)}) custom-call(s32[2]{0:T(128)S(1)} %pad_add_fusion.1.place, bf16[1024,512]{1,0:T(8,128)(2,1)S(1)} %collective-permute-done.5.refs_0_, bf16[1024,512]{1,0:T(8,128)(2,1)S(1)} %collective-permute-done.8.refs_1_, bf16[4096,1792]{1,0:T(8,128)(2,1)S(1)} %bitcast.53, ...), custom_call_target="tpu_custom_call" | custom-call | tf_op jit(solution)/shard_map/pallas_call | solution.py:107
  107.7 4.3 %shard_map.105 = (f32[512,512]{1,0:T(8,128)S(1)}, f32[512,512]{1,0:T(8,128)S(1)}, bf16[512,1024]{1,0:T(8,128)(2,1)S(1)}) custom-call(bf16[1024,768]{1,0:T(8,128)(2,1)S(1)} %shard_map.102.values.features.old_values, bf16[1024,768]{1,0:T(8,128)(2,1)S(1)} %shard_map.102.values.features.old_values, bf16[1024,1024]{1,0:T(8,128)(2,1)S(1)} %copy-done.2, ...), custom_call_target="tpu_custom_call" | custom-call | tf_op jit(solution)/shard_map/pallas_call | solution.py:310
  112.1 5.3 %shard_map.106 = (f32[512,512]{1,0:T(8,128)S(1)}, f32[512,512]{1,0:T(8,128)S(1)}, bf16[512,1024]{1,0:T(8,128)(2,1)S(1)}) custom-call(bf16[1024,768]{1,0:T(8,128)(2,1)S(1)} %shard_map.102.values.features.old_values, bf16[1024,768]{1,0:T(8,128)(2,1)S(1)} %shard_map.102.values.features.old_values, bf16[1024,1024]{1,0:T(8,128)(2,1)S(1)} %copy-done.2, ...), custom_call_target="tpu_custom_call" | custom-call | tf_op jit(solution)/shard_map/pallas_call | solution.py:310
  117.4 3.9 %shard_map.107 = (bf16[512,512]{1,0:T(8,128)(2,1)S(1)}, bf16[512,512]{1,0:T(8,128)(2,1)S(1)}) custom-call(s32[5]{0:T(128)S(1)} %pad_add_fusion.limits, f32[8,128]{1,0:T(8,128)S(1)} %broadcast_in_dim.6.refs_1_.first_doc, s32[1024,1]{1,0:T(8,128)S(1)} %copy.16.bounds, f32[4,4,160,128]{3,2,1,0:T(8,128)S(1)} %copy-done.11, ...), custom_call_target="tpu_custom_call" | custom-call | tf_op jit(solution)/shard_map/pallas_call | solution.py:373
  126.8 2.2 %collective-permute-start.18 = (bf16[512,512]{1,0:T(8,128)(2,1)S(1)}, bf16[512,512]{1,0:T(8,128)(2,1)S(1)}, u32[]{:S(2)}, u32[]{:S(2)}) collective-permute-start(bf16[512,512]{1,0:T(8,128)(2,1)S(1)} %fusion.13), channel_id=1, source_target_pairs={{0,6},{1,7},{2,0},{3,1},{4,2},{5,3},{6,4},{7,5},{8,14},{9,15},{10,... | collective-permute-start | bytes 1572872 | tf_op jit(solution)/shard_map/ppermute | solution.py:31
  130.8 10.1 %collective-permute-done.14 = bf16[512,512]{1,0:T(8,128)(2,1)S(1)} collective-permute-done((bf16[512,512]{1,0:T(8,128)(2,1)S(1)}, bf16[512,512]{1,0:T(8,128)(2,1)S(1)}, u32[]{:S(2)}, u32[]{:S(2)}) %collective-permute-start.14) | collective-permute-done | bytes 524320 | tf_op jit(solution)/shard_map/ppermute | solution.py:31
  141.4 10.6 %collective-permute-done.18 = bf16[512,512]{1,0:T(8,128)(2,1)S(1)} collective-permute-done((bf16[512,512]{1,0:T(8,128)(2,1)S(1)}, bf16[512,512]{1,0:T(8,128)(2,1)S(1)}, u32[]{:S(2)}, u32[]{:S(2)}) %collective-permute-start.18) | collective-permute-done | bytes 524320 | tf_op jit(solution)/shard_map/ppermute | solution.py:31
  154.7 8.7 %collective-permute-done.15 = bf16[512,512]{1,0:T(8,128)(2,1)S(1)} collective-permute-done((bf16[512,512]{1,0:T(8,128)(2,1)S(1)}, bf16[512,512]{1,0:T(8,128)(2,1)S(1)}, u32[]{:S(2)}, u32[]{:S(2)}) %collective-permute-start.15) | collective-permute-done | bytes 524320 | tf_op jit(solution)/shard_map/ppermute | solution.py:31
  163.9 10.6 %collective-permute-done.19 = bf16[512,512]{1,0:T(8,128)(2,1)S(1)} collective-permute-done((bf16[512,512]{1,0:T(8,128)(2,1)S(1)}, bf16[512,512]{1,0:T(8,128)(2,1)S(1)}, u32[]{:S(2)}, u32[]{:S(2)}) %collective-permute-start.19) | collective-permute-done | bytes 524320 | tf_op jit(solution)/shard_map/ppermute | solution.py:31
  175.0 1.8 collective-permute-start.20
  177.2 8.7 %collective-permute-done.16 = bf16[512,512]{1,0:T(8,128)(2,1)S(1)} collective-permute-done((bf16[512,512]{1,0:T(8,128)(2,1)S(1)}, bf16[512,512]{1,0:T(8,128)(2,1)S(1)}, u32[]{:S(2)}, u32[]{:S(2)}) %collective-permute-start.16) | collective-permute-done | bytes 524320 | tf_op jit(solution)/shard_map/ppermute | solution.py:31
  186.4 9.9 %collective-permute-done.20 = bf16[512,512]{1,0:T(8,128)(2,1)S(1)} collective-permute-done((bf16[512,512]{1,0:T(8,128)(2,1)S(1)}, bf16[512,512]{1,0:T(8,128)(2,1)S(1)}, u32[]{:S(2)}, u32[]{:S(2)}) %collective-permute-start.20) | collective-permute-done | bytes 524320 | tf_op jit(solution)/shard_map/ppermute | solution.py:31
  (117 shorter events, 32.7 us)
Async XLA Ops:
  0.0 9.4 %collective-permute-start.3 = (bf16[1024,512]{1,0:T(8,128)(2,1)}, bf16[1024,512]{1,0:T(8,128)(2,1)S(1)}, u32[]{:S(2)}, u32[]{:S(2)}) collective-permute-start(bf16[1024,512]{1,0:T(8,128)(2,1)} %refs_0_.1), channel_id=1, source_target_pairs={{0,1},{1,0},{2,3},{3,2},{4,5},{5,4},{6,7},{7,6},{8,9},{9,8},{10,11... | collective-permute-start | bytes 3145736 | tf_op jit(solution)/shard_map/ppermute | solution.py:37
  0.5 47.4 %collective-permute-start = (bf16[1024,512]{1,0:T(8,128)(2,1)}, bf16[1024,512]{1,0:T(8,128)(2,1)}, u32[]{:S(2)}, u32[]{:S(2)}) collective-permute-start(bf16[1024,512]{1,0:T(8,128)(2,1)} %refs_0_.1), channel_id=1, source_target_pairs={{0,6},{1,7},{2,0},{3,1},{4,2},{5,3},{6,4},{7,5},{8,14},{9,15},{10,... | collective-permute-start | bytes 3145736 | tf_op jit(solution)/shard_map/ppermute | solution.py:31
  5.1 46.8 %collective-permute-start.1 = (bf16[1024,512]{1,0:T(8,128)(2,1)}, bf16[1024,512]{1,0:T(8,128)(2,1)}, u32[]{:S(2)}, u32[]{:S(2)}) collective-permute-start(bf16[1024,512]{1,0:T(8,128)(2,1)} %refs_0_.1), channel_id=1, source_target_pairs={{0,2},{1,3},{2,4},{3,5},{4,6},{5,7},{6,0},{7,1},{8,10},{9,11},{10,... | collective-permute-start | bytes 3145736 | tf_op jit(solution)/shard_map/ppermute | solution.py:31
  5.9 42.0 %collective-permute-start.2 = (bf16[64,128]{1,0:T(8,128)(2,1)S(1)}, bf16[64,128]{1,0:T(8,128)(2,1)S(1)}, u32[]{:S(2)}, u32[]{:S(2)}) collective-permute-start(bf16[64,128]{1,0:T(8,128)(2,1)S(1)} %broadcast_in_dim.7), channel_id=1, source_target_pairs={{0,8},{8,16},{16,24},{1,9},{9,17},{17,25},{2,10},{10,18},{18,26},{... | collective-permute-start | bytes 49160 | tf_op jit(solution)/shard_map/ppermute | solution.py:419
  15.0 14.8 %copy-start.12 = (bf16[1024,512]{1,0:T(8,128)(2,1)S(1)}, bf16[1024,512]{1,0:T(8,128)(2,1)}, u32[]{:S(2)}) copy-start(bf16[1024,512]{1,0:T(8,128)(2,1)} %refs_0_.1) | copy-start | bytes 3145732
  15.0 28.8 %collective-permute-start.4 = (bf16[4,512,512]{2,1,0:T(8,128)(2,1)}, bf16[4,512,512]{2,1,0:T(8,128)(2,1)}, u32[]{:S(2)}, u32[]{:S(2)}) collective-permute-start(bf16[4,512,512]{2,1,0:T(8,128)(2,1)} %pad_maximum_fusion.1), channel_id=1, source_target_pairs={{0,1},{1,0},{2,3},{3,2},{4,5},{5,4},{6,7},{7,6},{8,9},{9,8},{10,11... | collective-permute-start | bytes 6291464 | tf_op jit(solution)/shard_map/ppermute | solution.py:37
  43.8 37.3 %slice-start = ((s8[14680064]{0:T(1024)(128)(4,1)}), s8[4194304]{0:T(1024)(128)(4,1)S(1)}, s32[]{:S(2)}) async-start(s8[14680064]{0:T(1024)(128)(4,1)} %bitcast.52), calls=%async_computation | async-start | bytes 8388608
  52.5 28.6 %slice-start.1 = ((s8[14680064]{0:T(1024)(128)(4,1)}), s8[4194304]{0:T(1024)(128)(4,1)S(1)}, s32[]{:S(2)}) async-start(s8[14680064]{0:T(1024)(128)(4,1)} %bitcast.52), calls=%async_computation.1 | async-start | bytes 8388608
  52.5 28.6 %slice-start.2 = ((s8[14680064]{0:T(1024)(128)(4,1)}), s8[4194304]{0:T(1024)(128)(4,1)S(1)}, s32[]{:S(2)}) async-start(s8[14680064]{0:T(1024)(128)(4,1)} %bitcast.52), calls=%async_computation.2 | async-start | bytes 8388608
  52.5 28.6 %slice-start.3 = ((s8[14680064]{0:T(1024)(128)(4,1)}), s8[2097152]{0:T(1024)(128)(4,1)S(1)}, s32[]{:S(2)}) async-start(s8[14680064]{0:T(1024)(128)(4,1)} %bitcast.52), calls=%async_computation.3 | async-start | bytes 4194304
  52.5 2.9 %collective-permute-start.6 = (bf16[1024,512]{1,0:T(8,128)(2,1)}, bf16[1024,512]{1,0:T(8,128)(2,1)S(1)}, u32[]{:S(2)}, u32[]{:S(2)}) collective-permute-start(bf16[1024,512]{1,0:T(8,128)(2,1)} %collective-permute-done.refs_0_), channel_id=1, source_target_pairs={{0,1},{1,0},{2,3},{3,2},{4,5},{5,4},{6,7},{7,6},{8,9},{9,8},{10,11... | collective-permute-start | bytes 3145736 | tf_op jit(solution)/shard_map/ppermute | solution.py:37
  52.6 4.4 %collective-permute-start.7 = (bf16[1024,512]{1,0:T(8,128)(2,1)}, bf16[1024,512]{1,0:T(8,128)(2,1)S(1)}, u32[]{:S(2)}, u32[]{:S(2)}) collective-permute-start(bf16[1024,512]{1,0:T(8,128)(2,1)} %collective-permute-done.1.refs_1_), channel_id=1, source_target_pairs={{0,1},{1,0},{2,3},{3,2},{4,5},{5,4},{6,7},{7,6},{8,9},{9,8},{10,11... | collective-permute-start | bytes 3145736 | tf_op jit(solution)/shard_map/ppermute | solution.py:37
  53.1 25.4 %collective-permute-start.5 = (bf16[1024,512]{1,0:T(8,128)(2,1)}, bf16[1024,512]{1,0:T(8,128)(2,1)S(1)}, u32[]{:S(2)}, u32[]{:S(2)}) collective-permute-start(bf16[1024,512]{1,0:T(8,128)(2,1)} %collective-permute-done.refs_0_), channel_id=1, source_target_pairs={{0,6},{1,7},{2,0},{3,1},{4,2},{5,3},{6,4},{7,5},{8,14},{9,15},{10,... | collective-permute-start | bytes 3145736 | tf_op jit(solution)/shard_map/ppermute | solution.py:31
  78.4 2.7 %collective-permute-start.8 = (bf16[1024,512]{1,0:T(8,128)(2,1)S(1)}, bf16[1024,512]{1,0:T(8,128)(2,1)S(1)}, u32[]{:S(2)}, u32[]{:S(2)}) collective-permute-start(bf16[1024,512]{1,0:T(8,128)(2,1)S(1)} %collective-permute-done.5.refs_0_), channel_id=1, source_target_pairs={{0,1},{1,0},{2,3},{3,2},{4,5},{5,4},{6,7},{7,6},{8,9},{9,8},{10,11... | collective-permute-start | bytes 3145736 | tf_op jit(solution)/shard_map/ppermute | solution.py:37
  81.1 16.9 %copy-start.4 = (f32[1024,1024]{1,0:T(8,128)S(1)}, f32[1024,1024]{1,0:T(8,128)}, u32[]{:S(2)}) copy-start(f32[1024,1024]{1,0:T(8,128)} %copy-done.3) | copy-start | bytes 12582916
  88.4 14.7 %copy-start.10 = (f32[4,4,160,128]{3,2,1,0:T(8,128)}, f32[4,4,160,128]{3,2,1,0:T(8,128)S(1)}, u32[]{:S(2)}) copy-start(f32[4,4,160,128]{3,2,1,0:T(8,128)S(1)} %get-tuple-element.57.prefix) | copy-start | bytes 3932164
  88.4 17.7 %copy-start.9 = (bf16[4,128,512]{2,1,0:T(8,128)(2,1)S(1)}, bf16[4,128,512]{2,1,0:T(8,128)(2,1)}, u32[]{:S(2)}) copy-start(bf16[4,128,512]{2,1,0:T(8,128)(2,1)} %constant.76.clone.expand) | copy-start | bytes 1572868
  88.4 17.8 %copy-start.13 = (bf16[4,128,256]{2,1,0:T(8,128)(2,1)S(1)}, bf16[4,128,256]{2,1,0:T(8,128)(2,1)}, u32[]{:S(2)}) copy-start(bf16[4,128,256]{2,1,0:T(8,128)(2,1)} %constant.79.clone.pick) | copy-start | bytes 786436
  88.4 23.7 %collective-permute-start.9 = (bf16[4,224,128]{2,1,0:T(8,128)(2,1)}, bf16[4,224,128]{2,1,0:T(8,128)(2,1)}, u32[]{:S(2)}, u32[]{:S(2)}) collective-permute-start(bf16[4,224,128]{2,1,0:T(8,128)(2,1)} %get-tuple-element.58), channel_id=1, source_target_pairs={{0,8},{8,16},{16,24},{1,9},{9,17},{17,25},{2,10},{10,18},{18,26},{... | collective-permute-start | bytes 688136 | tf_op jit(solution)/shard_map/ppermute | solution.py:471
  92.6 24.8 %collective-permute-start.11 = (bf16[4,224,128]{2,1,0:T(8,128)(2,1)}, bf16[4,224,128]{2,1,0:T(8,128)(2,1)}, u32[]{:S(2)}, u32[]{:S(2)}) collective-permute-start(bf16[4,224,128]{2,1,0:T(8,128)(2,1)} %get-tuple-element.58), channel_id=1, source_target_pairs={{0,16},{8,24},{1,17},{9,25},{2,18},{10,26},{3,19},{11,27},{4,20},{... | collective-permute-start | bytes 688136 | tf_op jit(solution)/shard_map/ppermute | solution.py:471
  96.0 21.4 %collective-permute-start.12 = (bf16[4,224,128]{2,1,0:T(8,128)(2,1)}, bf16[4,224,128]{2,1,0:T(8,128)(2,1)}, u32[]{:S(2)}, u32[]{:S(2)}) collective-permute-start(bf16[4,224,128]{2,1,0:T(8,128)(2,1)} %get-tuple-element.58), channel_id=1, source_target_pairs={{0,24},{1,25},{2,26},{3,27},{4,28},{5,29},{6,30},{7,31}} | collective-permute-start | bytes 688136 | tf_op jit(solution)/shard_map/ppermute | solution.py:471
  104.4 7.7 %collective-permute-start.10 = (bf16[64,1024]{1,0:T(8,128)(2,1)}, bf16[64,1024]{1,0:T(8,128)(2,1)S(1)}, u32[]{:S(2)}, u32[]{:S(2)}) collective-permute-start(bf16[64,1024]{1,0:T(8,128)(2,1)} %get-tuple-element.64), channel_id=1, source_target_pairs={{0,8},{8,16},{16,24},{1,9},{9,17},{17,25},{2,10},{10,18},{18,26},{... | collective-permute-start | bytes 393224 | tf_op jit(solution)/shard_map/ppermute | solution.py:478
  121.3 2.0 collective-permute-start.13
  121.4 4.5 %collective-permute-start.17 = (bf16[512,512]{1,0:T(8,128)(2,1)S(1)}, bf16[512,512]{1,0:T(8,128)(2,1)S(1)}, u32[]{:S(2)}, u32[]{:S(2)}) collective-permute-start(bf16[512,512]{1,0:T(8,128)(2,1)S(1)} %get-tuple-element.80), channel_id=1, source_target_pairs={{0,1},{1,0},{2,3},{3,2},{4,5},{5,4},{6,7},{7,6},{8,9},{9,8},{10,11... | collective-permute-start | bytes 1572872 | tf_op jit(solution)/shard_map/ppermute | solution.py:37
  124.2 16.7 %collective-permute-start.14 = (bf16[512,512]{1,0:T(8,128)(2,1)S(1)}, bf16[512,512]{1,0:T(8,128)(2,1)S(1)}, u32[]{:S(2)}, u32[]{:S(2)}) collective-permute-start(bf16[512,512]{1,0:T(8,128)(2,1)S(1)} %fusion.12), channel_id=1, source_target_pairs={{0,2},{1,3},{2,4},{3,5},{4,6},{5,7},{6,0},{7,1},{8,10},{9,11},{10,... | collective-permute-start | bytes 1572872 | tf_op jit(solution)/shard_map/ppermute | solution.py:31
  126.8 25.2 %collective-permute-start.18 = (bf16[512,512]{1,0:T(8,128)(2,1)S(1)}, bf16[512,512]{1,0:T(8,128)(2,1)S(1)}, u32[]{:S(2)}, u32[]{:S(2)}) collective-permute-start(bf16[512,512]{1,0:T(8,128)(2,1)S(1)} %fusion.13), channel_id=1, source_target_pairs={{0,6},{1,7},{2,0},{3,1},{4,2},{5,3},{6,4},{7,5},{8,14},{9,15},{10,... | collective-permute-start | bytes 1572872 | tf_op jit(solution)/shard_map/ppermute | solution.py:31
  130.4 23.9 %copy-start.17 = (bf16[512,512]{1,0:T(8,128)(2,1)S(1)}, bf16[512,512]{1,0:T(8,128)(2,1)}, u32[]{:S(2)}) copy-start(bf16[512,512]{1,0:T(8,128)(2,1)} %get-tuple-element.73) | copy-start | bytes 1572868
  141.3 22.1 %collective-permute-start.15 = (bf16[512,512]{1,0:T(8,128)(2,1)S(1)}, bf16[512,512]{1,0:T(8,128)(2,1)S(1)}, u32[]{:S(2)}, u32[]{:S(2)}) collective-permute-start(bf16[512,512]{1,0:T(8,128)(2,1)S(1)} %fusion.8), channel_id=1, source_target_pairs={{0,2},{1,3},{2,4},{3,5},{4,6},{5,7},{6,0},{7,1},{8,10},{9,11},{10,... | collective-permute-start | bytes 1572872 | tf_op jit(solution)/shard_map/ppermute | solution.py:31
  152.5 22.1 %collective-permute-start.19 = (bf16[512,512]{1,0:T(8,128)(2,1)S(1)}, bf16[512,512]{1,0:T(8,128)(2,1)S(1)}, u32[]{:S(2)}, u32[]{:S(2)}) collective-permute-start(bf16[512,512]{1,0:T(8,128)(2,1)S(1)} %fusion.11), channel_id=1, source_target_pairs={{0,6},{1,7},{2,0},{3,1},{4,2},{5,3},{6,4},{7,5},{8,14},{9,15},{10,... | collective-permute-start | bytes 1572872 | tf_op jit(solution)/shard_map/ppermute | solution.py:31
  154.7 31.2 %copy-start.23 = (bf16[512,512]{1,0:T(8,128)(2,1)S(1)}, bf16[512,512]{1,0:T(8,128)(2,1)}, u32[]{:S(2)}) copy-start(bf16[512,512]{1,0:T(8,128)(2,1)} %get-tuple-element.72) | copy-start | bytes 1572868
  163.8 22.1 %collective-permute-start.16 = (bf16[512,512]{1,0:T(8,128)(2,1)S(1)}, bf16[512,512]{1,0:T(8,128)(2,1)S(1)}, u32[]{:S(2)}, u32[]{:S(2)}) collective-permute-start(bf16[512,512]{1,0:T(8,128)(2,1)S(1)} %fusion.7), channel_id=1, source_target_pairs={{0,2},{1,3},{2,4},{3,5},{4,6},{5,7},{6,0},{7,1},{8,10},{9,11},{10,... | collective-permute-start | bytes 1572872 | tf_op jit(solution)/shard_map/ppermute | solution.py:31
  175.0 21.3 %collective-permute-start.20 = (bf16[512,512]{1,0:T(8,128)(2,1)S(1)}, bf16[512,512]{1,0:T(8,128)(2,1)S(1)}, u32[]{:S(2)}, u32[]{:S(2)}) collective-permute-start(bf16[512,512]{1,0:T(8,128)(2,1)S(1)} %fusion.10), channel_id=1, source_target_pairs={{0,6},{1,7},{2,0},{3,1},{4,2},{5,3},{6,4},{7,5},{8,14},{9,15},{10,... | collective-permute-start | bytes 1572872 | tf_op jit(solution)/shard_map/ppermute | solution.py:31
  (19 other events, 96.9 us)

commit v7 on v6

v7 whole, which is shorter than its diff:
```python
import functools

import jax
import jax.numpy as jnp
import numpy as np
from jax import lax
from jax.experimental import pallas as pl
from jax.experimental.pallas import tpu as pltpu
from jax.sharding import PartitionSpec as P

HEAD_DIM = 128
FEAT = 16
WIN = 64
PAIRS = [(i, j) for i in range(FEAT) for j in range(i, FEAT)]
WIDE = 256
CHUNK = 256
GROUP = 4
STATE = -(-(len(PAIRS) + FEAT + 1) // 16) * 16
SENT = STATE + 2 * WIN
VMEM = 24 * 1024 * 1024
TILE = 128
LANES = 128
F32 = jnp.float32
BF16 = jnp.bfloat16


def params():
    return pltpu.CompilerParams(vmem_limit_bytes=VMEM, dimension_semantics=("arbitrary",))


def ring(x, step, count):
    return lax.ppermute(
        x, "head", [(2 * z + c, 2 * ((z + step) % count) + c) for z in range(count) for c in (0, 1)]
    )


def swap(x, count):
    return lax.ppermute(x, "head", [(h, h ^ 1) for h in range(2 * count)])


def by_column(c, mine, theirs, both):
    width = mine[0].shape[1]
    for n in range(len(mine)):
        own = pl.multiple_of((2 * n + c) * width, width)
        other = pl.multiple_of((2 * n + 1 - c) * width, width)
        both[:, pl.ds(own, width)] = mine[n][...]
        both[:, pl.ds(other, width)] = theirs[n][...]


def project_kernel(chips, cuts, has_before, place, *refs):
    mine, theirs, weights = refs[:chips], refs[chips : 2 * chips], refs[2 * chips : 3 * chips]
    before = refs[3 * chips : 3 * chips + len(cuts)] if has_before else None
    outs, both = refs[-1 - len(cuts) : -1], refs[-1]
    width = mine[0].shape[1]
    c = place[1]
    step = pl.program_id(0)

    @pl.when(step == 0)
    def _():
        by_column(c, mine, theirs, both)

    def tile(k):
        total = before[k][...] if has_before else None
        for n in range(chips):
            rows = both[:, 2 * n * width : 2 * (n + 1) * width]
            part = jnp.dot(rows, weights[n][...], preferred_element_type=F32)
            total = part if total is None else total + part
        outs[k][...] = total.astype(outs[k].dtype)

    if len(cuts) == 1:
        tile(0)
    else:

        @pl.when(step < cuts[0])
        def _():
            tile(0)

        @pl.when(step >= cuts[0])
        def _():
            tile(1)


def project(place, chips, mine, theirs, weight, first, columns, before=None, dtype=F32):
    rows, width = mine[0].shape
    count = weight.shape[0] // (2 * width)
    size = 256
    start = first // size
    cuts = [n // size for n in columns]
    specs = [pl.BlockSpec((rows, width), lambda j, p: (0, 0))] * (2 * len(chips))
    for n in chips:
        specs.append(
            pl.BlockSpec(
                (2 * width, size), lambda j, p, n=n: (lax.rem(p[0] + n, count), start + j)
            )
        )
    results = [
        pl.BlockSpec(
            (rows, size),
            lambda j, p, at=sum(cuts[:k]), n=cuts[k]: (0, jnp.clip(j - at, 0, n - 1)),
        )
        for k in range(len(cuts))
    ]
    args = [*mine, *theirs] + [weight] * len(chips)
    if before is not None:
        specs += results
        args += before
    shapes = [jax.ShapeDtypeStruct((rows, n), dtype) for n in columns]
    return pl.pallas_call(
        functools.partial(project_kernel, len(chips), cuts, before is not None),
        grid_spec=pltpu.PrefetchScalarGridSpec(
            num_scalar_prefetch=1,
            grid=(sum(cuts),),
            in_specs=specs,
            out_specs=results,
            scratch_shapes=[pltpu.VMEM((rows, 2 * width * len(chips)), BF16)],
        ),
        out_shape=shapes,
        compiler_params=params(),
    )(place, *args)


def late_kernel(chips, heads, place, *refs):
    mine, theirs, weights = refs[:chips], refs[chips : 2 * chips], refs[2 * chips : 3 * chips]
    key_weights = refs[3 * chips : (3 + heads) * chips]
    before, *key_before = refs[(3 + heads) * chips : (3 + heads) * chips + 1 + heads]
    out, keys, both = refs[-3:]
    width = 2 * mine[0].shape[1]
    step = pl.program_id(0)

    @pl.when(step == 0)
    def _():
        by_column(place[1], mine, theirs, both)

    total = before[...]
    for n in range(chips):
        rows = both[:, n * width : (n + 1) * width]
        total += jnp.dot(rows, weights[n][...], preferred_element_type=F32)
    out[...] = total.astype(BF16)

    @pl.when(step == pl.num_programs(0) - 1)
    def _():
        last = slice(out.shape[0] - WIN, out.shape[0])
        for h in range(heads):
            tail = key_before[h][...]
            for n in range(chips):
                tail += jnp.dot(
                    both[last, n * width : (n + 1) * width], key_weights[n * heads + h][...],
                    preferred_element_type=F32,
                )
            keys[h] = tail.astype(BF16)


def project_late(place, chips, mine, theirs, weight, heads, before, window_before):
    rows, width = mine[0].shape
    count = weight.shape[0] // (2 * width)
    columns = before.shape[1]
    size = 256
    first = columns // HEAD_DIM + 1
    specs = [pl.BlockSpec((rows, width), lambda j, p: (0, 0))] * (2 * len(chips))
    for n in chips:
        specs.append(
            pl.BlockSpec((2 * width, size), lambda j, p, n=n: (lax.rem(p[0] + n, count), j))
        )
    for n in chips:
        for h in range(heads):
            specs.append(
                pl.BlockSpec(
                    (2 * width, HEAD_DIM),
                    lambda j, p, n=n, h=h: (lax.rem(p[0] + n, count), first + 2 * h),
                )
            )
    block = pl.BlockSpec((rows, size), lambda j, p: (0, j))
    specs.append(block)
    for h in range(heads):
        specs.append(pl.BlockSpec((WIN, HEAD_DIM), lambda j, p, h=h: (rows // WIN - 1, 2 * h + 1)))
    return pl.pallas_call(
        functools.partial(late_kernel, len(chips), heads),
        grid_spec=pltpu.PrefetchScalarGridSpec(
            num_scalar_prefetch=1,
            grid=(columns // size,),
            in_specs=specs,
            out_specs=[block, pl.BlockSpec((heads, WIN, HEAD_DIM), lambda j, p: (0, 0, 0))],
            scratch_shapes=[pltpu.VMEM((rows, 2 * width * len(chips)), BF16)],
        ),
        out_shape=[
            jax.ShapeDtypeStruct((rows, columns), BF16),
            jax.ShapeDtypeStruct((heads, WIN, HEAD_DIM), BF16),
        ],
        compiler_params=params(),
    )(place, *mine, *theirs, *[weight] * (len(chips) * (1 + heads)), before, *[window_before] * heads)


def expansions(heads):
    lanes = -(-heads * 2 * FEAT // LANES) * LANES
    maps = np.zeros((2, heads, lanes, 2 * WIDE), np.float32)
    rows = np.zeros((3, WIDE), np.float32)
    for h in range(heads):
        for side in (0, 1):
            base = h * 2 * FEAT + side * FEAT
            for n, (i, j) in enumerate(PAIRS):
                maps[side, h, base + i, n] = 1.0
                maps[side, h, base + j, WIDE + n] = 1.0
            for i in range(FEAT):
                maps[side, h, base + i, len(PAIRS) + i] = 1.0
    for n, (i, j) in enumerate(PAIRS):
        rows[2, n] = (2.0 * FEAT) ** -0.5 * (1.0 if i == j else 2.0**0.5)
    rows[1, len(PAIRS) : len(PAIRS) + FEAT + 1] = 1.0
    rows[0, len(PAIRS) + FEAT] = 1.0
    rows[2, len(PAIRS) : len(PAIRS) + FEAT] = FEAT**-0.25
    rows[2, len(PAIRS) + FEAT] = 1.0
    return maps.astype(jnp.bfloat16), rows


def picks(heads):
    lanes = -(-heads * 2 * FEAT // LANES) * LANES
    maps = np.zeros((heads, lanes, 256), np.float32)
    for h in range(heads):
        for i in range(FEAT):
            maps[h, h * 2 * FEAT + i, i] = 1.0
            maps[h, h * 2 * FEAT + FEAT + i, 128 + i] = 1.0
    return maps.astype(jnp.bfloat16)


def phi(features, expand, rows):
    factors = jnp.dot(features, expand, preferred_element_type=F32)
    left = factors[:, :WIDE] + rows[0:1]
    right = factors[:, WIDE:] + rows[1:2]
    return (left * right * rows[2:3]).astype(BF16)


def sums_kernel(limits, values, features, expand, rows, keys, prefix, end):
    chunks, heads = prefix.shape[:2]
    mark = lax.broadcasted_iota(jnp.int32, (STATE, HEAD_DIM), 0) == STATE - 1
    at = lax.broadcasted_iota(jnp.int32, (CHUNK, HEAD_DIM), 0)
    for h in range(heads):
        column = slice(h * HEAD_DIM, (h + 1) * HEAD_DIM)
        phi_key = phi(features[...], expand[h], rows[...])
        parts = []
        for n in range(chunks):
            here = slice(n * CHUNK, (n + 1) * CHUNK)
            kept = jnp.where(at + n * CHUNK >= limits[n], values[here, column].astype(F32), 0.0)
            parts.append(
                lax.dot_general(
                    phi_key[here], kept.astype(BF16), (((0,), (0,)), ((), ())),
                    preferred_element_type=F32,
                )[:STATE]
            )
        state = jnp.zeros((STATE, HEAD_DIM), F32)
        for n in range(chunks):
            prefix[n, h] = state
            state = parts[n] + jnp.where(limits[n] <= n * CHUNK, state, 0.0)
        end[h, :STATE] = jnp.where(mark, (limits[chunks] + 1).astype(F32), state).astype(BF16)
        end[h, STATE : STATE + WIN] = values[values.shape[0] - WIN :, column]
        end[h, STATE + WIN :] = keys[h]


def sums(limits, both, keys, expand, rows):
    heads = keys.shape[0]
    chunks = both.shape[0] // CHUNK
    group = min(GROUP, heads)
    count = both.shape[0]
    return pl.pallas_call(
        sums_kernel,
        grid_spec=pltpu.PrefetchScalarGridSpec(
            num_scalar_prefetch=1,
            grid=(heads // group,),
            in_specs=[
                pl.BlockSpec((count, group * HEAD_DIM), lambda g, _: (0, g)),
                pl.BlockSpec((count, LANES), lambda g, _: (0, heads)),
                pl.BlockSpec((group,) + expand.shape[1:], lambda g, _: (g, 0, 0)),
                pl.BlockSpec(rows.shape, lambda g, _: (0, 0)),
                pl.BlockSpec((group, WIN, HEAD_DIM), lambda g, _: (g, 0, 0)),
            ],
            out_specs=[
                pl.BlockSpec((chunks, group, STATE, HEAD_DIM), lambda g, _: (0, g, 0, 0)),
                pl.BlockSpec((group, SENT, HEAD_DIM), lambda g, _: (g, 0, 0)),
            ],
        ),
        out_shape=[
            jax.ShapeDtypeStruct((chunks, heads, STATE, HEAD_DIM), F32),
            jax.ShapeDtypeStruct((heads, SENT, HEAD_DIM), BF16),
        ],
        compiler_params=params(),
    )(limits, both, both, expand, rows, keys)


def windows(tiles):
    wide = TILE + WIN
    logits = jnp.concatenate(
        [
            lax.dot_general(q, k, (((1,), (1,)), ((), ())), preferred_element_type=F32)
            for q, k, _, _, _ in tiles
        ],
        0,
    )
    at = lax.broadcasted_iota(jnp.int32, (TILE, wide), 1)
    row = lax.broadcasted_iota(jnp.int32, (TILE, wide), 0)
    near = (at <= row + WIN) & (at > row)
    good = jnp.concatenate([near & (at >= first - start) for _, _, _, first, start in tiles], 0)
    logits = jnp.where(good, logits * HEAD_DIM**-0.5, -1e30)
    top = jnp.max(logits, 1, keepdims=True)
    weight = jnp.where(good, jnp.exp(logits - top), 0.0)
    probs = (weight / jnp.sum(weight, 1, keepdims=True)).astype(BF16)
    return [
        jnp.dot(probs[n * TILE : (n + 1) * TILE], tile[2], preferred_element_type=F32)
        for n, tile in enumerate(tiles)
    ]


def mix_kernel(
    chips, shifts, place, limits, values, features, window_before, bounds, pick, expand, rows, prefix,
    tail_docs, first_doc, *refs
):
    mine, theirs, weights = refs[:chips], refs[chips : 2 * chips], refs[2 * chips : 3 * chips]
    states = refs[3 * chips : 3 * chips + shifts]
    *outs, both, window = refs[3 * chips + shifts :]
    width = 2 * mine[0].shape[1]
    count = values.shape[0]
    half = count // 2

    @pl.when(pl.program_id(0) == 0)
    def _():
        by_column(place[1], mine, theirs, both)

    total = window_before[...]
    for n in range(chips):
        total += jnp.dot(
            both[:, n * width : (n + 1) * width], weights[n][...], preferred_element_type=F32
        )
    window[...] = total.astype(BF16)

    pair = jnp.dot(features[...], pick[0], preferred_element_type=F32).astype(BF16)
    phi_query = phi(features[...], expand[0], rows[...])
    chunks = count // CHUNK
    at = lax.broadcasted_iota(jnp.int32, (CHUNK, CHUNK), 1)
    row = lax.broadcasted_iota(jnp.int32, (CHUNK, CHUNK), 0)
    dots, good = [], []
    for n in range(chunks):
        here = slice(n * CHUNK, (n + 1) * CHUNK)
        dots.append(
            lax.dot_general(
                pair[here, :128], pair[here, 128:], (((1,), (1,)), ((), ())),
                preferred_element_type=F32,
            )
        )
        good.append((at <= row) & (at >= bounds[here] - n * CHUNK))
    dots, good = jnp.concatenate(dots, 0), jnp.concatenate(good, 0)
    score = dots * (dots * (0.5 / FEAT) + FEAT**-0.5) + 1.0
    score = jnp.where(good, score, 0.0).astype(BF16)

    same = jnp.where(tail_docs[...].astype(F32) == first_doc[0:1, :] + 1.0, 1.0, 0.0)
    in_tail = jnp.sum(same, 0, keepdims=True)[:, 0:1].astype(jnp.int32)
    tiles = []
    for n in range(count // TILE):
        near = slice(n * TILE - WIN, (n + 1) * TILE)
        first = bounds[n * TILE : (n + 1) * TILE]
        if n:
            keys, vals = window[near, HEAD_DIM:], values[near]
        else:
            keys = jnp.concatenate([states[0][0, STATE + WIN :], window[:TILE, HEAD_DIM:]], 0)
            vals = jnp.concatenate([states[0][0, STATE : STATE + WIN], values[:TILE]], 0)
            first = jnp.where(first == 0, -in_tail, first)
        tiles.append(
            (window[n * TILE : (n + 1) * TILE, :HEAD_DIM], keys, vals, first, n * TILE - WIN)
        )
    windowed = jnp.concatenate(windows(tiles), 0)

    unmarked = lax.broadcasted_iota(jnp.int32, (STATE, HEAD_DIM), 0) < STATE - 1
    incoming = jnp.zeros((STATE, HEAD_DIM), F32)
    for k in range(shifts):
        sent = states[k][0, :STATE].astype(F32)
        wanted = (sent[STATE - 1 :] == first_doc[0:1, :] + 1.0) & unmarked
        incoming += jnp.where(wanted, sent, 0.0)
    linear = []
    for n in range(chunks):
        here = slice(n * CHUNK, (n + 1) * CHUNK)
        state = incoming
        if n:
            state = jnp.where(limits[n - 1] <= 0, incoming, 0.0) + prefix[n, 0]
        state = jnp.concatenate([state, jnp.zeros((WIDE - STATE, HEAD_DIM), F32)], 0)
        carried = jnp.dot(phi_query[here], state.astype(BF16), preferred_element_type=F32)
        inner = jnp.dot(score[here], values[here], preferred_element_type=F32)
        linear.append(inner + jnp.where(bounds[here] <= n * CHUNK, carried, 0.0))
    linear = jnp.concatenate(linear, 0)
    mean = jnp.mean(linear * linear, 1, keepdims=True)
    mixed = (linear * lax.rsqrt(mean + 1e-5) + windowed).astype(BF16)
    outs[0][...] = mixed[:half]
    outs[1][...] = mixed[half:]


def mix(place, limits, chips, mine, theirs, weight, both, window_before, bounds, pick, expand, rows, prefix,
        tail_docs, first_doc, states):
    count, width = mine[0].shape
    heads = states[0].shape[0]
    half = count // 2
    ring_size = weight.shape[0] // (2 * width)
    tile = 2 * HEAD_DIM
    first = both.shape[1] // tile

    def full(a):
        return pl.BlockSpec(a.shape, lambda h, *_: (0,) * a.ndim)

    def per_head(a):
        return pl.BlockSpec((1,) + a.shape[1:], lambda h, *_: (h, 0, 0))

    specs = [
        pl.BlockSpec((count, HEAD_DIM), lambda h, *_: (0, h)),
        pl.BlockSpec((count, LANES), lambda h, *_: (0, heads)),
        pl.BlockSpec((count, tile), lambda h, *_: (0, h)),
        full(bounds), per_head(pick), per_head(expand), full(rows),
        pl.BlockSpec((prefix.shape[0], 1, STATE, HEAD_DIM), lambda h, *_: (0, h, 0, 0)),
        full(tail_docs), full(first_doc),
    ]
    specs += [full(mine[0])] * (2 * len(chips))
    for n in chips:
        specs.append(
            pl.BlockSpec(
                (2 * width, tile), lambda h, p, _, n=n: (lax.rem(p[0] + n, ring_size), first + h)
            )
        )
    specs += [per_head(a) for a in states]
    return pl.pallas_call(
        functools.partial(mix_kernel, len(chips), len(states)),
        grid_spec=pltpu.PrefetchScalarGridSpec(
            num_scalar_prefetch=2,
            grid=(heads,),
            in_specs=specs,
            out_specs=[pl.BlockSpec((half, HEAD_DIM), lambda h, *_: (0, h))] * 2,
            scratch_shapes=[
                pltpu.VMEM((count, 2 * width * len(chips)), BF16),
                pltpu.VMEM((count, tile), BF16),
            ],
        ),
        out_shape=[jax.ShapeDtypeStruct((half, heads * HEAD_DIM), BF16)] * 2,
        compiler_params=params(),
    )(place, limits, both, both, window_before, bounds, pick, expand, rows, prefix, tail_docs, first_doc,
      *mine, *theirs, *[weight] * len(chips), *states)


def after(x, *others):
    return lax.optimization_barrier((x, *others))[0]


def shards(tokens, doc_ids, w_feat, w_value, w_window, w_out):
    rows = tokens.shape[0]
    chunks = rows // CHUNK
    value_columns = w_value.shape[1]
    heads = value_columns // HEAD_DIM
    count = lax.axis_size("head") // 2
    blocks = lax.axis_size("ctx")
    me = lax.axis_index("head")
    z, c = me // 2, me % 2
    place = jnp.stack([z, c]).astype(jnp.int32)

    pieces = {0: tokens, 1: ring(tokens, -1, count), count - 1: ring(tokens, 1, count)}
    tokens_there = swap(tokens, count)

    docs = doc_ids.astype(F32)
    ends = jnp.concatenate([docs[CHUNK::CHUNK], docs[rows - 1 :]])
    limits = jnp.sum((docs[None, :] < ends[:, None]).astype(F32), 1).astype(jnp.int32)
    limits = jnp.concatenate([limits, doc_ids[rows - 1 :]])
    first = jnp.sum((docs[None, :] < docs[:, None]).astype(F32), 1, keepdims=True)
    bounds = first.astype(jnp.int32)
    first_doc = jnp.broadcast_to(docs[:1], (8, HEAD_DIM))
    tail_docs = jnp.broadcast_to((docs[rows - WIN :] + 1.0).astype(BF16)[:, None], (WIN, HEAD_DIM))
    onward = [(i, i + 1) for i in range(blocks - 1)]
    tail_docs = lax.ppermute(tail_docs, "ctx", onward)

    maps, scale_rows = expansions(heads)
    query_map, key_map = jnp.asarray(maps[0]), jnp.asarray(maps[1])
    scale_rows = jnp.asarray(scale_rows)
    pick = jnp.asarray(picks(heads))

    depth, columns = w_out.shape
    width = columns // (2 * count)

    rows_out = after(w_out, tokens_there)

    def cut(chip, core):
        return lax.dynamic_slice(rows_out, (0, (2 * chip + core) * width), (depth, width))

    other_rows = swap(jnp.stack([cut(chip, 1 - c) for chip in range(count)]), count)
    out_rows = []
    for n in range(count):
        chip = lax.rem(z + n, count)
        theirs = lax.dynamic_index_in_dim(other_rows, chip, 0, keepdims=False)
        out_rows += [cut(chip, c), theirs]

    used = value_columns + w_feat.shape[1]
    fv_columns = -(-used // 256) * 256
    weight = jnp.concatenate(
        [w_value, w_feat, jnp.zeros((w_value.shape[0], fv_columns - used), BF16), w_window], 1
    )
    all_columns = weight.shape[1]
    widths = (fv_columns, all_columns - fv_columns)
    part = project(place, (0,), [tokens], [tokens_there], weight, 0, widths)

    ready = lax.optimization_barrier(
        (pieces[1], pieces[count - 1], limits, bounds, first_doc, tail_docs, *part, *out_rows)
    )
    pieces[1], pieces[count - 1], limits, bounds, first_doc, tail_docs = ready[:6]
    part, out_rows = ready[6:8], ready[8:]

    for n in range(2, count // 2 + 1):
        pieces[n] = ring(pieces[n - 1], -1, count)
    for n in range(count - 2, count // 2, -1):
        pieces[n] = ring(pieces[n + 1], 1, count)
    near = (1, count - 1)
    mine = [pieces[n] for n in near]
    part = project(
        place, near, mine, [swap(p, count) for p in mine], weight, 0, widths, part
    )
    late = tuple(range(2, count - 1))
    *mine, fv_part, win_part = lax.optimization_barrier((*[pieces[n] for n in late], *part))
    theirs = [swap(p, count) for p in mine]
    both, keys = project_late(place, late, mine, theirs, weight, heads, fv_part, win_part)
    prefix, state = sums(limits, both, keys, key_map, scale_rows)
    states = [
        lax.ppermute(state, "ctx", [(i, i + k) for i in range(blocks - k)])
        for k in range(1, blocks)
    ]
    low, high = mix(
        place, limits, late, mine, theirs, weight, both, win_part, bounds, pick, query_map, scale_rows,
        prefix, tail_docs, first_doc, states,
    )

    def scattered(mixed, step):
        swapped = swap(mixed, count)
        sent = None
        for n in range(1, count + 1):
            at = 2 * (-step * n % count)
            total = jnp.dot(mixed, out_rows[at], preferred_element_type=F32)
            total += jnp.dot(swapped, out_rows[at + 1], preferred_element_type=F32)
            if sent is not None:
                total += ring(sent, step, count).astype(F32)
            sent = total.astype(BF16)
        return sent

    high_out = scattered(high, -1)
    low_out = scattered(low, 1)
    return jnp.concatenate([low_out, high_out], 0)


def solution(mesh):
    return jax.shard_map(
        shards,
        mesh=mesh,
        in_specs=(
            P("ctx", "head"),
            P("ctx"),
            P(None, "head"),
            P(None, "head"),
            P(None, "head"),
            P("head", None),
        ),
        out_specs=P("ctx", "head"),
        check_vma=False,
    )
```

time: 198 us -> 210 us (1.061)
  waiting for transfers between devices: 71.2 us -> 82.7 us
  local copies, waits for them, and re-layouts: 29.3 us -> 37.8 us
  Pallas kernels: 45.6 us -> 39 us
  starting transfers between devices: 30 us -> 27.9 us
    ppermute x3, waiting for transfers between devices: 0.01 us -> 9.68 us  [shards(): lax.ppermute(state, 'ctx', [(i, i + k) for i in range(blocks - k)])]
    pallas_call x4 -> x2, Pallas kernels: 28.3 us -> 19.8 us  [project(): pl.pallas_call(functools.partial(project_kernel, len(chips), cuts, before...]
    unnamed x60 -> x66, local copies, waits for them, and re-layouts: 18.3 us -> 26.4 us
    pallas_call x3 -> x2, Pallas kernels: 13.5 us -> 15.6 us  [the longest x1 11.6 us: mix(): pl.pallas_call(functools.partial(mix_kernel, len(chips), len(states)), gr...]
  transfers between devices with their start and end apart: 21 -> 20, of which waited for: 12 -> 14; matrix products, arithmetic and copies ran while one was open for 15% -> 15% of each run, Pallas kernels for 17% -> 9%
where the time goes in v7:
time: 210 us; the launch traced here: 209 us
  waiting for transfers between devices  82.7 us (39%)
  Pallas kernels  39 us (19%)
  local copies, waits for them, and re-layouts  37.8 us (18%)
  starting transfers between devices  27.9 us (13%)
  other arithmetic  14.1 us (7%)
  matrix products  7.07 us (3%)
    ppermute x9, waiting for transfers between devices, ring(): lax.ppermute(x, 'head', [(2 * z + c, 2 * ((z + step) % count) + c) for z...  66.8 us
    unnamed x66, local copies, waits for them, and re-layouts  26.4 us
    pallas_call x2, Pallas kernels, project(): pl.pallas_call(functools.partial(project_kernel, len(chips), cuts, before...  19.8 us
    ppermute x9, starting transfers between devices, ring(): lax.ppermute(x, 'head', [(2 * z + c, 2 * ((z + step) % count) + c) for z...  13.9 us
    pallas_call x1, Pallas kernels, mix(): pl.pallas_call(functools.partial(mix_kernel, len(chips), len(states)), gr...  11.6 us
    ppermute x3, waiting for transfers between devices, shards(): lax.ppermute(state, 'ctx', [(i, i + k) for i in range(blocks - k)])  9.68 us
    ppermute x3, starting transfers between devices, shards(): lax.ppermute(state, 'ctx', [(i, i + k) for i in range(blocks - k)])  8.96 us
    concatenate x1, other arithmetic, shards(): jnp.concatenate([w_value, w_feat, jnp.zeros((w_value.shape[0], fv_columns...  8.41 us
  transfers between devices with their start and end apart: 20, of which 14 were waited for; matrix products, arithmetic and copies ran while one was open for 15% of the time, Pallas kernels for 9%

profile of v7, /device:TPU:0, one launch (start us, length us, event | category | flops | bytes accessed | tf_op | source)
XLA Modules:
  0.0 209.1 jit_solution(10205541364276629026)
XLA Ops:
  0.5 4.6 %collective-permute-start = (bf16[1024,512]{1,0:T(8,128)(2,1)}, bf16[1024,512]{1,0:T(8,128)(2,1)}, u32[]{:S(2)}, u32[]{:S(2)}) collective-permute-start(bf16[1024,512]{1,0:T(8,128)(2,1)} %refs_0_.1), channel_id=1, source_target_pairs={{0,6},{1,7},{2,0},{3,1},{4,2},{5,3},{6,4},{7,5},{8,14},{9,15},{10,... | collective-permute-start | bytes 3145736 | tf_op jit(solution)/shard_map/ppermute | solution.py:32
  5.9 3.4 %collective-permute-start.2 = (bf16[64,128]{1,0:T(8,128)(2,1)S(1)}, bf16[64,128]{1,0:T(8,128)(2,1)S(1)}, u32[]{:S(2)}, u32[]{:S(2)}) collective-permute-start(bf16[64,128]{1,0:T(8,128)(2,1)S(1)} %broadcast_in_dim.7), channel_id=1, source_target_pairs={{0,8},{8,16},{16,24},{1,9},{9,17},{17,25},{2,10},{10,18},{18,26},{... | collective-permute-start | bytes 49160 | tf_op jit(solution)/shard_map/ppermute | solution.py:467
  9.4 3.9 %constant_dynamic-slice_fusion = (bf16[512,512]{1,0:T(8,128)(2,1)}, bf16[512,512]{1,0:T(8,128)(2,1)}, bf16[512,512]{1,0:T(8,128)(2,1)}, bf16[1,512,512]{2,1,0:T(...) fusion(bf16[512,4096]{1,0:T(8,128)(2,1)} %param.15, ...), kind=kLoop, calls=%fused_computation.35 | loop fusion | bytes 8388640 | tf_op jit(solution)/shard_map/dynamic_slice | solution.py:480
  17.1 8.4 %pad_maximum_fusion.refs_2_.refs_4_.refs_5_.refs_3_.refs_6_ = bf16[4096,1792]{1,0:T(8,128)(2,1)} fusion(bf16[4096,1024]{1,0:T(8,128)(2,1)S(1)} %copy-done.19, bf16[4096,128]{1,0:T(8,128)(2,1)} %param.12, bf16[4096,512]{1,0:T(8,128)(2,1)S(1)} %copy-done.28, bf16[1792]{0:T(1024)(128)(2,1)S(1)} %pad.8.clone), kind=kLoop, calls=%fused_computation | loop fusion | flops 58720256 | bytes 28315136 | tf_op jit(solution)/shard_map/concatenate | solution.py:491
  29.8 5.2 %copy-done = bf16[4096,1792]{1,0:T(8,128)(2,1)S(1)} copy-done((bf16[4096,1792]{1,0:T(8,128)(2,1)S(1)}, bf16[4096,1792]{1,0:T(8,128)(2,1)}, u32[]{:S(2)}) %copy-start) | copy-done | bytes 14680088
  35.0 6.8 %shard_map.100 = (f32[1024,768]{1,0:T(8,128)S(1)}, f32[1024,1024]{1,0:T(8,128)S(1)}) custom-call(s32[2]{0:T(128)S(1)} %pad_add_fusion.place, bf16[1024,512]{1,0:T(8,128)(2,1)S(1)} %copy-done.14, bf16[1024,512]{1,0:T(8,128)(2,1)S(1)} %collective-permute-done.3.refs_1_, bf16[4096,1792]{1,0:T(8,128)(2,1)S(1)} %copy-done), custom_call_target="tpu_custom_call" | custom-call | tf_op jit(solution)/shard_map/pallas_call | solution.py:108
  43.5 4.5 %dynamic-slice_bitcast_fusion = (bf16[512,512]{1,0:T(8,128)(2,1)}, bf16[512,512]{1,0:T(8,128)(2,1)}, bf16[512,512]{1,0:T(8,128)(2,1)}, bf16[512,512]{1,0:T(8,128)(2,1)}) fusion(bf16[4,512,512]{2,1,0:T(8,128)(2,1)} %collective-permute-done.4, s32[]{:T(128)S(6)} %select_n.61, s32[]{:T(128)S(6)} %select_n.59, s32[]{:T(128)S(6)} %select_n.57, s32[]{:T(128)S(6)} %select_n.55), kind=kLoop, calls=%fused_computation.26 | loop fusion | bytes 4194320 | tf_op jit(solution)/shard_map/jit(dynamic_index_in_dim)/squeeze | solution.py:486
  48.0 3.8 %collective-permute-done.1.refs_1_ = bf16[1024,512]{1,0:T(8,128)(2,1)} collective-permute-done((bf16[1024,512]{1,0:T(8,128)(2,1)}, bf16[1024,512]{1,0:T(8,128)(2,1)}, u32[]{:S(2)}, u32[]{:S(2)}) %collective-permute-start.1) | collective-permute-done | bytes 1048608 | tf_op jit(solution)/shard_map/ppermute | solution.py:32
  57.0 2.2 %copy-done.9 = f32[1024,1024]{1,0:T(8,128)S(1)} copy-done((f32[1024,1024]{1,0:T(8,128)S(1)}, f32[1024,1024]{1,0:T(8,128)}, u32[]{:S(2)}) %copy-start.9) | copy-done | bytes 4194328
  59.2 1.9 copy-done.11
  61.1 13.0 %shard_map.101 = (f32[1024,768]{1,0:T(8,128)S(1)}, f32[1024,1024]{1,0:T(8,128)S(1)}) custom-call(s32[2]{0:T(128)S(1)} %pad_add_fusion.place, bf16[1024,512]{1,0:T(8,128)(2,1)} %collective-permute-done.refs_0_, bf16[1024,512]{1,0:T(8,128)(2,1)} %collective-permute-done.1.refs_1_, bf16[1024,512]{1,0:T(8,128)(2,1)S(1)} %collective-permute-done.6.refs_2_, ...), custom_call_target="tpu_custom_call" | custom-call | tf_op jit(solution)/shard_map/pallas_call | solution.py:108
  74.1 4.4 %collective-permute-done.5.refs_0_ = bf16[1024,512]{1,0:T(8,128)(2,1)S(1)} collective-permute-done((bf16[1024,512]{1,0:T(8,128)(2,1)}, bf16[1024,512]{1,0:T(8,128)(2,1)S(1)}, u32[]{:S(2)}, u32[]{:S(2)}) %collective-permute-start.5) | collective-permute-done | bytes 1048608 | tf_op jit(solution)/shard_map/ppermute | solution.py:32
  78.5 2.7 %collective-permute-done.8.refs_1_ = bf16[1024,512]{1,0:T(8,128)(2,1)S(1)} collective-permute-done((bf16[1024,512]{1,0:T(8,128)(2,1)S(1)}, bf16[1024,512]{1,0:T(8,128)(2,1)S(1)}, u32[]{:S(2)}, u32[]{:S(2)}) %collective-permute-start.8) | collective-permute-done | bytes 1048608 | tf_op jit(solution)/shard_map/ppermute | solution.py:38
  81.2 4.0 %shard_map.102 = (bf16[1024,768]{1,0:T(8,128)(2,1)S(1)}, bf16[4,64,128]{2,1,0:T(8,128)(2,1)S(1)}) custom-call(s32[2]{0:T(128)S(1)} %pad_add_fusion.place, bf16[1024,512]{1,0:T(8,128)(2,1)S(1)} %collective-permute-done.5.refs_0_, bf16[1024,512]{1,0:T(8,128)(2,1)S(1)} %collective-permute-done.8.refs_1_, bf16[4096,1792]{1,0:T(8,128)(2,1)S(1)} %bitcast.53, ...), custom_call_target="tpu_custom_call" | custom-call | tf_op jit(solution)/shard_map/pallas_call | solution.py:176
  85.3 3.6 %shard_map.103 = (f32[4,4,160,128]{3,2,1,0:T(8,128)S(1)}, bf16[4,288,128]{2,1,0:T(8,128)(2,1)}) custom-call(s32[5]{0:T(128)S(1)} %pad_add_fusion.1.limits, bf16[1024,768]{1,0:T(8,128)(2,1)S(1)} %get-tuple-element.48.values.features, bf16[1024,768]{1,0:T(8,128)(2,1)S(1)} %get-tuple-element.48.values.features, bf16[4,128,512]{2,1,0:T(8,128)(2,1)S(1)} %copy-done.16, ...), custom_call_target="tpu_custom_call" | custom-call | tf_op jit(solution)/shard_map/pallas_call | solution.py:262
  91.2 3.4 %collective-permute-start.10 = (bf16[4,288,128]{2,1,0:T(8,128)(2,1)}, bf16[4,288,128]{2,1,0:T(8,128)(2,1)S(1)}, u32[]{:S(2)}, u32[]{:S(2)}) collective-permute-start(bf16[4,288,128]{2,1,0:T(8,128)(2,1)} %get-tuple-element.54), channel_id=1, source_target_pairs={{0,16},{8,24},{1,17},{9,25},{2,18},{10,26},{3,19},{11,27},{4,20},{... | collective-permute-start | bytes 884744 | tf_op jit(solution)/shard_map/ppermute | solution.py:519
  94.6 2.9 %collective-permute-start.11 = (bf16[4,288,128]{2,1,0:T(8,128)(2,1)}, bf16[4,288,128]{2,1,0:T(8,128)(2,1)}, u32[]{:S(2)}, u32[]{:S(2)}) collective-permute-start(bf16[4,288,128]{2,1,0:T(8,128)(2,1)} %get-tuple-element.54), channel_id=1, source_target_pairs={{0,24},{1,25},{2,26},{3,27},{4,28},{5,29},{6,30},{7,31}} | collective-permute-start | bytes 884744 | tf_op jit(solution)/shard_map/ppermute | solution.py:519
  97.5 2.6 %collective-permute-start.9 = (bf16[4,288,128]{2,1,0:T(8,128)(2,1)}, bf16[4,288,128]{2,1,0:T(8,128)(2,1)}, u32[]{:S(2)}, u32[]{:S(2)}) collective-permute-start(bf16[4,288,128]{2,1,0:T(8,128)(2,1)} %get-tuple-element.54), channel_id=1, source_target_pairs={{0,8},{8,16},{16,24},{1,9},{9,17},{17,25},{2,10},{10,18},{18,26},{... | collective-permute-start | bytes 884744 | tf_op jit(solution)/shard_map/ppermute | solution.py:519
  100.4 7.4 %collective-permute-done.10.refs_4_ = bf16[4,288,128]{2,1,0:T(8,128)(2,1)S(1)} collective-permute-done((bf16[4,288,128]{2,1,0:T(8,128)(2,1)}, bf16[4,288,128]{2,1,0:T(8,128)(2,1)S(1)}, u32[]{:S(2)}, u32[]{:S(2)}) %collective-permute-start.10) | collective-permute-done | bytes 294944 | tf_op jit(solution)/shard_map/ppermute | solution.py:519
  107.8 2.3 %collective-permute-done.9.refs_3_ = bf16[4,288,128]{2,1,0:T(8,128)(2,1)} collective-permute-done((bf16[4,288,128]{2,1,0:T(8,128)(2,1)}, bf16[4,288,128]{2,1,0:T(8,128)(2,1)}, u32[]{:S(2)}, u32[]{:S(2)}) %collective-permute-start.9) | collective-permute-done | bytes 294944 | tf_op jit(solution)/shard_map/ppermute | solution.py:519
  110.0 5.2 %copy-done.1 = bf16[4096,1792]{1,0:T(8,128)(2,1)S(1)} copy-done((bf16[4096,1792]{1,0:T(8,128)(2,1)S(1)}, bf16[4096,1792]{1,0:T(8,128)(2,1)}, u32[]{:S(2)}) %copy-start.1) | copy-done | bytes 14680088
  115.2 2.2 %copy-done.3 = f32[1024,1024]{1,0:T(8,128)S(1)} copy-done((f32[1024,1024]{1,0:T(8,128)S(1)}, f32[1024,1024]{1,0:T(8,128)}, u32[]{:S(2)}) %copy-start.3) | copy-done | bytes 4194328
  121.1 11.6 %shard_map.104 = (bf16[512,512]{1,0:T(8,128)(2,1)S(1)}, bf16[512,512]{1,0:T(8,128)(2,1)S(1)}) custom-call(s32[2]{0:T(128)S(1)} %pad_add_fusion.place, s32[5]{0:T(128)S(1)} %pad_add_fusion.1.limits, bf16[1024,768]{1,0:T(8,128)(2,1)S(1)} %copy-done.5, bf16[1024,768]{1,0:T(8,128)(2,1)S(1)} %copy-done.5, f32[1024,1024]{1,0:T(8,128)S(1)} %copy-done.3, ...), custom_call_target="tpu_custom_call" | custom-call | tf_op jit(solution)/shard_map/pallas_call | solution.py:422
  138.2 2.3 %collective-permute-start.17 = (bf16[512,512]{1,0:T(8,128)(2,1)S(1)}, bf16[512,512]{1,0:T(8,128)(2,1)S(1)}, u32[]{:S(2)}, u32[]{:S(2)}) collective-permute-start(bf16[512,512]{1,0:T(8,128)(2,1)S(1)} %fusion.13), channel_id=1, source_target_pairs={{0,6},{1,7},{2,0},{3,1},{4,2},{5,3},{6,4},{7,5},{8,14},{9,15},{10,... | collective-permute-start | bytes 1572872 | tf_op jit(solution)/shard_map/ppermute | solution.py:32
  142.2 10.0 %collective-permute-done.13 = bf16[512,512]{1,0:T(8,128)(2,1)S(1)} collective-permute-done((bf16[512,512]{1,0:T(8,128)(2,1)S(1)}, bf16[512,512]{1,0:T(8,128)(2,1)S(1)}, u32[]{:S(2)}, u32[]{:S(2)}) %collective-permute-start.13) | collective-permute-done | bytes 524320 | tf_op jit(solution)/shard_map/ppermute | solution.py:32
  152.8 10.6 %collective-permute-done.17 = bf16[512,512]{1,0:T(8,128)(2,1)S(1)} collective-permute-done((bf16[512,512]{1,0:T(8,128)(2,1)S(1)}, bf16[512,512]{1,0:T(8,128)(2,1)S(1)}, u32[]{:S(2)}, u32[]{:S(2)}) %collective-permute-start.17) | collective-permute-done | bytes 524320 | tf_op jit(solution)/shard_map/ppermute | solution.py:32
  163.8 1.8 collective-permute-start.18
  166.1 8.7 %collective-permute-done.14 = bf16[512,512]{1,0:T(8,128)(2,1)S(1)} collective-permute-done((bf16[512,512]{1,0:T(8,128)(2,1)S(1)}, bf16[512,512]{1,0:T(8,128)(2,1)S(1)}, u32[]{:S(2)}, u32[]{:S(2)}) %collective-permute-start.14) | collective-permute-done | bytes 524320 | tf_op jit(solution)/shard_map/ppermute | solution.py:32
  175.3 10.6 %collective-permute-done.18 = bf16[512,512]{1,0:T(8,128)(2,1)S(1)} collective-permute-done((bf16[512,512]{1,0:T(8,128)(2,1)S(1)}, bf16[512,512]{1,0:T(8,128)(2,1)S(1)}, u32[]{:S(2)}, u32[]{:S(2)}) %collective-permute-start.18) | collective-permute-done | bytes 524320 | tf_op jit(solution)/shard_map/ppermute | solution.py:32
  186.3 1.8 collective-permute-start.19
  188.5 8.7 %collective-permute-done.15 = bf16[512,512]{1,0:T(8,128)(2,1)S(1)} collective-permute-done((bf16[512,512]{1,0:T(8,128)(2,1)S(1)}, bf16[512,512]{1,0:T(8,128)(2,1)S(1)}, u32[]{:S(2)}, u32[]{:S(2)}) %collective-permute-start.15) | collective-permute-done | bytes 524320 | tf_op jit(solution)/shard_map/ppermute | solution.py:32
  197.7 9.9 %collective-permute-done.19 = bf16[512,512]{1,0:T(8,128)(2,1)S(1)} collective-permute-done((bf16[512,512]{1,0:T(8,128)(2,1)S(1)}, bf16[512,512]{1,0:T(8,128)(2,1)S(1)}, u32[]{:S(2)}, u32[]{:S(2)}) %collective-permute-start.19) | collective-permute-done | bytes 524320 | tf_op jit(solution)/shard_map/ppermute | solution.py:32
  (118 shorter events, 34.3 us)
Async XLA Ops:
  0.0 9.4 %collective-permute-start.3 = (bf16[1024,512]{1,0:T(8,128)(2,1)}, bf16[1024,512]{1,0:T(8,128)(2,1)S(1)}, u32[]{:S(2)}, u32[]{:S(2)}) collective-permute-start(bf16[1024,512]{1,0:T(8,128)(2,1)} %refs_0_.1), channel_id=1, source_target_pairs={{0,1},{1,0},{2,3},{3,2},{4,5},{5,4},{6,7},{7,6},{8,9},{9,8},{10,11... | collective-permute-start | bytes 3145736 | tf_op jit(solution)/shard_map/ppermute | solution.py:38
  0.5 47.6 %collective-permute-start = (bf16[1024,512]{1,0:T(8,128)(2,1)}, bf16[1024,512]{1,0:T(8,128)(2,1)}, u32[]{:S(2)}, u32[]{:S(2)}) collective-permute-start(bf16[1024,512]{1,0:T(8,128)(2,1)} %refs_0_.1), channel_id=1, source_target_pairs={{0,6},{1,7},{2,0},{3,1},{4,2},{5,3},{6,4},{7,5},{8,14},{9,15},{10,... | collective-permute-start | bytes 3145736 | tf_op jit(solution)/shard_map/ppermute | solution.py:32
  5.1 46.8 %collective-permute-start.1 = (bf16[1024,512]{1,0:T(8,128)(2,1)}, bf16[1024,512]{1,0:T(8,128)(2,1)}, u32[]{:S(2)}, u32[]{:S(2)}) collective-permute-start(bf16[1024,512]{1,0:T(8,128)(2,1)} %refs_0_.1), channel_id=1, source_target_pairs={{0,2},{1,3},{2,4},{3,5},{4,6},{5,7},{6,0},{7,1},{8,10},{9,11},{10,... | collective-permute-start | bytes 3145736 | tf_op jit(solution)/shard_map/ppermute | solution.py:32
  5.9 42.1 %collective-permute-start.2 = (bf16[64,128]{1,0:T(8,128)(2,1)S(1)}, bf16[64,128]{1,0:T(8,128)(2,1)S(1)}, u32[]{:S(2)}, u32[]{:S(2)}) collective-permute-start(bf16[64,128]{1,0:T(8,128)(2,1)S(1)} %broadcast_in_dim.7), channel_id=1, source_target_pairs={{0,8},{8,16},{16,24},{1,9},{9,17},{17,25},{2,10},{10,18},{18,26},{... | collective-permute-start | bytes 49160 | tf_op jit(solution)/shard_map/ppermute | solution.py:467
  15.0 14.8 %copy-start.14 = (bf16[1024,512]{1,0:T(8,128)(2,1)S(1)}, bf16[1024,512]{1,0:T(8,128)(2,1)}, u32[]{:S(2)}) copy-start(bf16[1024,512]{1,0:T(8,128)(2,1)} %refs_0_.1) | copy-start | bytes 3145732
  15.0 28.5 %collective-permute-start.4 = (bf16[4,512,512]{2,1,0:T(8,128)(2,1)}, bf16[4,512,512]{2,1,0:T(8,128)(2,1)}, u32[]{:S(2)}, u32[]{:S(2)}) collective-permute-start(bf16[4,512,512]{2,1,0:T(8,128)(2,1)} %pad_maximum_fusion.1), channel_id=1, source_target_pairs={{0,1},{1,0},{2,3},{3,2},{4,5},{5,4},{6,7},{7,6},{8,9},{9,8},{10,11... | collective-permute-start | bytes 6291464 | tf_op jit(solution)/shard_map/ppermute | solution.py:38
  43.5 37.6 %slice-start = ((s8[14680064]{0:T(1024)(128)(4,1)}), s8[4194304]{0:T(1024)(128)(4,1)S(1)}, s32[]{:S(2)}) async-start(s8[14680064]{0:T(1024)(128)(4,1)} %bitcast.52), calls=%async_computation | async-start | bytes 8388608
  52.5 28.6 %slice-start.1 = ((s8[14680064]{0:T(1024)(128)(4,1)}), s8[4194304]{0:T(1024)(128)(4,1)S(1)}, s32[]{:S(2)}) async-start(s8[14680064]{0:T(1024)(128)(4,1)} %bitcast.52), calls=%async_computation.1 | async-start | bytes 8388608
  52.5 28.6 %slice-start.2 = ((s8[14680064]{0:T(1024)(128)(4,1)}), s8[4194304]{0:T(1024)(128)(4,1)S(1)}, s32[]{:S(2)}) async-start(s8[14680064]{0:T(1024)(128)(4,1)} %bitcast.52), calls=%async_computation.2 | async-start | bytes 8388608
  52.6 28.6 %slice-start.3 = ((s8[14680064]{0:T(1024)(128)(4,1)}), s8[2097152]{0:T(1024)(128)(4,1)S(1)}, s32[]{:S(2)}) async-start(s8[14680064]{0:T(1024)(128)(4,1)} %bitcast.52), calls=%async_computation.3 | async-start | bytes 4194304
  52.6 2.9 %collective-permute-start.6 = (bf16[1024,512]{1,0:T(8,128)(2,1)}, bf16[1024,512]{1,0:T(8,128)(2,1)S(1)}, u32[]{:S(2)}, u32[]{:S(2)}) collective-permute-start(bf16[1024,512]{1,0:T(8,128)(2,1)} %collective-permute-done.refs_0_), channel_id=1, source_target_pairs={{0,1},{1,0},{2,3},{3,2},{4,5},{5,4},{6,7},{7,6},{8,9},{9,8},{10,11... | collective-permute-start | bytes 3145736 | tf_op jit(solution)/shard_map/ppermute | solution.py:38
  52.6 4.4 %collective-permute-start.7 = (bf16[1024,512]{1,0:T(8,128)(2,1)}, bf16[1024,512]{1,0:T(8,128)(2,1)S(1)}, u32[]{:S(2)}, u32[]{:S(2)}) collective-permute-start(bf16[1024,512]{1,0:T(8,128)(2,1)} %collective-permute-done.1.refs_1_), channel_id=1, source_target_pairs={{0,1},{1,0},{2,3},{3,2},{4,5},{5,4},{6,7},{7,6},{8,9},{9,8},{10,11... | collective-permute-start | bytes 3145736 | tf_op jit(solution)/shard_map/ppermute | solution.py:38
  53.1 25.4 %collective-permute-start.5 = (bf16[1024,512]{1,0:T(8,128)(2,1)}, bf16[1024,512]{1,0:T(8,128)(2,1)S(1)}, u32[]{:S(2)}, u32[]{:S(2)}) collective-permute-start(bf16[1024,512]{1,0:T(8,128)(2,1)} %collective-permute-done.refs_0_), channel_id=1, source_target_pairs={{0,6},{1,7},{2,0},{3,1},{4,2},{5,3},{6,4},{7,5},{8,14},{9,15},{10,... | collective-permute-start | bytes 3145736 | tf_op jit(solution)/shard_map/ppermute | solution.py:32
  78.5 2.7 %collective-permute-start.8 = (bf16[1024,512]{1,0:T(8,128)(2,1)S(1)}, bf16[1024,512]{1,0:T(8,128)(2,1)S(1)}, u32[]{:S(2)}, u32[]{:S(2)}) collective-permute-start(bf16[1024,512]{1,0:T(8,128)(2,1)S(1)} %collective-permute-done.5.refs_0_), channel_id=1, source_target_pairs={{0,1},{1,0},{2,3},{3,2},{4,5},{5,4},{6,7},{7,6},{8,9},{9,8},{10,11... | collective-permute-start | bytes 3145736 | tf_op jit(solution)/shard_map/ppermute | solution.py:38
  85.3 24.8 %copy-start.15 = (bf16[4,128,512]{2,1,0:T(8,128)(2,1)S(1)}, bf16[4,128,512]{2,1,0:T(8,128)(2,1)}, u32[]{:S(2)}) copy-start(bf16[4,128,512]{2,1,0:T(8,128)(2,1)} %constant.76.clone.expand) | copy-start | bytes 1572868
  85.3 24.8 %copy-start.7 = (bf16[1024,512]{1,0:T(8,128)(2,1)S(1)}, bf16[1024,512]{1,0:T(8,128)(2,1)}, u32[]{:S(2)}) copy-start(bf16[1024,512]{1,0:T(8,128)(2,1)} %copy-done.6) | copy-start | bytes 3145732
  91.2 16.6 %collective-permute-start.10 = (bf16[4,288,128]{2,1,0:T(8,128)(2,1)}, bf16[4,288,128]{2,1,0:T(8,128)(2,1)S(1)}, u32[]{:S(2)}, u32[]{:S(2)}) collective-permute-start(bf16[4,288,128]{2,1,0:T(8,128)(2,1)} %get-tuple-element.54), channel_id=1, source_target_pairs={{0,16},{8,24},{1,17},{9,25},{2,18},{10,26},{3,19},{11,27},{4,20},{... | collective-permute-start | bytes 884744 | tf_op jit(solution)/shard_map/ppermute | solution.py:519
  94.6 13.2 %collective-permute-start.11 = (bf16[4,288,128]{2,1,0:T(8,128)(2,1)}, bf16[4,288,128]{2,1,0:T(8,128)(2,1)}, u32[]{:S(2)}, u32[]{:S(2)}) collective-permute-start(bf16[4,288,128]{2,1,0:T(8,128)(2,1)} %get-tuple-element.54), channel_id=1, source_target_pairs={{0,24},{1,25},{2,26},{3,27},{4,28},{5,29},{6,30},{7,31}} | collective-permute-start | bytes 884744 | tf_op jit(solution)/shard_map/ppermute | solution.py:519
  97.5 12.5 %collective-permute-start.9 = (bf16[4,288,128]{2,1,0:T(8,128)(2,1)}, bf16[4,288,128]{2,1,0:T(8,128)(2,1)}, u32[]{:S(2)}, u32[]{:S(2)}) collective-permute-start(bf16[4,288,128]{2,1,0:T(8,128)(2,1)} %get-tuple-element.54), channel_id=1, source_target_pairs={{0,8},{8,16},{16,24},{1,9},{9,17},{17,25},{2,10},{10,18},{18,26},{... | collective-permute-start | bytes 884744 | tf_op jit(solution)/shard_map/ppermute | solution.py:519
  121.1 13.6 %copy-start.21 = (bf16[512,512]{1,0:T(8,128)(2,1)S(1)}, bf16[512,512]{1,0:T(8,128)(2,1)}, u32[]{:S(2)}) copy-start(bf16[512,512]{1,0:T(8,128)(2,1)} %get-tuple-element.63) | copy-start | bytes 1572868
  121.1 14.0 %copy-start.24 = (bf16[512,512]{1,0:T(8,128)(2,1)S(1)}, bf16[512,512]{1,0:T(8,128)(2,1)}, u32[]{:S(2)}) copy-start(bf16[512,512]{1,0:T(8,128)(2,1)} %get-tuple-element.62) | copy-start | bytes 1572868
  132.7 2.0 collective-permute-start.12
  132.8 4.5 %collective-permute-start.16 = (bf16[512,512]{1,0:T(8,128)(2,1)S(1)}, bf16[512,512]{1,0:T(8,128)(2,1)S(1)}, u32[]{:S(2)}, u32[]{:S(2)}) collective-permute-start(bf16[512,512]{1,0:T(8,128)(2,1)S(1)} %get-tuple-element.64), channel_id=1, source_target_pairs={{0,1},{1,0},{2,3},{3,2},{4,5},{5,4},{6,7},{7,6},{8,9},{9,8},{10,11... | collective-permute-start | bytes 1572872 | tf_op jit(solution)/shard_map/ppermute | solution.py:38
  135.6 16.7 %collective-permute-start.13 = (bf16[512,512]{1,0:T(8,128)(2,1)S(1)}, bf16[512,512]{1,0:T(8,128)(2,1)S(1)}, u32[]{:S(2)}, u32[]{:S(2)}) collective-permute-start(bf16[512,512]{1,0:T(8,128)(2,1)S(1)} %fusion.12), channel_id=1, source_target_pairs={{0,2},{1,3},{2,4},{3,5},{4,6},{5,7},{6,0},{7,1},{8,10},{9,11},{10,... | collective-permute-start | bytes 1572872 | tf_op jit(solution)/shard_map/ppermute | solution.py:32
  138.2 14.1 %copy-start.27 = (bf16[512,512]{1,0:T(8,128)(2,1)S(1)}, bf16[512,512]{1,0:T(8,128)(2,1)}, u32[]{:S(2)}) copy-start(bf16[512,512]{1,0:T(8,128)(2,1)} %get-tuple-element.60) | copy-start | bytes 1572868
  138.2 25.2 %collective-permute-start.17 = (bf16[512,512]{1,0:T(8,128)(2,1)S(1)}, bf16[512,512]{1,0:T(8,128)(2,1)S(1)}, u32[]{:S(2)}, u32[]{:S(2)}) collective-permute-start(bf16[512,512]{1,0:T(8,128)(2,1)S(1)} %fusion.13), channel_id=1, source_target_pairs={{0,6},{1,7},{2,0},{3,1},{4,2},{5,3},{6,4},{7,5},{8,14},{9,15},{10,... | collective-permute-start | bytes 1572872 | tf_op jit(solution)/shard_map/ppermute | solution.py:32
  141.8 23.9 %copy-start.20 = (bf16[512,512]{1,0:T(8,128)(2,1)S(1)}, bf16[512,512]{1,0:T(8,128)(2,1)}, u32[]{:S(2)}) copy-start(bf16[512,512]{1,0:T(8,128)(2,1)} %get-tuple-element.57) | copy-start | bytes 1572868
  152.7 22.0 %collective-permute-start.14 = (bf16[512,512]{1,0:T(8,128)(2,1)S(1)}, bf16[512,512]{1,0:T(8,128)(2,1)S(1)}, u32[]{:S(2)}, u32[]{:S(2)}) collective-permute-start(bf16[512,512]{1,0:T(8,128)(2,1)S(1)} %fusion.8), channel_id=1, source_target_pairs={{0,2},{1,3},{2,4},{3,5},{4,6},{5,7},{6,0},{7,1},{8,10},{9,11},{10,... | collective-permute-start | bytes 1572872 | tf_op jit(solution)/shard_map/ppermute | solution.py:32
  163.8 22.1 %collective-permute-start.18 = (bf16[512,512]{1,0:T(8,128)(2,1)S(1)}, bf16[512,512]{1,0:T(8,128)(2,1)S(1)}, u32[]{:S(2)}, u32[]{:S(2)}) collective-permute-start(bf16[512,512]{1,0:T(8,128)(2,1)S(1)} %fusion.11), channel_id=1, source_target_pairs={{0,6},{1,7},{2,0},{3,1},{4,2},{5,3},{6,4},{7,5},{8,14},{9,15},{10,... | collective-permute-start | bytes 1572872 | tf_op jit(solution)/shard_map/ppermute | solution.py:32
  166.0 31.2 %copy-start.26 = (bf16[512,512]{1,0:T(8,128)(2,1)S(1)}, bf16[512,512]{1,0:T(8,128)(2,1)}, u32[]{:S(2)}) copy-start(bf16[512,512]{1,0:T(8,128)(2,1)} %get-tuple-element.56) | copy-start | bytes 1572868
  175.2 22.1 %collective-permute-start.15 = (bf16[512,512]{1,0:T(8,128)(2,1)S(1)}, bf16[512,512]{1,0:T(8,128)(2,1)S(1)}, u32[]{:S(2)}, u32[]{:S(2)}) collective-permute-start(bf16[512,512]{1,0:T(8,128)(2,1)S(1)} %fusion.7), channel_id=1, source_target_pairs={{0,2},{1,3},{2,4},{3,5},{4,6},{5,7},{6,0},{7,1},{8,10},{9,11},{10,... | collective-permute-start | bytes 1572872 | tf_op jit(solution)/shard_map/ppermute | solution.py:32
  186.3 21.3 %collective-permute-start.19 = (bf16[512,512]{1,0:T(8,128)(2,1)S(1)}, bf16[512,512]{1,0:T(8,128)(2,1)S(1)}, u32[]{:S(2)}, u32[]{:S(2)}) collective-permute-start(bf16[512,512]{1,0:T(8,128)(2,1)S(1)} %fusion.10), channel_id=1, source_target_pairs={{0,6},{1,7},{2,0},{3,1},{4,2},{5,3},{6,4},{7,5},{8,14},{9,15},{10,... | collective-permute-start | bytes 1572872 | tf_op jit(solution)/shard_map/ppermute | solution.py:32
  (21 other events, 90.2 us)

commit v8 on v7

--- a/solution.py
+++ b/solution.py
@@ -24,8 +24,8 @@
 BF16 = jnp.bfloat16
 
 
-def params():
-    return pltpu.CompilerParams(vmem_limit_bytes=VMEM, dimension_semantics=("arbitrary",))
+def params(limit=VMEM):
+    return pltpu.CompilerParams(vmem_limit_bytes=limit, dimension_semantics=("arbitrary",))
 
 
 def ring(x, step, count):
@@ -80,7 +80,7 @@
             tile(1)
 
 
-def project(place, chips, mine, theirs, weight, first, columns, before=None, dtype=F32):
+def project(place, chips, mine, theirs, weight, first, columns, before=None, dtype=F32, limit=VMEM):
     rows, width = mine[0].shape
     count = weight.shape[0] // (2 * width)
     size = 256
@@ -115,7 +115,7 @@
             scratch_shapes=[pltpu.VMEM((rows, 2 * width * len(chips)), BF16)],
         ),
         out_shape=shapes,
-        compiler_params=params(),
+        compiler_params=params(limit),
     )(place, *args)
 
 
@@ -228,7 +228,7 @@
     return (left * right * rows[2:3]).astype(BF16)
 
 
-def sums_kernel(limits, values, features, expand, rows, keys, prefix, end):
+def sums_kernel(limits, values, features, expand, rows, keys, prefix, end, both):
     chunks, heads = prefix.shape[:2]
     mark = lax.broadcasted_iota(jnp.int32, (STATE, HEAD_DIM), 0) == STATE - 1
     at = lax.broadcasted_iota(jnp.int32, (CHUNK, HEAD_DIM), 0)
@@ -249,9 +249,11 @@
         for n in range(chunks):
             prefix[n, h] = state
             state = parts[n] + jnp.where(limits[n] <= n * CHUNK, state, 0.0)
-        end[h, :STATE] = jnp.where(mark, (limits[chunks] + 1).astype(F32), state).astype(BF16)
-        end[h, STATE : STATE + WIN] = values[values.shape[0] - WIN :, column]
-        end[h, STATE + WIN :] = keys[h]
+        sent = jnp.where(mark, (limits[chunks] + 1).astype(F32), state).astype(BF16)
+        end[h] = sent
+        both[h, :STATE] = sent
+        both[h, STATE : STATE + WIN] = values[values.shape[0] - WIN :, column]
+        both[h, STATE + WIN :] = keys[h]
 
 
 def sums(limits, both, keys, expand, rows):
@@ -273,11 +275,13 @@
             ],
             out_specs=[
                 pl.BlockSpec((chunks, group, STATE, HEAD_DIM), lambda g, _: (0, g, 0, 0)),
+                pl.BlockSpec((group, STATE, HEAD_DIM), lambda g, _: (g, 0, 0)),
                 pl.BlockSpec((group, SENT, HEAD_DIM), lambda g, _: (g, 0, 0)),
             ],
         ),
         out_shape=[
             jax.ShapeDtypeStruct((chunks, heads, STATE, HEAD_DIM), F32),
+            jax.ShapeDtypeStruct((heads, STATE, HEAD_DIM), BF16),
             jax.ShapeDtypeStruct((heads, SENT, HEAD_DIM), BF16),
         ],
         compiler_params=params(),
@@ -308,26 +312,11 @@
 
 
 def mix_kernel(
-    chips, shifts, place, limits, values, features, window_before, bounds, pick, expand, rows, prefix,
-    tail_docs, first_doc, *refs
+    shifts, limits, values, features, window, bounds, pick, expand, rows, prefix, tail_docs, first_doc, *refs
 ):
-    mine, theirs, weights = refs[:chips], refs[chips : 2 * chips], refs[2 * chips : 3 * chips]
-    states = refs[3 * chips : 3 * chips + shifts]
-    *outs, both, window = refs[3 * chips + shifts :]
-    width = 2 * mine[0].shape[1]
+    states, outs = refs[:shifts], refs[shifts:]
     count = values.shape[0]
     half = count // 2
-
-    @pl.when(pl.program_id(0) == 0)
-    def _():
-        by_column(place[1], mine, theirs, both)
-
-    total = window_before[...]
-    for n in range(chips):
-        total += jnp.dot(
-            both[:, n * width : (n + 1) * width], weights[n][...], preferred_element_type=F32
-        )
-    window[...] = total.astype(BF16)
 
     pair = jnp.dot(features[...], pick[0], preferred_element_type=F32).astype(BF16)
     phi_query = phi(features[...], expand[0], rows[...])
@@ -388,53 +377,36 @@
     outs[1][...] = mixed[half:]
 
 
-def mix(place, limits, chips, mine, theirs, weight, both, window_before, bounds, pick, expand, rows, prefix,
-        tail_docs, first_doc, states):
-    count, width = mine[0].shape
+def mix(limits, both, window, bounds, pick, expand, rows, prefix, tail_docs, first_doc, states):
+    count = both.shape[0]
     heads = states[0].shape[0]
     half = count // 2
-    ring_size = weight.shape[0] // (2 * width)
-    tile = 2 * HEAD_DIM
-    first = both.shape[1] // tile
 
     def full(a):
-        return pl.BlockSpec(a.shape, lambda h, *_: (0,) * a.ndim)
+        return pl.BlockSpec(a.shape, lambda h, _: (0,) * a.ndim)
 
     def per_head(a):
-        return pl.BlockSpec((1,) + a.shape[1:], lambda h, *_: (h, 0, 0))
-
-    specs = [
-        pl.BlockSpec((count, HEAD_DIM), lambda h, *_: (0, h)),
-        pl.BlockSpec((count, LANES), lambda h, *_: (0, heads)),
-        pl.BlockSpec((count, tile), lambda h, *_: (0, h)),
-        full(bounds), per_head(pick), per_head(expand), full(rows),
-        pl.BlockSpec((prefix.shape[0], 1, STATE, HEAD_DIM), lambda h, *_: (0, h, 0, 0)),
-        full(tail_docs), full(first_doc),
-    ]
-    specs += [full(mine[0])] * (2 * len(chips))
-    for n in chips:
-        specs.append(
-            pl.BlockSpec(
-                (2 * width, tile), lambda h, p, _, n=n: (lax.rem(p[0] + n, ring_size), first + h)
-            )
-        )
-    specs += [per_head(a) for a in states]
+        return pl.BlockSpec((1,) + a.shape[1:], lambda h, _: (h, 0, 0))
+
     return pl.pallas_call(
-        functools.partial(mix_kernel, len(chips), len(states)),
+        functools.partial(mix_kernel, len(states)),
         grid_spec=pltpu.PrefetchScalarGridSpec(
-            num_scalar_prefetch=2,
+            num_scalar_prefetch=1,
             grid=(heads,),
-            in_specs=specs,
-            out_specs=[pl.BlockSpec((half, HEAD_DIM), lambda h, *_: (0, h))] * 2,
-            scratch_shapes=[
-                pltpu.VMEM((count, 2 * width * len(chips)), BF16),
-                pltpu.VMEM((count, tile), BF16),
-            ],
+            in_specs=[
+                pl.BlockSpec((count, HEAD_DIM), lambda h, _: (0, h)),
+                pl.BlockSpec((count, LANES), lambda h, _: (0, heads)),
+                pl.BlockSpec((count, 2 * HEAD_DIM), lambda h, _: (0, h)),
+                full(bounds), per_head(pick), per_head(expand), full(rows),
+                pl.BlockSpec((prefix.shape[0], 1, STATE, HEAD_DIM), lambda h, _: (0, h, 0, 0)),
+                full(tail_docs), full(first_doc),
+            ]
+            + [per_head(a) for a in states],
+            out_specs=[pl.BlockSpec((half, HEAD_DIM), lambda h, _: (0, h))] * 2,
         ),
         out_shape=[jax.ShapeDtypeStruct((half, heads * HEAD_DIM), BF16)] * 2,
-        compiler_params=params(),
-    )(place, limits, both, both, window_before, bounds, pick, expand, rows, prefix, tail_docs, first_doc,
-      *mine, *theirs, *[weight] * len(chips), *states)
+        compiler_params=params(40 * 1024 * 1024),
+    )(limits, both, both, window, bounds, pick, expand, rows, prefix, tail_docs, first_doc, *states)
 
 
 def after(x, *others):
@@ -514,14 +486,19 @@
     *mine, fv_part, win_part = lax.optimization_barrier((*[pieces[n] for n in late], *part))
     theirs = [swap(p, count) for p in mine]
     both, keys = project_late(place, late, mine, theirs, weight, heads, fv_part, win_part)
-    prefix, state = sums(limits, both, keys, key_map, scale_rows)
+    prefix, state, state_and_tail = sums(limits, both, keys, key_map, scale_rows)
     states = [
-        lax.ppermute(state, "ctx", [(i, i + k) for i in range(blocks - k)])
+        lax.ppermute(
+            state_and_tail if k == 1 else state, "ctx", [(i, i + k) for i in range(blocks - k)]
+        )
         for k in range(1, blocks)
     ]
+    (window,) = project(
+        place, late, [after(mine[0], state), *mine[1:]], theirs, weight, fv_columns, widths[1:],
+        [win_part], BF16, 40 * 1024 * 1024,
+    )
     low, high = mix(
-        place, limits, late, mine, theirs, weight, both, win_part, bounds, pick, query_map, scale_rows,
-        prefix, tail_docs, first_doc, states,
+        limits, both, window, bounds, pick, query_map, scale_rows, prefix, tail_docs, first_doc, states
     )
 
     def scattered(mixed, step):

time: 210 us -> 193 us (0.919)
  waiting for transfers between devices: 82.7 us -> 73.2 us
  local copies, waits for them, and re-layouts: 37.8 us -> 28.8 us
  Pallas kernels: 39 us -> 41.7 us
    ppermute x3, waiting for transfers between devices: 9.68 us -> 0.01 us  [shards(): lax.ppermute(state_and_tail if k == 1 else state, 'ctx', [(i, i + k) for...]
    unnamed x66 -> x64, local copies, waits for them, and re-layouts: 26.4 us -> 17.6 us
    pallas_call x2 -> x3, Pallas kernels: 19.8 us -> 25.4 us  [project(): pl.pallas_call(functools.partial(project_kernel, len(chips), cuts, before...]
    pallas_call x1, Pallas kernels: 11.6 us -> 8.63 us  [mix(): pl.pallas_call(functools.partial(mix_kernel, len(states)), grid_spec=pltp...]
  transfers between devices with their start and end apart: 20 -> 20, of which waited for: 14 -> 12; matrix products, arithmetic and copies ran while one was open for 15% -> 16% of each run, Pallas kernels for 9% -> 13%
where the time goes in v8:
time: 193 us
  waiting for transfers between devices  73.2 us (38%)
  Pallas kernels  41.7 us (22%)
  local copies, waits for them, and re-layouts  28.8 us (15%)
  starting transfers between devices  27.2 us (14%)
  other arithmetic  14.1 us (7%)
  matrix products  6.96 us (4%)
    ppermute x9, waiting for transfers between devices, ring(): lax.ppermute(x, 'head', [(2 * z + c, 2 * ((z + step) % count) + c) for z...  67 us
    pallas_call x3, Pallas kernels, project(): pl.pallas_call(functools.partial(project_kernel, len(chips), cuts, before...  25.4 us
    unnamed x64, local copies, waits for them, and re-layouts  17.6 us
    ppermute x9, starting transfers between devices, ring(): lax.ppermute(x, 'head', [(2 * z + c, 2 * ((z + step) % count) + c) for z...  13.9 us
    pallas_call x1, Pallas kernels, mix(): pl.pallas_call(functools.partial(mix_kernel, len(states)), grid_spec=pltp...  8.63 us
    concatenate x1, other arithmetic, shards(): jnp.concatenate([w_value, w_feat, jnp.zeros((w_value.shape[0], fv_columns...  8.41 us
    ppermute x3, starting transfers between devices, shards(): lax.ppermute(state_and_tail if k == 1 else state, 'ctx', [(i, i + k) for...  8.3 us
    ppermute x7, waiting for transfers between devices, swap(): return lax.ppermute(x, 'head', [(h, h ^ 1) for h in range(2 * count)])  6.17 us
  transfers between devices with their start and end apart: 20, of which 12 were waited for; matrix products, arithmetic and copies ran while one was open for 16% of the time, Pallas kernels for 13%

profile of v8, /device:TPU:0, one launch (start us, length us, event | category | flops | bytes accessed | tf_op | source)
XLA Modules:
  0.0 192.6 jit_solution(12123317815826510579)
XLA Ops:
  0.5 4.6 %collective-permute-start = (bf16[1024,512]{1,0:T(8,128)(2,1)}, bf16[1024,512]{1,0:T(8,128)(2,1)}, u32[]{:S(2)}, u32[]{:S(2)}) collective-permute-start(bf16[1024,512]{1,0:T(8,128)(2,1)} %refs_0_.1), channel_id=1, source_target_pairs={{0,6},{1,7},{2,0},{3,1},{4,2},{5,3},{6,4},{7,5},{8,14},{9,15},{10,... | collective-permute-start | bytes 3145736 | tf_op jit(solution)/shard_map/ppermute | solution.py:32
  5.9 3.4 %collective-permute-start.2 = (bf16[64,128]{1,0:T(8,128)(2,1)S(1)}, bf16[64,128]{1,0:T(8,128)(2,1)S(1)}, u32[]{:S(2)}, u32[]{:S(2)}) collective-permute-start(bf16[64,128]{1,0:T(8,128)(2,1)S(1)} %broadcast_in_dim.7), channel_id=1, source_target_pairs={{0,8},{8,16},{16,24},{1,9},{9,17},{17,25},{2,10},{10,18},{18,26},{... | collective-permute-start | bytes 49160 | tf_op jit(solution)/shard_map/ppermute | solution.py:439
  9.4 3.9 %constant_dynamic-slice_fusion = (bf16[512,512]{1,0:T(8,128)(2,1)}, bf16[512,512]{1,0:T(8,128)(2,1)}, bf16[512,512]{1,0:T(8,128)(2,1)}, bf16[1,512,512]{2,1,0:T(...) fusion(bf16[512,4096]{1,0:T(8,128)(2,1)} %param.15, ...), kind=kLoop, calls=%fused_computation.35 | loop fusion | bytes 8388640 | tf_op jit(solution)/shard_map/dynamic_slice | solution.py:452
  17.1 8.4 %pad_maximum_fusion.refs_2_.refs_4_.refs_5_.refs_3_.refs_6_ = bf16[4096,1792]{1,0:T(8,128)(2,1)} fusion(bf16[4096,1024]{1,0:T(8,128)(2,1)S(1)} %copy-done.18, bf16[4096,128]{1,0:T(8,128)(2,1)} %param.12, bf16[4096,512]{1,0:T(8,128)(2,1)S(1)} %copy-done.27, bf16[1792]{0:T(1024)(128)(2,1)S(1)} %pad.8.clone), kind=kLoop, calls=%fused_computation | loop fusion | flops 58720256 | bytes 28315136 | tf_op jit(solution)/shard_map/concatenate | solution.py:463
  29.7 5.2 %copy-done = bf16[4096,1792]{1,0:T(8,128)(2,1)S(1)} copy-done((bf16[4096,1792]{1,0:T(8,128)(2,1)S(1)}, bf16[4096,1792]{1,0:T(8,128)(2,1)}, u32[]{:S(2)}) %copy-start) | copy-done | bytes 14680088
  34.9 6.8 %shard_map.100 = (f32[1024,768]{1,0:T(8,128)S(1)}, f32[1024,1024]{1,0:T(8,128)S(1)}) custom-call(s32[2]{0:T(128)S(1)} %pad_add_fusion.1.place, bf16[1024,512]{1,0:T(8,128)(2,1)S(1)} %copy-done.13, bf16[1024,512]{1,0:T(8,128)(2,1)S(1)} %collective-permute-done.3.refs_1_, bf16[4096,1792]{1,0:T(8,128)(2,1)S(1)} %copy-done), custom_call_target="tpu_custom_call" | custom-call | tf_op jit(solution)/shard_map/pallas_call | solution.py:108
  41.7 1.7 copy-done.9
  43.4 4.5 %dynamic-slice_bitcast_fusion = (bf16[512,512]{1,0:T(8,128)(2,1)}, bf16[512,512]{1,0:T(8,128)(2,1)}, bf16[512,512]{1,0:T(8,128)(2,1)}, bf16[512,512]{1,0:T(8,128)(2,1)}) fusion(bf16[4,512,512]{2,1,0:T(8,128)(2,1)} %collective-permute-done.4, s32[]{:T(128)S(6)} %select_n.61, s32[]{:T(128)S(6)} %select_n.59, s32[]{:T(128)S(6)} %select_n.57, s32[]{:T(128)S(6)} %select_n.55), kind=kLoop, calls=%fused_computation.26 | loop fusion | bytes 4194320 | tf_op jit(solution)/shard_map/jit(dynamic_index_in_dim)/squeeze | solution.py:458
  47.9 3.9 %collective-permute-done.1.refs_1_ = bf16[1024,512]{1,0:T(8,128)(2,1)} collective-permute-done((bf16[1024,512]{1,0:T(8,128)(2,1)}, bf16[1024,512]{1,0:T(8,128)(2,1)}, u32[]{:S(2)}, u32[]{:S(2)}) %collective-permute-start.1) | collective-permute-done | bytes 1048608 | tf_op jit(solution)/shard_map/ppermute | solution.py:32
  53.1 1.7 collective-permute-start.5
  56.9 2.2 %copy-done.8 = f32[1024,1024]{1,0:T(8,128)S(1)} copy-done((f32[1024,1024]{1,0:T(8,128)S(1)}, f32[1024,1024]{1,0:T(8,128)}, u32[]{:S(2)}) %copy-start.8) | copy-done | bytes 4194328
  59.1 1.9 copy-done.10
  61.0 13.0 %shard_map.101 = (f32[1024,768]{1,0:T(8,128)S(1)}, f32[1024,1024]{1,0:T(8,128)S(1)}) custom-call(s32[2]{0:T(128)S(1)} %pad_add_fusion.1.place, bf16[1024,512]{1,0:T(8,128)(2,1)} %collective-permute-done.refs_0_, bf16[1024,512]{1,0:T(8,128)(2,1)} %collective-permute-done.1.refs_1_, bf16[1024,512]{1,0:T(8,128)(2,1)S(1)} %collective-permute-done.6.refs_2_, ...), custom_call_target="tpu_custom_call" | custom-call | tf_op jit(solution)/shard_map/pallas_call | solution.py:108
  74.0 4.4 %collective-permute-done.5.refs_0_ = bf16[1024,512]{1,0:T(8,128)(2,1)S(1)} collective-permute-done((bf16[1024,512]{1,0:T(8,128)(2,1)}, bf16[1024,512]{1,0:T(8,128)(2,1)S(1)}, u32[]{:S(2)}, u32[]{:S(2)}) %collective-permute-start.5) | collective-permute-done | bytes 1048608 | tf_op jit(solution)/shard_map/ppermute | solution.py:32
  78.4 2.7 %collective-permute-done.8.refs_1_ = bf16[1024,512]{1,0:T(8,128)(2,1)S(1)} collective-permute-done((bf16[1024,512]{1,0:T(8,128)(2,1)S(1)}, bf16[1024,512]{1,0:T(8,128)(2,1)S(1)}, u32[]{:S(2)}, u32[]{:S(2)}) %collective-permute-start.8) | collective-permute-done | bytes 1048608 | tf_op jit(solution)/shard_map/ppermute | solution.py:38
  81.1 4.0 %shard_map.102 = (bf16[1024,768]{1,0:T(8,128)(2,1)S(1)}, bf16[4,64,128]{2,1,0:T(8,128)(2,1)S(1)}) custom-call(s32[2]{0:T(128)S(1)} %pad_add_fusion.1.place, bf16[1024,512]{1,0:T(8,128)(2,1)S(1)} %collective-permute-done.5.refs_0_, bf16[1024,512]{1,0:T(8,128)(2,1)S(1)} %collective-permute-done.8.refs_1_, bf16[4096,1792]{1,0:T(8,128)(2,1)S(1)} %bitcast.53, ...), custom_call_target="tpu_custom_call" | custom-call | tf_op jit(solution)/shard_map/pallas_call | solution.py:176
  85.2 3.6 %shard_map.103 = (f32[4,4,160,128]{3,2,1,0:T(8,128)S(1)}, bf16[4,160,128]{2,1,0:T(8,128)(2,1)S(1)}, bf16[4,288,128]{2,1,0:T(8,128)(2,1)}) custom-call(s32[5]{0:T(128)S(1)} %pad_add_fusion.limits, bf16[1024,768]{1,0:T(8,128)(2,1)S(1)} %get-tuple-element.50.values.features, bf16[1024,768]{1,0:T(8,128)(2,1)S(1)} %get-tuple-element.50.values.features, ...), custom_call_target="tpu_custom_call" | custom-call | tf_op jit(solution)/shard_map/pallas_call | solution.py:264
  91.1 3.4 %collective-permute-start.9 = (bf16[4,288,128]{2,1,0:T(8,128)(2,1)}, bf16[4,288,128]{2,1,0:T(8,128)(2,1)S(1)}, u32[]{:S(2)}, u32[]{:S(2)}) collective-permute-start(bf16[4,288,128]{2,1,0:T(8,128)(2,1)} %get-tuple-element.58), channel_id=1, source_target_pairs={{0,8},{8,16},{16,24},{1,9},{9,17},{17,25},{2,10},{10,18},{18,26},{... | collective-permute-start | bytes 884744 | tf_op jit(solution)/shard_map/ppermute | solution.py:491
  94.5 3.4 %collective-permute-start.10 = (bf16[4,160,128]{2,1,0:T(8,128)(2,1)S(1)}, bf16[4,160,128]{2,1,0:T(8,128)(2,1)S(1)}, u32[]{:S(2)}, u32[]{:S(2)}) collective-permute-start(bf16[4,160,128]{2,1,0:T(8,128)(2,1)S(1)} %get-tuple-element.52), channel_id=1, source_target_pairs={{0,16},{8,24},{1,17},{9,25},{2,18},{10,26},{3,19},{11,27},{4,20},{... | collective-permute-start | bytes 491528 | tf_op jit(solution)/shard_map/ppermute | solution.py:491
  99.6 2.2 %copy-done.2 = f32[1024,1024]{1,0:T(8,128)S(1)} copy-done((f32[1024,1024]{1,0:T(8,128)S(1)}, f32[1024,1024]{1,0:T(8,128)}, u32[]{:S(2)}) %copy-start.2) | copy-done | bytes 4194328
  101.8 5.6 %shard_map.104.window = bf16[1024,1024]{1,0:T(8,128)(2,1)S(1)} custom-call(s32[2]{0:T(128)S(1)} %pad_add_fusion.1.place, bf16[1024,512]{1,0:T(8,128)(2,1)S(1)} %collective-permute-done.5.refs_0_, bf16[1024,512]{1,0:T(8,128)(2,1)S(1)} %copy-done.6, bf16[4096,1792]{1,0:T(8,128)(2,1)} %pad_maximum_fusion.refs_2_.refs_4_.refs_5_.refs_3_.refs_6_, ...), custom_call_target="tpu_custom_call" | custom-call | tf_op jit(solution)/shard_map/pallas_call | solution.py:108
  107.5 8.6 %shard_map.105 = (bf16[512,512]{1,0:T(8,128)(2,1)S(1)}, bf16[512,512]{1,0:T(8,128)(2,1)S(1)}) custom-call(s32[5]{0:T(128)S(1)} %pad_add_fusion.limits, bf16[1024,768]{1,0:T(8,128)(2,1)S(1)} %copy-done.4, bf16[1024,768]{1,0:T(8,128)(2,1)S(1)} %copy-done.4, bf16[1024,1024]{1,0:T(8,128)(2,1)S(1)} %shard_map.104.window, s32[1024,1]{1,0:T(8,128)S(1)} %copy.12.bounds, ...), custom_call_target="tpu_custom_call" | custom-call | tf_op jit(solution)/shard_map/pallas_call | solution.py:391
  119.1 1.7 collective-permute-start.13
  121.6 2.3 %collective-permute-start.17 = (bf16[512,512]{1,0:T(8,128)(2,1)S(1)}, bf16[512,512]{1,0:T(8,128)(2,1)S(1)}, u32[]{:S(2)}, u32[]{:S(2)}) collective-permute-start(bf16[512,512]{1,0:T(8,128)(2,1)S(1)} %fusion.13), channel_id=1, source_target_pairs={{0,6},{1,7},{2,0},{3,1},{4,2},{5,3},{6,4},{7,5},{8,14},{9,15},{10,... | collective-permute-start | bytes 1572872 | tf_op jit(solution)/shard_map/ppermute | solution.py:32
  125.7 10.1 %collective-permute-done.13 = bf16[512,512]{1,0:T(8,128)(2,1)S(1)} collective-permute-done((bf16[512,512]{1,0:T(8,128)(2,1)S(1)}, bf16[512,512]{1,0:T(8,128)(2,1)S(1)}, u32[]{:S(2)}, u32[]{:S(2)}) %collective-permute-start.13) | collective-permute-done | bytes 524320 | tf_op jit(solution)/shard_map/ppermute | solution.py:32
  136.2 10.6 %collective-permute-done.17 = bf16[512,512]{1,0:T(8,128)(2,1)S(1)} collective-permute-done((bf16[512,512]{1,0:T(8,128)(2,1)S(1)}, bf16[512,512]{1,0:T(8,128)(2,1)S(1)}, u32[]{:S(2)}, u32[]{:S(2)}) %collective-permute-start.17) | collective-permute-done | bytes 524320 | tf_op jit(solution)/shard_map/ppermute | solution.py:32
  147.3 1.8 collective-permute-start.18
  149.5 8.7 %collective-permute-done.14 = bf16[512,512]{1,0:T(8,128)(2,1)S(1)} collective-permute-done((bf16[512,512]{1,0:T(8,128)(2,1)S(1)}, bf16[512,512]{1,0:T(8,128)(2,1)S(1)}, u32[]{:S(2)}, u32[]{:S(2)}) %collective-permute-start.14) | collective-permute-done | bytes 524320 | tf_op jit(solution)/shard_map/ppermute | solution.py:32
  158.7 10.6 %collective-permute-done.18 = bf16[512,512]{1,0:T(8,128)(2,1)S(1)} collective-permute-done((bf16[512,512]{1,0:T(8,128)(2,1)S(1)}, bf16[512,512]{1,0:T(8,128)(2,1)S(1)}, u32[]{:S(2)}, u32[]{:S(2)}) %collective-permute-start.18) | collective-permute-done | bytes 524320 | tf_op jit(solution)/shard_map/ppermute | solution.py:32
  169.8 1.8 collective-permute-start.19
  172.0 8.7 %collective-permute-done.15 = bf16[512,512]{1,0:T(8,128)(2,1)S(1)} collective-permute-done((bf16[512,512]{1,0:T(8,128)(2,1)S(1)}, bf16[512,512]{1,0:T(8,128)(2,1)S(1)}, u32[]{:S(2)}, u32[]{:S(2)}) %collective-permute-start.15) | collective-permute-done | bytes 524320 | tf_op jit(solution)/shard_map/ppermute | solution.py:32
  181.2 9.9 %collective-permute-done.19 = bf16[512,512]{1,0:T(8,128)(2,1)S(1)} collective-permute-done((bf16[512,512]{1,0:T(8,128)(2,1)S(1)}, bf16[512,512]{1,0:T(8,128)(2,1)S(1)}, u32[]{:S(2)}, u32[]{:S(2)}) %collective-permute-start.19) | collective-permute-done | bytes 524320 | tf_op jit(solution)/shard_map/ppermute | solution.py:32
  (117 shorter events, 26.7 us)
Async XLA Ops:
  0.0 9.4 %collective-permute-start.3 = (bf16[1024,512]{1,0:T(8,128)(2,1)}, bf16[1024,512]{1,0:T(8,128)(2,1)S(1)}, u32[]{:S(2)}, u32[]{:S(2)}) collective-permute-start(bf16[1024,512]{1,0:T(8,128)(2,1)} %refs_0_.1), channel_id=1, source_target_pairs={{0,1},{1,0},{2,3},{3,2},{4,5},{5,4},{6,7},{7,6},{8,9},{9,8},{10,11... | collective-permute-start | bytes 3145736 | tf_op jit(solution)/shard_map/ppermute | solution.py:38
  0.5 47.5 %collective-permute-start = (bf16[1024,512]{1,0:T(8,128)(2,1)}, bf16[1024,512]{1,0:T(8,128)(2,1)}, u32[]{:S(2)}, u32[]{:S(2)}) collective-permute-start(bf16[1024,512]{1,0:T(8,128)(2,1)} %refs_0_.1), channel_id=1, source_target_pairs={{0,6},{1,7},{2,0},{3,1},{4,2},{5,3},{6,4},{7,5},{8,14},{9,15},{10,... | collective-permute-start | bytes 3145736 | tf_op jit(solution)/shard_map/ppermute | solution.py:32
  5.1 46.8 %collective-permute-start.1 = (bf16[1024,512]{1,0:T(8,128)(2,1)}, bf16[1024,512]{1,0:T(8,128)(2,1)}, u32[]{:S(2)}, u32[]{:S(2)}) collective-permute-start(bf16[1024,512]{1,0:T(8,128)(2,1)} %refs_0_.1), channel_id=1, source_target_pairs={{0,2},{1,3},{2,4},{3,5},{4,6},{5,7},{6,0},{7,1},{8,10},{9,11},{10,... | collective-permute-start | bytes 3145736 | tf_op jit(solution)/shard_map/ppermute | solution.py:32
  5.9 42.0 %collective-permute-start.2 = (bf16[64,128]{1,0:T(8,128)(2,1)S(1)}, bf16[64,128]{1,0:T(8,128)(2,1)S(1)}, u32[]{:S(2)}, u32[]{:S(2)}) collective-permute-start(bf16[64,128]{1,0:T(8,128)(2,1)S(1)} %broadcast_in_dim.7), channel_id=1, source_target_pairs={{0,8},{8,16},{16,24},{1,9},{9,17},{17,25},{2,10},{10,18},{18,26},{... | collective-permute-start | bytes 49160 | tf_op jit(solution)/shard_map/ppermute | solution.py:439
  15.0 14.8 %copy-start.13 = (bf16[1024,512]{1,0:T(8,128)(2,1)S(1)}, bf16[1024,512]{1,0:T(8,128)(2,1)}, u32[]{:S(2)}) copy-start(bf16[1024,512]{1,0:T(8,128)(2,1)} %refs_0_.1) | copy-start | bytes 3145732
  15.0 28.5 %collective-permute-start.4 = (bf16[4,512,512]{2,1,0:T(8,128)(2,1)}, bf16[4,512,512]{2,1,0:T(8,128)(2,1)}, u32[]{:S(2)}, u32[]{:S(2)}) collective-permute-start(bf16[4,512,512]{2,1,0:T(8,128)(2,1)} %pad_maximum_fusion.1), channel_id=1, source_target_pairs={{0,1},{1,0},{2,3},{3,2},{4,5},{5,4},{6,7},{7,6},{8,9},{9,8},{10,11... | collective-permute-start | bytes 6291464 | tf_op jit(solution)/shard_map/ppermute | solution.py:38
  43.4 12.0 %copy-start.7 = (f32[1024,1024]{1,0:T(8,128)}, f32[1024,1024]{1,0:T(8,128)S(1)}, u32[]{:S(2)}) copy-start(f32[1024,1024]{1,0:T(8,128)S(1)} %get-tuple-element.44.refs_7_) | copy-start | bytes 12582916
  43.4 37.6 %slice-start = ((s8[14680064]{0:T(1024)(128)(4,1)}), s8[4194304]{0:T(1024)(128)(4,1)S(1)}, s32[]{:S(2)}) async-start(s8[14680064]{0:T(1024)(128)(4,1)} %bitcast.52), calls=%async_computation | async-start | bytes 8388608
  52.4 28.6 %slice-start.1 = ((s8[14680064]{0:T(1024)(128)(4,1)}), s8[4194304]{0:T(1024)(128)(4,1)S(1)}, s32[]{:S(2)}) async-start(s8[14680064]{0:T(1024)(128)(4,1)} %bitcast.52), calls=%async_computation.1 | async-start | bytes 8388608
  52.5 28.6 %slice-start.2 = ((s8[14680064]{0:T(1024)(128)(4,1)}), s8[4194304]{0:T(1024)(128)(4,1)S(1)}, s32[]{:S(2)}) async-start(s8[14680064]{0:T(1024)(128)(4,1)} %bitcast.52), calls=%async_computation.2 | async-start | bytes 8388608
  52.5 28.6 %slice-start.3 = ((s8[14680064]{0:T(1024)(128)(4,1)}), s8[2097152]{0:T(1024)(128)(4,1)S(1)}, s32[]{:S(2)}) async-start(s8[14680064]{0:T(1024)(128)(4,1)} %bitcast.52), calls=%async_computation.3 | async-start | bytes 4194304
  52.5 2.9 %collective-permute-start.6 = (bf16[1024,512]{1,0:T(8,128)(2,1)}, bf16[1024,512]{1,0:T(8,128)(2,1)S(1)}, u32[]{:S(2)}, u32[]{:S(2)}) collective-permute-start(bf16[1024,512]{1,0:T(8,128)(2,1)} %collective-permute-done.refs_0_), channel_id=1, source_target_pairs={{0,1},{1,0},{2,3},{3,2},{4,5},{5,4},{6,7},{7,6},{8,9},{9,8},{10,11... | collective-permute-start | bytes 3145736 | tf_op jit(solution)/shard_map/ppermute | solution.py:38
  52.6 4.4 %collective-permute-start.7 = (bf16[1024,512]{1,0:T(8,128)(2,1)}, bf16[1024,512]{1,0:T(8,128)(2,1)S(1)}, u32[]{:S(2)}, u32[]{:S(2)}) collective-permute-start(bf16[1024,512]{1,0:T(8,128)(2,1)} %collective-permute-done.1.refs_1_), channel_id=1, source_target_pairs={{0,1},{1,0},{2,3},{3,2},{4,5},{5,4},{6,7},{7,6},{8,9},{9,8},{10,11... | collective-permute-start | bytes 3145736 | tf_op jit(solution)/shard_map/ppermute | solution.py:38
  53.1 25.4 %collective-permute-start.5 = (bf16[1024,512]{1,0:T(8,128)(2,1)}, bf16[1024,512]{1,0:T(8,128)(2,1)S(1)}, u32[]{:S(2)}, u32[]{:S(2)}) collective-permute-start(bf16[1024,512]{1,0:T(8,128)(2,1)} %collective-permute-done.refs_0_), channel_id=1, source_target_pairs={{0,6},{1,7},{2,0},{3,1},{4,2},{5,3},{6,4},{7,5},{8,14},{9,15},{10,... | collective-permute-start | bytes 3145736 | tf_op jit(solution)/shard_map/ppermute | solution.py:32
  74.0 11.2 %copy-start.1 = (f32[1024,1024]{1,0:T(8,128)}, f32[1024,1024]{1,0:T(8,128)S(1)}, u32[]{:S(2)}) copy-start(f32[1024,1024]{1,0:T(8,128)S(1)} %get-tuple-element.49.refs_8_.refs_9_.refs_10_.refs_11_.refs_3_) | copy-start | bytes 12582916
  78.4 2.7 %collective-permute-start.8 = (bf16[1024,512]{1,0:T(8,128)(2,1)S(1)}, bf16[1024,512]{1,0:T(8,128)(2,1)S(1)}, u32[]{:S(2)}, u32[]{:S(2)}) collective-permute-start(bf16[1024,512]{1,0:T(8,128)(2,1)S(1)} %collective-permute-done.5.refs_0_), channel_id=1, source_target_pairs={{0,1},{1,0},{2,3},{3,2},{4,5},{5,4},{6,7},{7,6},{8,9},{9,8},{10,11... | collective-permute-start | bytes 3145736 | tf_op jit(solution)/shard_map/ppermute | solution.py:38
  85.2 14.4 %copy-start.6 = (bf16[1024,512]{1,0:T(8,128)(2,1)S(1)}, bf16[1024,512]{1,0:T(8,128)(2,1)}, u32[]{:S(2)}) copy-start(bf16[1024,512]{1,0:T(8,128)(2,1)} %copy-done.5) | copy-start | bytes 3145732
  91.1 16.4 %collective-permute-start.9 = (bf16[4,288,128]{2,1,0:T(8,128)(2,1)}, bf16[4,288,128]{2,1,0:T(8,128)(2,1)S(1)}, u32[]{:S(2)}, u32[]{:S(2)}) collective-permute-start(bf16[4,288,128]{2,1,0:T(8,128)(2,1)} %get-tuple-element.58), channel_id=1, source_target_pairs={{0,8},{8,16},{16,24},{1,9},{9,17},{17,25},{2,10},{10,18},{18,26},{... | collective-permute-start | bytes 884744 | tf_op jit(solution)/shard_map/ppermute | solution.py:491
  94.5 13.0 %collective-permute-start.10 = (bf16[4,160,128]{2,1,0:T(8,128)(2,1)S(1)}, bf16[4,160,128]{2,1,0:T(8,128)(2,1)S(1)}, u32[]{:S(2)}, u32[]{:S(2)}) collective-permute-start(bf16[4,160,128]{2,1,0:T(8,128)(2,1)S(1)} %get-tuple-element.52), channel_id=1, source_target_pairs={{0,16},{8,24},{1,17},{9,25},{2,18},{10,26},{3,19},{11,27},{4,20},{... | collective-permute-start | bytes 491528 | tf_op jit(solution)/shard_map/ppermute | solution.py:491
  97.9 9.6 %collective-permute-start.11 = (bf16[4,160,128]{2,1,0:T(8,128)(2,1)S(1)}, bf16[4,160,128]{2,1,0:T(8,128)(2,1)S(1)}, u32[]{:S(2)}, u32[]{:S(2)}) collective-permute-start(bf16[4,160,128]{2,1,0:T(8,128)(2,1)S(1)} %get-tuple-element.52), channel_id=1, source_target_pairs={{0,24},{1,25},{2,26},{3,27},{4,28},{5,29},{6,30},{7,31}} | collective-permute-start | bytes 491528 | tf_op jit(solution)/shard_map/ppermute | solution.py:491
  107.5 11.1 %copy-start.23 = (bf16[512,512]{1,0:T(8,128)(2,1)S(1)}, bf16[512,512]{1,0:T(8,128)(2,1)}, u32[]{:S(2)}) copy-start(bf16[512,512]{1,0:T(8,128)(2,1)} %get-tuple-element.66) | copy-start | bytes 1572868
  116.2 2.0 %collective-permute-start.12 = (bf16[512,512]{1,0:T(8,128)(2,1)S(1)}, bf16[512,512]{1,0:T(8,128)(2,1)S(1)}, u32[]{:S(2)}, u32[]{:S(2)}) collective-permute-start(bf16[512,512]{1,0:T(8,128)(2,1)S(1)} %get-tuple-element.59), channel_id=1, source_target_pairs={{0,1},{1,0},{2,3},{3,2},{4,5},{5,4},{6,7},{7,6},{8,9},{9,8},{10,11... | collective-permute-start | bytes 1572872 | tf_op jit(solution)/shard_map/ppermute | solution.py:38
  116.3 4.5 %collective-permute-start.16 = (bf16[512,512]{1,0:T(8,128)(2,1)S(1)}, bf16[512,512]{1,0:T(8,128)(2,1)S(1)}, u32[]{:S(2)}, u32[]{:S(2)}) collective-permute-start(bf16[512,512]{1,0:T(8,128)(2,1)S(1)} %get-tuple-element.68), channel_id=1, source_target_pairs={{0,1},{1,0},{2,3},{3,2},{4,5},{5,4},{6,7},{7,6},{8,9},{9,8},{10,11... | collective-permute-start | bytes 1572872 | tf_op jit(solution)/shard_map/ppermute | solution.py:38
  119.1 16.7 %collective-permute-start.13 = (bf16[512,512]{1,0:T(8,128)(2,1)S(1)}, bf16[512,512]{1,0:T(8,128)(2,1)S(1)}, u32[]{:S(2)}, u32[]{:S(2)}) collective-permute-start(bf16[512,512]{1,0:T(8,128)(2,1)S(1)} %fusion.12), channel_id=1, source_target_pairs={{0,2},{1,3},{2,4},{3,5},{4,6},{5,7},{6,0},{7,1},{8,10},{9,11},{10,... | collective-permute-start | bytes 1572872 | tf_op jit(solution)/shard_map/ppermute | solution.py:32
  121.6 14.1 %copy-start.26 = (bf16[512,512]{1,0:T(8,128)(2,1)S(1)}, bf16[512,512]{1,0:T(8,128)(2,1)}, u32[]{:S(2)}) copy-start(bf16[512,512]{1,0:T(8,128)(2,1)} %get-tuple-element.64) | copy-start | bytes 1572868
  121.6 25.2 %collective-permute-start.17 = (bf16[512,512]{1,0:T(8,128)(2,1)S(1)}, bf16[512,512]{1,0:T(8,128)(2,1)S(1)}, u32[]{:S(2)}, u32[]{:S(2)}) collective-permute-start(bf16[512,512]{1,0:T(8,128)(2,1)S(1)} %fusion.13), channel_id=1, source_target_pairs={{0,6},{1,7},{2,0},{3,1},{4,2},{5,3},{6,4},{7,5},{8,14},{9,15},{10,... | collective-permute-start | bytes 1572872 | tf_op jit(solution)/shard_map/ppermute | solution.py:32
  125.2 23.9 %copy-start.19 = (bf16[512,512]{1,0:T(8,128)(2,1)S(1)}, bf16[512,512]{1,0:T(8,128)(2,1)}, u32[]{:S(2)}) copy-start(bf16[512,512]{1,0:T(8,128)(2,1)} %get-tuple-element.61) | copy-start | bytes 1572868
  136.2 22.1 %collective-permute-start.14 = (bf16[512,512]{1,0:T(8,128)(2,1)S(1)}, bf16[512,512]{1,0:T(8,128)(2,1)S(1)}, u32[]{:S(2)}, u32[]{:S(2)}) collective-permute-start(bf16[512,512]{1,0:T(8,128)(2,1)S(1)} %fusion.8), channel_id=1, source_target_pairs={{0,2},{1,3},{2,4},{3,5},{4,6},{5,7},{6,0},{7,1},{8,10},{9,11},{10,... | collective-permute-start | bytes 1572872 | tf_op jit(solution)/shard_map/ppermute | solution.py:32
  147.3 22.1 %collective-permute-start.18 = (bf16[512,512]{1,0:T(8,128)(2,1)S(1)}, bf16[512,512]{1,0:T(8,128)(2,1)S(1)}, u32[]{:S(2)}, u32[]{:S(2)}) collective-permute-start(bf16[512,512]{1,0:T(8,128)(2,1)S(1)} %fusion.11), channel_id=1, source_target_pairs={{0,6},{1,7},{2,0},{3,1},{4,2},{5,3},{6,4},{7,5},{8,14},{9,15},{10,... | collective-permute-start | bytes 1572872 | tf_op jit(solution)/shard_map/ppermute | solution.py:32
  149.5 31.2 %copy-start.25 = (bf16[512,512]{1,0:T(8,128)(2,1)S(1)}, bf16[512,512]{1,0:T(8,128)(2,1)}, u32[]{:S(2)}) copy-start(bf16[512,512]{1,0:T(8,128)(2,1)} %get-tuple-element.60) | copy-start | bytes 1572868
  158.7 22.1 %collective-permute-start.15 = (bf16[512,512]{1,0:T(8,128)(2,1)S(1)}, bf16[512,512]{1,0:T(8,128)(2,1)S(1)}, u32[]{:S(2)}, u32[]{:S(2)}) collective-permute-start(bf16[512,512]{1,0:T(8,128)(2,1)S(1)} %fusion.7), channel_id=1, source_target_pairs={{0,2},{1,3},{2,4},{3,5},{4,6},{5,7},{6,0},{7,1},{8,10},{9,11},{10,... | collective-permute-start | bytes 1572872 | tf_op jit(solution)/shard_map/ppermute | solution.py:32
  169.8 21.3 %collective-permute-start.19 = (bf16[512,512]{1,0:T(8,128)(2,1)S(1)}, bf16[512,512]{1,0:T(8,128)(2,1)S(1)}, u32[]{:S(2)}, u32[]{:S(2)}) collective-permute-start(bf16[512,512]{1,0:T(8,128)(2,1)S(1)} %fusion.10), channel_id=1, source_target_pairs={{0,6},{1,7},{2,0},{3,1},{4,2},{5,3},{6,4},{7,5},{8,14},{9,15},{10,... | collective-permute-start | bytes 1572872 | tf_op jit(solution)/shard_map/ppermute | solution.py:32
  (20 other events, 91.5 us)

commit v9 on v8

--- a/solution.py
+++ b/solution.py
@@ -119,12 +119,15 @@
     )(place, *args)
 
 
-def late_kernel(chips, heads, place, *refs):
+def late_kernel(chips, place, limits, *refs):
     mine, theirs, weights = refs[:chips], refs[chips : 2 * chips], refs[2 * chips : 3 * chips]
+    out, prefix, end, with_tail, both = refs[-5:]
+    chunks, heads = prefix.shape[:2]
     key_weights = refs[3 * chips : (3 + heads) * chips]
     before, *key_before = refs[(3 + heads) * chips : (3 + heads) * chips + 1 + heads]
-    out, keys, both = refs[-3:]
+    expand, rows = refs[-7:-5]
     width = 2 * mine[0].shape[1]
+    size = before.shape[1]
     step = pl.program_id(0)
 
     @pl.when(step == 0)
@@ -133,13 +136,16 @@
 
     total = before[...]
     for n in range(chips):
-        rows = both[:, n * width : (n + 1) * width]
-        total += jnp.dot(rows, weights[n][...], preferred_element_type=F32)
-    out[...] = total.astype(BF16)
+        piece = both[:, n * width : (n + 1) * width]
+        total += jnp.dot(piece, weights[n][...], preferred_element_type=F32)
+    out[:, pl.ds(pl.multiple_of(step * size, size), size)] = total.astype(BF16)
 
     @pl.when(step == pl.num_programs(0) - 1)
     def _():
         last = slice(out.shape[0] - WIN, out.shape[0])
+        features = out[:, heads * HEAD_DIM : heads * HEAD_DIM + LANES]
+        mark = lax.broadcasted_iota(jnp.int32, (STATE, HEAD_DIM), 0) == STATE - 1
+        at = lax.broadcasted_iota(jnp.int32, (CHUNK, HEAD_DIM), 0)
         for h in range(heads):
             tail = key_before[h][...]
             for n in range(chips):
@@ -147,47 +153,75 @@
                     both[last, n * width : (n + 1) * width], key_weights[n * heads + h][...],
                     preferred_element_type=F32,
                 )
-            keys[h] = tail.astype(BF16)
-
-
-def project_late(place, chips, mine, theirs, weight, heads, before, window_before):
-    rows, width = mine[0].shape
-    count = weight.shape[0] // (2 * width)
+            column = slice(h * HEAD_DIM, (h + 1) * HEAD_DIM)
+            phi_key = phi(features, expand[h], rows[...])
+            parts = []
+            for n in range(chunks):
+                here = slice(n * CHUNK, (n + 1) * CHUNK)
+                kept = jnp.where(at + n * CHUNK >= limits[n], out[here, column].astype(F32), 0.0)
+                parts.append(
+                    lax.dot_general(
+                        phi_key[here], kept.astype(BF16), (((0,), (0,)), ((), ())),
+                        preferred_element_type=F32,
+                    )[:STATE]
+                )
+            state = jnp.zeros((STATE, HEAD_DIM), F32)
+            for n in range(chunks):
+                prefix[n, h] = state
+                state = parts[n] + jnp.where(limits[n] <= n * CHUNK, state, 0.0)
+            sent = jnp.where(mark, (limits[chunks] + 1).astype(F32), state).astype(BF16)
+            end[h] = sent
+            with_tail[h, :STATE] = sent
+            with_tail[h, STATE : STATE + WIN] = out[last, column]
+            with_tail[h, STATE + WIN :] = tail.astype(BF16)
+
+
+def project_late(place, limits, chips, mine, theirs, weight, heads, before, window_before, expand, rows):
+    count, width = mine[0].shape
+    ring_size = weight.shape[0] // (2 * width)
     columns = before.shape[1]
     size = 256
     first = columns // HEAD_DIM + 1
-    specs = [pl.BlockSpec((rows, width), lambda j, p: (0, 0))] * (2 * len(chips))
+
+    def full(a):
+        return pl.BlockSpec(a.shape, lambda j, *_: (0,) * len(a.shape))
+
+    specs = [full(mine[0])] * (2 * len(chips))
     for n in chips:
         specs.append(
-            pl.BlockSpec((2 * width, size), lambda j, p, n=n: (lax.rem(p[0] + n, count), j))
+            pl.BlockSpec((2 * width, size), lambda j, p, _, n=n: (lax.rem(p[0] + n, ring_size), j))
         )
     for n in chips:
         for h in range(heads):
             specs.append(
                 pl.BlockSpec(
                     (2 * width, HEAD_DIM),
-                    lambda j, p, n=n, h=h: (lax.rem(p[0] + n, count), first + 2 * h),
+                    lambda j, p, _, n=n, h=h: (lax.rem(p[0] + n, ring_size), first + 2 * h),
                 )
             )
-    block = pl.BlockSpec((rows, size), lambda j, p: (0, j))
-    specs.append(block)
+    specs.append(pl.BlockSpec((count, size), lambda j, *_: (0, j)))
     for h in range(heads):
-        specs.append(pl.BlockSpec((WIN, HEAD_DIM), lambda j, p, h=h: (rows // WIN - 1, 2 * h + 1)))
+        specs.append(pl.BlockSpec((WIN, HEAD_DIM), lambda j, *_, h=h: (count // WIN - 1, 2 * h + 1)))
+    specs += [full(expand), full(rows)]
+    shapes = [
+        jax.ShapeDtypeStruct((count, columns), BF16),
+        jax.ShapeDtypeStruct((count // CHUNK, heads, STATE, HEAD_DIM), F32),
+        jax.ShapeDtypeStruct((heads, STATE, HEAD_DIM), BF16),
+        jax.ShapeDtypeStruct((heads, SENT, HEAD_DIM), BF16),
+    ]
     return pl.pallas_call(
-        functools.partial(late_kernel, len(chips), heads),
+        functools.partial(late_kernel, len(chips)),
         grid_spec=pltpu.PrefetchScalarGridSpec(
-            num_scalar_prefetch=1,
+            num_scalar_prefetch=2,
             grid=(columns // size,),
             in_specs=specs,
-            out_specs=[block, pl.BlockSpec((heads, WIN, HEAD_DIM), lambda j, p: (0, 0, 0))],
-            scratch_shapes=[pltpu.VMEM((rows, 2 * width * len(chips)), BF16)],
+            out_specs=[full(a) for a in shapes],
+            scratch_shapes=[pltpu.VMEM((count, 2 * width * len(chips)), BF16)],
         ),
-        out_shape=[
-            jax.ShapeDtypeStruct((rows, columns), BF16),
-            jax.ShapeDtypeStruct((heads, WIN, HEAD_DIM), BF16),
-        ],
-        compiler_params=params(),
-    )(place, *mine, *theirs, *[weight] * (len(chips) * (1 + heads)), before, *[window_before] * heads)
+        out_shape=shapes,
+        compiler_params=params(50 * 1024 * 1024),
+    )(place, limits, *mine, *theirs, *[weight] * (len(chips) * (1 + heads)), before,
+      *[window_before] * heads, expand, rows)
 
 
 def expansions(heads):
@@ -226,66 +260,6 @@
     left = factors[:, :WIDE] + rows[0:1]
     right = factors[:, WIDE:] + rows[1:2]
     return (left * right * rows[2:3]).astype(BF16)
-
-
-def sums_kernel(limits, values, features, expand, rows, keys, prefix, end, both):
-    chunks, heads = prefix.shape[:2]
-    mark = lax.broadcasted_iota(jnp.int32, (STATE, HEAD_DIM), 0) == STATE - 1
-    at = lax.broadcasted_iota(jnp.int32, (CHUNK, HEAD_DIM), 0)
-    for h in range(heads):
-        column = slice(h * HEAD_DIM, (h + 1) * HEAD_DIM)
-        phi_key = phi(features[...], expand[h], rows[...])
-        parts = []
-        for n in range(chunks):
-            here = slice(n * CHUNK, (n + 1) * CHUNK)
-            kept = jnp.where(at + n * CHUNK >= limits[n], values[here, column].astype(F32), 0.0)
-            parts.append(
-                lax.dot_general(
-                    phi_key[here], kept.astype(BF16), (((0,), (0,)), ((), ())),
-                    preferred_element_type=F32,
-                )[:STATE]
-            )
-        state = jnp.zeros((STATE, HEAD_DIM), F32)
-        for n in range(chunks):
-            prefix[n, h] = state
-            state = parts[n] + jnp.where(limits[n] <= n * CHUNK, state, 0.0)
-        sent = jnp.where(mark, (limits[chunks] + 1).astype(F32), state).astype(BF16)
-        end[h] = sent
-        both[h, :STATE] = sent
-        both[h, STATE : STATE + WIN] = values[values.shape[0] - WIN :, column]
-        both[h, STATE + WIN :] = keys[h]
-
-
-def sums(limits, both, keys, expand, rows):
-    heads = keys.shape[0]
-    chunks = both.shape[0] // CHUNK
-    group = min(GROUP, heads)
-    count = both.shape[0]
-    return pl.pallas_call(
-        sums_kernel,
-        grid_spec=pltpu.PrefetchScalarGridSpec(
-            num_scalar_prefetch=1,
-            grid=(heads // group,),
-            in_specs=[
-                pl.BlockSpec((count, group * HEAD_DIM), lambda g, _: (0, g)),
-                pl.BlockSpec((count, LANES), lambda g, _: (0, heads)),
-                pl.BlockSpec((group,) + expand.shape[1:], lambda g, _: (g, 0, 0)),
-                pl.BlockSpec(rows.shape, lambda g, _: (0, 0)),
-                pl.BlockSpec((group, WIN, HEAD_DIM), lambda g, _: (g, 0, 0)),
-            ],
-            out_specs=[
-                pl.BlockSpec((chunks, group, STATE, HEAD_DIM), lambda g, _: (0, g, 0, 0)),
-                pl.BlockSpec((group, STATE, HEAD_DIM), lambda g, _: (g, 0, 0)),
-                pl.BlockSpec((group, SENT, HEAD_DIM), lambda g, _: (g, 0, 0)),
-            ],
-        ),
-        out_shape=[
-            jax.ShapeDtypeStruct((chunks, heads, STATE, HEAD_DIM), F32),
-            jax.ShapeDtypeStruct((heads, STATE, HEAD_DIM), BF16),
-            jax.ShapeDtypeStruct((heads, SENT, HEAD_DIM), BF16),
-        ],
-        compiler_params=params(),
-    )(limits, both, both, expand, rows, keys)
 
 
 def windows(tiles):
@@ -485,8 +459,9 @@
     late = tuple(range(2, count - 1))
     *mine, fv_part, win_part = lax.optimization_barrier((*[pieces[n] for n in late], *part))
     theirs = [swap(p, count) for p in mine]
-    both, keys = project_late(place, late, mine, theirs, weight, heads, fv_part, win_part)
-    prefix, state, state_and_tail = sums(limits, both, keys, key_map, scale_rows)
+    both, prefix, state, state_and_tail = project_late(
+        place, limits, late, mine, theirs, weight, heads, fv_part, win_part, key_map, scale_rows
+    )
     states = [
         lax.ppermute(
             state_and_tail if k == 1 else state, "ctx", [(i, i + k) for i in range(blocks - k)]

time: 193 us -> 192 us (level)
  local copies, waits for them, and re-layouts: 28.8 us -> 24.4 us
  waiting for transfers between devices: 73.2 us -> 75.7 us
    unnamed x64 -> x46, local copies, waits for them, and re-layouts: 17.6 us -> 14.5 us
    ppermute x9, waiting for transfers between devices: 67 us -> 69.8 us  [ring(): lax.ppermute(x, 'head', [(2 * z + c, 2 * ((z + step) % count) + c) for z...]
    pallas_call x2 -> x1, Pallas kernels: 7.64 us -> 9.43 us  [project_late(): pl.pallas_call(functools.partial(late_kernel, len(chips)), grid_spec=pltp...]
  transfers between devices with their start and end apart: 20 -> 20, of which waited for: 12 -> 12; matrix products, arithmetic and copies ran while one was open for 16% -> 15% of each run, Pallas kernels for 13% -> 13%
where the time goes in v9:
time: 192 us
  waiting for transfers between devices  75.7 us (39%)
  Pallas kernels  42.7 us (22%)
  starting transfers between devices  27.2 us (14%)
  local copies, waits for them, and re-layouts  24.4 us (13%)
  other arithmetic  14 us (7%)
  matrix products  7.01 us (4%)
    ppermute x9, waiting for transfers between devices, ring(): lax.ppermute(x, 'head', [(2 * z + c, 2 * ((z + step) % count) + c) for z...  69.8 us
    pallas_call x3, Pallas kernels, project(): pl.pallas_call(functools.partial(project_kernel, len(chips), cuts, before...  24.6 us
    unnamed x46, local copies, waits for them, and re-layouts  14.5 us
    ppermute x9, starting transfers between devices, ring(): lax.ppermute(x, 'head', [(2 * z + c, 2 * ((z + step) % count) + c) for z...  14 us
    pallas_call x1, Pallas kernels, project_late(): pl.pallas_call(functools.partial(late_kernel, len(chips)), grid_spec=pltp...  9.43 us
    pallas_call x1, Pallas kernels, mix(): pl.pallas_call(functools.partial(mix_kernel, len(states)), grid_spec=pltp...  8.62 us
    concatenate x1, other arithmetic, shards(): jnp.concatenate([w_value, w_feat, jnp.zeros((w_value.shape[0], fv_columns...  8.39 us
    ppermute x3, starting transfers between devices, shards(): lax.ppermute(state_and_tail if k == 1 else state, 'ctx', [(i, i + k) for...  8.3 us
  transfers between devices with their start and end apart: 20, of which 12 were waited for; matrix products, arithmetic and copies ran while one was open for 15% of the time, Pallas kernels for 13%

profile of v9, /device:TPU:0, one launch (start us, length us, event | category | flops | bytes accessed | tf_op | source)
XLA Modules:
  0.0 191.7 jit_solution(12960829337716761457)
XLA Ops:
  0.5 4.6 %collective-permute-start = (bf16[1024,512]{1,0:T(8,128)(2,1)}, bf16[1024,512]{1,0:T(8,128)(2,1)S(1)}, u32[]{:S(2)}, u32[]{:S(2)}) collective-permute-start(bf16[1024,512]{1,0:T(8,128)(2,1)} %refs_0_.1), channel_id=1, source_target_pairs={{0,6},{1,7},{2,0},{3,1},{4,2},{5,3},{6,4},{7,5},{8,14},{9,15},{10,... | collective-permute-start | bytes 3145736 | tf_op jit(solution)/shard_map/ppermute | solution.py:32
  5.9 3.4 %collective-permute-start.2 = (bf16[64,128]{1,0:T(8,128)(2,1)S(1)}, bf16[64,128]{1,0:T(8,128)(2,1)S(1)}, u32[]{:S(2)}, u32[]{:S(2)}) collective-permute-start(bf16[64,128]{1,0:T(8,128)(2,1)S(1)} %broadcast_in_dim.7), channel_id=1, source_target_pairs={{0,8},{8,16},{16,24},{1,9},{9,17},{17,25},{2,10},{10,18},{18,26},{... | collective-permute-start | bytes 49160 | tf_op jit(solution)/shard_map/ppermute | solution.py:413
  9.5 4.2 %constant_dynamic-slice_fusion = (bf16[512,512]{1,0:T(8,128)(2,1)}, bf16[512,512]{1,0:T(8,128)(2,1)}, bf16[512,512]{1,0:T(8,128)(2,1)}, bf16[1,512,512]{2,1,0:T(...) fusion(bf16[512,4096]{1,0:T(8,128)(2,1)} %param.15, ...), kind=kLoop, calls=%fused_computation.35 | loop fusion | bytes 8388640 | tf_op jit(solution)/shard_map/dynamic_slice | solution.py:426
  13.7 1.6 pad_maximum_fusion.1
  17.5 8.4 %pad_maximum_fusion.refs_2_.refs_4_.refs_5_.refs_3_.refs_6_ = bf16[4096,1792]{1,0:T(8,128)(2,1)} fusion(bf16[4096,1024]{1,0:T(8,128)(2,1)S(1)} %copy-done.13, bf16[4096,128]{1,0:T(8,128)(2,1)} %param.12, bf16[4096,512]{1,0:T(8,128)(2,1)S(1)} %copy-done.22, bf16[1792]{0:T(1024)(128)(2,1)S(1)} %pad.8.clone), kind=kLoop, calls=%fused_computation | loop fusion | flops 58720256 | bytes 28315136 | tf_op jit(solution)/shard_map/concatenate | solution.py:437
  30.1 5.2 %copy-done = bf16[4096,1792]{1,0:T(8,128)(2,1)S(1)} copy-done((bf16[4096,1792]{1,0:T(8,128)(2,1)S(1)}, bf16[4096,1792]{1,0:T(8,128)(2,1)}, u32[]{:S(2)}) %copy-start) | copy-done | bytes 14680088
  36.5 6.8 %shard_map.100 = (f32[1024,768]{1,0:T(8,128)S(1)}, f32[1024,1024]{1,0:T(8,128)S(1)}) custom-call(s32[2]{0:T(128)S(1)} %pad_add_fusion.1.place, bf16[1024,512]{1,0:T(8,128)(2,1)S(1)} %copy-done.6, bf16[1024,512]{1,0:T(8,128)(2,1)S(1)} %copy-done.8, bf16[4096,1792]{1,0:T(8,128)(2,1)S(1)} %copy-done), custom_call_target="tpu_custom_call" | custom-call | tf_op jit(solution)/shard_map/pallas_call | solution.py:108
  43.3 2.9 %dynamic-slice_bitcast_fusion = (bf16[512,512]{1,0:T(8,128)(2,1)}, bf16[512,512]{1,0:T(8,128)(2,1)}, bf16[512,512]{1,0:T(8,128)(2,1)}, bf16[512,512]{1,0:T(8,128)(2,1)}) fusion(bf16[4,512,512]{2,1,0:T(8,128)(2,1)} %collective-permute-done.4, s32[]{:T(128)S(6)} %select_n.61, s32[]{:T(128)S(6)} %select_n.59, s32[]{:T(128)S(6)} %select_n.57, s32[]{:T(128)S(6)} %select_n.55), kind=kLoop, calls=%fused_computation.26 | loop fusion | bytes 4194320 | tf_op jit(solution)/shard_map/jit(dynamic_index_in_dim)/squeeze | solution.py:432
  46.2 5.5 %collective-permute-done.1.refs_1_ = bf16[1024,512]{1,0:T(8,128)(2,1)S(1)} collective-permute-done((bf16[1024,512]{1,0:T(8,128)(2,1)}, bf16[1024,512]{1,0:T(8,128)(2,1)S(1)}, u32[]{:S(2)}, u32[]{:S(2)}) %collective-permute-start.1) | collective-permute-done | bytes 1048608 | tf_op jit(solution)/shard_map/ppermute | solution.py:32
  52.9 1.7 collective-permute-start.5
  55.0 1.5 collective-permute-done.7.refs_3_
  56.5 12.2 %shard_map.101 = (f32[1024,768]{1,0:T(8,128)S(1)}, f32[1024,1024]{1,0:T(8,128)S(1)}) custom-call(s32[2]{0:T(128)S(1)} %pad_add_fusion.1.place, bf16[1024,512]{1,0:T(8,128)(2,1)S(1)} %collective-permute-done.refs_0_, bf16[1024,512]{1,0:T(8,128)(2,1)S(1)} %collective-permute-done.1.refs_1_, bf16[1024,512]{1,0:T(8,128)(2,1)S(1)} %collective-permute-done.6.refs_2_, ...), custom_call_target="tpu_custom_call" | custom-call | tf_op jit(solution)/shard_map/pallas_call | solution.py:108
  68.8 2.0 %copy-done.1 = f32[1024,1024]{1,0:T(8,128)} copy-done((f32[1024,1024]{1,0:T(8,128)}, f32[1024,1024]{1,0:T(8,128)S(1)}, u32[]{:S(2)}) %copy-start.1) | copy-done | bytes 4194328
  70.8 1.7 copy-done.4
  72.4 5.6 %collective-permute-done.5.refs_0_ = bf16[1024,512]{1,0:T(8,128)(2,1)S(1)} collective-permute-done((bf16[1024,512]{1,0:T(8,128)(2,1)S(1)}, bf16[1024,512]{1,0:T(8,128)(2,1)S(1)}, u32[]{:S(2)}, u32[]{:S(2)}) %collective-permute-start.5) | collective-permute-done | bytes 1048608 | tf_op jit(solution)/shard_map/ppermute | solution.py:32
  78.0 2.7 %collective-permute-done.8.refs_1_ = bf16[1024,512]{1,0:T(8,128)(2,1)S(1)} collective-permute-done((bf16[1024,512]{1,0:T(8,128)(2,1)S(1)}, bf16[1024,512]{1,0:T(8,128)(2,1)S(1)}, u32[]{:S(2)}, u32[]{:S(2)}) %collective-permute-start.8) | collective-permute-done | bytes 1048608 | tf_op jit(solution)/shard_map/ppermute | solution.py:38
  80.7 9.4 %shard_map.102 = (bf16[1024,768]{1,0:T(8,128)(2,1)}, f32[4,4,160,128]{3,2,1,0:T(8,128)}, bf16[4,160,128]{2,1,0:T(8,128)(2,1)S(1)}, bf16[4,288,128]{2,1,0:T(8,128)(2,1)}) custom-call(s32[2]{0:T(128)S(1)} %pad_add_fusion.1.place, s32[5]{0:T(128)S(1)} %pad_add_fusion.limits, bf16[1024,512]{1,0:T(8,128)(2,1)S(1)} %collective-permute-done.5.refs_0_, ...), custom_call_target="tpu_custom_call" | custom-call | tf_op jit(solution)/shard_map/pallas_call | solution.py:212
  90.1 3.4 %collective-permute-start.9 = (bf16[4,288,128]{2,1,0:T(8,128)(2,1)}, bf16[4,288,128]{2,1,0:T(8,128)(2,1)S(1)}, u32[]{:S(2)}, u32[]{:S(2)}) collective-permute-start(bf16[4,288,128]{2,1,0:T(8,128)(2,1)} %get-tuple-element.56), channel_id=1, source_target_pairs={{0,8},{8,16},{16,24},{1,9},{9,17},{17,25},{2,10},{10,18},{18,26},{... | collective-permute-start | bytes 884744 | tf_op jit(solution)/shard_map/ppermute | solution.py:466
  93.5 3.4 %collective-permute-start.10 = (bf16[4,160,128]{2,1,0:T(8,128)(2,1)S(1)}, bf16[4,160,128]{2,1,0:T(8,128)(2,1)S(1)}, u32[]{:S(2)}, u32[]{:S(2)}) collective-permute-start(bf16[4,160,128]{2,1,0:T(8,128)(2,1)S(1)} %get-tuple-element.50), channel_id=1, source_target_pairs={{0,16},{8,24},{1,17},{9,25},{2,18},{10,26},{3,19},{11,27},{4,20},{... | collective-permute-start | bytes 491528 | tf_op jit(solution)/shard_map/ppermute | solution.py:466
  98.7 2.2 %copy-done.2 = f32[1024,1024]{1,0:T(8,128)S(1)} copy-done((f32[1024,1024]{1,0:T(8,128)S(1)}, f32[1024,1024]{1,0:T(8,128)}, u32[]{:S(2)}) %copy-start.2) | copy-done | bytes 4194328
  100.9 5.6 %shard_map.103.window = bf16[1024,1024]{1,0:T(8,128)(2,1)S(1)} custom-call(s32[2]{0:T(128)S(1)} %pad_add_fusion.1.place, bf16[1024,512]{1,0:T(8,128)(2,1)S(1)} %collective-permute-done.5.refs_0_, bf16[1024,512]{1,0:T(8,128)(2,1)S(1)} %collective-permute-done.8.refs_1_, bf16[4096,1792]{1,0:T(8,128)(2,1)} %pad_maximum_fusion.refs_2_.refs_4_.refs_5_.refs_3_.refs_6_, ...), custom_call_target="tpu_custom_call" | custom-call | tf_op jit(solution)/shard_map/pallas_call | solution.py:108
  106.6 8.6 %shard_map.104 = (bf16[512,512]{1,0:T(8,128)(2,1)S(1)}, bf16[512,512]{1,0:T(8,128)(2,1)S(1)}) custom-call(s32[5]{0:T(128)S(1)} %pad_add_fusion.limits, bf16[1024,768]{1,0:T(8,128)(2,1)S(1)} %copy-done.3, bf16[1024,768]{1,0:T(8,128)(2,1)S(1)} %copy-done.3, bf16[1024,1024]{1,0:T(8,128)(2,1)S(1)} %shard_map.103.window, s32[1024,1]{1,0:T(8,128)S(1)} %copy.12.bounds, ...), custom_call_target="tpu_custom_call" | custom-call | tf_op jit(solution)/shard_map/pallas_call | solution.py:365
  118.1 1.7 collective-permute-start.13
  120.7 2.3 %collective-permute-start.17 = (bf16[512,512]{1,0:T(8,128)(2,1)S(1)}, bf16[512,512]{1,0:T(8,128)(2,1)S(1)}, u32[]{:S(2)}, u32[]{:S(2)}) collective-permute-start(bf16[512,512]{1,0:T(8,128)(2,1)S(1)} %fusion.13), channel_id=1, source_target_pairs={{0,6},{1,7},{2,0},{3,1},{4,2},{5,3},{6,4},{7,5},{8,14},{9,15},{10,... | collective-permute-start | bytes 1572872 | tf_op jit(solution)/shard_map/ppermute | solution.py:32
  124.7 10.1 %collective-permute-done.13 = bf16[512,512]{1,0:T(8,128)(2,1)S(1)} collective-permute-done((bf16[512,512]{1,0:T(8,128)(2,1)S(1)}, bf16[512,512]{1,0:T(8,128)(2,1)S(1)}, u32[]{:S(2)}, u32[]{:S(2)}) %collective-permute-start.13) | collective-permute-done | bytes 524320 | tf_op jit(solution)/shard_map/ppermute | solution.py:32
  135.3 10.6 %collective-permute-done.17 = bf16[512,512]{1,0:T(8,128)(2,1)S(1)} collective-permute-done((bf16[512,512]{1,0:T(8,128)(2,1)S(1)}, bf16[512,512]{1,0:T(8,128)(2,1)S(1)}, u32[]{:S(2)}, u32[]{:S(2)}) %collective-permute-start.17) | collective-permute-done | bytes 524320 | tf_op jit(solution)/shard_map/ppermute | solution.py:32
  146.4 1.8 collective-permute-start.18
  148.6 8.7 %collective-permute-done.14 = bf16[512,512]{1,0:T(8,128)(2,1)S(1)} collective-permute-done((bf16[512,512]{1,0:T(8,128)(2,1)S(1)}, bf16[512,512]{1,0:T(8,128)(2,1)S(1)}, u32[]{:S(2)}, u32[]{:S(2)}) %collective-permute-start.14) | collective-permute-done | bytes 524320 | tf_op jit(solution)/shard_map/ppermute | solution.py:32
  157.8 10.6 %collective-permute-done.18 = bf16[512,512]{1,0:T(8,128)(2,1)S(1)} collective-permute-done((bf16[512,512]{1,0:T(8,128)(2,1)S(1)}, bf16[512,512]{1,0:T(8,128)(2,1)S(1)}, u32[]{:S(2)}, u32[]{:S(2)}) %collective-permute-start.18) | collective-permute-done | bytes 524320 | tf_op jit(solution)/shard_map/ppermute | solution.py:32
  168.9 1.8 collective-permute-start.19
  171.1 8.7 %collective-permute-done.15 = bf16[512,512]{1,0:T(8,128)(2,1)S(1)} collective-permute-done((bf16[512,512]{1,0:T(8,128)(2,1)S(1)}, bf16[512,512]{1,0:T(8,128)(2,1)S(1)}, u32[]{:S(2)}, u32[]{:S(2)}) %collective-permute-start.15) | collective-permute-done | bytes 524320 | tf_op jit(solution)/shard_map/ppermute | solution.py:32
  180.3 9.9 %collective-permute-done.19 = bf16[512,512]{1,0:T(8,128)(2,1)S(1)} collective-permute-done((bf16[512,512]{1,0:T(8,128)(2,1)S(1)}, bf16[512,512]{1,0:T(8,128)(2,1)S(1)}, u32[]{:S(2)}, u32[]{:S(2)}) %collective-permute-start.19) | collective-permute-done | bytes 524320 | tf_op jit(solution)/shard_map/ppermute | solution.py:32
  (97 shorter events, 22.4 us)
Async XLA Ops:
  0.0 9.4 %collective-permute-start.3 = (bf16[1024,512]{1,0:T(8,128)(2,1)}, bf16[1024,512]{1,0:T(8,128)(2,1)S(1)}, u32[]{:S(2)}, u32[]{:S(2)}) collective-permute-start(bf16[1024,512]{1,0:T(8,128)(2,1)} %refs_0_.1), channel_id=1, source_target_pairs={{0,1},{1,0},{2,3},{3,2},{4,5},{5,4},{6,7},{7,6},{8,9},{9,8},{10,11... | collective-permute-start | bytes 3145736 | tf_op jit(solution)/shard_map/ppermute | solution.py:38
  0.5 45.7 %collective-permute-start = (bf16[1024,512]{1,0:T(8,128)(2,1)}, bf16[1024,512]{1,0:T(8,128)(2,1)S(1)}, u32[]{:S(2)}, u32[]{:S(2)}) collective-permute-start(bf16[1024,512]{1,0:T(8,128)(2,1)} %refs_0_.1), channel_id=1, source_target_pairs={{0,6},{1,7},{2,0},{3,1},{4,2},{5,3},{6,4},{7,5},{8,14},{9,15},{10,... | collective-permute-start | bytes 3145736 | tf_op jit(solution)/shard_map/ppermute | solution.py:32
  5.1 46.7 %collective-permute-start.1 = (bf16[1024,512]{1,0:T(8,128)(2,1)}, bf16[1024,512]{1,0:T(8,128)(2,1)S(1)}, u32[]{:S(2)}, u32[]{:S(2)}) collective-permute-start(bf16[1024,512]{1,0:T(8,128)(2,1)} %refs_0_.1), channel_id=1, source_target_pairs={{0,2},{1,3},{2,4},{3,5},{4,6},{5,7},{6,0},{7,1},{8,10},{9,11},{10,... | collective-permute-start | bytes 3145736 | tf_op jit(solution)/shard_map/ppermute | solution.py:32
  5.9 40.3 %collective-permute-start.2 = (bf16[64,128]{1,0:T(8,128)(2,1)S(1)}, bf16[64,128]{1,0:T(8,128)(2,1)S(1)}, u32[]{:S(2)}, u32[]{:S(2)}) collective-permute-start(bf16[64,128]{1,0:T(8,128)(2,1)S(1)} %broadcast_in_dim.7), channel_id=1, source_target_pairs={{0,8},{8,16},{16,24},{1,9},{9,17},{17,25},{2,10},{10,18},{18,26},{... | collective-permute-start | bytes 49160 | tf_op jit(solution)/shard_map/ppermute | solution.py:413
  9.4 6.6 %copy-start.13 = (bf16[4096,1024]{1,0:T(8,128)(2,1)S(1)}, bf16[4096,1024]{1,0:T(8,128)(2,1)}, u32[]{:S(2)}) copy-start(bf16[4096,1024]{1,0:T(8,128)(2,1)} %param.14) | copy-start | bytes 25165828
  15.3 14.8 %copy-start.6 = (bf16[1024,512]{1,0:T(8,128)(2,1)S(1)}, bf16[1024,512]{1,0:T(8,128)(2,1)}, u32[]{:S(2)}) copy-start(bf16[1024,512]{1,0:T(8,128)(2,1)} %refs_0_.1) | copy-start | bytes 3145732
  15.3 28.0 %collective-permute-start.4 = (bf16[4,512,512]{2,1,0:T(8,128)(2,1)}, bf16[4,512,512]{2,1,0:T(8,128)(2,1)}, u32[]{:S(2)}, u32[]{:S(2)}) collective-permute-start(bf16[4,512,512]{2,1,0:T(8,128)(2,1)} %pad_maximum_fusion.1), channel_id=1, source_target_pairs={{0,1},{1,0},{2,3},{3,2},{4,5},{5,4},{6,7},{7,6},{8,9},{9,8},{10,11... | collective-permute-start | bytes 6291464 | tf_op jit(solution)/shard_map/ppermute | solution.py:38
  52.3 28.4 %copy-start.9 = (bf16[4,128,512]{2,1,0:T(8,128)(2,1)S(1)}, bf16[4,128,512]{2,1,0:T(8,128)(2,1)}, u32[]{:S(2)}) copy-start(bf16[4,128,512]{2,1,0:T(8,128)(2,1)} %constant.77.clone.refs_12_) | copy-start | bytes 1572868
  52.3 28.4 %copy-start.12 = (f32[3,256]{1,0:T(4,128)S(1)}, f32[3,256]{1,0:T(4,128)}, u32[]{:S(2)}) copy-start(f32[3,256]{1,0:T(4,128)} %constant.78.clone.refs_13_.rows) | copy-start | bytes 9220
  52.3 2.7 %collective-permute-start.6 = (bf16[1024,512]{1,0:T(8,128)(2,1)S(1)}, bf16[1024,512]{1,0:T(8,128)(2,1)S(1)}, u32[]{:S(2)}, u32[]{:S(2)}) collective-permute-start(bf16[1024,512]{1,0:T(8,128)(2,1)S(1)} %collective-permute-done.refs_0_), channel_id=1, source_target_pairs={{0,1},{1,0},{2,3},{3,2},{4,5},{5,4},{6,7},{7,6},{8,9},{9,8},{10,11... | collective-permute-start | bytes 3145736 | tf_op jit(solution)/shard_map/ppermute | solution.py:38
  52.4 4.1 %collective-permute-start.7 = (bf16[1024,512]{1,0:T(8,128)(2,1)S(1)}, bf16[1024,512]{1,0:T(8,128)(2,1)S(1)}, u32[]{:S(2)}, u32[]{:S(2)}) collective-permute-start(bf16[1024,512]{1,0:T(8,128)(2,1)S(1)} %collective-permute-done.1.refs_1_), channel_id=1, source_target_pairs={{0,1},{1,0},{2,3},{3,2},{4,5},{5,4},{6,7},{7,6},{8,9},{9,8},{10,11... | collective-permute-start | bytes 3145736 | tf_op jit(solution)/shard_map/ppermute | solution.py:38
  52.9 25.1 %collective-permute-start.5 = (bf16[1024,512]{1,0:T(8,128)(2,1)S(1)}, bf16[1024,512]{1,0:T(8,128)(2,1)S(1)}, u32[]{:S(2)}, u32[]{:S(2)}) collective-permute-start(bf16[1024,512]{1,0:T(8,128)(2,1)S(1)} %collective-permute-done.refs_0_), channel_id=1, source_target_pairs={{0,6},{1,7},{2,0},{3,1},{4,2},{5,3},{6,4},{7,5},{8,14},{9,15},{10,... | collective-permute-start | bytes 3145736 | tf_op jit(solution)/shard_map/ppermute | solution.py:32
  78.0 2.7 %collective-permute-start.8 = (bf16[1024,512]{1,0:T(8,128)(2,1)S(1)}, bf16[1024,512]{1,0:T(8,128)(2,1)S(1)}, u32[]{:S(2)}, u32[]{:S(2)}) collective-permute-start(bf16[1024,512]{1,0:T(8,128)(2,1)S(1)} %collective-permute-done.5.refs_0_), channel_id=1, source_target_pairs={{0,1},{1,0},{2,3},{3,2},{4,5},{5,4},{6,7},{7,6},{8,9},{9,8},{10,11... | collective-permute-start | bytes 3145736 | tf_op jit(solution)/shard_map/ppermute | solution.py:38
  90.1 16.4 %collective-permute-start.9 = (bf16[4,288,128]{2,1,0:T(8,128)(2,1)}, bf16[4,288,128]{2,1,0:T(8,128)(2,1)S(1)}, u32[]{:S(2)}, u32[]{:S(2)}) collective-permute-start(bf16[4,288,128]{2,1,0:T(8,128)(2,1)} %get-tuple-element.56), channel_id=1, source_target_pairs={{0,8},{8,16},{16,24},{1,9},{9,17},{17,25},{2,10},{10,18},{18,26},{... | collective-permute-start | bytes 884744 | tf_op jit(solution)/shard_map/ppermute | solution.py:466
  93.5 13.0 %collective-permute-start.10 = (bf16[4,160,128]{2,1,0:T(8,128)(2,1)S(1)}, bf16[4,160,128]{2,1,0:T(8,128)(2,1)S(1)}, u32[]{:S(2)}, u32[]{:S(2)}) collective-permute-start(bf16[4,160,128]{2,1,0:T(8,128)(2,1)S(1)} %get-tuple-element.50), channel_id=1, source_target_pairs={{0,16},{8,24},{1,17},{9,25},{2,18},{10,26},{3,19},{11,27},{4,20},{... | collective-permute-start | bytes 491528 | tf_op jit(solution)/shard_map/ppermute | solution.py:466
  97.0 9.6 %collective-permute-start.11 = (bf16[4,160,128]{2,1,0:T(8,128)(2,1)S(1)}, bf16[4,160,128]{2,1,0:T(8,128)(2,1)S(1)}, u32[]{:S(2)}, u32[]{:S(2)}) collective-permute-start(bf16[4,160,128]{2,1,0:T(8,128)(2,1)S(1)} %get-tuple-element.50), channel_id=1, source_target_pairs={{0,24},{1,25},{2,26},{3,27},{4,28},{5,29},{6,30},{7,31}} | collective-permute-start | bytes 491528 | tf_op jit(solution)/shard_map/ppermute | solution.py:466
  100.9 5.7 %copy-start.10 = (bf16[4,128,512]{2,1,0:T(8,128)(2,1)S(1)}, bf16[4,128,512]{2,1,0:T(8,128)(2,1)}, u32[]{:S(2)}) copy-start(bf16[4,128,512]{2,1,0:T(8,128)(2,1)} %constant.76.clone.expand) | copy-start | bytes 1572868
  100.9 5.7 %copy-start.11 = (bf16[4,128,256]{2,1,0:T(8,128)(2,1)S(1)}, bf16[4,128,256]{2,1,0:T(8,128)(2,1)}, u32[]{:S(2)}) copy-start(bf16[4,128,256]{2,1,0:T(8,128)(2,1)} %constant.79.clone.pick) | copy-start | bytes 786436
  106.6 10.7 %copy-start.15 = (bf16[512,512]{1,0:T(8,128)(2,1)S(1)}, bf16[512,512]{1,0:T(8,128)(2,1)}, u32[]{:S(2)}) copy-start(bf16[512,512]{1,0:T(8,128)(2,1)} %get-tuple-element.65) | copy-start | bytes 1572868
  106.6 11.1 %copy-start.18 = (bf16[512,512]{1,0:T(8,128)(2,1)S(1)}, bf16[512,512]{1,0:T(8,128)(2,1)}, u32[]{:S(2)}) copy-start(bf16[512,512]{1,0:T(8,128)(2,1)} %get-tuple-element.64) | copy-start | bytes 1572868
  115.2 2.0 %collective-permute-start.12 = (bf16[512,512]{1,0:T(8,128)(2,1)S(1)}, bf16[512,512]{1,0:T(8,128)(2,1)S(1)}, u32[]{:S(2)}, u32[]{:S(2)}) collective-permute-start(bf16[512,512]{1,0:T(8,128)(2,1)S(1)} %get-tuple-element.57), channel_id=1, source_target_pairs={{0,1},{1,0},{2,3},{3,2},{4,5},{5,4},{6,7},{7,6},{8,9},{9,8},{10,11... | collective-permute-start | bytes 1572872 | tf_op jit(solution)/shard_map/ppermute | solution.py:38
  115.3 4.5 %collective-permute-start.16 = (bf16[512,512]{1,0:T(8,128)(2,1)S(1)}, bf16[512,512]{1,0:T(8,128)(2,1)S(1)}, u32[]{:S(2)}, u32[]{:S(2)}) collective-permute-start(bf16[512,512]{1,0:T(8,128)(2,1)S(1)} %get-tuple-element.66), channel_id=1, source_target_pairs={{0,1},{1,0},{2,3},{3,2},{4,5},{5,4},{6,7},{7,6},{8,9},{9,8},{10,11... | collective-permute-start | bytes 1572872 | tf_op jit(solution)/shard_map/ppermute | solution.py:38
  117.7 5.7 %copy-start.16 = (bf16[512,512]{1,0:T(8,128)(2,1)S(1)}, bf16[512,512]{1,0:T(8,128)(2,1)}, u32[]{:S(2)}) copy-start(bf16[512,512]{1,0:T(8,128)(2,1)} %get-tuple-element.63) | copy-start | bytes 1572868
  118.1 16.7 %collective-permute-start.13 = (bf16[512,512]{1,0:T(8,128)(2,1)S(1)}, bf16[512,512]{1,0:T(8,128)(2,1)S(1)}, u32[]{:S(2)}, u32[]{:S(2)}) collective-permute-start(bf16[512,512]{1,0:T(8,128)(2,1)S(1)} %fusion.12), channel_id=1, source_target_pairs={{0,2},{1,3},{2,4},{3,5},{4,6},{5,7},{6,0},{7,1},{8,10},{9,11},{10,... | collective-permute-start | bytes 1572872 | tf_op jit(solution)/shard_map/ppermute | solution.py:32
  120.7 14.1 %copy-start.21 = (bf16[512,512]{1,0:T(8,128)(2,1)S(1)}, bf16[512,512]{1,0:T(8,128)(2,1)}, u32[]{:S(2)}) copy-start(bf16[512,512]{1,0:T(8,128)(2,1)} %get-tuple-element.62) | copy-start | bytes 1572868
  120.7 25.2 %collective-permute-start.17 = (bf16[512,512]{1,0:T(8,128)(2,1)S(1)}, bf16[512,512]{1,0:T(8,128)(2,1)S(1)}, u32[]{:S(2)}, u32[]{:S(2)}) collective-permute-start(bf16[512,512]{1,0:T(8,128)(2,1)S(1)} %fusion.13), channel_id=1, source_target_pairs={{0,6},{1,7},{2,0},{3,1},{4,2},{5,3},{6,4},{7,5},{8,14},{9,15},{10,... | collective-permute-start | bytes 1572872 | tf_op jit(solution)/shard_map/ppermute | solution.py:32
  124.3 23.9 %copy-start.14 = (bf16[512,512]{1,0:T(8,128)(2,1)S(1)}, bf16[512,512]{1,0:T(8,128)(2,1)}, u32[]{:S(2)}) copy-start(bf16[512,512]{1,0:T(8,128)(2,1)} %get-tuple-element.59) | copy-start | bytes 1572868
  135.2 22.1 %collective-permute-start.14 = (bf16[512,512]{1,0:T(8,128)(2,1)S(1)}, bf16[512,512]{1,0:T(8,128)(2,1)S(1)}, u32[]{:S(2)}, u32[]{:S(2)}) collective-permute-start(bf16[512,512]{1,0:T(8,128)(2,1)S(1)} %fusion.8), channel_id=1, source_target_pairs={{0,2},{1,3},{2,4},{3,5},{4,6},{5,7},{6,0},{7,1},{8,10},{9,11},{10,... | collective-permute-start | bytes 1572872 | tf_op jit(solution)/shard_map/ppermute | solution.py:32
  146.4 22.1 %collective-permute-start.18 = (bf16[512,512]{1,0:T(8,128)(2,1)S(1)}, bf16[512,512]{1,0:T(8,128)(2,1)S(1)}, u32[]{:S(2)}, u32[]{:S(2)}) collective-permute-start(bf16[512,512]{1,0:T(8,128)(2,1)S(1)} %fusion.11), channel_id=1, source_target_pairs={{0,6},{1,7},{2,0},{3,1},{4,2},{5,3},{6,4},{7,5},{8,14},{9,15},{10,... | collective-permute-start | bytes 1572872 | tf_op jit(solution)/shard_map/ppermute | solution.py:32
  148.6 31.2 %copy-start.20 = (bf16[512,512]{1,0:T(8,128)(2,1)S(1)}, bf16[512,512]{1,0:T(8,128)(2,1)}, u32[]{:S(2)}) copy-start(bf16[512,512]{1,0:T(8,128)(2,1)} %get-tuple-element.58) | copy-start | bytes 1572868
  157.8 22.1 %collective-permute-start.15 = (bf16[512,512]{1,0:T(8,128)(2,1)S(1)}, bf16[512,512]{1,0:T(8,128)(2,1)S(1)}, u32[]{:S(2)}, u32[]{:S(2)}) collective-permute-start(bf16[512,512]{1,0:T(8,128)(2,1)S(1)} %fusion.7), channel_id=1, source_target_pairs={{0,2},{1,3},{2,4},{3,5},{4,6},{5,7},{6,0},{7,1},{8,10},{9,11},{10,... | collective-permute-start | bytes 1572872 | tf_op jit(solution)/shard_map/ppermute | solution.py:32
  168.9 21.3 %collective-permute-start.19 = (bf16[512,512]{1,0:T(8,128)(2,1)S(1)}, bf16[512,512]{1,0:T(8,128)(2,1)S(1)}, u32[]{:S(2)}, u32[]{:S(2)}) collective-permute-start(bf16[512,512]{1,0:T(8,128)(2,1)S(1)} %fusion.10), channel_id=1, source_target_pairs={{0,6},{1,7},{2,0},{3,1},{4,2},{5,3},{6,4},{7,5},{8,14},{9,15},{10,... | collective-permute-start | bytes 1572872 | tf_op jit(solution)/shard_map/ppermute | solution.py:32
  (11 other events, 41.2 us)

commit v10 on v9

--- a/solution.py
+++ b/solution.py
@@ -407,7 +407,6 @@
     limits = jnp.concatenate([limits, doc_ids[rows - 1 :]])
     first = jnp.sum((docs[None, :] < docs[:, None]).astype(F32), 1, keepdims=True)
     bounds = first.astype(jnp.int32)
-    first_doc = jnp.broadcast_to(docs[:1], (8, HEAD_DIM))
     tail_docs = jnp.broadcast_to((docs[rows - WIN :] + 1.0).astype(BF16)[:, None], (WIN, HEAD_DIM))
     onward = [(i, i + 1) for i in range(blocks - 1)]
     tail_docs = lax.ppermute(tail_docs, "ctx", onward)
@@ -442,10 +441,10 @@
     part = project(place, (0,), [tokens], [tokens_there], weight, 0, widths)
 
     ready = lax.optimization_barrier(
-        (pieces[1], pieces[count - 1], limits, bounds, first_doc, tail_docs, *part, *out_rows)
-    )
-    pieces[1], pieces[count - 1], limits, bounds, first_doc, tail_docs = ready[:6]
-    part, out_rows = ready[6:8], ready[8:]
+        (pieces[1], pieces[count - 1], limits, bounds, tail_docs, *part, *out_rows)
+    )
+    pieces[1], pieces[count - 1], limits, bounds, tail_docs = ready[:5]
+    part, out_rows = ready[5:7], ready[7:]
 
     for n in range(2, count // 2 + 1):
         pieces[n] = ring(pieces[n - 1], -1, count)
@@ -457,7 +456,10 @@
         place, near, mine, [swap(p, count) for p in mine], weight, 0, widths, part
     )
     late = tuple(range(2, count - 1))
-    *mine, fv_part, win_part = lax.optimization_barrier((*[pieces[n] for n in late], *part))
+    first_doc = jnp.broadcast_to(after(docs[:1], *part), (8, HEAD_DIM))
+    *mine, fv_part, win_part, first_doc = lax.optimization_barrier(
+        (*[pieces[n] for n in late], *part, first_doc)
+    )
     theirs = [swap(p, count) for p in mine]
     both, prefix, state, state_and_tail = project_late(
         place, limits, late, mine, theirs, weight, heads, fv_part, win_part, key_map, scale_rows

time: 192 us -> 192 us (level)
  no operation moved by 1% of the time
where the time goes in v10:
time: 192 us
  waiting for transfers between devices  75.7 us (39%)
  Pallas kernels  42.7 us (22%)
  starting transfers between devices  27.2 us (14%)
  local copies, waits for them, and re-layouts  24.6 us (13%)
  other arithmetic  14 us (7%)
  matrix products  7.01 us (4%)
    ppermute x9, waiting for transfers between devices, ring(): lax.ppermute(x, 'head', [(2 * z + c, 2 * ((z + step) % count) + c) for z...  69.7 us
    pallas_call x3, Pallas kernels, project(): pl.pallas_call(functools.partial(project_kernel, len(chips), cuts, before...  24.6 us
    unnamed x46, local copies, waits for them, and re-layouts  14.5 us
    ppermute x9, starting transfers between devices, ring(): lax.ppermute(x, 'head', [(2 * z + c, 2 * ((z + step) % count) + c) for z...  13.9 us
    pallas_call x1, Pallas kernels, project_late(): pl.pallas_call(functools.partial(late_kernel, len(chips)), grid_spec=pltp...  9.43 us
    pallas_call x1, Pallas kernels, mix(): pl.pallas_call(functools.partial(mix_kernel, len(states)), grid_spec=pltp...  8.62 us
    concatenate x1, other arithmetic, shards(): jnp.concatenate([w_value, w_feat, jnp.zeros((w_value.shape[0], fv_columns...  8.39 us
    ppermute x3, starting transfers between devices, shards(): lax.ppermute(state_and_tail if k == 1 else state, 'ctx', [(i, i + k) for...  8.3 us
  transfers between devices with their start and end apart: 20, of which 12 were waited for; matrix products, arithmetic and copies ran while one was open for 15% of the time, Pallas kernels for 13%

profile of v10, /device:TPU:0, one launch (start us, length us, event | category | flops | bytes accessed | tf_op | source)
XLA Modules:
  0.0 191.8 jit_solution(9736633855623257413)
XLA Ops:
  0.5 4.6 %collective-permute-start = (bf16[1024,512]{1,0:T(8,128)(2,1)}, bf16[1024,512]{1,0:T(8,128)(2,1)S(1)}, u32[]{:S(2)}, u32[]{:S(2)}) collective-permute-start(bf16[1024,512]{1,0:T(8,128)(2,1)} %refs_0_.1), channel_id=1, source_target_pairs={{0,6},{1,7},{2,0},{3,1},{4,2},{5,3},{6,4},{7,5},{8,14},{9,15},{10,... | collective-permute-start | bytes 3145736 | tf_op jit(solution)/shard_map/ppermute | solution.py:32
  5.9 3.4 %collective-permute-start.2 = (bf16[64,128]{1,0:T(8,128)(2,1)S(1)}, bf16[64,128]{1,0:T(8,128)(2,1)S(1)}, u32[]{:S(2)}, u32[]{:S(2)}) collective-permute-start(bf16[64,128]{1,0:T(8,128)(2,1)S(1)} %broadcast_in_dim.6), channel_id=1, source_target_pairs={{0,8},{8,16},{16,24},{1,9},{9,17},{17,25},{2,10},{10,18},{18,26},{... | collective-permute-start | bytes 49160 | tf_op jit(solution)/shard_map/ppermute | solution.py:412
  9.5 4.2 %constant_dynamic-slice_fusion = (bf16[512,512]{1,0:T(8,128)(2,1)}, bf16[512,512]{1,0:T(8,128)(2,1)}, bf16[512,512]{1,0:T(8,128)(2,1)}, bf16[1,512,512]{2,1,0:T(...) fusion(bf16[512,4096]{1,0:T(8,128)(2,1)} %param.15, ...), kind=kLoop, calls=%fused_computation.35 | loop fusion | bytes 8388640 | tf_op jit(solution)/shard_map/dynamic_slice | solution.py:425
  13.7 1.6 pad_maximum_fusion.1
  17.5 8.4 %pad_maximum_fusion.refs_2_.refs_4_.refs_5_.refs_3_.refs_6_ = bf16[4096,1792]{1,0:T(8,128)(2,1)} fusion(bf16[4096,1024]{1,0:T(8,128)(2,1)S(1)} %copy-done.13, bf16[4096,128]{1,0:T(8,128)(2,1)} %param.12, bf16[4096,512]{1,0:T(8,128)(2,1)S(1)} %copy-done.22, bf16[1792]{0:T(1024)(128)(2,1)S(1)} %pad.8.clone), kind=kLoop, calls=%fused_computation | loop fusion | flops 58720256 | bytes 28315136 | tf_op jit(solution)/shard_map/concatenate | solution.py:436
  30.1 5.2 %copy-done = bf16[4096,1792]{1,0:T(8,128)(2,1)S(1)} copy-done((bf16[4096,1792]{1,0:T(8,128)(2,1)S(1)}, bf16[4096,1792]{1,0:T(8,128)(2,1)}, u32[]{:S(2)}) %copy-start) | copy-done | bytes 14680088
  36.5 6.8 %shard_map.100 = (f32[1024,768]{1,0:T(8,128)S(1)}, f32[1024,1024]{1,0:T(8,128)S(1)}) custom-call(s32[2]{0:T(128)S(1)} %pad_add_fusion.1.place, bf16[1024,512]{1,0:T(8,128)(2,1)S(1)} %copy-done.6, bf16[1024,512]{1,0:T(8,128)(2,1)S(1)} %copy-done.8, bf16[4096,1792]{1,0:T(8,128)(2,1)S(1)} %copy-done), custom_call_target="tpu_custom_call" | custom-call | tf_op jit(solution)/shard_map/pallas_call | solution.py:108
  43.3 2.9 %dynamic-slice_bitcast_fusion = (bf16[512,512]{1,0:T(8,128)(2,1)}, bf16[512,512]{1,0:T(8,128)(2,1)}, bf16[512,512]{1,0:T(8,128)(2,1)}, bf16[512,512]{1,0:T(8,128)(2,1)}) fusion(bf16[4,512,512]{2,1,0:T(8,128)(2,1)} %collective-permute-done.4, s32[]{:T(128)S(6)} %select_n.61, s32[]{:T(128)S(6)} %select_n.59, s32[]{:T(128)S(6)} %select_n.57, s32[]{:T(128)S(6)} %select_n.55), kind=kLoop, calls=%fused_computation.26 | loop fusion | bytes 4194320 | tf_op jit(solution)/shard_map/jit(dynamic_index_in_dim)/squeeze | solution.py:431
  46.2 5.5 %collective-permute-done.1.refs_1_ = bf16[1024,512]{1,0:T(8,128)(2,1)S(1)} collective-permute-done((bf16[1024,512]{1,0:T(8,128)(2,1)}, bf16[1024,512]{1,0:T(8,128)(2,1)S(1)}, u32[]{:S(2)}, u32[]{:S(2)}) %collective-permute-start.1) | collective-permute-done | bytes 1048608 | tf_op jit(solution)/shard_map/ppermute | solution.py:32
  52.2 1.7 collective-permute-start.5
  54.4 1.5 collective-permute-done.7.refs_3_
  55.9 12.2 %shard_map.101 = (f32[1024,768]{1,0:T(8,128)S(1)}, f32[1024,1024]{1,0:T(8,128)S(1)}) custom-call(s32[2]{0:T(128)S(1)} %pad_add_fusion.1.place, bf16[1024,512]{1,0:T(8,128)(2,1)S(1)} %collective-permute-done.refs_0_, bf16[1024,512]{1,0:T(8,128)(2,1)S(1)} %collective-permute-done.1.refs_1_, bf16[1024,512]{1,0:T(8,128)(2,1)S(1)} %collective-permute-done.6.refs_2_, ...), custom_call_target="tpu_custom_call" | custom-call | tf_op jit(solution)/shard_map/pallas_call | solution.py:108
  68.1 2.0 %copy-done.1 = f32[1024,1024]{1,0:T(8,128)} copy-done((f32[1024,1024]{1,0:T(8,128)}, f32[1024,1024]{1,0:T(8,128)S(1)}, u32[]{:S(2)}) %copy-start.1) | copy-done | bytes 4194328
  70.1 1.7 copy-done.4
  71.8 5.6 %collective-permute-done.5.refs_0_ = bf16[1024,512]{1,0:T(8,128)(2,1)S(1)} collective-permute-done((bf16[1024,512]{1,0:T(8,128)(2,1)S(1)}, bf16[1024,512]{1,0:T(8,128)(2,1)S(1)}, u32[]{:S(2)}, u32[]{:S(2)}) %collective-permute-start.5) | collective-permute-done | bytes 1048608 | tf_op jit(solution)/shard_map/ppermute | solution.py:32
  78.1 2.6 %collective-permute-done.8.refs_1_ = bf16[1024,512]{1,0:T(8,128)(2,1)S(1)} collective-permute-done((bf16[1024,512]{1,0:T(8,128)(2,1)S(1)}, bf16[1024,512]{1,0:T(8,128)(2,1)S(1)}, u32[]{:S(2)}, u32[]{:S(2)}) %collective-permute-start.8) | collective-permute-done | bytes 1048608 | tf_op jit(solution)/shard_map/ppermute | solution.py:38
  80.8 9.4 %shard_map.102 = (bf16[1024,768]{1,0:T(8,128)(2,1)}, f32[4,4,160,128]{3,2,1,0:T(8,128)}, bf16[4,160,128]{2,1,0:T(8,128)(2,1)S(1)}, bf16[4,288,128]{2,1,0:T(8,128)(2,1)}) custom-call(s32[2]{0:T(128)S(1)} %pad_add_fusion.1.place, s32[5]{0:T(128)S(1)} %pad_add_fusion.limits, bf16[1024,512]{1,0:T(8,128)(2,1)S(1)} %collective-permute-done.5.refs_0_, ...), custom_call_target="tpu_custom_call" | custom-call | tf_op jit(solution)/shard_map/pallas_call | solution.py:212
  90.2 3.4 %collective-permute-start.9 = (bf16[4,288,128]{2,1,0:T(8,128)(2,1)}, bf16[4,288,128]{2,1,0:T(8,128)(2,1)S(1)}, u32[]{:S(2)}, u32[]{:S(2)}) collective-permute-start(bf16[4,288,128]{2,1,0:T(8,128)(2,1)} %get-tuple-element.58), channel_id=1, source_target_pairs={{0,8},{8,16},{16,24},{1,9},{9,17},{17,25},{2,10},{10,18},{18,26},{... | collective-permute-start | bytes 884744 | tf_op jit(solution)/shard_map/ppermute | solution.py:468
  93.6 3.4 %collective-permute-start.10 = (bf16[4,160,128]{2,1,0:T(8,128)(2,1)S(1)}, bf16[4,160,128]{2,1,0:T(8,128)(2,1)S(1)}, u32[]{:S(2)}, u32[]{:S(2)}) collective-permute-start(bf16[4,160,128]{2,1,0:T(8,128)(2,1)S(1)} %get-tuple-element.52), channel_id=1, source_target_pairs={{0,16},{8,24},{1,17},{9,25},{2,18},{10,26},{3,19},{11,27},{4,20},{... | collective-permute-start | bytes 491528 | tf_op jit(solution)/shard_map/ppermute | solution.py:468
  98.8 2.2 %copy-done.2 = f32[1024,1024]{1,0:T(8,128)S(1)} copy-done((f32[1024,1024]{1,0:T(8,128)S(1)}, f32[1024,1024]{1,0:T(8,128)}, u32[]{:S(2)}) %copy-start.2) | copy-done | bytes 4194328
  101.0 5.6 %shard_map.103.window = bf16[1024,1024]{1,0:T(8,128)(2,1)S(1)} custom-call(s32[2]{0:T(128)S(1)} %pad_add_fusion.1.place, bf16[1024,512]{1,0:T(8,128)(2,1)S(1)} %collective-permute-done.5.refs_0_, bf16[1024,512]{1,0:T(8,128)(2,1)S(1)} %collective-permute-done.8.refs_1_, bf16[4096,1792]{1,0:T(8,128)(2,1)} %pad_maximum_fusion.refs_2_.refs_4_.refs_5_.refs_3_.refs_6_, ...), custom_call_target="tpu_custom_call" | custom-call | tf_op jit(solution)/shard_map/pallas_call | solution.py:108
  106.7 8.6 %shard_map.104 = (bf16[512,512]{1,0:T(8,128)(2,1)S(1)}, bf16[512,512]{1,0:T(8,128)(2,1)S(1)}) custom-call(s32[5]{0:T(128)S(1)} %pad_add_fusion.limits, bf16[1024,768]{1,0:T(8,128)(2,1)S(1)} %copy-done.3, bf16[1024,768]{1,0:T(8,128)(2,1)S(1)} %copy-done.3, bf16[1024,1024]{1,0:T(8,128)(2,1)S(1)} %shard_map.103.window, s32[1024,1]{1,0:T(8,128)S(1)} %copy.12.bounds, ...), custom_call_target="tpu_custom_call" | custom-call | tf_op jit(solution)/shard_map/pallas_call | solution.py:365
  118.2 1.7 collective-permute-start.13
  120.8 2.2 %collective-permute-start.17 = (bf16[512,512]{1,0:T(8,128)(2,1)S(1)}, bf16[512,512]{1,0:T(8,128)(2,1)S(1)}, u32[]{:S(2)}, u32[]{:S(2)}) collective-permute-start(bf16[512,512]{1,0:T(8,128)(2,1)S(1)} %fusion.13), channel_id=1, source_target_pairs={{0,6},{1,7},{2,0},{3,1},{4,2},{5,3},{6,4},{7,5},{8,14},{9,15},{10,... | collective-permute-start | bytes 1572872 | tf_op jit(solution)/shard_map/ppermute | solution.py:32
  124.8 10.1 %collective-permute-done.13 = bf16[512,512]{1,0:T(8,128)(2,1)S(1)} collective-permute-done((bf16[512,512]{1,0:T(8,128)(2,1)S(1)}, bf16[512,512]{1,0:T(8,128)(2,1)S(1)}, u32[]{:S(2)}, u32[]{:S(2)}) %collective-permute-start.13) | collective-permute-done | bytes 524320 | tf_op jit(solution)/shard_map/ppermute | solution.py:32
  135.4 10.6 %collective-permute-done.17 = bf16[512,512]{1,0:T(8,128)(2,1)S(1)} collective-permute-done((bf16[512,512]{1,0:T(8,128)(2,1)S(1)}, bf16[512,512]{1,0:T(8,128)(2,1)S(1)}, u32[]{:S(2)}, u32[]{:S(2)}) %collective-permute-start.17) | collective-permute-done | bytes 524320 | tf_op jit(solution)/shard_map/ppermute | solution.py:32
  146.5 1.8 collective-permute-start.18
  148.7 8.7 %collective-permute-done.14 = bf16[512,512]{1,0:T(8,128)(2,1)S(1)} collective-permute-done((bf16[512,512]{1,0:T(8,128)(2,1)S(1)}, bf16[512,512]{1,0:T(8,128)(2,1)S(1)}, u32[]{:S(2)}, u32[]{:S(2)}) %collective-permute-start.14) | collective-permute-done | bytes 524320 | tf_op jit(solution)/shard_map/ppermute | solution.py:32
  157.9 10.6 %collective-permute-done.18 = bf16[512,512]{1,0:T(8,128)(2,1)S(1)} collective-permute-done((bf16[512,512]{1,0:T(8,128)(2,1)S(1)}, bf16[512,512]{1,0:T(8,128)(2,1)S(1)}, u32[]{:S(2)}, u32[]{:S(2)}) %collective-permute-start.18) | collective-permute-done | bytes 524320 | tf_op jit(solution)/shard_map/ppermute | solution.py:32
  169.0 1.8 collective-permute-start.19
  171.2 8.7 %collective-permute-done.15 = bf16[512,512]{1,0:T(8,128)(2,1)S(1)} collective-permute-done((bf16[512,512]{1,0:T(8,128)(2,1)S(1)}, bf16[512,512]{1,0:T(8,128)(2,1)S(1)}, u32[]{:S(2)}, u32[]{:S(2)}) %collective-permute-start.15) | collective-permute-done | bytes 524320 | tf_op jit(solution)/shard_map/ppermute | solution.py:32
  180.4 9.9 %collective-permute-done.19 = bf16[512,512]{1,0:T(8,128)(2,1)S(1)} collective-permute-done((bf16[512,512]{1,0:T(8,128)(2,1)S(1)}, bf16[512,512]{1,0:T(8,128)(2,1)S(1)}, u32[]{:S(2)}, u32[]{:S(2)}) %collective-permute-start.19) | collective-permute-done | bytes 524320 | tf_op jit(solution)/shard_map/ppermute | solution.py:32
  (97 shorter events, 22.5 us)
Async XLA Ops:
  0.0 9.4 %collective-permute-start.3 = (bf16[1024,512]{1,0:T(8,128)(2,1)}, bf16[1024,512]{1,0:T(8,128)(2,1)S(1)}, u32[]{:S(2)}, u32[]{:S(2)}) collective-permute-start(bf16[1024,512]{1,0:T(8,128)(2,1)} %refs_0_.1), channel_id=1, source_target_pairs={{0,1},{1,0},{2,3},{3,2},{4,5},{5,4},{6,7},{7,6},{8,9},{9,8},{10,11... | collective-permute-start | bytes 3145736 | tf_op jit(solution)/shard_map/ppermute | solution.py:38
  0.5 45.8 %collective-permute-start = (bf16[1024,512]{1,0:T(8,128)(2,1)}, bf16[1024,512]{1,0:T(8,128)(2,1)S(1)}, u32[]{:S(2)}, u32[]{:S(2)}) collective-permute-start(bf16[1024,512]{1,0:T(8,128)(2,1)} %refs_0_.1), channel_id=1, source_target_pairs={{0,6},{1,7},{2,0},{3,1},{4,2},{5,3},{6,4},{7,5},{8,14},{9,15},{10,... | collective-permute-start | bytes 3145736 | tf_op jit(solution)/shard_map/ppermute | solution.py:32
  5.1 46.7 %collective-permute-start.1 = (bf16[1024,512]{1,0:T(8,128)(2,1)}, bf16[1024,512]{1,0:T(8,128)(2,1)S(1)}, u32[]{:S(2)}, u32[]{:S(2)}) collective-permute-start(bf16[1024,512]{1,0:T(8,128)(2,1)} %refs_0_.1), channel_id=1, source_target_pairs={{0,2},{1,3},{2,4},{3,5},{4,6},{5,7},{6,0},{7,1},{8,10},{9,11},{10,... | collective-permute-start | bytes 3145736 | tf_op jit(solution)/shard_map/ppermute | solution.py:32
  5.9 40.3 %collective-permute-start.2 = (bf16[64,128]{1,0:T(8,128)(2,1)S(1)}, bf16[64,128]{1,0:T(8,128)(2,1)S(1)}, u32[]{:S(2)}, u32[]{:S(2)}) collective-permute-start(bf16[64,128]{1,0:T(8,128)(2,1)S(1)} %broadcast_in_dim.6), channel_id=1, source_target_pairs={{0,8},{8,16},{16,24},{1,9},{9,17},{17,25},{2,10},{10,18},{18,26},{... | collective-permute-start | bytes 49160 | tf_op jit(solution)/shard_map/ppermute | solution.py:412
  9.4 6.6 %copy-start.13 = (bf16[4096,1024]{1,0:T(8,128)(2,1)S(1)}, bf16[4096,1024]{1,0:T(8,128)(2,1)}, u32[]{:S(2)}) copy-start(bf16[4096,1024]{1,0:T(8,128)(2,1)} %param.14) | copy-start | bytes 25165828
  15.3 14.8 %copy-start.6 = (bf16[1024,512]{1,0:T(8,128)(2,1)S(1)}, bf16[1024,512]{1,0:T(8,128)(2,1)}, u32[]{:S(2)}) copy-start(bf16[1024,512]{1,0:T(8,128)(2,1)} %refs_0_.1) | copy-start | bytes 3145732
  15.3 28.0 %collective-permute-start.4 = (bf16[4,512,512]{2,1,0:T(8,128)(2,1)}, bf16[4,512,512]{2,1,0:T(8,128)(2,1)}, u32[]{:S(2)}, u32[]{:S(2)}) collective-permute-start(bf16[4,512,512]{2,1,0:T(8,128)(2,1)} %pad_maximum_fusion.1), channel_id=1, source_target_pairs={{0,1},{1,0},{2,3},{3,2},{4,5},{5,4},{6,7},{7,6},{8,9},{9,8},{10,11... | collective-permute-start | bytes 6291464 | tf_op jit(solution)/shard_map/ppermute | solution.py:38
  51.7 29.1 %copy-start.9 = (bf16[4,128,512]{2,1,0:T(8,128)(2,1)S(1)}, bf16[4,128,512]{2,1,0:T(8,128)(2,1)}, u32[]{:S(2)}) copy-start(bf16[4,128,512]{2,1,0:T(8,128)(2,1)} %constant.77.clone.refs_12_) | copy-start | bytes 1572868
  51.7 29.1 %copy-start.12 = (f32[3,256]{1,0:T(4,128)S(1)}, f32[3,256]{1,0:T(4,128)}, u32[]{:S(2)}) copy-start(f32[3,256]{1,0:T(4,128)} %constant.78.clone.refs_13_.rows) | copy-start | bytes 9220
  51.7 2.7 %collective-permute-start.6 = (bf16[1024,512]{1,0:T(8,128)(2,1)S(1)}, bf16[1024,512]{1,0:T(8,128)(2,1)S(1)}, u32[]{:S(2)}, u32[]{:S(2)}) collective-permute-start(bf16[1024,512]{1,0:T(8,128)(2,1)S(1)} %collective-permute-done.refs_0_), channel_id=1, source_target_pairs={{0,1},{1,0},{2,3},{3,2},{4,5},{5,4},{6,7},{7,6},{8,9},{9,8},{10,11... | collective-permute-start | bytes 3145736 | tf_op jit(solution)/shard_map/ppermute | solution.py:38
  51.7 4.2 %collective-permute-start.7 = (bf16[1024,512]{1,0:T(8,128)(2,1)S(1)}, bf16[1024,512]{1,0:T(8,128)(2,1)S(1)}, u32[]{:S(2)}, u32[]{:S(2)}) collective-permute-start(bf16[1024,512]{1,0:T(8,128)(2,1)S(1)} %collective-permute-done.1.refs_1_), channel_id=1, source_target_pairs={{0,1},{1,0},{2,3},{3,2},{4,5},{5,4},{6,7},{7,6},{8,9},{9,8},{10,11... | collective-permute-start | bytes 3145736 | tf_op jit(solution)/shard_map/ppermute | solution.py:38
  52.2 25.1 %collective-permute-start.5 = (bf16[1024,512]{1,0:T(8,128)(2,1)S(1)}, bf16[1024,512]{1,0:T(8,128)(2,1)S(1)}, u32[]{:S(2)}, u32[]{:S(2)}) collective-permute-start(bf16[1024,512]{1,0:T(8,128)(2,1)S(1)} %collective-permute-done.refs_0_), channel_id=1, source_target_pairs={{0,6},{1,7},{2,0},{3,1},{4,2},{5,3},{6,4},{7,5},{8,14},{9,15},{10,... | collective-permute-start | bytes 3145736 | tf_op jit(solution)/shard_map/ppermute | solution.py:32
  78.1 2.7 %collective-permute-start.8 = (bf16[1024,512]{1,0:T(8,128)(2,1)S(1)}, bf16[1024,512]{1,0:T(8,128)(2,1)S(1)}, u32[]{:S(2)}, u32[]{:S(2)}) collective-permute-start(bf16[1024,512]{1,0:T(8,128)(2,1)S(1)} %collective-permute-done.5.refs_0_), channel_id=1, source_target_pairs={{0,1},{1,0},{2,3},{3,2},{4,5},{5,4},{6,7},{7,6},{8,9},{9,8},{10,11... | collective-permute-start | bytes 3145736 | tf_op jit(solution)/shard_map/ppermute | solution.py:38
  90.2 16.4 %collective-permute-start.9 = (bf16[4,288,128]{2,1,0:T(8,128)(2,1)}, bf16[4,288,128]{2,1,0:T(8,128)(2,1)S(1)}, u32[]{:S(2)}, u32[]{:S(2)}) collective-permute-start(bf16[4,288,128]{2,1,0:T(8,128)(2,1)} %get-tuple-element.58), channel_id=1, source_target_pairs={{0,8},{8,16},{16,24},{1,9},{9,17},{17,25},{2,10},{10,18},{18,26},{... | collective-permute-start | bytes 884744 | tf_op jit(solution)/shard_map/ppermute | solution.py:468
  93.6 13.0 %collective-permute-start.10 = (bf16[4,160,128]{2,1,0:T(8,128)(2,1)S(1)}, bf16[4,160,128]{2,1,0:T(8,128)(2,1)S(1)}, u32[]{:S(2)}, u32[]{:S(2)}) collective-permute-start(bf16[4,160,128]{2,1,0:T(8,128)(2,1)S(1)} %get-tuple-element.52), channel_id=1, source_target_pairs={{0,16},{8,24},{1,17},{9,25},{2,18},{10,26},{3,19},{11,27},{4,20},{... | collective-permute-start | bytes 491528 | tf_op jit(solution)/shard_map/ppermute | solution.py:468
  97.1 9.5 %collective-permute-start.11 = (bf16[4,160,128]{2,1,0:T(8,128)(2,1)S(1)}, bf16[4,160,128]{2,1,0:T(8,128)(2,1)S(1)}, u32[]{:S(2)}, u32[]{:S(2)}) collective-permute-start(bf16[4,160,128]{2,1,0:T(8,128)(2,1)S(1)} %get-tuple-element.52), channel_id=1, source_target_pairs={{0,24},{1,25},{2,26},{3,27},{4,28},{5,29},{6,30},{7,31}} | collective-permute-start | bytes 491528 | tf_op jit(solution)/shard_map/ppermute | solution.py:468
  101.0 5.7 %copy-start.10 = (bf16[4,128,512]{2,1,0:T(8,128)(2,1)S(1)}, bf16[4,128,512]{2,1,0:T(8,128)(2,1)}, u32[]{:S(2)}) copy-start(bf16[4,128,512]{2,1,0:T(8,128)(2,1)} %constant.76.clone.expand) | copy-start | bytes 1572868
  101.0 5.7 %copy-start.11 = (bf16[4,128,256]{2,1,0:T(8,128)(2,1)S(1)}, bf16[4,128,256]{2,1,0:T(8,128)(2,1)}, u32[]{:S(2)}) copy-start(bf16[4,128,256]{2,1,0:T(8,128)(2,1)} %constant.79.clone.pick) | copy-start | bytes 786436
  106.7 10.7 %copy-start.15 = (bf16[512,512]{1,0:T(8,128)(2,1)S(1)}, bf16[512,512]{1,0:T(8,128)(2,1)}, u32[]{:S(2)}) copy-start(bf16[512,512]{1,0:T(8,128)(2,1)} %get-tuple-element.67) | copy-start | bytes 1572868
  106.7 11.1 %copy-start.18 = (bf16[512,512]{1,0:T(8,128)(2,1)S(1)}, bf16[512,512]{1,0:T(8,128)(2,1)}, u32[]{:S(2)}) copy-start(bf16[512,512]{1,0:T(8,128)(2,1)} %get-tuple-element.66) | copy-start | bytes 1572868
  115.3 2.0 %collective-permute-start.12 = (bf16[512,512]{1,0:T(8,128)(2,1)S(1)}, bf16[512,512]{1,0:T(8,128)(2,1)S(1)}, u32[]{:S(2)}, u32[]{:S(2)}) collective-permute-start(bf16[512,512]{1,0:T(8,128)(2,1)S(1)} %get-tuple-element.59), channel_id=1, source_target_pairs={{0,1},{1,0},{2,3},{3,2},{4,5},{5,4},{6,7},{7,6},{8,9},{9,8},{10,11... | collective-permute-start | bytes 1572872 | tf_op jit(solution)/shard_map/ppermute | solution.py:38
  115.4 4.5 %collective-permute-start.16 = (bf16[512,512]{1,0:T(8,128)(2,1)S(1)}, bf16[512,512]{1,0:T(8,128)(2,1)S(1)}, u32[]{:S(2)}, u32[]{:S(2)}) collective-permute-start(bf16[512,512]{1,0:T(8,128)(2,1)S(1)} %get-tuple-element.68), channel_id=1, source_target_pairs={{0,1},{1,0},{2,3},{3,2},{4,5},{5,4},{6,7},{7,6},{8,9},{9,8},{10,11... | collective-permute-start | bytes 1572872 | tf_op jit(solution)/shard_map/ppermute | solution.py:38
  117.8 5.7 %copy-start.16 = (bf16[512,512]{1,0:T(8,128)(2,1)S(1)}, bf16[512,512]{1,0:T(8,128)(2,1)}, u32[]{:S(2)}) copy-start(bf16[512,512]{1,0:T(8,128)(2,1)} %get-tuple-element.65) | copy-start | bytes 1572868
  118.2 16.7 %collective-permute-start.13 = (bf16[512,512]{1,0:T(8,128)(2,1)S(1)}, bf16[512,512]{1,0:T(8,128)(2,1)S(1)}, u32[]{:S(2)}, u32[]{:S(2)}) collective-permute-start(bf16[512,512]{1,0:T(8,128)(2,1)S(1)} %fusion.12), channel_id=1, source_target_pairs={{0,2},{1,3},{2,4},{3,5},{4,6},{5,7},{6,0},{7,1},{8,10},{9,11},{10,... | collective-permute-start | bytes 1572872 | tf_op jit(solution)/shard_map/ppermute | solution.py:32
  120.8 14.1 %copy-start.21 = (bf16[512,512]{1,0:T(8,128)(2,1)S(1)}, bf16[512,512]{1,0:T(8,128)(2,1)}, u32[]{:S(2)}) copy-start(bf16[512,512]{1,0:T(8,128)(2,1)} %get-tuple-element.64) | copy-start | bytes 1572868
  120.8 25.2 %collective-permute-start.17 = (bf16[512,512]{1,0:T(8,128)(2,1)S(1)}, bf16[512,512]{1,0:T(8,128)(2,1)S(1)}, u32[]{:S(2)}, u32[]{:S(2)}) collective-permute-start(bf16[512,512]{1,0:T(8,128)(2,1)S(1)} %fusion.13), channel_id=1, source_target_pairs={{0,6},{1,7},{2,0},{3,1},{4,2},{5,3},{6,4},{7,5},{8,14},{9,15},{10,... | collective-permute-start | bytes 1572872 | tf_op jit(solution)/shard_map/ppermute | solution.py:32
  124.4 23.9 %copy-start.14 = (bf16[512,512]{1,0:T(8,128)(2,1)S(1)}, bf16[512,512]{1,0:T(8,128)(2,1)}, u32[]{:S(2)}) copy-start(bf16[512,512]{1,0:T(8,128)(2,1)} %get-tuple-element.61) | copy-start | bytes 1572868
  135.3 22.1 %collective-permute-start.14 = (bf16[512,512]{1,0:T(8,128)(2,1)S(1)}, bf16[512,512]{1,0:T(8,128)(2,1)S(1)}, u32[]{:S(2)}, u32[]{:S(2)}) collective-permute-start(bf16[512,512]{1,0:T(8,128)(2,1)S(1)} %fusion.8), channel_id=1, source_target_pairs={{0,2},{1,3},{2,4},{3,5},{4,6},{5,7},{6,0},{7,1},{8,10},{9,11},{10,... | collective-permute-start | bytes 1572872 | tf_op jit(solution)/shard_map/ppermute | solution.py:32
  146.5 22.1 %collective-permute-start.18 = (bf16[512,512]{1,0:T(8,128)(2,1)S(1)}, bf16[512,512]{1,0:T(8,128)(2,1)S(1)}, u32[]{:S(2)}, u32[]{:S(2)}) collective-permute-start(bf16[512,512]{1,0:T(8,128)(2,1)S(1)} %fusion.11), channel_id=1, source_target_pairs={{0,6},{1,7},{2,0},{3,1},{4,2},{5,3},{6,4},{7,5},{8,14},{9,15},{10,... | collective-permute-start | bytes 1572872 | tf_op jit(solution)/shard_map/ppermute | solution.py:32
  148.7 31.2 %copy-start.20 = (bf16[512,512]{1,0:T(8,128)(2,1)S(1)}, bf16[512,512]{1,0:T(8,128)(2,1)}, u32[]{:S(2)}) copy-start(bf16[512,512]{1,0:T(8,128)(2,1)} %get-tuple-element.60) | copy-start | bytes 1572868
  157.9 22.1 %collective-permute-start.15 = (bf16[512,512]{1,0:T(8,128)(2,1)S(1)}, bf16[512,512]{1,0:T(8,128)(2,1)S(1)}, u32[]{:S(2)}, u32[]{:S(2)}) collective-permute-start(bf16[512,512]{1,0:T(8,128)(2,1)S(1)} %fusion.7), channel_id=1, source_target_pairs={{0,2},{1,3},{2,4},{3,5},{4,6},{5,7},{6,0},{7,1},{8,10},{9,11},{10,... | collective-permute-start | bytes 1572872 | tf_op jit(solution)/shard_map/ppermute | solution.py:32
  169.0 21.3 %collective-permute-start.19 = (bf16[512,512]{1,0:T(8,128)(2,1)S(1)}, bf16[512,512]{1,0:T(8,128)(2,1)S(1)}, u32[]{:S(2)}, u32[]{:S(2)}) collective-permute-start(bf16[512,512]{1,0:T(8,128)(2,1)S(1)} %fusion.10), channel_id=1, source_target_pairs={{0,6},{1,7},{2,0},{3,1},{4,2},{5,3},{6,4},{7,5},{8,14},{9,15},{10,... | collective-permute-start | bytes 1572872 | tf_op jit(solution)/shard_map/ppermute | solution.py:32
  (11 other events, 41.2 us)

commit v11 on v9

--- a/solution.py
+++ b/solution.py
@@ -311,7 +311,7 @@
     score = dots * (dots * (0.5 / FEAT) + FEAT**-0.5) + 1.0
     score = jnp.where(good, score, 0.0).astype(BF16)
 
-    same = jnp.where(tail_docs[...].astype(F32) == first_doc[0:1, :] + 1.0, 1.0, 0.0)
+    same = jnp.where(tail_docs[...].astype(F32) == first_doc[0:1, 0:1] + 1.0, 1.0, 0.0)
     in_tail = jnp.sum(same, 0, keepdims=True)[:, 0:1].astype(jnp.int32)
     tiles = []
     for n in range(count // TILE):
@@ -332,7 +332,7 @@
     incoming = jnp.zeros((STATE, HEAD_DIM), F32)
     for k in range(shifts):
         sent = states[k][0, :STATE].astype(F32)
-        wanted = (sent[STATE - 1 :] == first_doc[0:1, :] + 1.0) & unmarked
+        wanted = (sent[STATE - 1 :] == first_doc[0:1, 0:1] + 1.0) & unmarked
         incoming += jnp.where(wanted, sent, 0.0)
     linear = []
     for n in range(chunks):
@@ -407,7 +407,7 @@
     limits = jnp.concatenate([limits, doc_ids[rows - 1 :]])
     first = jnp.sum((docs[None, :] < docs[:, None]).astype(F32), 1, keepdims=True)
     bounds = first.astype(jnp.int32)
-    first_doc = jnp.broadcast_to(docs[:1], (8, HEAD_DIM))
+    first_doc = docs.reshape(-1, LANES)
     tail_docs = jnp.broadcast_to((docs[rows - WIN :] + 1.0).astype(BF16)[:, None], (WIN, HEAD_DIM))
     onward = [(i, i + 1) for i in range(blocks - 1)]
     tail_docs = lax.ppermute(tail_docs, "ctx", onward)

time: 192 us -> 192 us (level)
  no operation moved by 1% of the time
where the time goes in v11:
time: 192 us; the launch traced here: 191 us
  waiting for transfers between devices  76 us (40%)
  Pallas kernels  42.8 us (22%)
  starting transfers between devices  27.1 us (14%)
  local copies, waits for them, and re-layouts  23.8 us (12%)
  other arithmetic  13.9 us (7%)
  matrix products  7.01 us (4%)
    ppermute x9, waiting for transfers between devices, ring(): lax.ppermute(x, 'head', [(2 * z + c, 2 * ((z + step) % count) + c) for z...  70 us
    pallas_call x3, Pallas kernels, project(): pl.pallas_call(functools.partial(project_kernel, len(chips), cuts, before...  24.6 us
    unnamed x46, local copies, waits for them, and re-layouts  14.5 us
    ppermute x9, starting transfers between devices, ring(): lax.ppermute(x, 'head', [(2 * z + c, 2 * ((z + step) % count) + c) for z...  13.9 us
    pallas_call x1, Pallas kernels, project_late(): pl.pallas_call(functools.partial(late_kernel, len(chips)), grid_spec=pltp...  9.43 us
    pallas_call x1, Pallas kernels, mix(): pl.pallas_call(functools.partial(mix_kernel, len(states)), grid_spec=pltp...  8.76 us
    concatenate x1, other arithmetic, shards(): jnp.concatenate([w_value, w_feat, jnp.zeros((w_value.shape[0], fv_columns...  8.39 us
    ppermute x3, starting transfers between devices, shards(): lax.ppermute(state_and_tail if k == 1 else state, 'ctx', [(i, i + k) for...  8.3 us
  transfers between devices with their start and end apart: 20, of which 12 were waited for; matrix products, arithmetic and copies ran while one was open for 15% of the time, Pallas kernels for 13%

profile of v11, /device:TPU:0, one launch (start us, length us, event | category | flops | bytes accessed | tf_op | source)
XLA Modules:
  0.0 191.2 jit_solution(5812593351179232231)
XLA Ops:
  0.5 4.6 %collective-permute-start = (bf16[1024,512]{1,0:T(8,128)(2,1)}, bf16[1024,512]{1,0:T(8,128)(2,1)S(1)}, u32[]{:S(2)}, u32[]{:S(2)}) collective-permute-start(bf16[1024,512]{1,0:T(8,128)(2,1)} %refs_0_.1), channel_id=1, source_target_pairs={{0,6},{1,7},{2,0},{3,1},{4,2},{5,3},{6,4},{7,5},{8,14},{9,15},{10,... | collective-permute-start | bytes 3145736 | tf_op jit(solution)/shard_map/ppermute | solution.py:32
  5.9 3.4 %collective-permute-start.2 = (bf16[64,128]{1,0:T(8,128)(2,1)S(1)}, bf16[64,128]{1,0:T(8,128)(2,1)S(1)}, u32[]{:S(2)}, u32[]{:S(2)}) collective-permute-start(bf16[64,128]{1,0:T(8,128)(2,1)S(1)} %broadcast_in_dim.4), channel_id=1, source_target_pairs={{0,8},{8,16},{16,24},{1,9},{9,17},{17,25},{2,10},{10,18},{18,26},{... | collective-permute-start | bytes 49160 | tf_op jit(solution)/shard_map/ppermute | solution.py:413
  9.5 4.2 %constant_dynamic-slice_fusion = (bf16[512,512]{1,0:T(8,128)(2,1)}, bf16[512,512]{1,0:T(8,128)(2,1)}, bf16[512,512]{1,0:T(8,128)(2,1)}, bf16[1,512,512]{2,1,0:T(...) fusion(bf16[512,4096]{1,0:T(8,128)(2,1)} %param.15, ...), kind=kLoop, calls=%fused_computation.35 | loop fusion | bytes 8388640 | tf_op jit(solution)/shard_map/dynamic_slice | solution.py:426
  13.7 1.6 pad_maximum_fusion.1
  17.5 8.4 %pad_maximum_fusion.refs_2_.refs_4_.refs_5_.refs_3_.refs_6_ = bf16[4096,1792]{1,0:T(8,128)(2,1)} fusion(bf16[4096,1024]{1,0:T(8,128)(2,1)S(1)} %copy-done.13, bf16[4096,128]{1,0:T(8,128)(2,1)} %param.12, bf16[4096,512]{1,0:T(8,128)(2,1)S(1)} %copy-done.22, bf16[1792]{0:T(1024)(128)(2,1)S(1)} %pad.8.clone), kind=kLoop, calls=%fused_computation | loop fusion | flops 58720256 | bytes 28315136 | tf_op jit(solution)/shard_map/concatenate | solution.py:437
  29.9 5.2 %copy-done = bf16[4096,1792]{1,0:T(8,128)(2,1)S(1)} copy-done((bf16[4096,1792]{1,0:T(8,128)(2,1)S(1)}, bf16[4096,1792]{1,0:T(8,128)(2,1)}, u32[]{:S(2)}) %copy-start) | copy-done | bytes 14680088
  36.3 6.8 %shard_map.100 = (f32[1024,768]{1,0:T(8,128)S(1)}, f32[1024,1024]{1,0:T(8,128)S(1)}) custom-call(s32[2]{0:T(128)S(1)} %pad_add_fusion.1.place, bf16[1024,512]{1,0:T(8,128)(2,1)S(1)} %copy-done.6, bf16[1024,512]{1,0:T(8,128)(2,1)S(1)} %copy-done.8, bf16[4096,1792]{1,0:T(8,128)(2,1)S(1)} %copy-done), custom_call_target="tpu_custom_call" | custom-call | tf_op jit(solution)/shard_map/pallas_call | solution.py:108
  43.1 2.9 %dynamic-slice_bitcast_fusion = (bf16[512,512]{1,0:T(8,128)(2,1)}, bf16[512,512]{1,0:T(8,128)(2,1)}, bf16[512,512]{1,0:T(8,128)(2,1)}, bf16[512,512]{1,0:T(8,128)(2,1)}) fusion(bf16[4,512,512]{2,1,0:T(8,128)(2,1)} %collective-permute-done.4, s32[]{:T(128)S(6)} %select_n.61, s32[]{:T(128)S(6)} %select_n.59, s32[]{:T(128)S(6)} %select_n.57, s32[]{:T(128)S(6)} %select_n.55), kind=kLoop, calls=%fused_computation.26 | loop fusion | bytes 4194320 | tf_op jit(solution)/shard_map/jit(dynamic_index_in_dim)/squeeze | solution.py:432
  46.0 5.7 %collective-permute-done.1.refs_1_ = bf16[1024,512]{1,0:T(8,128)(2,1)S(1)} collective-permute-done((bf16[1024,512]{1,0:T(8,128)(2,1)}, bf16[1024,512]{1,0:T(8,128)(2,1)S(1)}, u32[]{:S(2)}, u32[]{:S(2)}) %collective-permute-start.1) | collective-permute-done | bytes 1048608 | tf_op jit(solution)/shard_map/ppermute | solution.py:32
  52.2 1.7 collective-permute-start.5
  54.4 1.5 collective-permute-done.7.refs_3_
  55.9 12.2 %shard_map.101 = (f32[1024,768]{1,0:T(8,128)S(1)}, f32[1024,1024]{1,0:T(8,128)S(1)}) custom-call(s32[2]{0:T(128)S(1)} %pad_add_fusion.1.place, bf16[1024,512]{1,0:T(8,128)(2,1)S(1)} %collective-permute-done.refs_0_, bf16[1024,512]{1,0:T(8,128)(2,1)S(1)} %collective-permute-done.1.refs_1_, bf16[1024,512]{1,0:T(8,128)(2,1)S(1)} %collective-permute-done.6.refs_2_, ...), custom_call_target="tpu_custom_call" | custom-call | tf_op jit(solution)/shard_map/pallas_call | solution.py:108
  68.1 2.0 %copy-done.1 = f32[1024,1024]{1,0:T(8,128)} copy-done((f32[1024,1024]{1,0:T(8,128)}, f32[1024,1024]{1,0:T(8,128)S(1)}, u32[]{:S(2)}) %copy-start.1) | copy-done | bytes 4194328
  70.1 1.7 copy-done.4
  71.8 5.6 %collective-permute-done.5.refs_0_ = bf16[1024,512]{1,0:T(8,128)(2,1)S(1)} collective-permute-done((bf16[1024,512]{1,0:T(8,128)(2,1)S(1)}, bf16[1024,512]{1,0:T(8,128)(2,1)S(1)}, u32[]{:S(2)}, u32[]{:S(2)}) %collective-permute-start.5) | collective-permute-done | bytes 1048608 | tf_op jit(solution)/shard_map/ppermute | solution.py:32
  77.4 2.7 %collective-permute-done.8.refs_1_ = bf16[1024,512]{1,0:T(8,128)(2,1)S(1)} collective-permute-done((bf16[1024,512]{1,0:T(8,128)(2,1)S(1)}, bf16[1024,512]{1,0:T(8,128)(2,1)S(1)}, u32[]{:S(2)}, u32[]{:S(2)}) %collective-permute-start.8) | collective-permute-done | bytes 1048608 | tf_op jit(solution)/shard_map/ppermute | solution.py:38
  80.0 9.4 %shard_map.102 = (bf16[1024,768]{1,0:T(8,128)(2,1)}, f32[4,4,160,128]{3,2,1,0:T(8,128)}, bf16[4,160,128]{2,1,0:T(8,128)(2,1)S(1)}, bf16[4,288,128]{2,1,0:T(8,128)(2,1)}) custom-call(s32[2]{0:T(128)S(1)} %pad_add_fusion.1.place, s32[5]{0:T(128)S(1)} %pad_add_fusion.limits, bf16[1024,512]{1,0:T(8,128)(2,1)S(1)} %collective-permute-done.5.refs_0_, ...), custom_call_target="tpu_custom_call" | custom-call | tf_op jit(solution)/shard_map/pallas_call | solution.py:212
  89.5 3.4 %collective-permute-start.9 = (bf16[4,288,128]{2,1,0:T(8,128)(2,1)}, bf16[4,288,128]{2,1,0:T(8,128)(2,1)S(1)}, u32[]{:S(2)}, u32[]{:S(2)}) collective-permute-start(bf16[4,288,128]{2,1,0:T(8,128)(2,1)} %get-tuple-element.56), channel_id=1, source_target_pairs={{0,8},{8,16},{16,24},{1,9},{9,17},{17,25},{2,10},{10,18},{18,26},{... | collective-permute-start | bytes 884744 | tf_op jit(solution)/shard_map/ppermute | solution.py:466
  92.9 3.4 %collective-permute-start.10 = (bf16[4,160,128]{2,1,0:T(8,128)(2,1)S(1)}, bf16[4,160,128]{2,1,0:T(8,128)(2,1)S(1)}, u32[]{:S(2)}, u32[]{:S(2)}) collective-permute-start(bf16[4,160,128]{2,1,0:T(8,128)(2,1)S(1)} %get-tuple-element.50), channel_id=1, source_target_pairs={{0,16},{8,24},{1,17},{9,25},{2,18},{10,26},{3,19},{11,27},{4,20},{... | collective-permute-start | bytes 491528 | tf_op jit(solution)/shard_map/ppermute | solution.py:466
  98.0 2.2 %copy-done.2 = f32[1024,1024]{1,0:T(8,128)S(1)} copy-done((f32[1024,1024]{1,0:T(8,128)S(1)}, f32[1024,1024]{1,0:T(8,128)}, u32[]{:S(2)}) %copy-start.2) | copy-done | bytes 4194328
  100.2 5.6 %shard_map.103.window = bf16[1024,1024]{1,0:T(8,128)(2,1)S(1)} custom-call(s32[2]{0:T(128)S(1)} %pad_add_fusion.1.place, bf16[1024,512]{1,0:T(8,128)(2,1)S(1)} %collective-permute-done.5.refs_0_, bf16[1024,512]{1,0:T(8,128)(2,1)S(1)} %collective-permute-done.8.refs_1_, bf16[4096,1792]{1,0:T(8,128)(2,1)} %pad_maximum_fusion.refs_2_.refs_4_.refs_5_.refs_3_.refs_6_, ...), custom_call_target="tpu_custom_call" | custom-call | tf_op jit(solution)/shard_map/pallas_call | solution.py:108
  105.9 8.8 %shard_map.104 = (bf16[512,512]{1,0:T(8,128)(2,1)S(1)}, bf16[512,512]{1,0:T(8,128)(2,1)S(1)}) custom-call(s32[5]{0:T(128)S(1)} %pad_add_fusion.limits, bf16[1024,768]{1,0:T(8,128)(2,1)S(1)} %copy-done.3, bf16[1024,768]{1,0:T(8,128)(2,1)S(1)} %copy-done.3, bf16[1024,1024]{1,0:T(8,128)(2,1)S(1)} %shard_map.103.window, s32[1024,1]{1,0:T(8,128)S(1)} %copy.12.bounds, ...), custom_call_target="tpu_custom_call" | custom-call | tf_op jit(solution)/shard_map/pallas_call | solution.py:365
  117.6 1.7 collective-permute-start.13
  120.2 2.3 %collective-permute-start.17 = (bf16[512,512]{1,0:T(8,128)(2,1)S(1)}, bf16[512,512]{1,0:T(8,128)(2,1)S(1)}, u32[]{:S(2)}, u32[]{:S(2)}) collective-permute-start(bf16[512,512]{1,0:T(8,128)(2,1)S(1)} %fusion.13), channel_id=1, source_target_pairs={{0,6},{1,7},{2,0},{3,1},{4,2},{5,3},{6,4},{7,5},{8,14},{9,15},{10,... | collective-permute-start | bytes 1572872 | tf_op jit(solution)/shard_map/ppermute | solution.py:32
  124.2 10.1 %collective-permute-done.13 = bf16[512,512]{1,0:T(8,128)(2,1)S(1)} collective-permute-done((bf16[512,512]{1,0:T(8,128)(2,1)S(1)}, bf16[512,512]{1,0:T(8,128)(2,1)S(1)}, u32[]{:S(2)}, u32[]{:S(2)}) %collective-permute-start.13) | collective-permute-done | bytes 524320 | tf_op jit(solution)/shard_map/ppermute | solution.py:32
  134.8 10.6 %collective-permute-done.17 = bf16[512,512]{1,0:T(8,128)(2,1)S(1)} collective-permute-done((bf16[512,512]{1,0:T(8,128)(2,1)S(1)}, bf16[512,512]{1,0:T(8,128)(2,1)S(1)}, u32[]{:S(2)}, u32[]{:S(2)}) %collective-permute-start.17) | collective-permute-done | bytes 524320 | tf_op jit(solution)/shard_map/ppermute | solution.py:32
  145.9 1.8 collective-permute-start.18
  148.1 8.7 %collective-permute-done.14 = bf16[512,512]{1,0:T(8,128)(2,1)S(1)} collective-permute-done((bf16[512,512]{1,0:T(8,128)(2,1)S(1)}, bf16[512,512]{1,0:T(8,128)(2,1)S(1)}, u32[]{:S(2)}, u32[]{:S(2)}) %collective-permute-start.14) | collective-permute-done | bytes 524320 | tf_op jit(solution)/shard_map/ppermute | solution.py:32
  157.3 10.6 %collective-permute-done.18 = bf16[512,512]{1,0:T(8,128)(2,1)S(1)} collective-permute-done((bf16[512,512]{1,0:T(8,128)(2,1)S(1)}, bf16[512,512]{1,0:T(8,128)(2,1)S(1)}, u32[]{:S(2)}, u32[]{:S(2)}) %collective-permute-start.18) | collective-permute-done | bytes 524320 | tf_op jit(solution)/shard_map/ppermute | solution.py:32
  168.4 1.8 collective-permute-start.19
  170.6 8.7 %collective-permute-done.15 = bf16[512,512]{1,0:T(8,128)(2,1)S(1)} collective-permute-done((bf16[512,512]{1,0:T(8,128)(2,1)S(1)}, bf16[512,512]{1,0:T(8,128)(2,1)S(1)}, u32[]{:S(2)}, u32[]{:S(2)}) %collective-permute-start.15) | collective-permute-done | bytes 524320 | tf_op jit(solution)/shard_map/ppermute | solution.py:32
  179.8 9.9 %collective-permute-done.19 = bf16[512,512]{1,0:T(8,128)(2,1)S(1)} collective-permute-done((bf16[512,512]{1,0:T(8,128)(2,1)S(1)}, bf16[512,512]{1,0:T(8,128)(2,1)S(1)}, u32[]{:S(2)}, u32[]{:S(2)}) %collective-permute-start.19) | collective-permute-done | bytes 524320 | tf_op jit(solution)/shard_map/ppermute | solution.py:32
  (96 shorter events, 21.5 us)
Async XLA Ops:
  0.0 9.4 %collective-permute-start.3 = (bf16[1024,512]{1,0:T(8,128)(2,1)}, bf16[1024,512]{1,0:T(8,128)(2,1)S(1)}, u32[]{:S(2)}, u32[]{:S(2)}) collective-permute-start(bf16[1024,512]{1,0:T(8,128)(2,1)} %refs_0_.1), channel_id=1, source_target_pairs={{0,1},{1,0},{2,3},{3,2},{4,5},{5,4},{6,7},{7,6},{8,9},{9,8},{10,11... | collective-permute-start | bytes 3145736 | tf_op jit(solution)/shard_map/ppermute | solution.py:38
  0.5 45.5 %collective-permute-start = (bf16[1024,512]{1,0:T(8,128)(2,1)}, bf16[1024,512]{1,0:T(8,128)(2,1)S(1)}, u32[]{:S(2)}, u32[]{:S(2)}) collective-permute-start(bf16[1024,512]{1,0:T(8,128)(2,1)} %refs_0_.1), channel_id=1, source_target_pairs={{0,6},{1,7},{2,0},{3,1},{4,2},{5,3},{6,4},{7,5},{8,14},{9,15},{10,... | collective-permute-start | bytes 3145736 | tf_op jit(solution)/shard_map/ppermute | solution.py:32
  5.1 46.7 %collective-permute-start.1 = (bf16[1024,512]{1,0:T(8,128)(2,1)}, bf16[1024,512]{1,0:T(8,128)(2,1)S(1)}, u32[]{:S(2)}, u32[]{:S(2)}) collective-permute-start(bf16[1024,512]{1,0:T(8,128)(2,1)} %refs_0_.1), channel_id=1, source_target_pairs={{0,2},{1,3},{2,4},{3,5},{4,6},{5,7},{6,0},{7,1},{8,10},{9,11},{10,... | collective-permute-start | bytes 3145736 | tf_op jit(solution)/shard_map/ppermute | solution.py:32
  5.9 40.1 %collective-permute-start.2 = (bf16[64,128]{1,0:T(8,128)(2,1)S(1)}, bf16[64,128]{1,0:T(8,128)(2,1)S(1)}, u32[]{:S(2)}, u32[]{:S(2)}) collective-permute-start(bf16[64,128]{1,0:T(8,128)(2,1)S(1)} %broadcast_in_dim.4), channel_id=1, source_target_pairs={{0,8},{8,16},{16,24},{1,9},{9,17},{17,25},{2,10},{10,18},{18,26},{... | collective-permute-start | bytes 49160 | tf_op jit(solution)/shard_map/ppermute | solution.py:413
  9.4 6.6 %copy-start.13 = (bf16[4096,1024]{1,0:T(8,128)(2,1)S(1)}, bf16[4096,1024]{1,0:T(8,128)(2,1)}, u32[]{:S(2)}) copy-start(bf16[4096,1024]{1,0:T(8,128)(2,1)} %param.14) | copy-start | bytes 25165828
  15.3 14.6 %copy-start.6 = (bf16[1024,512]{1,0:T(8,128)(2,1)S(1)}, bf16[1024,512]{1,0:T(8,128)(2,1)}, u32[]{:S(2)}) copy-start(bf16[1024,512]{1,0:T(8,128)(2,1)} %refs_0_.1) | copy-start | bytes 3145732
  15.3 27.8 %collective-permute-start.4 = (bf16[4,512,512]{2,1,0:T(8,128)(2,1)}, bf16[4,512,512]{2,1,0:T(8,128)(2,1)}, u32[]{:S(2)}, u32[]{:S(2)}) collective-permute-start(bf16[4,512,512]{2,1,0:T(8,128)(2,1)} %pad_maximum_fusion.1), channel_id=1, source_target_pairs={{0,1},{1,0},{2,3},{3,2},{4,5},{5,4},{6,7},{7,6},{8,9},{9,8},{10,11... | collective-permute-start | bytes 6291464 | tf_op jit(solution)/shard_map/ppermute | solution.py:38
  51.7 28.3 %copy-start.9 = (bf16[4,128,512]{2,1,0:T(8,128)(2,1)S(1)}, bf16[4,128,512]{2,1,0:T(8,128)(2,1)}, u32[]{:S(2)}) copy-start(bf16[4,128,512]{2,1,0:T(8,128)(2,1)} %constant.77.clone.refs_12_) | copy-start | bytes 1572868
  51.7 28.3 %copy-start.12 = (f32[3,256]{1,0:T(4,128)S(1)}, f32[3,256]{1,0:T(4,128)}, u32[]{:S(2)}) copy-start(f32[3,256]{1,0:T(4,128)} %constant.78.clone.refs_13_.rows) | copy-start | bytes 9220
  51.7 2.7 %collective-permute-start.6 = (bf16[1024,512]{1,0:T(8,128)(2,1)S(1)}, bf16[1024,512]{1,0:T(8,128)(2,1)S(1)}, u32[]{:S(2)}, u32[]{:S(2)}) collective-permute-start(bf16[1024,512]{1,0:T(8,128)(2,1)S(1)} %collective-permute-done.refs_0_), channel_id=1, source_target_pairs={{0,1},{1,0},{2,3},{3,2},{4,5},{5,4},{6,7},{7,6},{8,9},{9,8},{10,11... | collective-permute-start | bytes 3145736 | tf_op jit(solution)/shard_map/ppermute | solution.py:38
  51.7 4.2 %collective-permute-start.7 = (bf16[1024,512]{1,0:T(8,128)(2,1)S(1)}, bf16[1024,512]{1,0:T(8,128)(2,1)S(1)}, u32[]{:S(2)}, u32[]{:S(2)}) collective-permute-start(bf16[1024,512]{1,0:T(8,128)(2,1)S(1)} %collective-permute-done.1.refs_1_), channel_id=1, source_target_pairs={{0,1},{1,0},{2,3},{3,2},{4,5},{5,4},{6,7},{7,6},{8,9},{9,8},{10,11... | collective-permute-start | bytes 3145736 | tf_op jit(solution)/shard_map/ppermute | solution.py:38
  52.2 25.1 %collective-permute-start.5 = (bf16[1024,512]{1,0:T(8,128)(2,1)S(1)}, bf16[1024,512]{1,0:T(8,128)(2,1)S(1)}, u32[]{:S(2)}, u32[]{:S(2)}) collective-permute-start(bf16[1024,512]{1,0:T(8,128)(2,1)S(1)} %collective-permute-done.refs_0_), channel_id=1, source_target_pairs={{0,6},{1,7},{2,0},{3,1},{4,2},{5,3},{6,4},{7,5},{8,14},{9,15},{10,... | collective-permute-start | bytes 3145736 | tf_op jit(solution)/shard_map/ppermute | solution.py:32
  77.4 2.7 %collective-permute-start.8 = (bf16[1024,512]{1,0:T(8,128)(2,1)S(1)}, bf16[1024,512]{1,0:T(8,128)(2,1)S(1)}, u32[]{:S(2)}, u32[]{:S(2)}) collective-permute-start(bf16[1024,512]{1,0:T(8,128)(2,1)S(1)} %collective-permute-done.5.refs_0_), channel_id=1, source_target_pairs={{0,1},{1,0},{2,3},{3,2},{4,5},{5,4},{6,7},{7,6},{8,9},{9,8},{10,11... | collective-permute-start | bytes 3145736 | tf_op jit(solution)/shard_map/ppermute | solution.py:38
  89.5 16.4 %collective-permute-start.9 = (bf16[4,288,128]{2,1,0:T(8,128)(2,1)}, bf16[4,288,128]{2,1,0:T(8,128)(2,1)S(1)}, u32[]{:S(2)}, u32[]{:S(2)}) collective-permute-start(bf16[4,288,128]{2,1,0:T(8,128)(2,1)} %get-tuple-element.56), channel_id=1, source_target_pairs={{0,8},{8,16},{16,24},{1,9},{9,17},{17,25},{2,10},{10,18},{18,26},{... | collective-permute-start | bytes 884744 | tf_op jit(solution)/shard_map/ppermute | solution.py:466
  92.9 13.0 %collective-permute-start.10 = (bf16[4,160,128]{2,1,0:T(8,128)(2,1)S(1)}, bf16[4,160,128]{2,1,0:T(8,128)(2,1)S(1)}, u32[]{:S(2)}, u32[]{:S(2)}) collective-permute-start(bf16[4,160,128]{2,1,0:T(8,128)(2,1)S(1)} %get-tuple-element.50), channel_id=1, source_target_pairs={{0,16},{8,24},{1,17},{9,25},{2,18},{10,26},{3,19},{11,27},{4,20},{... | collective-permute-start | bytes 491528 | tf_op jit(solution)/shard_map/ppermute | solution.py:466
  96.3 9.6 %collective-permute-start.11 = (bf16[4,160,128]{2,1,0:T(8,128)(2,1)S(1)}, bf16[4,160,128]{2,1,0:T(8,128)(2,1)S(1)}, u32[]{:S(2)}, u32[]{:S(2)}) collective-permute-start(bf16[4,160,128]{2,1,0:T(8,128)(2,1)S(1)} %get-tuple-element.50), channel_id=1, source_target_pairs={{0,24},{1,25},{2,26},{3,27},{4,28},{5,29},{6,30},{7,31}} | collective-permute-start | bytes 491528 | tf_op jit(solution)/shard_map/ppermute | solution.py:466
  100.2 5.7 %copy-start.10 = (bf16[4,128,512]{2,1,0:T(8,128)(2,1)S(1)}, bf16[4,128,512]{2,1,0:T(8,128)(2,1)}, u32[]{:S(2)}) copy-start(bf16[4,128,512]{2,1,0:T(8,128)(2,1)} %constant.76.clone.expand) | copy-start | bytes 1572868
  100.2 5.7 %copy-start.11 = (bf16[4,128,256]{2,1,0:T(8,128)(2,1)S(1)}, bf16[4,128,256]{2,1,0:T(8,128)(2,1)}, u32[]{:S(2)}) copy-start(bf16[4,128,256]{2,1,0:T(8,128)(2,1)} %constant.79.clone.pick) | copy-start | bytes 786436
  105.9 10.8 %copy-start.15 = (bf16[512,512]{1,0:T(8,128)(2,1)S(1)}, bf16[512,512]{1,0:T(8,128)(2,1)}, u32[]{:S(2)}) copy-start(bf16[512,512]{1,0:T(8,128)(2,1)} %get-tuple-element.65) | copy-start | bytes 1572868
  105.9 11.2 %copy-start.18 = (bf16[512,512]{1,0:T(8,128)(2,1)S(1)}, bf16[512,512]{1,0:T(8,128)(2,1)}, u32[]{:S(2)}) copy-start(bf16[512,512]{1,0:T(8,128)(2,1)} %get-tuple-element.64) | copy-start | bytes 1572868
  114.7 2.0 %collective-permute-start.12 = (bf16[512,512]{1,0:T(8,128)(2,1)S(1)}, bf16[512,512]{1,0:T(8,128)(2,1)S(1)}, u32[]{:S(2)}, u32[]{:S(2)}) collective-permute-start(bf16[512,512]{1,0:T(8,128)(2,1)S(1)} %get-tuple-element.57), channel_id=1, source_target_pairs={{0,1},{1,0},{2,3},{3,2},{4,5},{5,4},{6,7},{7,6},{8,9},{9,8},{10,11... | collective-permute-start | bytes 1572872 | tf_op jit(solution)/shard_map/ppermute | solution.py:38
  114.8 4.5 %collective-permute-start.16 = (bf16[512,512]{1,0:T(8,128)(2,1)S(1)}, bf16[512,512]{1,0:T(8,128)(2,1)S(1)}, u32[]{:S(2)}, u32[]{:S(2)}) collective-permute-start(bf16[512,512]{1,0:T(8,128)(2,1)S(1)} %get-tuple-element.66), channel_id=1, source_target_pairs={{0,1},{1,0},{2,3},{3,2},{4,5},{5,4},{6,7},{7,6},{8,9},{9,8},{10,11... | collective-permute-start | bytes 1572872 | tf_op jit(solution)/shard_map/ppermute | solution.py:38
  117.2 5.7 %copy-start.16 = (bf16[512,512]{1,0:T(8,128)(2,1)S(1)}, bf16[512,512]{1,0:T(8,128)(2,1)}, u32[]{:S(2)}) copy-start(bf16[512,512]{1,0:T(8,128)(2,1)} %get-tuple-element.63) | copy-start | bytes 1572868
  117.6 16.7 %collective-permute-start.13 = (bf16[512,512]{1,0:T(8,128)(2,1)S(1)}, bf16[512,512]{1,0:T(8,128)(2,1)S(1)}, u32[]{:S(2)}, u32[]{:S(2)}) collective-permute-start(bf16[512,512]{1,0:T(8,128)(2,1)S(1)} %fusion.12), channel_id=1, source_target_pairs={{0,2},{1,3},{2,4},{3,5},{4,6},{5,7},{6,0},{7,1},{8,10},{9,11},{10,... | collective-permute-start | bytes 1572872 | tf_op jit(solution)/shard_map/ppermute | solution.py:32
  120.2 14.1 %copy-start.21 = (bf16[512,512]{1,0:T(8,128)(2,1)S(1)}, bf16[512,512]{1,0:T(8,128)(2,1)}, u32[]{:S(2)}) copy-start(bf16[512,512]{1,0:T(8,128)(2,1)} %get-tuple-element.62) | copy-start | bytes 1572868
  120.2 25.2 %collective-permute-start.17 = (bf16[512,512]{1,0:T(8,128)(2,1)S(1)}, bf16[512,512]{1,0:T(8,128)(2,1)S(1)}, u32[]{:S(2)}, u32[]{:S(2)}) collective-permute-start(bf16[512,512]{1,0:T(8,128)(2,1)S(1)} %fusion.13), channel_id=1, source_target_pairs={{0,6},{1,7},{2,0},{3,1},{4,2},{5,3},{6,4},{7,5},{8,14},{9,15},{10,... | collective-permute-start | bytes 1572872 | tf_op jit(solution)/shard_map/ppermute | solution.py:32
  123.8 23.9 %copy-start.14 = (bf16[512,512]{1,0:T(8,128)(2,1)S(1)}, bf16[512,512]{1,0:T(8,128)(2,1)}, u32[]{:S(2)}) copy-start(bf16[512,512]{1,0:T(8,128)(2,1)} %get-tuple-element.59) | copy-start | bytes 1572868
  134.7 22.1 %collective-permute-start.14 = (bf16[512,512]{1,0:T(8,128)(2,1)S(1)}, bf16[512,512]{1,0:T(8,128)(2,1)S(1)}, u32[]{:S(2)}, u32[]{:S(2)}) collective-permute-start(bf16[512,512]{1,0:T(8,128)(2,1)S(1)} %fusion.8), channel_id=1, source_target_pairs={{0,2},{1,3},{2,4},{3,5},{4,6},{5,7},{6,0},{7,1},{8,10},{9,11},{10,... | collective-permute-start | bytes 1572872 | tf_op jit(solution)/shard_map/ppermute | solution.py:32
  145.9 22.1 %collective-permute-start.18 = (bf16[512,512]{1,0:T(8,128)(2,1)S(1)}, bf16[512,512]{1,0:T(8,128)(2,1)S(1)}, u32[]{:S(2)}, u32[]{:S(2)}) collective-permute-start(bf16[512,512]{1,0:T(8,128)(2,1)S(1)} %fusion.11), channel_id=1, source_target_pairs={{0,6},{1,7},{2,0},{3,1},{4,2},{5,3},{6,4},{7,5},{8,14},{9,15},{10,... | collective-permute-start | bytes 1572872 | tf_op jit(solution)/shard_map/ppermute | solution.py:32
  148.1 31.2 %copy-start.20 = (bf16[512,512]{1,0:T(8,128)(2,1)S(1)}, bf16[512,512]{1,0:T(8,128)(2,1)}, u32[]{:S(2)}) copy-start(bf16[512,512]{1,0:T(8,128)(2,1)} %get-tuple-element.58) | copy-start | bytes 1572868
  157.2 22.1 %collective-permute-start.15 = (bf16[512,512]{1,0:T(8,128)(2,1)S(1)}, bf16[512,512]{1,0:T(8,128)(2,1)S(1)}, u32[]{:S(2)}, u32[]{:S(2)}) collective-permute-start(bf16[512,512]{1,0:T(8,128)(2,1)S(1)} %fusion.7), channel_id=1, source_target_pairs={{0,2},{1,3},{2,4},{3,5},{4,6},{5,7},{6,0},{7,1},{8,10},{9,11},{10,... | collective-permute-start | bytes 1572872 | tf_op jit(solution)/shard_map/ppermute | solution.py:32
  168.4 21.3 %collective-permute-start.19 = (bf16[512,512]{1,0:T(8,128)(2,1)S(1)}, bf16[512,512]{1,0:T(8,128)(2,1)S(1)}, u32[]{:S(2)}, u32[]{:S(2)}) collective-permute-start(bf16[512,512]{1,0:T(8,128)(2,1)S(1)} %fusion.10), channel_id=1, source_target_pairs={{0,6},{1,7},{2,0},{3,1},{4,2},{5,3},{6,4},{7,5},{8,14},{9,15},{10,... | collective-permute-start | bytes 1572872 | tf_op jit(solution)/shard_map/ppermute | solution.py:32
  (11 other events, 41.2 us)
